TPU v7x, 128 devices: a whole 4x4x4 slice. The times are simulated.
128 devices in a mesh: depth: 8 (over x_lo, y), row: 4 (over x_hi, core), col: 4 (over z).
Axes of the slice: x: 4 (x_hi: 2, x_lo: 2; x = x_hi * 2 + x_lo), y: 4, z: 4, core: 2. Of those that a mesh axis runs over, the one named last changes fastest.
Arguments:
- grad_out: bfloat16 [2048, 12288], P(('depth', 'col'), 'row'), may hold values from -6 to 6
- pre_act: bfloat16 [2048, 24576], P('col', 'depth'), may hold values from -8 to 8
- w_down: bfloat16 [24576, 12288], P(('depth', 'col'), 'row'), may hold values from -0.0546875 to 0.0546875
Outputs:
- grad_pre: bfloat16 [2048, 24576], P('row', ('depth', 'col'))
- grad_down: bfloat16 [24576, 12288], P(('depth', 'col'), 'row')
All inputs are finite; a program needn't handle non-finite values.
Results may differ from a plain program's by a relative error of at most 0.0048.
Values may be sent and summed in bfloat16 or wider, within the bound.
No kernel may reach another device: no remote copies, remote signals or barrier semaphores. Data moves between devices by JAX's collectives and lax.ppermute only.
A program may use at most 128 MiB of HBM per device.

v0:
```python
import math

import jax
import jax.numpy as jnp
from jax import lax
from jax.sharding import PartitionSpec as P

gelu_const = math.sqrt(2.0 / math.pi)


def gelu_parts(pre):
    inner = gelu_const * (pre + 0.044715 * pre * pre * pre)
    bend = jnp.tanh(inner)
    value = 0.5 * pre * (1.0 + bend)
    derivative = 0.5 * (1.0 + bend) + 0.5 * pre * (1.0 - bend * bend) * gelu_const * (
        1.0 + 3.0 * 0.044715 * pre * pre
    )
    return (value, derivative)


def local(grad_out, pre_act, w_down):
    pre_all = lax.all_to_all(pre_act, "col", split_axis=1, concat_axis=0, tiled=True)
    value, derivative = gelu_parts(pre_all.astype(jnp.float32))
    activated = value.astype(jnp.bfloat16)
    share_rows = pre_all.shape[0] // lax.axis_size("row")
    first_row = lax.axis_index("row") * share_rows
    slope_mine = lax.dynamic_slice_in_dim(derivative, first_row, share_rows, 0)
    gathered = lax.all_gather(grad_out, ("depth", "col"), axis=0, tiled=True)
    weight_sum = lax.dot_general(
        activated, gathered, (((0,), (0,)), ((), ())), preferred_element_type=jnp.float32
    )
    hidden_grad = lax.psum_scatter(
        lax.dot_general(
            gathered, w_down, (((1,), (1,)), ((), ())), preferred_element_type=jnp.float32
        ),
        "row",
        scatter_dimension=0,
        tiled=True,
    )
    grad_pre = (hidden_grad * slope_mine).astype(jnp.bfloat16)
    return (grad_pre, weight_sum.astype(jnp.bfloat16))


def solution(mesh):
    placed = (P(("depth", "col"), "row"), P("col", "depth"), P(("depth", "col"), "row"))
    return jax.shard_map(
        local,
        mesh=mesh,
        in_specs=placed,
        out_specs=(P("row", ("depth", "col")), P(("depth", "col"), "row")),
        check_vma=False,
    )
```

profile of v0, /device:TPU:1, one launch (start us, length us, event | category | flops | bytes accessed | tf_op | source)
XLA Modules:
  0.0 280.4 jit_solution(2442440417147552971)
XLA Ops:
  7.2 0.0 all-gather.2.cloned.1.call-start
  7.2 0.7 all-gather.2.cloned.1.call-update
  7.9 0.0 reduce-scatter.2.cloned.1.call-start
  7.9 164.6 %all-gather.2.cloned.1.call-done = bf16[2048,3072]{1,0:T(8,128)(2,1)} async-done(((bf16[64,3072]{1,0:T(8,128)(2,1)}), bf16[2048,3072]{1,0:T(8,128)(2,1)}) %all-gather.2.cloned.1.call-update) | async-done | bytes 12582928 | tf_op jit(solution)/shard_map/all_gather | solution.py:28
  172.6 15.9 %fusion.9 = f32[2048,768]{1,0:T(8,128)} fusion(bf16[2048,3072]{1,0:T(8,128)(2,1)} %all-gather.2.cloned.1.call-done, bf16[768,3072]{1,0:T(8,128)(2,1)} %param.5), kind=kOutput, calls=%fused_computation.19 | convolution fusion | flops 9663676416 | bytes 23592960 | tf_op jit(solution)/shard_map/dot_general | solution.py:33
  188.5 0.0 copy-start.2
  188.5 0.0 reduce-scatter.2.cloned.1.call-update
  188.5 1.9 copy-done.2
  190.4 1.9 copy.8
  192.3 3.7 %all-to-all-start = ((bf16[512,4,768]{2,0,1:T(8,128)(2,1)}), bf16[512,4,768]{2,0,1:T(8,128)(2,1)S(1)}, u32[]{:S(2)}, u32[]{:S(2)}) async-start(bf16[512,4,768]{2,0,1:T(8,128)(2,1)} %bitcast.14), calls=%async_computation.1 | async-start | bytes 6291456 | tf_op jit(solution)/shard_map/all_to_all | solution.py:22
  196.0 20.9 %all-to-all-done = bf16[512,4,768]{2,0,1:T(8,128)(2,1)S(1)} async-done(((bf16[512,4,768]{2,0,1:T(8,128)(2,1)}), bf16[512,4,768]{2,0,1:T(8,128)(2,1)S(1)}, u32[]{:S(2)}, u32[]{:S(2)}) %all-to-all-start) | async-done | bytes 3145760 | tf_op jit(solution)/shard_map/all_to_all | solution.py:22
  216.9 3.3 %convert_element_type.25 = f32[512,4,768]{2,0,1:T(8,128)} convert(bf16[512,4,768]{2,0,1:T(8,128)(2,1)S(1)} %all-to-all-done) | non-fusion elementwise | flops 1572864 | bytes 9437184 | tf_op jit(solution)/shard_map/convert_element_type | solution.py:23
  220.2 3.5 %fusion.1 = (f32[2048,768]{1,0:T(8,128)S(1)}, f32[2048,768]{1,0:T(8,128)}, f32[2048,768]{1,0:T(8,128)S(1)}) fusion(bf16[512,4,768]{2,0,1:T(8,128)(2,1)S(1)} %all-to-all-done), kind=kLoop, calls=%fused_computation.2 | loop fusion | flops 12582912 | bytes 22020096 | tf_op jit(solution)/shard_map/tanh | solution.py:13
  223.7 0.0 copy-start
  223.7 0.0 copy-start.1
  223.7 2.6 copy-done
  226.3 1.9 copy-done.1
  228.3 15.8 %convolution_convert_fusion = bf16[768,3072]{1,0:T(8,128)(2,1)} fusion(bf16[2048,3072]{1,0:T(8,128)(2,1)} %all-gather.2.cloned.1.call-done, f32[2048,768]{1,0:T(8,128)S(1)} %get-tuple-element.4, f32[2048,768]{1,0:T(8,128)S(1)} %get-tuple-element.2), kind=kOutput, calls=%fused_computation.4 | convolution fusion | flops 9670754304 | bytes 29884416 | tf_op jit(solution)/shard_map/dot_general | solution.py:29
  244.1 24.7 %reduce-scatter.2.cloned.1.call-done = f32[512,768]{1,0:T(8,128)} async-done(((f32[2048,768]{1,0:T(8,128)}), f32[512,768]{1,0:T(8,128)}) %reduce-scatter.2.cloned.1.call-update) | async-done | bytes 1572880 | tf_op jit(solution)/shard_map/reduce_scatter | solution.py:32
  268.8 4.8 %fusion.6 = bf16[512,768]{1,0:T(8,128)(2,1)} fusion(f32[512,768]{1,0:T(8,128)} %reduce-scatter.2.cloned.1.call-done, f32[2048,768]{1,0:T(8,128)} %get-tuple-element.3, s32[]{:T(128)S(6)} %select_n.3, f32[2048,768]{1,0:T(8,128)} %copy-done.1, f32[2048,768]{1,0:T(8,128)} %bitcast.15, f32[2048,768]{1,0:T(8,128)} %copy-done), kind=kLoop, calls=%fused_computation.13 | loop fusion | flops 4718592 | bytes 8650756 | tf_op jit(solution)/shard_map/convert_element_type | solution.py:40
Async XLA Ops:
  7.2 165.4 %all-gather.2.cloned.1.call-start = ((), (), s32[]{:S(2)}) async-start(), calls=%async_computation.2 | async-start | bytes 12976128 | tf_op jit(solution)/shard_map/all_gather | solution.py:28
  7.9 260.9 %reduce-scatter.2.cloned.1.call-start = ((), (), s32[]{:S(2)}) async-start(), calls=%async_computation.3 | async-start | bytes 7864320 | tf_op jit(solution)/shard_map/reduce_scatter | solution.py:32
  188.5 1.9 copy-start.2
  192.3 24.7 %all-to-all-start = ((bf16[512,4,768]{2,0,1:T(8,128)(2,1)}), bf16[512,4,768]{2,0,1:T(8,128)(2,1)S(1)}, u32[]{:S(2)}, u32[]{:S(2)}) async-start(bf16[512,4,768]{2,0,1:T(8,128)(2,1)} %bitcast.14), calls=%async_computation.1 | async-start | bytes 6291456 | tf_op jit(solution)/shard_map/all_to_all | solution.py:22
  223.7 2.6 copy-start
  223.7 4.6 %copy-start.1 = (f32[2048,768]{1,0:T(8,128)}, f32[2048,768]{1,0:T(8,128)S(1)}, u32[]{:S(2)}) copy-start(f32[2048,768]{1,0:T(8,128)S(1)} %get-tuple-element.4) | copy-start | bytes 18874372
Sparse Core Ops, SparseCore 0:
  9.6 162.8 all-gather.1
  188.6 80.0 reduce-scatter.1
where the time goes:
time: 281 us; the launch traced here: 280 us
  waiting for transfers between devices  211 us (75%)
  matrix products  31.8 us (11%)
  between operations  14.1 us (5%)
  other arithmetic  11.5 us (4%)
  local copies, waits for them, and re-layouts  8.31 us (3%)
  starting transfers between devices  3.78 us (1%)
    all_gather x1, waiting for transfers between devices, local(): gathered = lax.all_gather(grad_out, ('depth', 'col'), axis=0, tiled=True)  165 us
    reduce_scatter x1, waiting for transfers between devices, local(): lax.psum_scatter(lax.dot_general(gathered, w_down, (((1,), (1,)), ((), ()...  24.7 us
    all_to_all x1, waiting for transfers between devices, local(): lax.all_to_all(pre_act, 'col', split_axis=1, concat_axis=0, tiled=True)  20.9 us
    dot_general x1, matrix products, local(): lax.dot_general(gathered, w_down, (((1,), (1,)), ((), ())), preferred_ele...  15.9 us
    dot_general x1, matrix products, local(): lax.dot_general(activated, gathered, (((0,), (0,)), ((), ())), preferred_...  15.8 us
    unnamed x6, local copies, waits for them, and re-layouts  6.44 us
  transfers between devices with their start and end apart: 3, of which 3 were waited for; matrix products, arithmetic and copies ran while one was open for 9% of the time, Pallas kernels for 0%

commit v1 on v0

v1 whole, which is shorter than its diff:
```python
import functools
import math

import jax
import jax.numpy as jnp
import numpy as np
from jax import lax
from jax.experimental import pallas as pl
from jax.experimental.pallas import tpu as pltpu
from jax.sharding import PartitionSpec as P

gelu_const = math.sqrt(2.0 / math.pi)

SHARDS = 32
ROWS = 64
FEATS = 3072
HID = 768
X, Y0, Y1, Z0, Z1 = 16, 4, 12, 1, 3
DIMS = (X, Y0, Z0, Y1, Z1)
WIDTHS = (640, 512, 640, 640, 640)
OFFSETS = tuple(int(v) for v in np.cumsum((0,) + WIDTHS)[:-1])
CHAINS = len(WIDTHS)
ORDERS = tuple(tuple(DIMS[(p + k) % 5] for k in range(5)) for p in range(CHAINS))
PARTS = (48, 16)
STARTS = (0, 48)


def place_table():
    table = np.zeros((CHAINS, SHARDS), np.int32)
    for p, order in enumerate(ORDERS):
        for i in range(SHARDS):
            delta = 0
            for k, mask in enumerate(order):
                if i >> k & 1:
                    delta ^= mask
            table[p, delta] = i
    return table.reshape(-1)


def swap(x, mask):
    if mask >= 4:
        return lax.ppermute(x, "depth", [(i, i ^ (mask >> 2)) for i in range(8)])
    return lax.ppermute(x, "col", [(i, i ^ mask) for i in range(4)])


def swap_row(x, mask):
    return lax.ppermute(x, "row", [(i, i ^ mask) for i in range(4)])


def params(mib):
    return pltpu.CompilerParams(vmem_limit_bytes=mib * 1024 * 1024)


ANY = pl.BlockSpec(memory_space=pl.ANY)
VMEM = pl.BlockSpec(memory_space=pltpu.VMEM)
SMEM = pl.BlockSpec(memory_space=pltpu.SMEM)


def gelu_kernel(where, pre, got_a, got_b, got_c, other, *refs):
    outs, (buf, sems), acts = refs[:4], refs[4:6], refs[6:]
    act_t, slopes = outs[:2], outs[2:]
    row, col = where[0], where[1]
    core = row % 2
    quarter, half = SHARDS * ROWS // 4, SHARDS * ROWS // 8
    copies = [
        pltpu.make_async_copy(
            pre.at[:, pl.ds(pl.multiple_of(col * HID, HID), HID)],
            buf.at[pl.ds(pl.multiple_of(col * quarter, quarter), quarter)],
            sems.at[0],
        )
    ]
    for j, (got, mask) in enumerate(((got_a, Z0), (got_b, Z1), (got_c, Z0 ^ Z1))):
        base = (col ^ mask) * quarter
        copies.append(
            pltpu.make_async_copy(
                got, buf.at[pl.ds(pl.multiple_of(base + core * half, half), half)], sems.at[1 + 2 * j]
            )
        )
        copies.append(
            pltpu.make_async_copy(
                other.at[pl.ds(j * half, half)],
                buf.at[pl.ds(pl.multiple_of(base + (1 - core) * half, half), half)],
                sems.at[2 + 2 * j],
            )
        )
    for c in copies:
        c.start()
    for c in copies:
        c.wait()

    def one_shard(s, carry):
        v = buf[pl.ds(pl.multiple_of(s * ROWS, ROWS), ROWS), :].astype(jnp.float32)
        bend = jnp.tanh(gelu_const * (v + 0.044715 * v * v * v))
        a = (0.5 * v * (1.0 + bend)).astype(jnp.bfloat16)
        for part in range(2):
            n, at = PARTS[part], STARTS[part]
            acts[part][pl.ds(pl.multiple_of(s * n, 16), n), :] = a[at : at + n]
        return carry

    lax.fori_loop(0, SHARDS, one_shard, 0)

    def one_slope(s, carry):
        at_row = pl.multiple_of(row * quarter + s * ROWS, ROWS)
        v = buf[pl.ds(at_row, ROWS), :].astype(jnp.float32)
        bend = jnp.tanh(gelu_const * (v + 0.044715 * v * v * v))
        d = 0.5 * (1.0 + bend) + 0.5 * v * (1.0 - bend * bend) * gelu_const * (1.0 + 3.0 * 0.044715 * v * v)
        for part in range(2):
            n, at = PARTS[part], STARTS[part]
            slopes[part][s] = d[at : at + n]
        return carry

    lax.fori_loop(0, SHARDS // 4, one_slope, 0)

    for part in range(2):

        def one_turn(j, carry, part=part):
            at = pl.multiple_of(j * 128, 128)
            act_t[part][:, pl.ds(at, 128)] = acts[part][pl.ds(at, 128), :].T
            return carry

        lax.fori_loop(0, SHARDS * PARTS[part] // 128, one_turn, 0)


def gelu_call(where, pre, got, other):
    tokens = [SHARDS * n for n in PARTS]
    return pl.pallas_call(
        gelu_kernel,
        out_shape=[jax.ShapeDtypeStruct((HID, t), jnp.bfloat16) for t in tokens]
        + [jax.ShapeDtypeStruct((SHARDS // 4, n, HID), jnp.float32) for n in PARTS],
        in_specs=[SMEM] + [ANY] * 5,
        out_specs=[VMEM] * 4,
        scratch_shapes=[pltpu.VMEM((SHARDS * ROWS, HID), jnp.bfloat16), pltpu.SemaphoreType.DMA((7,))]
        + [pltpu.VMEM((t, HID), jnp.bfloat16) for t in tokens],
        compiler_params=params(32),
        cost_estimate=pl.CostEstimate(flops=2048 * HID * 40, bytes_accessed=16 << 20, transcendentals=2048 * HID),
        name="gelu",
    )(where, pre, *got, other)


def hidden_kernel(n, where, table, w, *refs):
    blocks = refs[: 2 * CHAINS]
    keep, send, gathered, g, in_sems, out_sems = refs[2 * CHAINS :]
    row, mine = where[0], where[2]
    per = SHARDS // 4
    order = [(1, 1), (0, 1), (1, 0), (0, 0)]
    quarters = [row ^ (2 * a + b) for a, b in order]

    for t, q in enumerate(quarters):

        def fetch(k, carry, t=t, q=q):
            s = q * per + k
            for p in range(CHAINS):
                i = table[p * SHARDS + (s ^ mine)]
                for side in range(2):

                    @pl.when(i // 16 == side)
                    def _(p=p, side=side, i=i):
                        pltpu.make_async_copy(
                            blocks[2 * p + side].at[i % 16],
                            g.at[s, :, pl.ds(OFFSETS[p], WIDTHS[p])],
                            in_sems.at[t],
                        ).start()

            return carry

        lax.fori_loop(0, per, fetch, 0)

    outs = []
    for t, q in enumerate(quarters):
        a, b = order[t]
        here = g.at[pl.ds(pl.multiple_of(q * per, per), per)]
        pltpu.make_async_copy(here, here, in_sems.at[t]).wait()
        out = pltpu.make_async_copy(here, gathered.at[pl.ds(pl.multiple_of(q * per, per), per)], out_sems.at[t])
        out.start()
        outs.append(out)
        lhs = here[...].reshape(per * n, FEATS)
        h = lax.dot_general(lhs, w[...], (((1,), (1,)), ((), ())), preferred_element_type=jnp.float32)
        if b:
            send[a] = h.astype(jnp.bfloat16).reshape(per, n, HID)
        else:
            keep[a] = h.reshape(per, n, HID)
    for out in outs:
        out.wait()


def hidden_call(part, where, table, w, blocks):
    n = PARTS[part]
    per = SHARDS // 4
    return pl.pallas_call(
        functools.partial(hidden_kernel, n),
        out_shape=[
            jax.ShapeDtypeStruct((2, per, n, HID), jnp.float32),
            jax.ShapeDtypeStruct((2, per, n, HID), jnp.bfloat16),
            jax.ShapeDtypeStruct((SHARDS, n, FEATS), jnp.bfloat16),
        ],
        in_specs=[SMEM, SMEM, VMEM] + [ANY] * (2 * CHAINS),
        out_specs=[VMEM, VMEM, ANY],
        scratch_shapes=[
            pltpu.VMEM((SHARDS, n, FEATS), jnp.bfloat16),
            pltpu.SemaphoreType.DMA((4,)),
            pltpu.SemaphoreType.DMA((4,)),
        ],
        compiler_params=params(40),
        cost_estimate=pl.CostEstimate(
            flops=2 * SHARDS * n * FEATS * HID, bytes_accessed=SHARDS * n * FEATS * 4, transcendentals=0
        ),
        name="hidden",
    )(where, table, w, *blocks)


def down_kernel(at_a, at_b, g_a, g_b, *refs):
    out = refs[-1]
    acc = jnp.dot(at_a[...], g_a[...], preferred_element_type=jnp.float32)
    acc += jnp.dot(at_b[...], g_b[...], preferred_element_type=jnp.float32)
    out[...] = acc.astype(jnp.bfloat16)


def down_call(acts, gathered, first, count, base=None):
    wide = 512
    tokens = [SHARDS * n for n in PARTS]
    in_specs = [pl.BlockSpec((HID, t), lambda j: (0, 0)) for t in tokens]
    in_specs += [pl.BlockSpec((t, wide), lambda j: (0, j + first)) for t in tokens]
    args = [*acts, *(g.reshape(t, FEATS) for g, t in zip(gathered, tokens))]
    aliases = {}
    if base is not None:
        in_specs.append(ANY)
        args.append(base)
        aliases = {4: 0}
    return pl.pallas_call(
        down_kernel,
        grid=(count,),
        out_shape=jax.ShapeDtypeStruct((HID, FEATS), jnp.bfloat16),
        in_specs=in_specs,
        out_specs=pl.BlockSpec((HID, wide), lambda j: (0, j + first)),
        input_output_aliases=aliases,
        compiler_params=params(40),
        cost_estimate=pl.CostEstimate(
            flops=2 * 2048 * HID * wide * count, bytes_accessed=count * wide * 2 * (2048 + HID), transcendentals=0
        ),
        name="down",
    )(*args)


def local(grad_out, pre_act, w_down):
    depth, row, col = (lax.axis_index(a) for a in ("depth", "row", "col"))
    where = jnp.stack([row, col, depth * 4 + col]).astype(jnp.int32)
    table = jnp.asarray(place_table())
    core = row % 2

    blocks = []
    for p in range(CHAINS):
        blocks.append(grad_out[:, OFFSETS[p] : OFFSETS[p] + WIDTHS[p]].reshape(1, ROWS, WIDTHS[p]))
    for k in range(3):
        got = [swap(blocks[p], ORDERS[p][k]) for p in range(CHAINS)]
        blocks = [jnp.concatenate([b, r], 0) for b, r in zip(blocks, got)]
    got = [swap(blocks[p], ORDERS[p][3]) for p in range(CHAINS)]
    own, came = ([], []), ([], [])
    for part in range(2):
        rows = slice(STARTS[part], STARTS[part] + PARTS[part])
        for p in range(CHAINS):
            own[part].append(jnp.concatenate([blocks[p][:, rows], got[p][:, rows]], 0))
    for part in range(2):
        for p in range(CHAINS):
            came[part].append(swap(own[part][p], ORDERS[p][4]))

    half = pre_act.shape[0] // 2
    fetched = []
    for mask in (Z0, Z1, Z0 ^ Z1):
        chunk = lax.dynamic_slice(pre_act, (core * half, (col ^ mask) * HID), (half, HID))
        fetched.append(swap(chunk, mask))
    other = swap_row(jnp.concatenate(fetched, 0), 1)
    act_a, act_b, slope_a, slope_b = gelu_call(where, pre_act, fetched, other)

    done, gathered = [], []
    for part in range(2):
        pairs = [b for p in range(CHAINS) for b in (own[part][p], came[part][p])]
        keep, send, g = hidden_call(part, where, table, w_down, pairs)
        gathered.append(g)
        total = keep + swap_row(send, 1).astype(jnp.float32)
        far = swap_row(total[1].astype(jnp.bfloat16), 2)
        done.append((total[0], far))
    grad_down = down_call((act_a, act_b), gathered, 0, 2)
    grad_down = down_call((act_a, act_b), gathered, 2, 4, grad_down)
    parts = [
        ((mine + far.astype(jnp.float32)) * slope).astype(jnp.bfloat16)
        for (mine, far), slope in zip(done, (slope_a, slope_b))
    ]
    grad_pre = jnp.concatenate(parts, 1).reshape(512, HID)
    return (grad_pre, grad_down)


def solution(mesh):
    placed = (P(("depth", "col"), "row"), P("col", "depth"), P(("depth", "col"), "row"))
    return jax.shard_map(
        local,
        mesh=mesh,
        in_specs=placed,
        out_specs=(P("row", ("depth", "col")), P(("depth", "col"), "row")),
        check_vma=False,
    )
```

time: 281 us -> 173 us (0.62)
  waiting for transfers between devices: 211 us -> 30.5 us
  Pallas kernels: 0 us -> 51.4 us
  starting transfers between devices: 3.78 us -> 49.5 us
  matrix products: 31.8 us -> 0 us
  local copies, waits for them, and re-layouts: 8.31 us -> 25.3 us
  between operations: 14.1 us -> 1.25 us
    all_gather x1 -> x0, waiting for transfers between devices: 165 us -> none  [local(): gathered = lax.all_gather(grad_out, ('depth', 'col'), axis=0, tiled=True)]
    pallas_call x0 -> x5, Pallas kernels: none -> 51.4 us  [the longest x2 28.9 us: hidden_call(): pl.pallas_call(functools.partial(hidden_kernel, n), out_shape=[jax.ShapeD...]
    ppermute x0 -> x38, starting transfers between devices: none -> 49.5 us  [the longest x18 18.3 us: swap(): return lax.ppermute(x, 'depth', [(i, i ^ mask >> 2) for i in range(8)])]
    dot_general x2 -> x0, matrix products: 31.8 us -> none  [the longest x1 15.9 us: local(): lax.dot_general(gathered, w_down, (((1,), (1,)), ((), ())), preferred_ele...]
    ppermute x0 -> x38, waiting for transfers between devices: none -> 30.5 us  [the longest x15 16.1 us: swap(): return lax.ppermute(x, 'col', [(i, i ^ mask) for i in range(4)])]
    reduce_scatter x1 -> x0, waiting for transfers between devices: 24.7 us -> none  [local(): lax.psum_scatter(lax.dot_general(gathered, w_down, (((1,), (1,)), ((), ()...]
    all_to_all x1 -> x0, waiting for transfers between devices: 20.9 us -> none  [local(): lax.all_to_all(pre_act, 'col', split_axis=1, concat_axis=0, tiled=True)]
    slice x0 -> x20, local copies, waits for them, and re-layouts: none -> 16.1 us  [local(): own[part].append(jnp.concatenate([blocks[p][:, rows], got[p][:, rows]], 0))]
  transfers between devices with their start and end apart: 3 -> 38, of which waited for: 3 -> 8; matrix products, arithmetic and copies ran while one was open for 9% -> 17% of each run, Pallas kernels for 0% -> 30%
where the time goes in v1:
time: 173 us; the launch traced here: 172 us
  Pallas kernels  51.4 us (30%)
  starting transfers between devices  49.5 us (29%)
  waiting for transfers between devices  30.5 us (18%)
  local copies, waits for them, and re-layouts  25.3 us (15%)
  other arithmetic  14.2 us (8%)
    pallas_call x2, Pallas kernels, hidden_call(): pl.pallas_call(functools.partial(hidden_kernel, n), out_shape=[jax.ShapeD...  28.9 us
    ppermute x18, starting transfers between devices, swap(): return lax.ppermute(x, 'depth', [(i, i ^ mask >> 2) for i in range(8)])  18.3 us
    ppermute x15, starting transfers between devices, swap(): return lax.ppermute(x, 'col', [(i, i ^ mask) for i in range(4)])  17 us
    slice x20, local copies, waits for them, and re-layouts, local(): own[part].append(jnp.concatenate([blocks[p][:, rows], got[p][:, rows]], 0))  16.1 us
    ppermute x15, waiting for transfers between devices, swap(): return lax.ppermute(x, 'col', [(i, i ^ mask) for i in range(4)])  16.1 us
    pallas_call x2, Pallas kernels, down_call(): pl.pallas_call(down_kernel, grid=(count,), out_shape=jax.ShapeDtypeStruct...  15.4 us
    ppermute x5, starting transfers between devices, swap_row(): return lax.ppermute(x, 'row', [(i, i ^ mask) for i in range(4)])  14.3 us
    ppermute x18, waiting for transfers between devices, swap(): return lax.ppermute(x, 'depth', [(i, i ^ mask >> 2) for i in range(8)])  8.71 us
  transfers between devices with their start and end apart: 38, of which 8 were waited for; matrix products, arithmetic and copies ran while one was open for 17% of the time, Pallas kernels for 30%

profile of v1, /device:TPU:1, one launch (start us, length us, event | category | flops | bytes accessed | tf_op | source)
XLA Modules:
  0.0 172.1 jit_solution(12827585471311987726)
XLA Ops:
  1.5 2.1 %collective-permute-start.5 = (bf16[1,64,512]{2,1,0:T(8,128)(2,1)S(1)}, bf16[1,64,512]{2,1,0:T(8,128)(2,1)S(1)}, u32[]{:S(2)}, u32[]{:S(2)}) collective-permute-start(bf16[1,64,512]{2,1,0:T(8,128)(2,1)S(1)} %slice_bitcast_fusion.6), channel_id=1, source_target_pairs={{0,16},{16,0},{32,48},{48,32},{64,80},{80,64},{96,112},{112,96},{1... | collective-permute-start | bytes 196616 | tf_op jit(solution)/shard_map/ppermute | solution.py:42
  4.7 3.8 %collective-permute-start.20 = (bf16[1,64,640]{2,1,0:T(8,128)(2,1)S(1)}, bf16[1,64,640]{2,1,0:T(8,128)(2,1)S(1)}, u32[]{:S(2)}, u32[]{:S(2)}) collective-permute-start(bf16[1,64,640]{2,1,0:T(8,128)(2,1)S(1)} %get-tuple-element.25), channel_id=1, source_target_pairs={{0,3},{1,2},{2,1},{3,0},{4,7},{5,6},{6,5},{7,4},{8,11},{9,10},{10,... | collective-permute-start | bytes 245768 | tf_op jit(solution)/shard_map/ppermute | solution.py:43
  9.7 1.9 %collective-permute-start.15 = (bf16[1,64,640]{2,1,0:T(8,128)(2,1)S(1)}, bf16[1,64,640]{2,1,0:T(8,128)(2,1)S(1)}, u32[]{:S(2)}, u32[]{:S(2)}) collective-permute-start(bf16[1,64,640]{2,1,0:T(8,128)(2,1)S(1)} %get-tuple-element.28), channel_id=1, source_target_pairs={{0,48},{16,32},{32,16},{48,0},{64,112},{80,96},{96,80},{112,64},{1... | collective-permute-start | bytes 245768 | tf_op jit(solution)/shard_map/ppermute | solution.py:42
  11.6 1.5 collective-permute-start.6
  14.4 2.0 %collective-permute-start.16 = (bf16[2,64,640]{2,1,0:T(8,128)(2,1)S(1)}, bf16[2,64,640]{2,1,0:T(8,128)(2,1)S(1)}, u32[]{:S(2)}, u32[]{:S(2)}) collective-permute-start(bf16[2,64,640]{2,1,0:T(8,128)(2,1)S(1)} %pad_maximum_fusion.24), channel_id=1, source_target_pairs={{0,3},{1,2},{2,1},{3,0},{4,7},{5,6},{6,5},{7,4},{8,11},{9,10},{10,... | collective-permute-start | bytes 491528 | tf_op jit(solution)/shard_map/ppermute | solution.py:43
  17.7 2.2 %collective-permute-done.16 = bf16[2,64,640]{2,1,0:T(8,128)(2,1)S(1)} collective-permute-done((bf16[2,64,640]{2,1,0:T(8,128)(2,1)S(1)}, bf16[2,64,640]{2,1,0:T(8,128)(2,1)S(1)}, u32[]{:S(2)}, u32[]{:S(2)}) %collective-permute-start.16) | collective-permute-done | bytes 163872 | tf_op jit(solution)/shard_map/ppermute | solution.py:43
  22.8 3.0 %collective-permute-done.7 = bf16[4,64,512]{2,1,0:T(8,128)(2,1)S(1)} collective-permute-done((bf16[4,64,512]{2,1,0:T(8,128)(2,1)S(1)}, bf16[4,64,512]{2,1,0:T(8,128)(2,1)S(1)}, u32[]{:S(2)}, u32[]{:S(2)}) %collective-permute-start.7) | collective-permute-done | bytes 262176 | tf_op jit(solution)/shard_map/ppermute | solution.py:42
  28.5 2.2 %collective-permute-start.3 = (bf16[8,64,640]{2,1,0:T(8,128)(2,1)}, bf16[8,64,640]{2,1,0:T(8,128)(2,1)}, u32[]{:S(2)}, u32[]{:S(2)}) collective-permute-start(bf16[8,64,640]{2,1,0:T(8,128)(2,1)} %pad_maximum_fusion.7), channel_id=1, source_target_pairs={{0,48},{16,32},{32,16},{48,0},{64,112},{80,96},{96,80},{112,64},{1... | collective-permute-start | bytes 1966088 | tf_op jit(solution)/shard_map/ppermute | solution.py:42
  41.0 5.7 %collective-permute-done.22 = bf16[4,64,640]{2,1,0:T(8,128)(2,1)S(1)} collective-permute-done((bf16[4,64,640]{2,1,0:T(8,128)(2,1)}, bf16[4,64,640]{2,1,0:T(8,128)(2,1)S(1)}, u32[]{:S(2)}, u32[]{:S(2)}) %collective-permute-start.22) | collective-permute-done | bytes 327712 | tf_op jit(solution)/shard_map/ppermute | solution.py:42
  50.1 2.6 %collective-permute-start.23 = (bf16[8,64,640]{2,1,0:T(8,128)(2,1)S(1)}, bf16[8,64,640]{2,1,0:T(8,128)(2,1)S(1)}, u32[]{:S(2)}, u32[]{:S(2)}) collective-permute-start(bf16[8,64,640]{2,1,0:T(8,128)(2,1)S(1)} %pad_maximum_fusion.10), channel_id=1, source_target_pairs={{0,1},{1,0},{2,3},{3,2},{4,5},{5,4},{6,7},{7,6},{8,9},{9,8},{10,11... | collective-permute-start | bytes 1966088 | tf_op jit(solution)/shard_map/ppermute | solution.py:43
  64.7 2.8 %collective-permute-done.28.got_b = bf16[256,768]{1,0:T(8,128)(2,1)S(1)} collective-permute-done((bf16[256,768]{1,0:T(8,128)(2,1)S(1)}, bf16[256,768]{1,0:T(8,128)(2,1)S(1)}, u32[]{:S(2)}, u32[]{:S(2)}) %collective-permute-start.28) | collective-permute-done | bytes 393248 | tf_op jit(solution)/shard_map/ppermute | solution.py:43
  67.5 2.2 %collective-permute-start.31 = (bf16[16,16,640]{2,1,0:T(8,128)(2,1)S(1)}, bf16[16,16,640]{2,1,0:T(8,128)(2,1)S(1)}, u32[]{:S(2)}, u32[]{:S(2)}) collective-permute-start(bf16[16,16,640]{2,1,0:T(8,128)(2,1)S(1)} %pad_maximum_fusion.16.refs_0_), channel_id=1, source_target_pairs={{0,3},{1,2},{2,1},{3,0},{4,7},{5,6},{6,5},{7,4},{8,11},{9,10},{10,... | collective-permute-start | bytes 983048 | tf_op jit(solution)/shard_map/ppermute | solution.py:43
  71.5 7.2 %collective-permute-done.27.got_a = bf16[256,768]{1,0:T(8,128)(2,1)S(1)} collective-permute-done((bf16[256,768]{1,0:T(8,128)(2,1)S(1)}, bf16[256,768]{1,0:T(8,128)(2,1)S(1)}, u32[]{:S(2)}, u32[]{:S(2)}) %collective-permute-start.27) | collective-permute-done | bytes 393248 | tf_op jit(solution)/shard_map/ppermute | solution.py:43
  82.6 3.1 %collective-permute-done.34.refs_7_ = bf16[16,16,640]{2,1,0:T(8,128)(2,1)S(1)} collective-permute-done((bf16[16,16,640]{2,1,0:T(8,128)(2,1)S(1)}, bf16[16,16,640]{2,1,0:T(8,128)(2,1)S(1)}, u32[]{:S(2)}, u32[]{:S(2)}) %collective-permute-start.34) | collective-permute-done | bytes 327712 | tf_op jit(solution)/shard_map/ppermute | solution.py:43
  90.2 1.8 %collective-permute-start.9 = (bf16[16,48,512]{2,1,0:T(8,128)(2,1)}, bf16[16,48,512]{2,1,0:T(8,128)(2,1)}, u32[]{:S(2)}, u32[]{:S(2)}) collective-permute-start(bf16[16,48,512]{2,1,0:T(8,128)(2,1)} %pad_maximum_fusion.5.refs_2_), channel_id=1, source_target_pairs={{0,64},{16,80},{32,96},{48,112},{64,0},{80,16},{96,32},{112,48},{1... | collective-permute-start | bytes 2359304 | tf_op jit(solution)/shard_map/ppermute | solution.py:42
  93.8 2.3 %copy-done.15 = bf16[768,3072]{1,0:T(8,128)(2,1)S(1)} copy-done((bf16[768,3072]{1,0:T(8,128)(2,1)S(1)}, bf16[768,3072]{1,0:T(8,128)(2,1)}, u32[]{:S(2)}) %copy-start.15) | copy-done | bytes 4718616
  99.0 14.2 %hidden.3 = (f32[2,8,16,768]{3,2,1,0:T(8,128)S(1)}, bf16[2,8,16,768]{3,2,1,0:T(8,128)(2,1)S(1)}, bf16[32,16,3072]{2,1,0:T(8,128)(2,1)S(1)}) custom-call(s32[3]{0:T(128)S(1)} %pad_add_fusion.where, s32[160]{0:T(256)S(1)} %copy-done.26, bf16[768,3072]{1,0:T(8,128)(2,1)S(1)} %copy-done.15, bf16[16,16,640]{2,1,0:T(8,128)(2,1)S(1)} %copy-done.8, ...), custom_call_target="tpu_custom_call" | custom-call | flops 2415919104 | bytes 6291456 | tf_op jit(solution)/shard_map/hidden/pallas_call | solution.py:189
  113.3 9.3 %collective-permute-start.30 = (bf16[768,768]{1,0:T(8,128)(2,1)S(1)}, bf16[768,768]{1,0:T(8,128)(2,1)S(1)}, u32[]{:S(2)}, u32[]{:S(2)}) collective-permute-start(bf16[768,768]{1,0:T(8,128)(2,1)S(1)} %pad_maximum_fusion), channel_id=1, source_target_pairs={{0,4},{4,0},{8,12},{12,8},{1,5},{5,1},{9,13},{13,9},{2,6},{6,2},{1... | collective-permute-start | bytes 3538952 | tf_op jit(solution)/shard_map/ppermute | solution.py:47
  122.7 14.7 %hidden.2 = (f32[2,8,48,768]{3,2,1,0:T(8,128)S(1)}, bf16[2,8,48,768]{3,2,1,0:T(8,128)(2,1)S(1)}, bf16[32,48,3072]{2,1,0:T(8,128)(2,1)}) custom-call(s32[3]{0:T(128)S(1)} %pad_add_fusion.where, s32[160]{0:T(256)S(1)} %copy-done.26, bf16[768,3072]{1,0:T(8,128)(2,1)} %w.3, bf16[16,48,640]{2,1,0:T(8,128)(2,1)} %pad_maximum_fusion.1.refs_0_, ...), custom_call_target="tpu_custom_call" | custom-call | flops 7247757312 | bytes 18874368 | tf_op jit(solution)/shard_map/hidden/pallas_call | solution.py:189
  138.0 3.5 %collective-permute-start.37 = (bf16[8,16,768]{2,1,0:T(8,128)(2,1)S(1)}, bf16[8,16,768]{2,1,0:T(8,128)(2,1)S(1)}, u32[]{:S(2)}, u32[]{:S(2)}) collective-permute-start(bf16[8,16,768]{2,1,0:T(8,128)(2,1)S(1)} %fusion.7), channel_id=1, source_target_pairs={{0,8},{4,12},{8,0},{12,4},{1,9},{5,13},{9,1},{13,5},{2,10},{6,14},... | collective-permute-start | bytes 589832 | tf_op jit(solution)/shard_map/ppermute | solution.py:47
  141.4 7.1 %gelu.1 = (bf16[768,1536]{1,0:T(8,128)(2,1)S(1)}, bf16[768,512]{1,0:T(8,128)(2,1)S(1)}, f32[8,48,768]{2,1,0:T(8,128)S(1)}, f32[8,16,768]{2,1,0:T(8,128)S(1)}) custom-call(s32[3]{0:T(128)S(1)} %pad_add_fusion.where, bf16[512,3072]{1,0:T(8,128)(2,1)S(1)} %copy-done, bf16[256,768]{1,0:T(8,128)(2,1)S(1)} %copy-done.4, bf16[256,768]{1,0:T(8,128)(2,1)S(1)} %copy-done.2, ...), custom_call_target="tpu_custom_call" | custom-call | flops 62914560 | bytes 16777216 | tf_op jit(solution)/shard_map/gelu/pallas_call | solution.py:126
  148.6 5.9 %down.2.refs_0_ = bf16[768,3072]{1,0:T(8,128)(2,1)} custom-call(bf16[768,1536]{1,0:T(8,128)(2,1)S(1)} %get-tuple-element.18.at_a, bf16[768,512]{1,0:T(8,128)(2,1)S(1)} %get-tuple-element.19.at_b, bf16[1536,3072]{1,0:T(8,128)(2,1)} %bitcast.38, bf16[512,3072]{1,0:T(8,128)(2,1)S(1)} %bitcast.36), custom_call_target="tpu_custom_call" | custom-call | flops 3221225472 | bytes 5767168 | tf_op jit(solution)/shard_map/down/pallas_call | solution.py:229
  155.8 9.5 %down.3 = bf16[768,3072]{1,0:T(8,128)(2,1)} custom-call(bf16[768,1536]{1,0:T(8,128)(2,1)S(1)} %get-tuple-element.18.at_a, bf16[768,512]{1,0:T(8,128)(2,1)S(1)} %get-tuple-element.19.at_b, bf16[1536,3072]{1,0:T(8,128)(2,1)} %bitcast.39, bf16[512,3072]{1,0:T(8,128)(2,1)S(1)} %bitcast.37, bf16[768,3072]{1,0:T(8,128)(2,1)} %down.2.refs_0_), custom_call_target="tpu_custom_call", output_to_operand_aliasing={{}: (4, {})} | custom-call | flops 6442450944 | bytes 11534336 | tf_op jit(solution)/shard_map/down/pallas_call | solution.py:229
  165.3 5.7 %collective-permute-done.26 = bf16[8,48,768]{2,1,0:T(8,128)(2,1)S(1)} collective-permute-done((bf16[8,48,768]{2,1,0:T(8,128)(2,1)S(1)}, bf16[8,48,768]{2,1,0:T(8,128)(2,1)S(1)}, u32[]{:S(2)}, u32[]{:S(2)}) %collective-permute-start.26) | collective-permute-done | bytes 589856 | tf_op jit(solution)/shard_map/ppermute | solution.py:47
  (182 shorter events, 54.6 us)
Async XLA Ops:
  13.2 18.9 %collective-permute-start.21 = (bf16[2,64,640]{2,1,0:T(8,128)(2,1)S(1)}, bf16[2,64,640]{2,1,0:T(8,128)(2,1)S(1)}, u32[]{:S(2)}, u32[]{:S(2)}) collective-permute-start(bf16[2,64,640]{2,1,0:T(8,128)(2,1)S(1)} %pad_maximum_fusion.25), channel_id=1, source_target_pairs={{0,64},{16,80},{32,96},{48,112},{64,0},{80,16},{96,32},{112,48},{1... | collective-permute-start | bytes 491528 | tf_op jit(solution)/shard_map/ppermute | solution.py:42
  26.6 23.5 %collective-permute-start.8 = (bf16[8,64,512]{2,1,0:T(8,128)(2,1)}, bf16[8,64,512]{2,1,0:T(8,128)(2,1)}, u32[]{:S(2)}, u32[]{:S(2)}) collective-permute-start(bf16[8,64,512]{2,1,0:T(8,128)(2,1)} %pad_maximum_fusion.11), channel_id=1, source_target_pairs={{0,3},{1,2},{2,1},{3,0},{4,7},{5,6},{6,5},{7,4},{8,11},{9,10},{10,... | collective-permute-start | bytes 1572872 | tf_op jit(solution)/shard_map/ppermute | solution.py:43
  27.6 26.1 %collective-permute-start.18 = (bf16[8,64,640]{2,1,0:T(8,128)(2,1)}, bf16[8,64,640]{2,1,0:T(8,128)(2,1)}, u32[]{:S(2)}, u32[]{:S(2)}) collective-permute-start(bf16[8,64,640]{2,1,0:T(8,128)(2,1)} %pad_maximum_fusion.9), channel_id=1, source_target_pairs={{0,16},{16,0},{32,48},{48,32},{64,80},{80,64},{96,112},{112,96},{1... | collective-permute-start | bytes 1966088 | tf_op jit(solution)/shard_map/ppermute | solution.py:42
  28.5 27.3 %collective-permute-start.3 = (bf16[8,64,640]{2,1,0:T(8,128)(2,1)}, bf16[8,64,640]{2,1,0:T(8,128)(2,1)}, u32[]{:S(2)}, u32[]{:S(2)}) collective-permute-start(bf16[8,64,640]{2,1,0:T(8,128)(2,1)} %pad_maximum_fusion.7), channel_id=1, source_target_pairs={{0,48},{16,32},{32,16},{48,0},{64,112},{80,96},{96,80},{112,64},{1... | collective-permute-start | bytes 1966088 | tf_op jit(solution)/shard_map/ppermute | solution.py:42
  31.7 26.5 %collective-permute-start.13 = (bf16[8,64,640]{2,1,0:T(8,128)(2,1)}, bf16[8,64,640]{2,1,0:T(8,128)(2,1)}, u32[]{:S(2)}, u32[]{:S(2)}) collective-permute-start(bf16[8,64,640]{2,1,0:T(8,128)(2,1)} %pad_maximum_fusion.8), channel_id=1, source_target_pairs={{0,64},{16,80},{32,96},{48,112},{64,0},{80,16},{96,32},{112,48},{1... | collective-permute-start | bytes 1966088 | tf_op jit(solution)/shard_map/ppermute | solution.py:42
  33.0 13.7 %collective-permute-start.22 = (bf16[4,64,640]{2,1,0:T(8,128)(2,1)}, bf16[4,64,640]{2,1,0:T(8,128)(2,1)S(1)}, u32[]{:S(2)}, u32[]{:S(2)}) collective-permute-start(bf16[4,64,640]{2,1,0:T(8,128)(2,1)} %pad_maximum_fusion.15), channel_id=1, source_target_pairs={{0,16},{16,0},{32,48},{48,32},{64,80},{80,64},{96,112},{112,96},{1... | collective-permute-start | bytes 983048 | tf_op jit(solution)/shard_map/ppermute | solution.py:42
  47.4 16.5 %collective-permute-start.29 = (bf16[256,768]{1,0:T(8,128)(2,1)S(1)}, bf16[256,768]{1,0:T(8,128)(2,1)S(1)}, u32[]{:S(2)}, u32[]{:S(2)}) collective-permute-start(bf16[256,768]{1,0:T(8,128)(2,1)S(1)} %get-tuple-element.22), channel_id=1, source_target_pairs={{0,2},{1,3},{2,0},{3,1},{4,6},{5,7},{6,4},{7,5},{8,10},{9,11},{10,... | collective-permute-start | bytes 1179656 | tf_op jit(solution)/shard_map/ppermute | solution.py:43
  50.1 20.2 %collective-permute-start.23 = (bf16[8,64,640]{2,1,0:T(8,128)(2,1)S(1)}, bf16[8,64,640]{2,1,0:T(8,128)(2,1)S(1)}, u32[]{:S(2)}, u32[]{:S(2)}) collective-permute-start(bf16[8,64,640]{2,1,0:T(8,128)(2,1)S(1)} %pad_maximum_fusion.10), channel_id=1, source_target_pairs={{0,1},{1,0},{2,3},{3,2},{4,5},{5,4},{6,7},{7,6},{8,9},{9,8},{10,11... | collective-permute-start | bytes 1966088 | tf_op jit(solution)/shard_map/ppermute | solution.py:43
  53.7 13.8 %collective-permute-start.28 = (bf16[256,768]{1,0:T(8,128)(2,1)S(1)}, bf16[256,768]{1,0:T(8,128)(2,1)S(1)}, u32[]{:S(2)}, u32[]{:S(2)}) collective-permute-start(bf16[256,768]{1,0:T(8,128)(2,1)S(1)} %get-tuple-element.23), channel_id=1, source_target_pairs={{0,3},{1,2},{2,1},{3,0},{4,7},{5,6},{6,5},{7,4},{8,11},{9,10},{10,... | collective-permute-start | bytes 1179656 | tf_op jit(solution)/shard_map/ppermute | solution.py:43
  55.8 22.9 %collective-permute-start.27 = (bf16[256,768]{1,0:T(8,128)(2,1)S(1)}, bf16[256,768]{1,0:T(8,128)(2,1)S(1)}, u32[]{:S(2)}, u32[]{:S(2)}) collective-permute-start(bf16[256,768]{1,0:T(8,128)(2,1)S(1)} %get-tuple-element.24), channel_id=1, source_target_pairs={{0,1},{1,0},{2,3},{3,2},{4,5},{5,4},{6,7},{7,6},{8,9},{9,8},{10,11... | collective-permute-start | bytes 1179656 | tf_op jit(solution)/shard_map/ppermute | solution.py:43
  58.2 23.1 %collective-permute-start.32 = (bf16[16,16,512]{2,1,0:T(8,128)(2,1)S(1)}, bf16[16,16,512]{2,1,0:T(8,128)(2,1)S(1)}, u32[]{:S(2)}, u32[]{:S(2)}) collective-permute-start(bf16[16,16,512]{2,1,0:T(8,128)(2,1)S(1)} %pad_maximum_fusion.21.refs_2_), channel_id=1, source_target_pairs={{0,64},{16,80},{32,96},{48,112},{64,0},{80,16},{96,32},{112,48},{1... | collective-permute-start | bytes 786440 | tf_op jit(solution)/shard_map/ppermute | solution.py:42
  64.0 21.8 %collective-permute-start.34 = (bf16[16,16,640]{2,1,0:T(8,128)(2,1)S(1)}, bf16[16,16,640]{2,1,0:T(8,128)(2,1)S(1)}, u32[]{:S(2)}, u32[]{:S(2)}) collective-permute-start(bf16[16,16,640]{2,1,0:T(8,128)(2,1)S(1)} %pad_maximum_fusion.18.refs_6_), channel_id=1, source_target_pairs={{0,1},{1,0},{2,3},{3,2},{4,5},{5,4},{6,7},{7,6},{8,9},{9,8},{10,11... | collective-permute-start | bytes 983048 | tf_op jit(solution)/shard_map/ppermute | solution.py:43
  67.5 18.3 %collective-permute-start.31 = (bf16[16,16,640]{2,1,0:T(8,128)(2,1)S(1)}, bf16[16,16,640]{2,1,0:T(8,128)(2,1)S(1)}, u32[]{:S(2)}, u32[]{:S(2)}) collective-permute-start(bf16[16,16,640]{2,1,0:T(8,128)(2,1)S(1)} %pad_maximum_fusion.16.refs_0_), channel_id=1, source_target_pairs={{0,3},{1,2},{2,1},{3,0},{4,7},{5,6},{6,5},{7,4},{8,11},{9,10},{10,... | collective-permute-start | bytes 983048 | tf_op jit(solution)/shard_map/ppermute | solution.py:43
  70.3 15.6 %collective-permute-start.33 = (bf16[16,16,640]{2,1,0:T(8,128)(2,1)S(1)}, bf16[16,16,640]{2,1,0:T(8,128)(2,1)S(1)}, u32[]{:S(2)}, u32[]{:S(2)}) collective-permute-start(bf16[16,16,640]{2,1,0:T(8,128)(2,1)S(1)} %pad_maximum_fusion.17.refs_4_), channel_id=1, source_target_pairs={{0,16},{16,0},{32,48},{48,32},{64,80},{80,64},{96,112},{112,96},{1... | collective-permute-start | bytes 983048 | tf_op jit(solution)/shard_map/ppermute | solution.py:42
  78.8 10.7 %collective-permute-start.35 = (bf16[16,16,640]{2,1,0:T(8,128)(2,1)S(1)}, bf16[16,16,640]{2,1,0:T(8,128)(2,1)S(1)}, u32[]{:S(2)}, u32[]{:S(2)}) collective-permute-start(bf16[16,16,640]{2,1,0:T(8,128)(2,1)S(1)} %pad_maximum_fusion.19.refs_8_), channel_id=1, source_target_pairs={{0,48},{16,32},{32,16},{48,0},{64,112},{80,96},{96,80},{112,64},{1... | collective-permute-start | bytes 983048 | tf_op jit(solution)/shard_map/ppermute | solution.py:42
  81.3 41.2 %collective-permute-start.24 = (bf16[16,48,640]{2,1,0:T(8,128)(2,1)}, bf16[16,48,640]{2,1,0:T(8,128)(2,1)}, u32[]{:S(2)}, u32[]{:S(2)}) collective-permute-start(bf16[16,48,640]{2,1,0:T(8,128)(2,1)} %pad_maximum_fusion.4.refs_8_), channel_id=1, source_target_pairs={{0,48},{16,32},{32,16},{48,0},{64,112},{80,96},{96,80},{112,64},{1... | collective-permute-start | bytes 2949128 | tf_op jit(solution)/shard_map/ppermute | solution.py:42
  85.8 36.9 %collective-permute-start.14 = (bf16[16,48,640]{2,1,0:T(8,128)(2,1)}, bf16[16,48,640]{2,1,0:T(8,128)(2,1)}, u32[]{:S(2)}, u32[]{:S(2)}) collective-permute-start(bf16[16,48,640]{2,1,0:T(8,128)(2,1)} %pad_maximum_fusion.2.refs_4_), channel_id=1, source_target_pairs={{0,16},{16,0},{32,48},{48,32},{64,80},{80,64},{96,112},{112,96},{1... | collective-permute-start | bytes 2949128 | tf_op jit(solution)/shard_map/ppermute | solution.py:42
  85.8 36.9 %collective-permute-start.4 = (bf16[16,48,640]{2,1,0:T(8,128)(2,1)}, bf16[16,48,640]{2,1,0:T(8,128)(2,1)}, u32[]{:S(2)}, u32[]{:S(2)}) collective-permute-start(bf16[16,48,640]{2,1,0:T(8,128)(2,1)} %pad_maximum_fusion.1.refs_0_), channel_id=1, source_target_pairs={{0,3},{1,2},{2,1},{3,0},{4,7},{5,6},{6,5},{7,4},{8,11},{9,10},{10,... | collective-permute-start | bytes 2949128 | tf_op jit(solution)/shard_map/ppermute | solution.py:43
  85.9 36.7 %collective-permute-start.19 = (bf16[16,48,640]{2,1,0:T(8,128)(2,1)}, bf16[16,48,640]{2,1,0:T(8,128)(2,1)}, u32[]{:S(2)}, u32[]{:S(2)}) collective-permute-start(bf16[16,48,640]{2,1,0:T(8,128)(2,1)} %pad_maximum_fusion.3.refs_6_), channel_id=1, source_target_pairs={{0,1},{1,0},{2,3},{3,2},{4,5},{5,4},{6,7},{7,6},{8,9},{9,8},{10,11... | collective-permute-start | bytes 2949128 | tf_op jit(solution)/shard_map/ppermute | solution.py:43
  90.2 23.0 %collective-permute-start.9 = (bf16[16,48,512]{2,1,0:T(8,128)(2,1)}, bf16[16,48,512]{2,1,0:T(8,128)(2,1)}, u32[]{:S(2)}, u32[]{:S(2)}) collective-permute-start(bf16[16,48,512]{2,1,0:T(8,128)(2,1)} %pad_maximum_fusion.5.refs_2_), channel_id=1, source_target_pairs={{0,64},{16,80},{32,96},{48,112},{64,0},{80,16},{96,32},{112,48},{1... | collective-permute-start | bytes 2359304 | tf_op jit(solution)/shard_map/ppermute | solution.py:42
  113.3 28.2 %collective-permute-start.30 = (bf16[768,768]{1,0:T(8,128)(2,1)S(1)}, bf16[768,768]{1,0:T(8,128)(2,1)S(1)}, u32[]{:S(2)}, u32[]{:S(2)}) collective-permute-start(bf16[768,768]{1,0:T(8,128)(2,1)S(1)} %pad_maximum_fusion), channel_id=1, source_target_pairs={{0,4},{4,0},{8,12},{12,8},{1,5},{5,1},{9,13},{13,9},{2,6},{6,2},{1... | collective-permute-start | bytes 3538952 | tf_op jit(solution)/shard_map/ppermute | solution.py:47
  122.6 15.3 %collective-permute-start.36 = (bf16[2,8,16,768]{3,2,1,0:T(8,128)(2,1)S(1)}, bf16[2,8,16,768]{3,2,1,0:T(8,128)(2,1)S(1)}, u32[]{:S(2)}, u32[]{:S(2)}) collective-permute-start(bf16[2,8,16,768]{3,2,1,0:T(8,128)(2,1)S(1)} %get-tuple-element.16), channel_id=1, source_target_pairs={{0,4},{4,0},{8,12},{12,8},{1,5},{5,1},{9,13},{13,9},{2,6},{6,2},{1... | collective-permute-start | bytes 1179656 | tf_op jit(solution)/shard_map/ppermute | solution.py:47
  137.4 17.1 %collective-permute-start.25 = (bf16[2,8,48,768]{3,2,1,0:T(8,128)(2,1)S(1)}, bf16[2,8,48,768]{3,2,1,0:T(8,128)(2,1)S(1)}, u32[]{:S(2)}, u32[]{:S(2)}) collective-permute-start(bf16[2,8,48,768]{3,2,1,0:T(8,128)(2,1)S(1)} %get-tuple-element.13), channel_id=1, source_target_pairs={{0,4},{4,0},{8,12},{12,8},{1,5},{5,1},{9,13},{13,9},{2,6},{6,2},{1... | collective-permute-start | bytes 3538952 | tf_op jit(solution)/shard_map/ppermute | solution.py:47
  154.8 16.1 %collective-permute-start.26 = (bf16[8,48,768]{2,1,0:T(8,128)(2,1)S(1)}, bf16[8,48,768]{2,1,0:T(8,128)(2,1)S(1)}, u32[]{:S(2)}, u32[]{:S(2)}) collective-permute-start(bf16[8,48,768]{2,1,0:T(8,128)(2,1)S(1)} %fusion.3), channel_id=1, source_target_pairs={{0,8},{4,12},{8,0},{12,4},{1,9},{5,13},{9,1},{13,5},{2,10},{6,14},... | collective-permute-start | bytes 1769480 | tf_op jit(solution)/shard_map/ppermute | solution.py:47
  (48 other events, 324.2 us)

commit v2 on v1

--- a/solution.py
+++ b/solution.py
@@ -16,8 +16,8 @@
 FEATS = 3072
 HID = 768
 X, Y0, Y1, Z0, Z1 = 16, 4, 12, 1, 3
-DIMS = (X, Y0, Z0, Y1, Z1)
-WIDTHS = (640, 512, 640, 640, 640)
+DIMS = (Z0, Y0, Z1, Y1, X)
+WIDTHS = (512, 640, 640, 640, 640)
 OFFSETS = tuple(int(v) for v in np.cumsum((0,) + WIDTHS)[:-1])
 CHAINS = len(WIDTHS)
 ORDERS = tuple(tuple(DIMS[(p + k) % 5] for k in range(5)) for p in range(CHAINS))
@@ -25,16 +25,12 @@
 STARTS = (0, 48)
 
 
-def place_table():
-    table = np.zeros((CHAINS, SHARDS), np.int32)
-    for p, order in enumerate(ORDERS):
-        for i in range(SHARDS):
-            delta = 0
-            for k, mask in enumerate(order):
-                if i >> k & 1:
-                    delta ^= mask
-            table[p, delta] = i
-    return table.reshape(-1)
+def mask_of(c):
+    mask = 0
+    for k in range(5):
+        if c >> k & 1:
+            mask ^= DIMS[k]
+    return mask
 
 
 def swap(x, mask):
@@ -56,10 +52,75 @@
 SMEM = pl.BlockSpec(memory_space=pltpu.SMEM)
 
 
-def gelu_kernel(where, pre, got_a, got_b, got_c, other, *refs):
+def cut_kernel(where, grad_out, pre, *refs):
+    outs, chunks, sem = refs[:CHAINS], refs[CHAINS:-1], refs[-1]
+    row, col = where[0], where[1]
+    copies = [
+        pltpu.make_async_copy(grad_out.at[:, pl.ds(OFFSETS[p], WIDTHS[p])], outs[p].at[0], sem.at[p])
+        for p in range(CHAINS)
+    ]
+    half = SHARDS * ROWS // 8
+    for j, mask in enumerate((Z0, Z1, Z0 ^ Z1)):
+        here = pre.at[
+            pl.ds(pl.multiple_of(row % 2 * half, half), half), pl.ds(pl.multiple_of((col ^ mask) * HID, HID), HID)
+        ]
+        copies.append(pltpu.make_async_copy(here, chunks[j], sem.at[CHAINS + j]))
+    for c in copies:
+        c.start()
+    for c in copies:
+        c.wait()
+
+
+def cut_call(where, grad_out, pre):
+    return pl.pallas_call(
+        cut_kernel,
+        out_shape=[jax.ShapeDtypeStruct((1, ROWS, w), jnp.bfloat16) for w in WIDTHS]
+        + [jax.ShapeDtypeStruct((SHARDS * ROWS // 8, HID), jnp.bfloat16)] * 3,
+        in_specs=[SMEM, ANY, ANY],
+        out_specs=[ANY] * (CHAINS + 3),
+        scratch_shapes=[pltpu.SemaphoreType.DMA((CHAINS + 3,))],
+        compiler_params=params(1),
+        name="cut",
+    )(where, grad_out, pre)
+
+
+def grow_kernel(rows, *refs):
+    own, got, sem = refs[:CHAINS], refs[CHAINS : 2 * CHAINS], refs[-1]
+    outs = refs[2 * CHAINS : -1]
+    copies = []
+    for part, (at, n) in enumerate(rows):
+        for p in range(CHAINS):
+            out = outs[part * CHAINS + p]
+            blocks = own[p].shape[0]
+            for side, src in enumerate((own[p], got[p])):
+                copies.append(
+                    pltpu.make_async_copy(
+                        src.at[:, pl.ds(at, n)], out.at[pl.ds(side * blocks, blocks)], sem.at[len(copies)]
+                    )
+                )
+    for c in copies:
+        c.start()
+    for c in copies:
+        c.wait()
+
+
+def grow_call(own, got, rows=((0, ROWS),)):
+    blocks = own[0].shape[0]
+    return pl.pallas_call(
+        functools.partial(grow_kernel, rows),
+        out_shape=[jax.ShapeDtypeStruct((2 * blocks, n, w), jnp.bfloat16) for _, n in rows for w in WIDTHS],
+        in_specs=[ANY] * (2 * CHAINS),
+        out_specs=[ANY] * (len(rows) * CHAINS),
+        scratch_shapes=[pltpu.SemaphoreType.DMA((2 * CHAINS * len(rows),))],
+        compiler_params=params(1),
+        name="grow",
+    )(*own, *got)
+
+
+def gelu_kernel(where, table, pre, got_a, got_b, got_c, other, *refs):
     outs, (buf, sems), acts = refs[:4], refs[4:6], refs[6:]
     act_t, slopes = outs[:2], outs[2:]
-    row, col = where[0], where[1]
+    row, col, mine = where[0], where[1], where[2]
     core = row % 2
     quarter, half = SHARDS * ROWS // 4, SHARDS * ROWS // 8
     copies = [
@@ -89,7 +150,7 @@
         c.wait()
 
     def one_shard(s, carry):
-        v = buf[pl.ds(pl.multiple_of(s * ROWS, ROWS), ROWS), :].astype(jnp.float32)
+        v = buf[pl.ds(pl.multiple_of((mine ^ table[s]) * ROWS, ROWS), ROWS), :].astype(jnp.float32)
         bend = jnp.tanh(gelu_const * (v + 0.044715 * v * v * v))
         a = (0.5 * v * (1.0 + bend)).astype(jnp.bfloat16)
         for part in range(2):
@@ -121,69 +182,66 @@
         lax.fori_loop(0, SHARDS * PARTS[part] // 128, one_turn, 0)
 
 
-def gelu_call(where, pre, got, other):
+def gelu_call(where, table, pre, got, other):
     tokens = [SHARDS * n for n in PARTS]
     return pl.pallas_call(
         gelu_kernel,
         out_shape=[jax.ShapeDtypeStruct((HID, t), jnp.bfloat16) for t in tokens]
         + [jax.ShapeDtypeStruct((SHARDS // 4, n, HID), jnp.float32) for n in PARTS],
-        in_specs=[SMEM] + [ANY] * 5,
+        in_specs=[SMEM, SMEM] + [ANY] * 5,
         out_specs=[VMEM] * 4,
         scratch_shapes=[pltpu.VMEM((SHARDS * ROWS, HID), jnp.bfloat16), pltpu.SemaphoreType.DMA((7,))]
         + [pltpu.VMEM((t, HID), jnp.bfloat16) for t in tokens],
-        compiler_params=params(32),
+        compiler_params=params(20),
         cost_estimate=pl.CostEstimate(flops=2048 * HID * 40, bytes_accessed=16 << 20, transcendentals=2048 * HID),
         name="gelu",
-    )(where, pre, *got, other)
-
-
-def hidden_kernel(n, where, table, w, *refs):
+    )(where, table, pre, *got, other)
+
+
+def pieces(p, side):
+    every = slice(None)
+    if p == 0:
+        return [((every,) * 4, (side,) + (every,) * 4)]
+    if p == 1:
+        return [((every,) * 4, (every,) * 4 + (side,))]
+    if p == 2:
+        return [((i,) + (every,) * 3, (every,) * 3 + (side, i)) for i in range(2)]
+    if p == 3:
+        return [((every,) * 2 + (i, j), (i, j, side) + (every,) * 2) for i in range(2) for j in range(2)]
+    return [((every,) * 3 + (i,), (i, side) + (every,) * 3) for i in range(2)]
+
+
+def hidden_kernel(n, where, w, *refs):
     blocks = refs[: 2 * CHAINS]
-    keep, send, gathered, g, in_sems, out_sems = refs[2 * CHAINS :]
+    keep, send, gathered, g, in_sem, out_sem = refs[2 * CHAINS :]
     row, mine = where[0], where[2]
     per = SHARDS // 4
-    order = [(1, 1), (0, 1), (1, 0), (0, 0)]
-    quarters = [row ^ (2 * a + b) for a, b in order]
-
-    for t, q in enumerate(quarters):
-
-        def fetch(k, carry, t=t, q=q):
-            s = q * per + k
-            for p in range(CHAINS):
-                i = table[p * SHARDS + (s ^ mine)]
-                for side in range(2):
-
-                    @pl.when(i // 16 == side)
-                    def _(p=p, side=side, i=i):
-                        pltpu.make_async_copy(
-                            blocks[2 * p + side].at[i % 16],
-                            g.at[s, :, pl.ds(OFFSETS[p], WIDTHS[p])],
-                            in_sems.at[t],
-                        ).start()
-
-            return carry
-
-        lax.fori_loop(0, per, fetch, 0)
-
-    outs = []
-    for t, q in enumerate(quarters):
-        a, b = order[t]
-        here = g.at[pl.ds(pl.multiple_of(q * per, per), per)]
-        pltpu.make_async_copy(here, here, in_sems.at[t]).wait()
-        out = pltpu.make_async_copy(here, gathered.at[pl.ds(pl.multiple_of(q * per, per), per)], out_sems.at[t])
-        out.start()
-        outs.append(out)
-        lhs = here[...].reshape(per * n, FEATS)
+    for p in range(CHAINS):
+        for side in range(2):
+            for src, dst in pieces(p, side):
+                pltpu.make_async_copy(
+                    blocks[2 * p + side].at[src],
+                    g.at[dst + (slice(None), pl.ds(OFFSETS[p], WIDTHS[p]))],
+                    in_sem,
+                ).start()
+    pltpu.make_async_copy(g, g, in_sem).wait()
+    out = pltpu.make_async_copy(g, gathered, out_sem)
+    out.start()
+    for a, b in ((1, 1), (0, 1), (1, 0), (0, 0)):
+        off_x = (mine // 16) ^ (row // 2) ^ a
+        off_y = (mine // 8 % 2) ^ (row % 2) ^ b
+        lhs = g[off_x, off_y].reshape(per * n, FEATS)
         h = lax.dot_general(lhs, w[...], (((1,), (1,)), ((), ())), preferred_element_type=jnp.float32)
-        if b:
-            send[a] = h.astype(jnp.bfloat16).reshape(per, n, HID)
-        else:
-            keep[a] = h.reshape(per, n, HID)
-    for out in outs:
-        out.wait()
-
-
-def hidden_call(part, where, table, w, blocks):
+        for j in range(per):
+            slot = (mine % 8) ^ (mask_of(j) % 8) ^ (off_y * 4)
+            if b:
+                send[a, slot] = h[j * n : (j + 1) * n].astype(jnp.bfloat16)
+            else:
+                keep[a, slot] = h[j * n : (j + 1) * n]
+    out.wait()
+
+
+def hidden_call(part, where, w, blocks):
     n = PARTS[part]
     per = SHARDS // 4
     return pl.pallas_call(
@@ -191,21 +249,21 @@
         out_shape=[
             jax.ShapeDtypeStruct((2, per, n, HID), jnp.float32),
             jax.ShapeDtypeStruct((2, per, n, HID), jnp.bfloat16),
-            jax.ShapeDtypeStruct((SHARDS, n, FEATS), jnp.bfloat16),
+            jax.ShapeDtypeStruct((2,) * 5 + (n, FEATS), jnp.bfloat16),
         ],
-        in_specs=[SMEM, SMEM, VMEM] + [ANY] * (2 * CHAINS),
+        in_specs=[SMEM, VMEM] + [ANY] * (2 * CHAINS),
         out_specs=[VMEM, VMEM, ANY],
         scratch_shapes=[
-            pltpu.VMEM((SHARDS, n, FEATS), jnp.bfloat16),
-            pltpu.SemaphoreType.DMA((4,)),
-            pltpu.SemaphoreType.DMA((4,)),
+            pltpu.VMEM((2,) * 5 + (n, FEATS), jnp.bfloat16),
+            pltpu.SemaphoreType.DMA,
+            pltpu.SemaphoreType.DMA,
         ],
-        compiler_params=params(40),
+        compiler_params=params(10 + n // 3),
         cost_estimate=pl.CostEstimate(
             flops=2 * SHARDS * n * FEATS * HID, bytes_accessed=SHARDS * n * FEATS * 4, transcendentals=0
         ),
         name="hidden",
-    )(where, table, w, *blocks)
+    )(where, w, *(b.reshape((2,) * 4 + b.shape[1:]) for b in blocks))
 
 
 def down_kernel(at_a, at_b, g_a, g_b, *refs):
@@ -233,7 +291,7 @@
         in_specs=in_specs,
         out_specs=pl.BlockSpec((HID, wide), lambda j: (0, j + first)),
         input_output_aliases=aliases,
-        compiler_params=params(40),
+        compiler_params=params(24),
         cost_estimate=pl.CostEstimate(
             flops=2 * 2048 * HID * wide * count, bytes_accessed=count * wide * 2 * (2048 + HID), transcendentals=0
         ),
@@ -244,37 +302,27 @@
 def local(grad_out, pre_act, w_down):
     depth, row, col = (lax.axis_index(a) for a in ("depth", "row", "col"))
     where = jnp.stack([row, col, depth * 4 + col]).astype(jnp.int32)
-    table = jnp.asarray(place_table())
-    core = row % 2
-
-    blocks = []
-    for p in range(CHAINS):
-        blocks.append(grad_out[:, OFFSETS[p] : OFFSETS[p] + WIDTHS[p]].reshape(1, ROWS, WIDTHS[p]))
+    table = jnp.asarray([mask_of(c) for c in range(SHARDS)], jnp.int32)
+
+    cuts = cut_call(where, grad_out, pre_act)
+    blocks, chunks = cuts[:CHAINS], cuts[CHAINS:]
+    fetched = [swap(chunk, mask) for chunk, mask in zip(chunks, (Z0, Z1, Z0 ^ Z1))]
     for k in range(3):
         got = [swap(blocks[p], ORDERS[p][k]) for p in range(CHAINS)]
-        blocks = [jnp.concatenate([b, r], 0) for b, r in zip(blocks, got)]
+        blocks = grow_call(blocks, got)
     got = [swap(blocks[p], ORDERS[p][3]) for p in range(CHAINS)]
-    own, came = ([], []), ([], [])
-    for part in range(2):
-        rows = slice(STARTS[part], STARTS[part] + PARTS[part])
-        for p in range(CHAINS):
-            own[part].append(jnp.concatenate([blocks[p][:, rows], got[p][:, rows]], 0))
-    for part in range(2):
-        for p in range(CHAINS):
-            came[part].append(swap(own[part][p], ORDERS[p][4]))
-
-    half = pre_act.shape[0] // 2
-    fetched = []
-    for mask in (Z0, Z1, Z0 ^ Z1):
-        chunk = lax.dynamic_slice(pre_act, (core * half, (col ^ mask) * HID), (half, HID))
-        fetched.append(swap(chunk, mask))
+    grown = grow_call(blocks, got, tuple(zip(STARTS, PARTS)))
+    own = grown[:CHAINS], grown[CHAINS:]
+    came = [[swap(own[part][p], ORDERS[p][4]) for p in range(CHAINS)] for part in range(2)]
+
     other = swap_row(jnp.concatenate(fetched, 0), 1)
-    act_a, act_b, slope_a, slope_b = gelu_call(where, pre_act, fetched, other)
+    act_a, act_b, slope_a, slope_b = gelu_call(where, table, pre_act, fetched, other)
+    came[0][0], act_a = lax.optimization_barrier((came[0][0], act_a))
 
     done, gathered = [], []
     for part in range(2):
         pairs = [b for p in range(CHAINS) for b in (own[part][p], came[part][p])]
-        keep, send, g = hidden_call(part, where, table, w_down, pairs)
+        keep, send, g = hidden_call(part, where, w_down, pairs)
         gathered.append(g)
         total = keep + swap_row(send, 1).astype(jnp.float32)
         far = swap_row(total[1].astype(jnp.bfloat16), 2)

time: 173 us -> 164 us (0.948)
  starting transfers between devices: 49.5 us -> 65.8 us
  local copies, waits for them, and re-layouts: 25.3 us -> 9.47 us
  other arithmetic: 14.2 us -> 1.74 us
  waiting for transfers between devices: 30.5 us -> 40.8 us
  Pallas kernels: 51.4 us -> 44.2 us
    ppermute x5, starting transfers between devices: 14.3 us -> 36.1 us  [swap_row(): return lax.ppermute(x, 'row', [(i, i ^ mask) for i in range(4)])]
    slice x20 -> x0, local copies, waits for them, and re-layouts: 16.1 us -> none  [local(): own[part].append(jnp.concatenate([blocks[p][:, rows], got[p][:, rows]], 0))]
    pallas_call x2, Pallas kernels: 28.9 us -> 17.5 us  [hidden_call(): pl.pallas_call(functools.partial(hidden_kernel, n), out_shape=[jax.ShapeD...]
    concatenate x25 -> x0, other arithmetic: 11.2 us -> none  [the longest x15 5.71 us: local(): blocks = [jnp.concatenate([b, r], 0) for b, r in zip(blocks, got)]]
    ppermute x15, waiting for transfers between devices: 16.1 us -> 25.1 us  [swap(): return lax.ppermute(x, 'col', [(i, i ^ mask) for i in range(4)])]
    pallas_call x0 -> x5, Pallas kernels: none -> 6.06 us  [the longest x4 5.25 us: grow_call(): pl.pallas_call(functools.partial(grow_kernel, rows), out_shape=[jax.Shape...]
    ppermute x18, starting transfers between devices: 18.3 us -> 13 us  [swap(): return lax.ppermute(x, 'depth', [(i, i ^ mask >> 2) for i in range(8)])]
    ppermute x5, waiting for transfers between devices: 5.66 us -> 8.38 us  [swap_row(): return lax.ppermute(x, 'row', [(i, i ^ mask) for i in range(4)])]
  transfers between devices with their start and end apart: 38 -> 38, of which waited for: 8 -> 15; matrix products, arithmetic and copies ran while one was open for 17% -> 0% of each run, Pallas kernels for 30% -> 25%
where the time goes in v2:
time: 164 us; the launch traced here: 163 us
  starting transfers between devices  65.8 us (40%)
  Pallas kernels  44.2 us (27%)
  waiting for transfers between devices  40.8 us (25%)
  local copies, waits for them, and re-layouts  9.47 us (6%)
  other arithmetic  1.74 us (1%)
    ppermute x5, starting transfers between devices, swap_row(): return lax.ppermute(x, 'row', [(i, i ^ mask) for i in range(4)])  36.1 us
    ppermute x15, waiting for transfers between devices, swap(): return lax.ppermute(x, 'col', [(i, i ^ mask) for i in range(4)])  25.1 us
    pallas_call x2, Pallas kernels, hidden_call(): pl.pallas_call(functools.partial(hidden_kernel, n), out_shape=[jax.ShapeD...  17.5 us
    ppermute x15, starting transfers between devices, swap(): return lax.ppermute(x, 'col', [(i, i ^ mask) for i in range(4)])  16.6 us
    pallas_call x2, Pallas kernels, down_call(): pl.pallas_call(down_kernel, grid=(count,), out_shape=jax.ShapeDtypeStruct...  13.4 us
    ppermute x18, starting transfers between devices, swap(): return lax.ppermute(x, 'depth', [(i, i ^ mask >> 2) for i in range(8)])  13 us
    unnamed x22, local copies, waits for them, and re-layouts  9.39 us
    ppermute x5, waiting for transfers between devices, swap_row(): return lax.ppermute(x, 'row', [(i, i ^ mask) for i in range(4)])  8.38 us
  transfers between devices with their start and end apart: 38, of which 15 were waited for; matrix products, arithmetic and copies ran while one was open for 0% of the time, Pallas kernels for 25%

profile of v2, /device:TPU:1, one launch (start us, length us, event | category | flops | bytes accessed | tf_op | source)
XLA Modules:
  0.0 162.9 jit_solution(17895617231194152991)
XLA Ops:
  4.4 2.2 %collective-permute-start.1 = (bf16[1,64,640]{2,1,0:T(8,128)(2,1)S(1)}, bf16[1,64,640]{2,1,0:T(8,128)(2,1)S(1)}, u32[]{:S(2)}, u32[]{:S(2)}) collective-permute-start(bf16[1,64,640]{2,1,0:T(8,128)(2,1)S(1)} %get-tuple-element.48.refs_1_), channel_id=1, source_target_pairs={{0,16},{16,0},{32,48},{48,32},{64,80},{80,64},{96,112},{112,96},{1... | collective-permute-start | bytes 245768 | tf_op jit(solution)/shard_map/ppermute | solution.py:38
  6.6 3.8 %collective-permute-start.2 = (bf16[1,64,640]{2,1,0:T(8,128)(2,1)S(1)}, bf16[1,64,640]{2,1,0:T(8,128)(2,1)S(1)}, u32[]{:S(2)}, u32[]{:S(2)}) collective-permute-start(bf16[1,64,640]{2,1,0:T(8,128)(2,1)S(1)} %get-tuple-element.49.refs_2_), channel_id=1, source_target_pairs={{0,3},{1,2},{2,1},{3,0},{4,7},{5,6},{6,5},{7,4},{8,11},{9,10},{10,... | collective-permute-start | bytes 245768 | tf_op jit(solution)/shard_map/ppermute | solution.py:39
  13.5 3.4 %collective-permute-done.refs_5_ = bf16[1,64,512]{2,1,0:T(8,128)(2,1)S(1)} collective-permute-done((bf16[1,64,512]{2,1,0:T(8,128)(2,1)S(1)}, bf16[1,64,512]{2,1,0:T(8,128)(2,1)S(1)}, u32[]{:S(2)}, u32[]{:S(2)}) %collective-permute-start) | collective-permute-done | bytes 65568 | tf_op jit(solution)/shard_map/ppermute | solution.py:39
  19.6 3.5 %collective-permute-done.5.refs_5_ = bf16[2,64,512]{2,1,0:T(8,128)(2,1)S(1)} collective-permute-done((bf16[2,64,512]{2,1,0:T(8,128)(2,1)S(1)}, bf16[2,64,512]{2,1,0:T(8,128)(2,1)S(1)}, u32[]{:S(2)}, u32[]{:S(2)}) %collective-permute-start.5) | collective-permute-done | bytes 131104 | tf_op jit(solution)/shard_map/ppermute | solution.py:38
  23.6 2.1 %grow.5 = (bf16[4,64,512]{2,1,0:T(8,128)(2,1)S(1)}, bf16[4,64,640]{2,1,0:T(8,128)(2,1)S(1)}, bf16[4,64,640]{2,1,0:T(8,128)(2,1)S(1)}, bf16[4,64,640]{2,1,0:T(8,128)(2,1)S(1)}, bf16[4,64,640]{2,1,0:T(8,128)(2,1)S(1)}) custom-call(bf16[2,64,512]{2,1,0:T(8,128)(2,1)S(1)} %get-tuple-element.52.refs_0_, bf16[2,64,640]{2,1,0:T(8,128)(2,1)S(1)} %get-tuple-element.53.refs_1_, ...), custom_call_target="tpu_custom_call" | custom-call | tf_op jit(solution)/shard_map/grow/pallas_call | solution.py:109
  29.0 2.6 %collective-permute-start.10 = (bf16[4,64,512]{2,1,0:T(8,128)(2,1)S(1)}, bf16[4,64,512]{2,1,0:T(8,128)(2,1)S(1)}, u32[]{:S(2)}, u32[]{:S(2)}) collective-permute-start(bf16[4,64,512]{2,1,0:T(8,128)(2,1)S(1)} %get-tuple-element.57.refs_0_), channel_id=1, source_target_pairs={{0,3},{1,2},{2,1},{3,0},{4,7},{5,6},{6,5},{7,4},{8,11},{9,10},{10,... | collective-permute-start | bytes 786440 | tf_op jit(solution)/shard_map/ppermute | solution.py:39
  32.2 3.6 %collective-permute-done.10.refs_5_ = bf16[4,64,512]{2,1,0:T(8,128)(2,1)S(1)} collective-permute-done((bf16[4,64,512]{2,1,0:T(8,128)(2,1)S(1)}, bf16[4,64,512]{2,1,0:T(8,128)(2,1)S(1)}, u32[]{:S(2)}, u32[]{:S(2)}) %collective-permute-start.10) | collective-permute-done | bytes 262176 | tf_op jit(solution)/shard_map/ppermute | solution.py:39
  36.2 2.1 %collective-permute-start.22 = (bf16[256,768]{1,0:T(8,128)(2,1)S(1)}, bf16[256,768]{1,0:T(8,128)(2,1)S(1)}, u32[]{:S(2)}, u32[]{:S(2)}) collective-permute-start(bf16[256,768]{1,0:T(8,128)(2,1)S(1)} %get-tuple-element.69), channel_id=1, source_target_pairs={{0,3},{1,2},{2,1},{3,0},{4,7},{5,6},{6,5},{7,4},{8,11},{9,10},{10,... | collective-permute-start | bytes 1179656 | tf_op jit(solution)/shard_map/ppermute | solution.py:39
  41.6 3.7 %collective-permute-done.21.got_a = bf16[256,768]{1,0:T(8,128)(2,1)S(1)} collective-permute-done((bf16[256,768]{1,0:T(8,128)(2,1)S(1)}, bf16[256,768]{1,0:T(8,128)(2,1)S(1)}, u32[]{:S(2)}, u32[]{:S(2)}) %collective-permute-start.21) | collective-permute-done | bytes 393248 | tf_op jit(solution)/shard_map/ppermute | solution.py:39
  45.4 8.7 %collective-permute-done.23.got_c = bf16[256,768]{1,0:T(8,128)(2,1)S(1)} collective-permute-done((bf16[256,768]{1,0:T(8,128)(2,1)S(1)}, bf16[256,768]{1,0:T(8,128)(2,1)S(1)}, u32[]{:S(2)}, u32[]{:S(2)}) %collective-permute-start.23) | collective-permute-done | bytes 393248 | tf_op jit(solution)/shard_map/ppermute | solution.py:39
  55.9 11.3 %collective-permute-start.24 = (bf16[768,768]{1,0:T(8,128)(2,1)S(1)}, bf16[768,768]{1,0:T(8,128)(2,1)S(1)}, u32[]{:S(2)}, u32[]{:S(2)}) collective-permute-start(bf16[768,768]{1,0:T(8,128)(2,1)S(1)} %pad_maximum_fusion), channel_id=1, source_target_pairs={{0,4},{4,0},{8,12},{12,8},{1,5},{5,1},{9,13},{13,9},{2,6},{6,2},{1... | collective-permute-start | bytes 3538952 | tf_op jit(solution)/shard_map/ppermute | solution.py:43
  72.2 2.8 %collective-permute-done.31 = bf16[16,16,512]{2,1,0:T(8,128)(2,1)S(1)} collective-permute-done((bf16[16,16,512]{2,1,0:T(8,128)(2,1)S(1)}, bf16[16,16,512]{2,1,0:T(8,128)(2,1)S(1)}, u32[]{:S(2)}, u32[]{:S(2)}) %collective-permute-start.31) | collective-permute-done | bytes 262176 | tf_op jit(solution)/shard_map/ppermute | solution.py:38
  76.9 3.5 %collective-permute-done.34 = bf16[16,16,640]{2,1,0:T(8,128)(2,1)S(1)} collective-permute-done((bf16[16,16,640]{2,1,0:T(8,128)(2,1)S(1)}, bf16[16,16,640]{2,1,0:T(8,128)(2,1)S(1)}, u32[]{:S(2)}, u32[]{:S(2)}) %collective-permute-start.34) | collective-permute-done | bytes 327712 | tf_op jit(solution)/shard_map/ppermute | solution.py:39
  83.3 7.5 %hidden.3 = (f32[2,8,16,768]{3,2,1,0:T(8,128)S(1)}, bf16[2,8,16,768]{3,2,1,0:T(8,128)(2,1)S(1)}, bf16[2,2,2,2,2,16,3072]{6,5,4,3,2,1,0:T(8,128)(2,1)S(1)}) custom-call(s32[3]{0:T(128)S(1)} %pad_add_fusion.where, bf16[768,3072]{1,0:T(8,128)(2,1)S(1)} %bitcast.51, bf16[2,2,2,2,16,512]{5,4,3,2,1,0:T(8,128)(2,1)S(1)} %bitcast.70, ...), custom_call_target="tpu_custom_call" | custom-call | flops 2415919104 | bytes 6291456 | tf_op jit(solution)/shard_map/hidden/pallas_call | solution.py:247
  90.7 7.2 %gelu.1 = (bf16[768,1536]{1,0:T(8,128)(2,1)S(1)}, bf16[768,512]{1,0:T(8,128)(2,1)S(1)}, f32[8,48,768]{2,1,0:T(8,128)S(1)}, f32[8,16,768]{2,1,0:T(8,128)S(1)}) custom-call(s32[3]{0:T(128)S(1)} %pad_add_fusion.where, s32[32]{0:T(128)S(1)} %copy-done.3, bf16[512,3072]{1,0:T(8,128)(2,1)S(1)} %copy-done.1, bf16[256,768]{1,0:T(8,128)(2,1)S(1)} %collective-permute-done.21.got_a, ...), custom_call_target="tpu_custom_call" | custom-call | flops 62914560 | bytes 16777216 | tf_op jit(solution)/shard_map/gelu/pallas_call | solution.py:187
  98.8 18.9 %collective-permute-start.36 = (bf16[2,8,16,768]{3,2,1,0:T(8,128)(2,1)S(1)}, bf16[2,8,16,768]{3,2,1,0:T(8,128)(2,1)S(1)}, u32[]{:S(2)}, u32[]{:S(2)}) collective-permute-start(bf16[2,8,16,768]{3,2,1,0:T(8,128)(2,1)S(1)} %get-tuple-element.86), channel_id=1, source_target_pairs={{0,4},{4,0},{8,12},{12,8},{1,5},{5,1},{9,13},{13,9},{2,6},{6,2},{1... | collective-permute-start | bytes 1179656 | tf_op jit(solution)/shard_map/ppermute | solution.py:43
  118.7 2.3 %copy-done.4 = bf16[768,3072]{1,0:T(8,128)(2,1)S(1)} copy-done((bf16[768,3072]{1,0:T(8,128)(2,1)S(1)}, bf16[768,3072]{1,0:T(8,128)(2,1)}, u32[]{:S(2)}) %copy-start.4) | copy-done | bytes 4718616
  123.4 10.1 %hidden.2 = (f32[2,8,48,768]{3,2,1,0:T(8,128)S(1)}, bf16[2,8,48,768]{3,2,1,0:T(8,128)(2,1)S(1)}, bf16[2,2,2,2,2,48,3072]{6,5,4,3,2,1,0:T(8,128)(2,1)S(1)}) custom-call(s32[3]{0:T(128)S(1)} %pad_add_fusion.where, bf16[768,3072]{1,0:T(8,128)(2,1)S(1)} %copy-done.4, bf16[2,2,2,2,48,512]{5,4,3,2,1,0:T(8,128)(2,1)S(1)} %bitcast.60, ...), custom_call_target="tpu_custom_call" | custom-call | flops 7247757312 | bytes 18874368 | tf_op jit(solution)/shard_map/hidden/pallas_call | solution.py:247
  133.7 3.0 %collective-permute-start.37 = (bf16[8,16,768]{2,1,0:T(8,128)(2,1)S(1)}, bf16[8,16,768]{2,1,0:T(8,128)(2,1)S(1)}, u32[]{:S(2)}, u32[]{:S(2)}) collective-permute-start(bf16[8,16,768]{2,1,0:T(8,128)(2,1)S(1)} %fusion.7), channel_id=1, source_target_pairs={{0,8},{4,12},{8,0},{12,4},{1,9},{5,13},{9,1},{13,5},{2,10},{6,14},... | collective-permute-start | bytes 589832 | tf_op jit(solution)/shard_map/ppermute | solution.py:43
  136.7 4.7 %collective-permute-done.37 = bf16[8,16,768]{2,1,0:T(8,128)(2,1)S(1)} collective-permute-done((bf16[8,16,768]{2,1,0:T(8,128)(2,1)S(1)}, bf16[8,16,768]{2,1,0:T(8,128)(2,1)S(1)}, u32[]{:S(2)}, u32[]{:S(2)}) %collective-permute-start.37) | collective-permute-done | bytes 196640 | tf_op jit(solution)/shard_map/ppermute | solution.py:43
  141.5 4.8 %down.2.refs_0_ = bf16[768,3072]{1,0:T(8,128)(2,1)} custom-call(bf16[768,1536]{1,0:T(8,128)(2,1)S(1)} %get-tuple-element.88.at_a, bf16[768,512]{1,0:T(8,128)(2,1)S(1)} %get-tuple-element.89.at_b, bf16[1536,3072]{1,0:T(8,128)(2,1)S(1)} %bitcast.46, bf16[512,3072]{1,0:T(8,128)(2,1)S(1)} %bitcast.48), custom_call_target="tpu_custom_call" | custom-call | flops 3221225472 | bytes 5767168 | tf_op jit(solution)/shard_map/down/pallas_call | solution.py:287
  146.7 2.8 %collective-permute-start.30 = (bf16[8,48,768]{2,1,0:T(8,128)(2,1)S(1)}, bf16[8,48,768]{2,1,0:T(8,128)(2,1)S(1)}, u32[]{:S(2)}, u32[]{:S(2)}) collective-permute-start(bf16[8,48,768]{2,1,0:T(8,128)(2,1)S(1)} %fusion.3), channel_id=1, source_target_pairs={{0,8},{4,12},{8,0},{12,4},{1,9},{5,13},{9,1},{13,5},{2,10},{6,14},... | collective-permute-start | bytes 1769480 | tf_op jit(solution)/shard_map/ppermute | solution.py:43
  149.5 8.6 %down.3 = bf16[768,3072]{1,0:T(8,128)(2,1)} custom-call(bf16[768,1536]{1,0:T(8,128)(2,1)S(1)} %get-tuple-element.88.at_a, bf16[768,512]{1,0:T(8,128)(2,1)S(1)} %get-tuple-element.89.at_b, bf16[1536,3072]{1,0:T(8,128)(2,1)S(1)} %bitcast.47, bf16[512,3072]{1,0:T(8,128)(2,1)S(1)} %bitcast.49, bf16[768,3072]{1,0:T(8,128)(2,1)} %down.2.refs_0_), custom_call_target="tpu_custom_call", output_to_operand_aliasing={{}: (4, {})} | custom-call | flops 6442450944 | bytes 11534336 | tf_op jit(solution)/shard_map/down/pallas_call | solution.py:287
  158.1 3.6 %collective-permute-done.30 = bf16[8,48,768]{2,1,0:T(8,128)(2,1)S(1)} collective-permute-done((bf16[8,48,768]{2,1,0:T(8,128)(2,1)S(1)}, bf16[8,48,768]{2,1,0:T(8,128)(2,1)S(1)}, u32[]{:S(2)}, u32[]{:S(2)}) %collective-permute-start.30) | collective-permute-done | bytes 589856 | tf_op jit(solution)/shard_map/ppermute | solution.py:43
  (94 shorter events, 35.2 us)
Async XLA Ops:
  4.4 12.5 %collective-permute-start.1 = (bf16[1,64,640]{2,1,0:T(8,128)(2,1)S(1)}, bf16[1,64,640]{2,1,0:T(8,128)(2,1)S(1)}, u32[]{:S(2)}, u32[]{:S(2)}) collective-permute-start(bf16[1,64,640]{2,1,0:T(8,128)(2,1)S(1)} %get-tuple-element.48.refs_1_), channel_id=1, source_target_pairs={{0,16},{16,0},{32,48},{48,32},{64,80},{80,64},{96,112},{112,96},{1... | collective-permute-start | bytes 245768 | tf_op jit(solution)/shard_map/ppermute | solution.py:38
  6.6 10.3 %collective-permute-start.2 = (bf16[1,64,640]{2,1,0:T(8,128)(2,1)S(1)}, bf16[1,64,640]{2,1,0:T(8,128)(2,1)S(1)}, u32[]{:S(2)}, u32[]{:S(2)}) collective-permute-start(bf16[1,64,640]{2,1,0:T(8,128)(2,1)S(1)} %get-tuple-element.49.refs_2_), channel_id=1, source_target_pairs={{0,3},{1,2},{2,1},{3,0},{4,7},{5,6},{6,5},{7,4},{8,11},{9,10},{10,... | collective-permute-start | bytes 245768 | tf_op jit(solution)/shard_map/ppermute | solution.py:39
  25.7 10.5 %collective-permute-start.11 = (bf16[4,64,640]{2,1,0:T(8,128)(2,1)S(1)}, bf16[4,64,640]{2,1,0:T(8,128)(2,1)S(1)}, u32[]{:S(2)}, u32[]{:S(2)}) collective-permute-start(bf16[4,64,640]{2,1,0:T(8,128)(2,1)S(1)} %get-tuple-element.58.refs_1_), channel_id=1, source_target_pairs={{0,48},{16,32},{32,16},{48,0},{64,112},{80,96},{96,80},{112,64},{1... | collective-permute-start | bytes 983048 | tf_op jit(solution)/shard_map/ppermute | solution.py:38
  27.4 10.9 %collective-permute-start.12 = (bf16[4,64,640]{2,1,0:T(8,128)(2,1)S(1)}, bf16[4,64,640]{2,1,0:T(8,128)(2,1)S(1)}, u32[]{:S(2)}, u32[]{:S(2)}) collective-permute-start(bf16[4,64,640]{2,1,0:T(8,128)(2,1)S(1)} %get-tuple-element.59.refs_2_), channel_id=1, source_target_pairs={{0,64},{16,80},{32,96},{48,112},{64,0},{80,16},{96,32},{112,48},{1... | collective-permute-start | bytes 983048 | tf_op jit(solution)/shard_map/ppermute | solution.py:38
  31.6 8.0 %collective-permute-start.13 = (bf16[4,64,640]{2,1,0:T(8,128)(2,1)S(1)}, bf16[4,64,640]{2,1,0:T(8,128)(2,1)S(1)}, u32[]{:S(2)}, u32[]{:S(2)}) collective-permute-start(bf16[4,64,640]{2,1,0:T(8,128)(2,1)S(1)} %get-tuple-element.60.refs_3_), channel_id=1, source_target_pairs={{0,1},{1,0},{2,3},{3,2},{4,5},{5,4},{6,7},{7,6},{8,9},{9,8},{10,11... | collective-permute-start | bytes 983048 | tf_op jit(solution)/shard_map/ppermute | solution.py:39
  35.7 9.5 %collective-permute-start.21 = (bf16[256,768]{1,0:T(8,128)(2,1)S(1)}, bf16[256,768]{1,0:T(8,128)(2,1)S(1)}, u32[]{:S(2)}, u32[]{:S(2)}) collective-permute-start(bf16[256,768]{1,0:T(8,128)(2,1)S(1)} %get-tuple-element.68), channel_id=1, source_target_pairs={{0,1},{1,0},{2,3},{3,2},{4,5},{5,4},{6,7},{7,6},{8,9},{9,8},{10,11... | collective-permute-start | bytes 1179656 | tf_op jit(solution)/shard_map/ppermute | solution.py:39
  36.2 9.2 %collective-permute-start.22 = (bf16[256,768]{1,0:T(8,128)(2,1)S(1)}, bf16[256,768]{1,0:T(8,128)(2,1)S(1)}, u32[]{:S(2)}, u32[]{:S(2)}) collective-permute-start(bf16[256,768]{1,0:T(8,128)(2,1)S(1)} %get-tuple-element.69), channel_id=1, source_target_pairs={{0,3},{1,2},{2,1},{3,0},{4,7},{5,6},{6,5},{7,4},{8,11},{9,10},{10,... | collective-permute-start | bytes 1179656 | tf_op jit(solution)/shard_map/ppermute | solution.py:39
  38.3 15.8 %collective-permute-start.23 = (bf16[256,768]{1,0:T(8,128)(2,1)S(1)}, bf16[256,768]{1,0:T(8,128)(2,1)S(1)}, u32[]{:S(2)}, u32[]{:S(2)}) collective-permute-start(bf16[256,768]{1,0:T(8,128)(2,1)S(1)} %get-tuple-element.70), channel_id=1, source_target_pairs={{0,2},{1,3},{2,0},{3,1},{4,6},{5,7},{6,4},{7,5},{8,10},{9,11},{10,... | collective-permute-start | bytes 1179656 | tf_op jit(solution)/shard_map/ppermute | solution.py:39
  40.6 15.3 %collective-permute-start.15 = (bf16[8,64,512]{2,1,0:T(8,128)(2,1)S(1)}, bf16[8,64,512]{2,1,0:T(8,128)(2,1)S(1)}, u32[]{:S(2)}, u32[]{:S(2)}) collective-permute-start(bf16[8,64,512]{2,1,0:T(8,128)(2,1)S(1)} %get-tuple-element.62.refs_0_), channel_id=1, source_target_pairs={{0,48},{16,32},{32,16},{48,0},{64,112},{80,96},{96,80},{112,64},{1... | collective-permute-start | bytes 1572872 | tf_op jit(solution)/shard_map/ppermute | solution.py:38
  40.7 26.5 %collective-permute-start.16 = (bf16[8,64,640]{2,1,0:T(8,128)(2,1)S(1)}, bf16[8,64,640]{2,1,0:T(8,128)(2,1)S(1)}, u32[]{:S(2)}, u32[]{:S(2)}) collective-permute-start(bf16[8,64,640]{2,1,0:T(8,128)(2,1)S(1)} %get-tuple-element.63.refs_1_), channel_id=1, source_target_pairs={{0,64},{16,80},{32,96},{48,112},{64,0},{80,16},{96,32},{112,48},{1... | collective-permute-start | bytes 1966088 | tf_op jit(solution)/shard_map/ppermute | solution.py:38
  45.3 22.5 %collective-permute-start.17 = (bf16[8,64,640]{2,1,0:T(8,128)(2,1)S(1)}, bf16[8,64,640]{2,1,0:T(8,128)(2,1)S(1)}, u32[]{:S(2)}, u32[]{:S(2)}) collective-permute-start(bf16[8,64,640]{2,1,0:T(8,128)(2,1)S(1)} %get-tuple-element.64.refs_2_), channel_id=1, source_target_pairs={{0,1},{1,0},{2,3},{3,2},{4,5},{5,4},{6,7},{7,6},{8,9},{9,8},{10,11... | collective-permute-start | bytes 1966088 | tf_op jit(solution)/shard_map/ppermute | solution.py:39
  45.4 22.4 %collective-permute-start.18 = (bf16[8,64,640]{2,1,0:T(8,128)(2,1)S(1)}, bf16[8,64,640]{2,1,0:T(8,128)(2,1)S(1)}, u32[]{:S(2)}, u32[]{:S(2)}) collective-permute-start(bf16[8,64,640]{2,1,0:T(8,128)(2,1)S(1)} %get-tuple-element.65.refs_3_), channel_id=1, source_target_pairs={{0,16},{16,0},{32,48},{48,32},{64,80},{80,64},{96,112},{112,96},{1... | collective-permute-start | bytes 1966088 | tf_op jit(solution)/shard_map/ppermute | solution.py:38
  54.1 14.3 %collective-permute-start.19 = (bf16[8,64,640]{2,1,0:T(8,128)(2,1)S(1)}, bf16[8,64,640]{2,1,0:T(8,128)(2,1)S(1)}, u32[]{:S(2)}, u32[]{:S(2)}) collective-permute-start(bf16[8,64,640]{2,1,0:T(8,128)(2,1)S(1)} %get-tuple-element.66.refs_4_), channel_id=1, source_target_pairs={{0,3},{1,2},{2,1},{3,0},{4,7},{5,6},{6,5},{7,4},{8,11},{9,10},{10,... | collective-permute-start | bytes 1966088 | tf_op jit(solution)/shard_map/ppermute | solution.py:39
  55.9 27.0 %collective-permute-start.24 = (bf16[768,768]{1,0:T(8,128)(2,1)S(1)}, bf16[768,768]{1,0:T(8,128)(2,1)S(1)}, u32[]{:S(2)}, u32[]{:S(2)}) collective-permute-start(bf16[768,768]{1,0:T(8,128)(2,1)S(1)} %pad_maximum_fusion), channel_id=1, source_target_pairs={{0,4},{4,0},{8,12},{12,8},{1,5},{5,1},{9,13},{13,9},{2,6},{6,2},{1... | collective-permute-start | bytes 3538952 | tf_op jit(solution)/shard_map/ppermute | solution.py:43
  70.4 10.0 %collective-permute-start.34 = (bf16[16,16,640]{2,1,0:T(8,128)(2,1)S(1)}, bf16[16,16,640]{2,1,0:T(8,128)(2,1)S(1)}, u32[]{:S(2)}, u32[]{:S(2)}) collective-permute-start(bf16[16,16,640]{2,1,0:T(8,128)(2,1)S(1)} %get-tuple-element.83), channel_id=1, source_target_pairs={{0,3},{1,2},{2,1},{3,0},{4,7},{5,6},{6,5},{7,4},{8,11},{9,10},{10,... | collective-permute-start | bytes 983048 | tf_op jit(solution)/shard_map/ppermute | solution.py:39
  76.4 41.4 %collective-permute-start.25 = (bf16[16,48,640]{2,1,0:T(8,128)(2,1)S(1)}, bf16[16,48,640]{2,1,0:T(8,128)(2,1)S(1)}, u32[]{:S(2)}, u32[]{:S(2)}) collective-permute-start(bf16[16,48,640]{2,1,0:T(8,128)(2,1)S(1)} %get-tuple-element.73), channel_id=1, source_target_pairs={{0,1},{1,0},{2,3},{3,2},{4,5},{5,4},{6,7},{7,6},{8,9},{9,8},{10,11... | collective-permute-start | bytes 2949128 | tf_op jit(solution)/shard_map/ppermute | solution.py:39
  76.8 40.9 %collective-permute-start.26 = (bf16[16,48,640]{2,1,0:T(8,128)(2,1)S(1)}, bf16[16,48,640]{2,1,0:T(8,128)(2,1)S(1)}, u32[]{:S(2)}, u32[]{:S(2)}) collective-permute-start(bf16[16,48,640]{2,1,0:T(8,128)(2,1)S(1)} %get-tuple-element.74), channel_id=1, source_target_pairs={{0,16},{16,0},{32,48},{48,32},{64,80},{80,64},{96,112},{112,96},{1... | collective-permute-start | bytes 2949128 | tf_op jit(solution)/shard_map/ppermute | solution.py:38
  80.3 37.4 %collective-permute-start.27 = (bf16[16,48,640]{2,1,0:T(8,128)(2,1)S(1)}, bf16[16,48,640]{2,1,0:T(8,128)(2,1)S(1)}, u32[]{:S(2)}, u32[]{:S(2)}) collective-permute-start(bf16[16,48,640]{2,1,0:T(8,128)(2,1)S(1)} %get-tuple-element.75), channel_id=1, source_target_pairs={{0,3},{1,2},{2,1},{3,0},{4,7},{5,6},{6,5},{7,4},{8,11},{9,10},{10,... | collective-permute-start | bytes 2949128 | tf_op jit(solution)/shard_map/ppermute | solution.py:39
  82.2 36.5 %collective-permute-start.28 = (bf16[16,48,640]{2,1,0:T(8,128)(2,1)S(1)}, bf16[16,48,640]{2,1,0:T(8,128)(2,1)S(1)}, u32[]{:S(2)}, u32[]{:S(2)}) collective-permute-start(bf16[16,48,640]{2,1,0:T(8,128)(2,1)S(1)} %get-tuple-element.76), channel_id=1, source_target_pairs={{0,48},{16,32},{32,16},{48,0},{64,112},{80,96},{96,80},{112,64},{1... | collective-permute-start | bytes 2949128 | tf_op jit(solution)/shard_map/ppermute | solution.py:38
  82.9 15.1 %collective-permute-start.20 = (bf16[16,48,512]{2,1,0:T(8,128)(2,1)S(1)}, bf16[16,48,512]{2,1,0:T(8,128)(2,1)S(1)}, u32[]{:S(2)}, u32[]{:S(2)}) collective-permute-start(bf16[16,48,512]{2,1,0:T(8,128)(2,1)S(1)} %get-tuple-element.67), channel_id=1, source_target_pairs={{0,64},{16,80},{32,96},{48,112},{64,0},{80,16},{96,32},{112,48},{1... | collective-permute-start | bytes 2359304 | tf_op jit(solution)/shard_map/ppermute | solution.py:38
  98.8 34.7 %collective-permute-start.36 = (bf16[2,8,16,768]{3,2,1,0:T(8,128)(2,1)S(1)}, bf16[2,8,16,768]{3,2,1,0:T(8,128)(2,1)S(1)}, u32[]{:S(2)}, u32[]{:S(2)}) collective-permute-start(bf16[2,8,16,768]{3,2,1,0:T(8,128)(2,1)S(1)} %get-tuple-element.86), channel_id=1, source_target_pairs={{0,4},{4,0},{8,12},{12,8},{1,5},{5,1},{9,13},{13,9},{2,6},{6,2},{1... | collective-permute-start | bytes 1179656 | tf_op jit(solution)/shard_map/ppermute | solution.py:43
  133.5 12.8 %collective-permute-start.29 = (bf16[2,8,48,768]{3,2,1,0:T(8,128)(2,1)S(1)}, bf16[2,8,48,768]{3,2,1,0:T(8,128)(2,1)S(1)}, u32[]{:S(2)}, u32[]{:S(2)}) collective-permute-start(bf16[2,8,48,768]{3,2,1,0:T(8,128)(2,1)S(1)} %get-tuple-element.78), channel_id=1, source_target_pairs={{0,4},{4,0},{8,12},{12,8},{1,5},{5,1},{9,13},{13,9},{2,6},{6,2},{1... | collective-permute-start | bytes 3538952 | tf_op jit(solution)/shard_map/ppermute | solution.py:43
  133.7 7.8 %collective-permute-start.37 = (bf16[8,16,768]{2,1,0:T(8,128)(2,1)S(1)}, bf16[8,16,768]{2,1,0:T(8,128)(2,1)S(1)}, u32[]{:S(2)}, u32[]{:S(2)}) collective-permute-start(bf16[8,16,768]{2,1,0:T(8,128)(2,1)S(1)} %fusion.7), channel_id=1, source_target_pairs={{0,8},{4,12},{8,0},{12,4},{1,9},{5,13},{9,1},{13,5},{2,10},{6,14},... | collective-permute-start | bytes 589832 | tf_op jit(solution)/shard_map/ppermute | solution.py:43
  146.7 15.1 %collective-permute-start.30 = (bf16[8,48,768]{2,1,0:T(8,128)(2,1)S(1)}, bf16[8,48,768]{2,1,0:T(8,128)(2,1)S(1)}, u32[]{:S(2)}, u32[]{:S(2)}) collective-permute-start(bf16[8,48,768]{2,1,0:T(8,128)(2,1)S(1)} %fusion.3), channel_id=1, source_target_pairs={{0,8},{4,12},{8,0},{12,4},{1,9},{5,13},{9,1},{13,5},{2,10},{6,14},... | collective-permute-start | bytes 1769480 | tf_op jit(solution)/shard_map/ppermute | solution.py:43
  (25 other events, 191.3 us)

commit v3 on v2

v3 whole, which is shorter than its diff:
```python
import functools
import math

import jax
import jax.numpy as jnp
import numpy as np
from jax import lax
from jax.experimental import pallas as pl
from jax.experimental.pallas import tpu as pltpu
from jax.sharding import PartitionSpec as P

gelu_const = math.sqrt(2.0 / math.pi)

SHARDS = 32
ROWS = 64
FEATS = 3072
HID = 768
X, Y0, Y1, Z0, Z1 = 16, 4, 12, 1, 3
DIMS = (Z0, Y0, Z1, Y1, X)
WIDTHS = (512, 640, 640, 640, 640)
OFFSETS = tuple(int(v) for v in np.cumsum((0,) + WIDTHS)[:-1])
CHAINS = len(WIDTHS)
ORDERS = tuple(tuple(DIMS[(p + k) % 5] for k in range(5)) for p in range(CHAINS))
PARTS = (32, 32)
STARTS = (0, 32)


def mask_of(c):
    mask = 0
    for k in range(5):
        if c >> k & 1:
            mask ^= DIMS[k]
    return mask


def swap(x, mask):
    if mask >= 4:
        return lax.ppermute(x, "depth", [(i, i ^ (mask >> 2)) for i in range(8)])
    return lax.ppermute(x, "col", [(i, i ^ mask) for i in range(4)])


def swap_row(x, mask):
    return lax.ppermute(x, "row", [(i, i ^ mask) for i in range(4)])


def in_hbm(x):
    return pltpu.with_memory_space_constraint(x, pltpu.HBM)


def params(mib):
    return pltpu.CompilerParams(vmem_limit_bytes=mib * 1024 * 1024)


TINY = pl.CostEstimate(flops=1, bytes_accessed=1, transcendentals=0)
ANY = pl.BlockSpec(memory_space=pl.ANY)
VMEM = pl.BlockSpec(memory_space=pltpu.VMEM)
SMEM = pl.BlockSpec(memory_space=pltpu.SMEM)


def cut_kernel(where, grad_out, pre, *refs):
    outs, chunks, sem = refs[:CHAINS], refs[CHAINS], refs[-1]
    row = where[0]
    copies = [
        pltpu.make_async_copy(grad_out.at[:, pl.ds(OFFSETS[p], WIDTHS[p])], outs[p].at[0], sem.at[p])
        for p in range(CHAINS)
    ]
    half = SHARDS * ROWS // 8
    for z in range(4):
        here = pre.at[pl.ds(pl.multiple_of(row % 2 * half, half), half), pl.ds(z * HID, HID)]
        copies.append(pltpu.make_async_copy(here, chunks.at[z], sem.at[CHAINS + z]))
    for c in copies:
        c.start()
    for c in copies:
        c.wait()


def cut_call(where, grad_out, pre):
    return pl.pallas_call(
        cut_kernel,
        out_shape=[jax.ShapeDtypeStruct((1, ROWS, w), jnp.bfloat16) for w in WIDTHS]
        + [jax.ShapeDtypeStruct((4, SHARDS * ROWS // 8, HID), jnp.bfloat16)],
        in_specs=[SMEM, ANY, ANY],
        out_specs=[ANY] * (CHAINS + 1),
        scratch_shapes=[pltpu.SemaphoreType.DMA((CHAINS + 4,))],
        compiler_params=params(1),
        cost_estimate=TINY,
        name="cut",
    )(where, in_hbm(grad_out), in_hbm(pre))


def grow_kernel(rows, *refs):
    own, got, sem = refs[:CHAINS], refs[CHAINS : 2 * CHAINS], refs[-1]
    outs = refs[-1 - len(rows) * CHAINS : -1]
    copies = []
    for part, (at, n) in enumerate(rows):
        for p in range(CHAINS):
            out = outs[part * CHAINS + p]
            blocks = own[p].shape[0]
            for side, src in enumerate((own[p], got[p])):
                copies.append((src.at[:, pl.ds(at, n)], out.at[pl.ds(side * blocks, blocks)]))
    copies = [pltpu.make_async_copy(*c, sem.at[i]) for i, c in enumerate(copies)]
    for c in copies:
        c.start()
    for c in copies:
        c.wait()


def grow_call(own, got, rows=((0, ROWS),), after=()):
    blocks = own[0].shape[0]
    shape = pltpu.HBM if len(rows) > 1 else jax.ShapeDtypeStruct
    return pl.pallas_call(
        functools.partial(grow_kernel, rows),
        out_shape=[shape((2 * blocks, n, w), jnp.bfloat16) for _, n in rows for w in WIDTHS],
        in_specs=[ANY] * (2 * CHAINS + len(after)),
        out_specs=[ANY] * (len(rows) * CHAINS),
        scratch_shapes=[pltpu.SemaphoreType.DMA((2 * CHAINS * len(rows),))],
        compiler_params=params(1),
        cost_estimate=TINY,
        name="grow",
    )(*own, *got, *after)


def gelu_kernel(where, table, fetched, other, *refs):
    outs, (buf, sems), acts = refs[:4], refs[4:6], refs[6:]
    act_t, slopes = outs[:2], outs[2:]
    row, mine = where[0], where[2]
    core = row % 2
    quarter, half = SHARDS * ROWS // 4, SHARDS * ROWS // 8
    copies = []
    for z in range(4):
        for side, src in ((core, fetched), (1 - core, other)):
            at = pl.multiple_of(z * quarter + side * half, half)
            copies.append(pltpu.make_async_copy(src.at[z], buf.at[pl.ds(at, half)], sems.at[len(copies)]))
    for c in copies:
        c.start()
    for c in copies:
        c.wait()

    def one_shard(s, carry):
        v = buf[pl.ds(pl.multiple_of((mine ^ table[s]) * ROWS, ROWS), ROWS), :].astype(jnp.float32)
        bend = jnp.tanh(gelu_const * (v + 0.044715 * v * v * v))
        a = (0.5 * v * (1.0 + bend)).astype(jnp.bfloat16)
        for part in range(2):
            n, at = PARTS[part], STARTS[part]
            acts[part][pl.ds(pl.multiple_of(s * n, 16), n), :] = a[at : at + n]
        return carry

    lax.fori_loop(0, SHARDS, one_shard, 0)

    def one_slope(s, carry):
        at_row = pl.multiple_of(row * quarter + s * ROWS, ROWS)
        v = buf[pl.ds(at_row, ROWS), :].astype(jnp.float32)
        bend = jnp.tanh(gelu_const * (v + 0.044715 * v * v * v))
        d = 0.5 * (1.0 + bend) + 0.5 * v * (1.0 - bend * bend) * gelu_const * (1.0 + 3.0 * 0.044715 * v * v)
        for part in range(2):
            n, at = PARTS[part], STARTS[part]
            slopes[part][s] = d[at : at + n]
        return carry

    lax.fori_loop(0, SHARDS // 4, one_slope, 0)

    for part in range(2):

        def one_turn(j, carry, part=part):
            at = pl.multiple_of(j * 128, 128)
            act_t[part][:, pl.ds(at, 128)] = acts[part][pl.ds(at, 128), :].T
            return carry

        lax.fori_loop(0, SHARDS * PARTS[part] // 128, one_turn, 0)


def gelu_call(where, table, fetched, other):
    tokens = [SHARDS * n for n in PARTS]
    return pl.pallas_call(
        gelu_kernel,
        out_shape=[jax.ShapeDtypeStruct((HID, t), jnp.bfloat16) for t in tokens]
        + [jax.ShapeDtypeStruct((SHARDS // 4, n, HID), jnp.float32) for n in PARTS],
        in_specs=[SMEM, SMEM, ANY, ANY],
        out_specs=[VMEM] * 4,
        scratch_shapes=[pltpu.VMEM((SHARDS * ROWS, HID), jnp.bfloat16), pltpu.SemaphoreType.DMA((8,))]
        + [pltpu.VMEM((t, HID), jnp.bfloat16) for t in tokens],
        compiler_params=params(20),
        cost_estimate=TINY,
        name="gelu",
    )(where, table, fetched, other)


def pieces(p, side):
    every = slice(None)
    if p == 0:
        return [((every,) * 4, (side,) + (every,) * 4)]
    if p == 1:
        return [((every,) * 4, (every,) * 4 + (side,))]
    if p == 2:
        return [((i,) + (every,) * 3, (every,) * 3 + (side, i)) for i in range(2)]
    if p == 3:
        return [((every,) * 2 + (i, j), (i, j, side) + (every,) * 2) for i in range(2) for j in range(2)]
    return [((every,) * 3 + (i,), (i, side) + (every,) * 3) for i in range(2)]


def hidden_kernel(n, where, w_far, *refs):
    blocks = refs[: 2 * CHAINS]
    keep, send, gathered, g, w, hs, sems = refs[-7:]
    row, mine = where[0], where[2]
    per = SHARDS // 4
    weights = pltpu.make_async_copy(w_far, w, sems.at[0])
    weights.start()
    for p in range(CHAINS):
        for side in range(2):
            for src, dst in pieces(p, side):
                pltpu.make_async_copy(
                    blocks[2 * p + side].at[src],
                    g.at[dst + (slice(None), pl.ds(OFFSETS[p], WIDTHS[p]))],
                    sems.at[1],
                ).start()
    pltpu.make_async_copy(g, g, sems.at[1]).wait()
    weights.wait()
    out = pltpu.make_async_copy(g, gathered, sems.at[2])
    out.start()
    for i in range(2):
        h = lax.dot_general(
            g[i].reshape(2 * per * n, FEATS), w[...], (((1,), (1,)), ((), ())), preferred_element_type=jnp.float32
        )
        hs[i] = h.reshape(2, per, n, HID)
    for a, b in ((1, 1), (0, 1), (1, 0), (0, 0)):
        off_x = (mine // 16) ^ (row // 2) ^ a
        off_y = (mine // 8 % 2) ^ (row % 2) ^ b
        for j in range(per):
            slot = (mine % 8) ^ (mask_of(j) % 8) ^ (off_y * 4)
            if b:
                send[a, slot] = hs[off_x, off_y, j].astype(jnp.bfloat16)
            else:
                keep[a, slot] = hs[off_x, off_y, j]
    out.wait()


def hidden_call(part, where, w, blocks, after=()):
    n = PARTS[part]
    per = SHARDS // 4
    return pl.pallas_call(
        functools.partial(hidden_kernel, n),
        out_shape=[
            jax.ShapeDtypeStruct((2, per, n, HID), jnp.float32),
            jax.ShapeDtypeStruct((2, per, n, HID), jnp.bfloat16),
            pltpu.HBM((2,) * 5 + (n, FEATS), jnp.bfloat16),
        ],
        in_specs=[SMEM] + [ANY] * (1 + 2 * CHAINS + len(after)),
        out_specs=[VMEM, VMEM, ANY],
        scratch_shapes=[
            pltpu.VMEM((2,) * 5 + (n, FEATS), jnp.bfloat16),
            pltpu.VMEM((HID, FEATS), jnp.bfloat16),
            pltpu.VMEM((2, 2, per, n, HID), jnp.float32),
            pltpu.SemaphoreType.DMA((3,)),
        ],
        compiler_params=params(14 + n // 2),
        cost_estimate=pl.CostEstimate(
            flops=2 * SHARDS * n * FEATS * HID, bytes_accessed=SHARDS * n * FEATS * 4, transcendentals=0
        ),
        name="hidden",
    )(where, w, *(f(b.reshape((2,) * 4 + b.shape[1:])) for b, f in zip(blocks, (in_hbm, lambda x: x) * CHAINS)), *after)


def total_kernel(keep, got, *refs):
    mine, far = refs[-2:]
    mine[...] = keep[0] + got[0].astype(jnp.float32)
    far[...] = (keep[1] + got[1].astype(jnp.float32)).astype(jnp.bfloat16)


def total_call(keep, got, after=()):
    return pl.pallas_call(
        total_kernel,
        out_shape=[
            jax.ShapeDtypeStruct(keep.shape[1:], jnp.float32),
            jax.ShapeDtypeStruct(keep.shape[1:], jnp.bfloat16),
        ],
        in_specs=[VMEM, VMEM] + [ANY] * len(after),
        out_specs=[VMEM, VMEM],
        compiler_params=params(8),
        cost_estimate=TINY,
        name="total",
    )(keep, got, *after)


def down_kernel(at_a, at_b, g_a, g_b, *refs):
    out = refs[-1]
    acc = jnp.dot(at_a[...], g_a[...], preferred_element_type=jnp.float32)
    acc += jnp.dot(at_b[...], g_b[...], preferred_element_type=jnp.float32)
    out[...] = acc.astype(jnp.bfloat16)


def down_call(acts, gathered, first, count, base=None):
    wide = 512
    tokens = [SHARDS * n for n in PARTS]
    in_specs = [pl.BlockSpec((HID, t), lambda j: (0, 0)) for t in tokens]
    in_specs += [pl.BlockSpec((t, wide), lambda j: (0, j + first)) for t in tokens]
    args = [*acts, *(in_hbm(g.reshape(t, FEATS)) for g, t in zip(gathered, tokens))]
    aliases = {}
    if base is not None:
        in_specs.append(ANY)
        args.append(in_hbm(base))
        aliases = {4: 0}
    return pl.pallas_call(
        down_kernel,
        grid=(count,),
        out_shape=pltpu.HBM((HID, FEATS), jnp.bfloat16),
        in_specs=in_specs,
        out_specs=pl.BlockSpec((HID, wide), lambda j: (0, j + first)),
        input_output_aliases=aliases,
        compiler_params=params(24),
        cost_estimate=pl.CostEstimate(
            flops=2 * 2048 * HID * wide * count, bytes_accessed=count * wide * 2 * (2048 + HID), transcendentals=0
        ),
        name="down",
    )(*args)


def local(grad_out, pre_act, w_down):
    depth, row, col = (lax.axis_index(a) for a in ("depth", "row", "col"))
    where = jnp.stack([row, col, depth * 4 + col]).astype(jnp.int32)
    table = jnp.asarray([mask_of(c) for c in range(SHARDS)], jnp.int32)

    *blocks, chunks = cut_call(where, grad_out, pre_act)
    fetched = lax.all_to_all(chunks, "col", split_axis=0, concat_axis=0, tiled=True)
    got = [swap(blocks[p], ORDERS[p][0]) for p in range(CHAINS)]
    blocks = grow_call(blocks, got)
    got = [swap(blocks[p], ORDERS[p][1]) for p in range(CHAINS)]
    blocks = grow_call(blocks, got, after=(fetched,))
    got = [swap(blocks[p], ORDERS[p][2]) for p in range(CHAINS)]
    other = swap_row(fetched, 1)
    blocks = grow_call(blocks, got, after=(other,))
    got = [swap(blocks[p], ORDERS[p][3]) for p in range(CHAINS)]
    act_a, act_b, slope_a, slope_b = gelu_call(where, table, fetched, other)
    grown = grow_call(blocks, got, tuple(zip(STARTS, PARTS)), after=(slope_a,))
    own = grown[:CHAINS], grown[CHAINS:]
    came = [[swap(own[part][p], ORDERS[p][4]) for p in range(CHAINS)] for part in range(2)]

    pairs = [[b for p in range(CHAINS) for b in (own[part][p], came[part][p])] for part in range(2)]
    keep_a, send_a, g_a = hidden_call(0, where, w_down, pairs[0])
    keep_b, send_b, g_b = hidden_call(1, where, w_down, pairs[1], after=(keep_a,))
    mine_a, far_a = total_call(keep_a, swap_row(send_a, 1), after=(keep_b,))
    far_a = swap_row(far_a, 2)
    grad_down = down_call((act_a, act_b), (g_a, g_b), 0, 2)
    mine_b, far_b = total_call(keep_b, swap_row(send_b, 1), after=(in_hbm(grad_down),))
    far_b = swap_row(far_b, 2)
    grad_down = down_call((act_a, act_b), (g_a, g_b), 2, 4, grad_down)
    done = (mine_a, far_a), (mine_b, far_b)
    parts = [
        ((mine + far.astype(jnp.float32)) * slope).astype(jnp.bfloat16)
        for (mine, far), slope in zip(done, (slope_a, slope_b))
    ]
    grad_pre = jnp.concatenate(parts, 1).reshape(512, HID)
    return (grad_pre, grad_down)


def solution(mesh):
    placed = (P(("depth", "col"), "row"), P("col", "depth"), P(("depth", "col"), "row"))
    return jax.shard_map(
        local,
        mesh=mesh,
        in_specs=placed,
        out_specs=(P("row", ("depth", "col")), P(("depth", "col"), "row")),
        check_vma=False,
    )
```

time: 164 us -> 157 us (0.957)
  blocking collectives: 0 us -> 25.5 us
  starting transfers between devices: 65.8 us -> 45 us
  local copies, waits for them, and re-layouts: 9.47 us -> 0.01 us
  waiting for transfers between devices: 40.8 us -> 35.1 us
  Pallas kernels: 44.2 us -> 48.8 us
    all_to_all x0 -> x1, blocking collectives: none -> 25.5 us  [local(): lax.all_to_all(chunks, 'col', split_axis=0, concat_axis=0, tiled=True)]
    ppermute x15 -> x12, waiting for transfers between devices: 25.1 us -> 6.72 us  [swap(): return lax.ppermute(x, 'col', [(i, i ^ mask) for i in range(4)])]
    ppermute x5, starting transfers between devices: 36.1 us -> 19 us  [swap_row(): return lax.ppermute(x, 'row', [(i, i ^ mask) for i in range(4)])]
    ppermute x18, waiting for transfers between devices: 7.34 us -> 21.3 us  [swap(): return lax.ppermute(x, 'depth', [(i, i ^ mask >> 2) for i in range(8)])]
    unnamed x22 -> x6, local copies, waits for them, and re-layouts: 9.39 us -> 0.01 us
    ppermute x15 -> x12, starting transfers between devices: 16.6 us -> 9.96 us  [swap(): return lax.ppermute(x, 'col', [(i, i ^ mask) for i in range(4)])]
    pallas_call x6 -> x8, Pallas kernels: 18.6 us -> 23 us  [the longest x2 15.8 us: down_call(): pl.pallas_call(down_kernel, grid=(count,), out_shape=pltpu.HBM((HID, FEAT...]
    ppermute x18, starting transfers between devices: 13 us -> 16.1 us  [swap(): return lax.ppermute(x, 'depth', [(i, i ^ mask >> 2) for i in range(8)])]
  transfers between devices with their start and end apart: 38 -> 35, of which waited for: 15 -> 17; matrix products, arithmetic and copies ran while one was open for 0% -> 0% of each run, Pallas kernels for 25% -> 27%
where the time goes in v3:
time: 157 us; the launch traced here: 156 us
  Pallas kernels  48.8 us (31%)
  starting transfers between devices  45 us (29%)
  waiting for transfers between devices  35.1 us (22%)
  blocking collectives  25.5 us (16%)
    all_to_all x1, blocking collectives, local(): lax.all_to_all(chunks, 'col', split_axis=0, concat_axis=0, tiled=True)  25.5 us
    ppermute x18, waiting for transfers between devices, swap(): return lax.ppermute(x, 'depth', [(i, i ^ mask >> 2) for i in range(8)])  21.3 us
    ppermute x5, starting transfers between devices, swap_row(): return lax.ppermute(x, 'row', [(i, i ^ mask) for i in range(4)])  19 us
    ppermute x18, starting transfers between devices, swap(): return lax.ppermute(x, 'depth', [(i, i ^ mask >> 2) for i in range(8)])  16.1 us
    pallas_call x2, Pallas kernels, hidden_call(): pl.pallas_call(functools.partial(hidden_kernel, n), out_shape=[jax.ShapeD...  16 us
    pallas_call x2, Pallas kernels, down_call(): pl.pallas_call(down_kernel, grid=(count,), out_shape=pltpu.HBM((HID, FEAT...  15.8 us
    ppermute x12, starting transfers between devices, swap(): return lax.ppermute(x, 'col', [(i, i ^ mask) for i in range(4)])  9.96 us
    pallas_call x1, Pallas kernels, gelu_call(): pl.pallas_call(gelu_kernel, out_shape=[jax.ShapeDtypeStruct((HID, t), jnp...  7.57 us
  transfers between devices with their start and end apart: 35, of which 17 were waited for; matrix products, arithmetic and copies ran while one was open for 0% of the time, Pallas kernels for 27%

profile of v3, /device:TPU:1, one launch (start us, length us, event | category | flops | bytes accessed | tf_op | source)
XLA Modules:
  0.0 156.4 jit_solution(11740068725210091879)
XLA Ops:
  0.7 2.2 %cut.1 = (bf16[1,64,512]{2,1,0:T(8,128)(2,1)S(1)}, bf16[1,64,640]{2,1,0:T(8,128)(2,1)S(1)}, bf16[1,64,640]{2,1,0:T(8,128)(2,1)S(1)}, bf16[1,64,640]{2,1,0:T(8,12...) custom-call(s32[3]{0:T(128)S(1)} %pad_add_fusion.where, bf16[64,3072]{1,0:T(8,128)(2,1)} %grad_out.1, ...), custom_call_target="tpu_custom_call" | custom-call | flops 1 | bytes 1 | tf_op jit(solution)/shard_map/cut/pallas_call | solution.py:78
  2.9 25.5 %all_to_all.5.refs_10_.fetched = bf16[4,256,768]{2,1,0:T(8,128)(2,1)S(1)} all-to-all(bf16[4,256,768]{2,1,0:T(8,128)(2,1)S(1)} %get-tuple-element.57), channel_id=1, replica_groups=mesh['depth'=8,'row'=4,'col'=4] {'col'}, dimensions={0} | all-to-all | bytes 3145728 | tf_op jit(solution)/shard_map/all_to_all | solution.py:323
  28.4 1.9 %collective-permute-start.15 = (bf16[4,256,768]{2,1,0:T(8,128)(2,1)S(1)}, bf16[4,256,768]{2,1,0:T(8,128)(2,1)S(1)}, u32[]{:S(2)}, u32[]{:S(2)}) collective-permute-start(bf16[4,256,768]{2,1,0:T(8,128)(2,1)S(1)} %all_to_all.5.refs_10_.fetched), channel_id=1, source_target_pairs={{0,4},{4,0},{8,12},{12,8},{1,5},{5,1},{9,13},{13,9},{2,6},{6,2},{1... | collective-permute-start | bytes 4718600 | tf_op jit(solution)/shard_map/ppermute | solution.py:43
  32.4 1.9 %collective-permute-start.3 = (bf16[1,64,640]{2,1,0:T(8,128)(2,1)S(1)}, bf16[1,64,640]{2,1,0:T(8,128)(2,1)S(1)}, u32[]{:S(2)}, u32[]{:S(2)}) collective-permute-start(bf16[1,64,640]{2,1,0:T(8,128)(2,1)S(1)} %get-tuple-element.50.refs_3_), channel_id=1, source_target_pairs={{0,48},{16,32},{32,16},{48,0},{64,112},{80,96},{96,80},{112,64},{1... | collective-permute-start | bytes 245768 | tf_op jit(solution)/shard_map/ppermute | solution.py:38
  41.3 1.5 collective-permute-start.7
  45.1 1.8 %collective-permute-done.7.refs_7_ = bf16[2,64,640]{2,1,0:T(8,128)(2,1)S(1)} collective-permute-done((bf16[2,64,640]{2,1,0:T(8,128)(2,1)S(1)}, bf16[2,64,640]{2,1,0:T(8,128)(2,1)S(1)}, u32[]{:S(2)}, u32[]{:S(2)}) %collective-permute-start.7) | collective-permute-done | bytes 163872 | tf_op jit(solution)/shard_map/ppermute | solution.py:38
  48.5 2.1 %grow.5 = (bf16[4,64,512]{2,1,0:T(8,128)(2,1)S(1)}, bf16[4,64,640]{2,1,0:T(8,128)(2,1)S(1)}, bf16[4,64,640]{2,1,0:T(8,128)(2,1)S(1)}, bf16[4,64,640]{2,1,0:T(8,128)(2,1)S(1)}, bf16[4,64,640]{2,1,0:T(8,128)(2,1)S(1)}) custom-call(bf16[2,64,512]{2,1,0:T(8,128)(2,1)S(1)} %get-tuple-element.52.refs_0_, bf16[2,64,640]{2,1,0:T(8,128)(2,1)S(1)} %get-tuple-element.53.refs_1_, ...), custom_call_target="tpu_custom_call" | custom-call | flops 1 | bytes 1 | tf_op jit(solution)/shard_map/grow/pallas_call | solution.py:111
  50.6 1.7 %collective-permute-start.10 = (bf16[4,64,512]{2,1,0:T(8,128)(2,1)S(1)}, bf16[4,64,512]{2,1,0:T(8,128)(2,1)S(1)}, u32[]{:S(2)}, u32[]{:S(2)}) collective-permute-start(bf16[4,64,512]{2,1,0:T(8,128)(2,1)S(1)} %get-tuple-element.58.refs_0_), channel_id=1, source_target_pairs={{0,3},{1,2},{2,1},{3,0},{4,7},{5,6},{6,5},{7,4},{8,11},{9,10},{10,... | collective-permute-start | bytes 786440 | tf_op jit(solution)/shard_map/ppermute | solution.py:39
  53.8 3.3 %collective-permute-done.10.refs_5_ = bf16[4,64,512]{2,1,0:T(8,128)(2,1)S(1)} collective-permute-done((bf16[4,64,512]{2,1,0:T(8,128)(2,1)S(1)}, bf16[4,64,512]{2,1,0:T(8,128)(2,1)S(1)}, u32[]{:S(2)}, u32[]{:S(2)}) %collective-permute-start.10) | collective-permute-done | bytes 262176 | tf_op jit(solution)/shard_map/ppermute | solution.py:39
  57.2 2.4 %collective-permute-done.11.refs_6_ = bf16[4,64,640]{2,1,0:T(8,128)(2,1)S(1)} collective-permute-done((bf16[4,64,640]{2,1,0:T(8,128)(2,1)S(1)}, bf16[4,64,640]{2,1,0:T(8,128)(2,1)S(1)}, u32[]{:S(2)}, u32[]{:S(2)}) %collective-permute-start.11) | collective-permute-done | bytes 327712 | tf_op jit(solution)/shard_map/ppermute | solution.py:38
  60.0 3.3 %collective-permute-done.14.refs_9_ = bf16[4,64,640]{2,1,0:T(8,128)(2,1)S(1)} collective-permute-done((bf16[4,64,640]{2,1,0:T(8,128)(2,1)S(1)}, bf16[4,64,640]{2,1,0:T(8,128)(2,1)S(1)}, u32[]{:S(2)}, u32[]{:S(2)}) %collective-permute-start.14) | collective-permute-done | bytes 327712 | tf_op jit(solution)/shard_map/ppermute | solution.py:38
  65.1 1.7 %collective-permute-start.20 = (bf16[8,64,640]{2,1,0:T(8,128)(2,1)S(1)}, bf16[8,64,640]{2,1,0:T(8,128)(2,1)S(1)}, u32[]{:S(2)}, u32[]{:S(2)}) collective-permute-start(bf16[8,64,640]{2,1,0:T(8,128)(2,1)S(1)} %get-tuple-element.67.refs_4_), channel_id=1, source_target_pairs={{0,3},{1,2},{2,1},{3,0},{4,7},{5,6},{6,5},{7,4},{8,11},{9,10},{10,... | collective-permute-start | bytes 1966088 | tf_op jit(solution)/shard_map/ppermute | solution.py:39
  68.2 7.6 %gelu.1 = (bf16[768,1024]{1,0:T(8,128)(2,1)S(1)}, bf16[768,1024]{1,0:T(8,128)(2,1)S(1)}, f32[8,32,768]{2,1,0:T(8,128)S(1)}, f32[8,32,768]{2,1,0:T(8,128)S(1)}) custom-call(s32[3]{0:T(128)S(1)} %pad_add_fusion.where, s32[32]{0:T(128)S(1)} %copy-done, bf16[4,256,768]{2,1,0:T(8,128)(2,1)S(1)} %all_to_all.5.refs_10_.fetched, ...), custom_call_target="tpu_custom_call" | custom-call | flops 1 | bytes 1 | tf_op jit(solution)/shard_map/gelu/pallas_call | solution.py:174
  76.6 2.8 %grow.7 = (bf16[16,32,512]{2,1,0:T(8,128)(2,1)}, bf16[16,32,640]{2,1,0:T(8,128)(2,1)}, bf16[16,32,640]{2,1,0:T(8,128)(2,1)}, bf16[16,32,640]{2,1,0:T(8,128)(2,1)...) custom-call(bf16[8,64,512]{2,1,0:T(8,128)(2,1)S(1)} %get-tuple-eleme, ...), custom_call_target="tpu_custom_call" | custom-call | flops 1 | bytes 1 | tf_op jit(solution)/shard_map/grow/pallas_call | solution.py:111
  80.2 1.9 %collective-permute-start.24 = (bf16[16,32,640]{2,1,0:T(8,128)(2,1)}, bf16[16,32,640]{2,1,0:T(8,128)(2,1)S(1)}, u32[]{:S(2)}, u32[]{:S(2)}) collective-permute-start(bf16[16,32,640]{2,1,0:T(8,128)(2,1)} %get-tuple-element.72), channel_id=1, source_target_pairs={{0,3},{1,2},{2,1},{3,0},{4,7},{5,6},{6,5},{7,4},{8,11},{9,10},{10,... | collective-permute-start | bytes 1966088 | tf_op jit(solution)/shard_map/ppermute | solution.py:39
  83.7 6.7 %collective-permute-done.21 = bf16[16,32,512]{2,1,0:T(8,128)(2,1)S(1)} collective-permute-done((bf16[16,32,512]{2,1,0:T(8,128)(2,1)}, bf16[16,32,512]{2,1,0:T(8,128)(2,1)S(1)}, u32[]{:S(2)}, u32[]{:S(2)}) %collective-permute-start.21) | collective-permute-done | bytes 524320 | tf_op jit(solution)/shard_map/ppermute | solution.py:38
  94.9 8.0 %hidden.2 = (f32[2,8,32,768]{3,2,1,0:T(8,128)S(1)}, bf16[2,8,32,768]{3,2,1,0:T(8,128)(2,1)S(1)}, bf16[2,2,2,2,2,32,3072]{6,5,4,3,2,1,0:T(8,128)(2,1)}) custom-call(s32[3]{0:T(128)S(1)} %pad_add_fusion.where, bf16[768,3072]{1,0:T(8,128)(2,1)S(1)} %bitcast.27, bf16[2,2,2,2,32,512]{5,4,3,2,1,0:T(8,128)(2,1)} %bitcast.52, ...), custom_call_target="tpu_custom_call" | custom-call | flops 4831838208 | bytes 12582912 | tf_op jit(solution)/shard_map/hidden/pallas_call | solution.py:240
  102.9 4.0 %collective-permute-done.27 = bf16[16,32,512]{2,1,0:T(8,128)(2,1)S(1)} collective-permute-done((bf16[16,32,512]{2,1,0:T(8,128)(2,1)}, bf16[16,32,512]{2,1,0:T(8,128)(2,1)S(1)}, u32[]{:S(2)}, u32[]{:S(2)}) %collective-permute-start.27) | collective-permute-done | bytes 524320 | tf_op jit(solution)/shard_map/ppermute | solution.py:38
  106.9 13.9 %collective-permute-start.26 = (bf16[2,8,32,768]{3,2,1,0:T(8,128)(2,1)S(1)}, bf16[2,8,32,768]{3,2,1,0:T(8,128)(2,1)S(1)}, u32[]{:S(2)}, u32[]{:S(2)}) collective-permute-start(bf16[2,8,32,768]{3,2,1,0:T(8,128)(2,1)S(1)} %get-tuple-element.75), channel_id=1, source_target_pairs={{0,4},{4,0},{8,12},{12,8},{1,5},{5,1},{9,13},{13,9},{2,6},{6,2},{1... | collective-permute-start | bytes 2359304 | tf_op jit(solution)/shard_map/ppermute | solution.py:43
  120.8 8.0 %hidden.3 = (f32[2,8,32,768]{3,2,1,0:T(8,128)S(1)}, bf16[2,8,32,768]{3,2,1,0:T(8,128)(2,1)S(1)}, bf16[2,2,2,2,2,32,3072]{6,5,4,3,2,1,0:T(8,128)(2,1)}) custom-call(s32[3]{0:T(128)S(1)} %pad_add_fusion.where, bf16[768,3072]{1,0:T(8,128)(2,1)S(1)} %bitcast.27, bf16[2,2,2,2,32,512]{5,4,3,2,1,0:T(8,128)(2,1)} %bitcast.51, ...), custom_call_target="tpu_custom_call" | custom-call | flops 4831838208 | bytes 12582912 | tf_op jit(solution)/shard_map/hidden/pallas_call | solution.py:240
  128.9 6.1 %down.2.refs_0_ = bf16[768,3072]{1,0:T(8,128)(2,1)} custom-call(bf16[768,1024]{1,0:T(8,128)(2,1)S(1)} %get-tuple-element.85.at_a, bf16[768,1024]{1,0:T(8,128)(2,1)S(1)} %get-tuple-element.86.at_b, bf16[1024,3072]{1,0:T(8,128)(2,1)} %bitcast.38, bf16[1024,3072]{1,0:T(8,128)(2,1)} %bitcast.40), custom_call_target="tpu_custom_call" | custom-call | flops 3221225472 | bytes 5767168 | tf_op jit(solution)/shard_map/down/pallas_call | solution.py:302
  135.1 2.4 %collective-permute-start.32 = (bf16[8,32,768]{2,1,0:T(8,128)(2,1)S(1)}, bf16[8,32,768]{2,1,0:T(8,128)(2,1)S(1)}, u32[]{:S(2)}, u32[]{:S(2)}) collective-permute-start(bf16[8,32,768]{2,1,0:T(8,128)(2,1)S(1)} %get-tuple-element.83), channel_id=1, source_target_pairs={{0,8},{4,12},{8,0},{12,4},{1,9},{5,13},{9,1},{13,5},{2,10},{6,14},... | collective-permute-start | bytes 1179656 | tf_op jit(solution)/shard_map/ppermute | solution.py:43
  138.4 9.7 %down.3 = bf16[768,3072]{1,0:T(8,128)(2,1)} custom-call(bf16[768,1024]{1,0:T(8,128)(2,1)S(1)} %get-tuple-element.85.at_a, bf16[768,1024]{1,0:T(8,128)(2,1)S(1)} %get-tuple-element.86.at_b, bf16[1024,3072]{1,0:T(8,128)(2,1)} %bitcast.39, bf16[1024,3072]{1,0:T(8,128)(2,1)} %bitcast.41, bf16[768,3072]{1,0:T(8,128)(2,1)} %down.2.refs_0_), custom_call_target="tpu_custom_call", output_to_operand_aliasing={{}: (4, {})} | custom-call | flops 6442450944 | bytes 11534336 | tf_op jit(solution)/shard_map/down/pallas_call | solution.py:302
  148.2 7.1 %collective-permute-done.34 = bf16[8,32,768]{2,1,0:T(8,128)(2,1)S(1)} collective-permute-done((bf16[8,32,768]{2,1,0:T(8,128)(2,1)S(1)}, bf16[8,32,768]{2,1,0:T(8,128)(2,1)S(1)}, u32[]{:S(2)}, u32[]{:S(2)}) %collective-permute-start.34) | collective-permute-done | bytes 393248 | tf_op jit(solution)/shard_map/ppermute | solution.py:43
  (70 shorter events, 28.1 us)
Async XLA Ops:
  28.4 35.0 %collective-permute-start.15 = (bf16[4,256,768]{2,1,0:T(8,128)(2,1)S(1)}, bf16[4,256,768]{2,1,0:T(8,128)(2,1)S(1)}, u32[]{:S(2)}, u32[]{:S(2)}) collective-permute-start(bf16[4,256,768]{2,1,0:T(8,128)(2,1)S(1)} %all_to_all.5.refs_10_.fetched), channel_id=1, source_target_pairs={{0,4},{4,0},{8,12},{12,8},{1,5},{5,1},{9,13},{13,9},{2,6},{6,2},{1... | collective-permute-start | bytes 4718600 | tf_op jit(solution)/shard_map/ppermute | solution.py:43
  50.6 6.5 %collective-permute-start.10 = (bf16[4,64,512]{2,1,0:T(8,128)(2,1)S(1)}, bf16[4,64,512]{2,1,0:T(8,128)(2,1)S(1)}, u32[]{:S(2)}, u32[]{:S(2)}) collective-permute-start(bf16[4,64,512]{2,1,0:T(8,128)(2,1)S(1)} %get-tuple-element.58.refs_0_), channel_id=1, source_target_pairs={{0,3},{1,2},{2,1},{3,0},{4,7},{5,6},{6,5},{7,4},{8,11},{9,10},{10,... | collective-permute-start | bytes 786440 | tf_op jit(solution)/shard_map/ppermute | solution.py:39
  52.2 7.4 %collective-permute-start.11 = (bf16[4,64,640]{2,1,0:T(8,128)(2,1)S(1)}, bf16[4,64,640]{2,1,0:T(8,128)(2,1)S(1)}, u32[]{:S(2)}, u32[]{:S(2)}) collective-permute-start(bf16[4,64,640]{2,1,0:T(8,128)(2,1)S(1)} %get-tuple-element.59.refs_1_), channel_id=1, source_target_pairs={{0,48},{16,32},{32,16},{48,0},{64,112},{80,96},{96,80},{112,64},{1... | collective-permute-start | bytes 983048 | tf_op jit(solution)/shard_map/ppermute | solution.py:38
  52.9 6.8 %collective-permute-start.12 = (bf16[4,64,640]{2,1,0:T(8,128)(2,1)S(1)}, bf16[4,64,640]{2,1,0:T(8,128)(2,1)S(1)}, u32[]{:S(2)}, u32[]{:S(2)}) collective-permute-start(bf16[4,64,640]{2,1,0:T(8,128)(2,1)S(1)} %get-tuple-element.60.refs_2_), channel_id=1, source_target_pairs={{0,64},{16,80},{32,96},{48,112},{64,0},{80,16},{96,32},{112,48},{1... | collective-permute-start | bytes 983048 | tf_op jit(solution)/shard_map/ppermute | solution.py:38
  53.8 6.2 %collective-permute-start.13 = (bf16[4,64,640]{2,1,0:T(8,128)(2,1)S(1)}, bf16[4,64,640]{2,1,0:T(8,128)(2,1)S(1)}, u32[]{:S(2)}, u32[]{:S(2)}) collective-permute-start(bf16[4,64,640]{2,1,0:T(8,128)(2,1)S(1)} %get-tuple-element.61.refs_3_), channel_id=1, source_target_pairs={{0,1},{1,0},{2,3},{3,2},{4,5},{5,4},{6,7},{7,6},{8,9},{9,8},{10,11... | collective-permute-start | bytes 983048 | tf_op jit(solution)/shard_map/ppermute | solution.py:39
  64.3 11.8 %collective-permute-start.17 = (bf16[8,64,640]{2,1,0:T(8,128)(2,1)S(1)}, bf16[8,64,640]{2,1,0:T(8,128)(2,1)S(1)}, u32[]{:S(2)}, u32[]{:S(2)}) collective-permute-start(bf16[8,64,640]{2,1,0:T(8,128)(2,1)S(1)} %get-tuple-element.64.refs_1_), channel_id=1, source_target_pairs={{0,64},{16,80},{32,96},{48,112},{64,0},{80,16},{96,32},{112,48},{1... | collective-permute-start | bytes 1966088 | tf_op jit(solution)/shard_map/ppermute | solution.py:38
  64.6 11.4 %collective-permute-start.18 = (bf16[8,64,640]{2,1,0:T(8,128)(2,1)S(1)}, bf16[8,64,640]{2,1,0:T(8,128)(2,1)S(1)}, u32[]{:S(2)}, u32[]{:S(2)}) collective-permute-start(bf16[8,64,640]{2,1,0:T(8,128)(2,1)S(1)} %get-tuple-element.65.refs_2_), channel_id=1, source_target_pairs={{0,1},{1,0},{2,3},{3,2},{4,5},{5,4},{6,7},{7,6},{8,9},{9,8},{10,11... | collective-permute-start | bytes 1966088 | tf_op jit(solution)/shard_map/ppermute | solution.py:39
  64.6 12.0 %collective-permute-start.19 = (bf16[8,64,640]{2,1,0:T(8,128)(2,1)S(1)}, bf16[8,64,640]{2,1,0:T(8,128)(2,1)S(1)}, u32[]{:S(2)}, u32[]{:S(2)}) collective-permute-start(bf16[8,64,640]{2,1,0:T(8,128)(2,1)S(1)} %get-tuple-element.66.refs_3_), channel_id=1, source_target_pairs={{0,16},{16,0},{32,48},{48,32},{64,80},{80,64},{96,112},{112,96},{1... | collective-permute-start | bytes 1966088 | tf_op jit(solution)/shard_map/ppermute | solution.py:38
  65.1 11.5 %collective-permute-start.20 = (bf16[8,64,640]{2,1,0:T(8,128)(2,1)S(1)}, bf16[8,64,640]{2,1,0:T(8,128)(2,1)S(1)}, u32[]{:S(2)}, u32[]{:S(2)}) collective-permute-start(bf16[8,64,640]{2,1,0:T(8,128)(2,1)S(1)} %get-tuple-element.67.refs_4_), channel_id=1, source_target_pairs={{0,3},{1,2},{2,1},{3,0},{4,7},{5,6},{6,5},{7,4},{8,11},{9,10},{10,... | collective-permute-start | bytes 1966088 | tf_op jit(solution)/shard_map/ppermute | solution.py:39
  66.8 9.2 %collective-permute-start.16 = (bf16[8,64,512]{2,1,0:T(8,128)(2,1)S(1)}, bf16[8,64,512]{2,1,0:T(8,128)(2,1)S(1)}, u32[]{:S(2)}, u32[]{:S(2)}) collective-permute-start(bf16[8,64,512]{2,1,0:T(8,128)(2,1)S(1)} %get-tuple-element.63.refs_0_), channel_id=1, source_target_pairs={{0,48},{16,32},{32,16},{48,0},{64,112},{80,96},{96,80},{112,64},{1... | collective-permute-start | bytes 1572872 | tf_op jit(solution)/shard_map/ppermute | solution.py:38
  79.4 11.3 %collective-permute-start.22 = (bf16[16,32,640]{2,1,0:T(8,128)(2,1)}, bf16[16,32,640]{2,1,0:T(8,128)(2,1)S(1)}, u32[]{:S(2)}, u32[]{:S(2)}) collective-permute-start(bf16[16,32,640]{2,1,0:T(8,128)(2,1)} %get-tuple-element.70), channel_id=1, source_target_pairs={{0,1},{1,0},{2,3},{3,2},{4,5},{5,4},{6,7},{7,6},{8,9},{9,8},{10,11... | collective-permute-start | bytes 1966088 | tf_op jit(solution)/shard_map/ppermute | solution.py:39
  79.9 11.4 %collective-permute-start.23 = (bf16[16,32,640]{2,1,0:T(8,128)(2,1)}, bf16[16,32,640]{2,1,0:T(8,128)(2,1)S(1)}, u32[]{:S(2)}, u32[]{:S(2)}) collective-permute-start(bf16[16,32,640]{2,1,0:T(8,128)(2,1)} %get-tuple-element.71), channel_id=1, source_target_pairs={{0,16},{16,0},{32,48},{48,32},{64,80},{80,64},{96,112},{112,96},{1... | collective-permute-start | bytes 1966088 | tf_op jit(solution)/shard_map/ppermute | solution.py:38
  80.2 12.6 %collective-permute-start.24 = (bf16[16,32,640]{2,1,0:T(8,128)(2,1)}, bf16[16,32,640]{2,1,0:T(8,128)(2,1)S(1)}, u32[]{:S(2)}, u32[]{:S(2)}) collective-permute-start(bf16[16,32,640]{2,1,0:T(8,128)(2,1)} %get-tuple-element.72), channel_id=1, source_target_pairs={{0,3},{1,2},{2,1},{3,0},{4,7},{5,6},{6,5},{7,4},{8,11},{9,10},{10,... | collective-permute-start | bytes 1966088 | tf_op jit(solution)/shard_map/ppermute | solution.py:39
  82.1 8.2 %collective-permute-start.21 = (bf16[16,32,512]{2,1,0:T(8,128)(2,1)}, bf16[16,32,512]{2,1,0:T(8,128)(2,1)S(1)}, u32[]{:S(2)}, u32[]{:S(2)}) collective-permute-start(bf16[16,32,512]{2,1,0:T(8,128)(2,1)} %get-tuple-element.69), channel_id=1, source_target_pairs={{0,64},{16,80},{32,96},{48,112},{64,0},{80,16},{96,32},{112,48},{1... | collective-permute-start | bytes 1572872 | tf_op jit(solution)/shard_map/ppermute | solution.py:38
  83.0 11.2 %collective-permute-start.25 = (bf16[16,32,640]{2,1,0:T(8,128)(2,1)}, bf16[16,32,640]{2,1,0:T(8,128)(2,1)S(1)}, u32[]{:S(2)}, u32[]{:S(2)}) collective-permute-start(bf16[16,32,640]{2,1,0:T(8,128)(2,1)} %get-tuple-element.73), channel_id=1, source_target_pairs={{0,48},{16,32},{32,16},{48,0},{64,112},{80,96},{96,80},{112,64},{1... | collective-permute-start | bytes 1966088 | tf_op jit(solution)/shard_map/ppermute | solution.py:38
  90.3 30.4 %collective-permute-start.28 = (bf16[16,32,640]{2,1,0:T(8,128)(2,1)}, bf16[16,32,640]{2,1,0:T(8,128)(2,1)S(1)}, u32[]{:S(2)}, u32[]{:S(2)}) collective-permute-start(bf16[16,32,640]{2,1,0:T(8,128)(2,1)} %get-tuple-element.77), channel_id=1, source_target_pairs={{0,1},{1,0},{2,3},{3,2},{4,5},{5,4},{6,7},{7,6},{8,9},{9,8},{10,11... | collective-permute-start | bytes 1966088 | tf_op jit(solution)/shard_map/ppermute | solution.py:39
  90.7 30.1 %collective-permute-start.29 = (bf16[16,32,640]{2,1,0:T(8,128)(2,1)}, bf16[16,32,640]{2,1,0:T(8,128)(2,1)S(1)}, u32[]{:S(2)}, u32[]{:S(2)}) collective-permute-start(bf16[16,32,640]{2,1,0:T(8,128)(2,1)} %get-tuple-element.78), channel_id=1, source_target_pairs={{0,16},{16,0},{32,48},{48,32},{64,80},{80,64},{96,112},{112,96},{1... | collective-permute-start | bytes 1966088 | tf_op jit(solution)/shard_map/ppermute | solution.py:38
  91.3 29.5 %collective-permute-start.30 = (bf16[16,32,640]{2,1,0:T(8,128)(2,1)}, bf16[16,32,640]{2,1,0:T(8,128)(2,1)S(1)}, u32[]{:S(2)}, u32[]{:S(2)}) collective-permute-start(bf16[16,32,640]{2,1,0:T(8,128)(2,1)} %get-tuple-element.79), channel_id=1, source_target_pairs={{0,3},{1,2},{2,1},{3,0},{4,7},{5,6},{6,5},{7,4},{8,11},{9,10},{10,... | collective-permute-start | bytes 1966088 | tf_op jit(solution)/shard_map/ppermute | solution.py:39
  92.8 28.0 %collective-permute-start.31 = (bf16[16,32,640]{2,1,0:T(8,128)(2,1)}, bf16[16,32,640]{2,1,0:T(8,128)(2,1)S(1)}, u32[]{:S(2)}, u32[]{:S(2)}) collective-permute-start(bf16[16,32,640]{2,1,0:T(8,128)(2,1)} %get-tuple-element.80), channel_id=1, source_target_pairs={{0,48},{16,32},{32,16},{48,0},{64,112},{80,96},{96,80},{112,64},{1... | collective-permute-start | bytes 1966088 | tf_op jit(solution)/shard_map/ppermute | solution.py:38
  94.1 12.7 %collective-permute-start.27 = (bf16[16,32,512]{2,1,0:T(8,128)(2,1)}, bf16[16,32,512]{2,1,0:T(8,128)(2,1)S(1)}, u32[]{:S(2)}, u32[]{:S(2)}) collective-permute-start(bf16[16,32,512]{2,1,0:T(8,128)(2,1)} %get-tuple-element.76), channel_id=1, source_target_pairs={{0,64},{16,80},{32,96},{48,112},{64,0},{80,16},{96,32},{112,48},{1... | collective-permute-start | bytes 1572872 | tf_op jit(solution)/shard_map/ppermute | solution.py:38
  106.9 28.1 %collective-permute-start.26 = (bf16[2,8,32,768]{3,2,1,0:T(8,128)(2,1)S(1)}, bf16[2,8,32,768]{3,2,1,0:T(8,128)(2,1)S(1)}, u32[]{:S(2)}, u32[]{:S(2)}) collective-permute-start(bf16[2,8,32,768]{3,2,1,0:T(8,128)(2,1)S(1)} %get-tuple-element.75), channel_id=1, source_target_pairs={{0,4},{4,0},{8,12},{12,8},{1,5},{5,1},{9,13},{13,9},{2,6},{6,2},{1... | collective-permute-start | bytes 2359304 | tf_op jit(solution)/shard_map/ppermute | solution.py:43
  128.8 8.7 %collective-permute-start.33 = (bf16[2,8,32,768]{3,2,1,0:T(8,128)(2,1)S(1)}, bf16[2,8,32,768]{3,2,1,0:T(8,128)(2,1)S(1)}, u32[]{:S(2)}, u32[]{:S(2)}) collective-permute-start(bf16[2,8,32,768]{3,2,1,0:T(8,128)(2,1)S(1)} %get-tuple-element.84), channel_id=1, source_target_pairs={{0,4},{4,0},{8,12},{12,8},{1,5},{5,1},{9,13},{13,9},{2,6},{6,2},{1... | collective-permute-start | bytes 2359304 | tf_op jit(solution)/shard_map/ppermute | solution.py:43
  135.1 13.0 %collective-permute-start.32 = (bf16[8,32,768]{2,1,0:T(8,128)(2,1)S(1)}, bf16[8,32,768]{2,1,0:T(8,128)(2,1)S(1)}, u32[]{:S(2)}, u32[]{:S(2)}) collective-permute-start(bf16[8,32,768]{2,1,0:T(8,128)(2,1)S(1)} %get-tuple-element.83), channel_id=1, source_target_pairs={{0,8},{4,12},{8,0},{12,4},{1,9},{5,13},{9,1},{13,5},{2,10},{6,14},... | collective-permute-start | bytes 1179656 | tf_op jit(solution)/shard_map/ppermute | solution.py:43
  137.7 17.7 %collective-permute-start.34 = (bf16[8,32,768]{2,1,0:T(8,128)(2,1)S(1)}, bf16[8,32,768]{2,1,0:T(8,128)(2,1)S(1)}, u32[]{:S(2)}, u32[]{:S(2)}) collective-permute-start(bf16[8,32,768]{2,1,0:T(8,128)(2,1)S(1)} %get-tuple-element.90), channel_id=1, source_target_pairs={{0,8},{4,12},{8,0},{12,4},{1,9},{5,13},{9,1},{13,5},{2,10},{6,14},... | collective-permute-start | bytes 1179656 | tf_op jit(solution)/shard_map/ppermute | solution.py:43
  (14 other events, 123.9 us)

commit v4 on v3

--- a/solution.py
+++ b/solution.py
@@ -20,7 +20,9 @@
 WIDTHS = (512, 640, 640, 640, 640)
 OFFSETS = tuple(int(v) for v in np.cumsum((0,) + WIDTHS)[:-1])
 CHAINS = len(WIDTHS)
+HOPS = (Z0, Z1, Z0 ^ Z1)
 ORDERS = tuple(tuple(DIMS[(p + k) % 5] for k in range(5)) for p in range(CHAINS))
+TIED = 4
 PARTS = (32, 32)
 STARTS = (0, 32)
 
@@ -58,16 +60,18 @@
 
 
 def cut_kernel(where, grad_out, pre, *refs):
-    outs, chunks, sem = refs[:CHAINS], refs[CHAINS], refs[-1]
-    row = where[0]
+    outs, chunks, sem = refs[:CHAINS], refs[CHAINS:-1], refs[-1]
+    row, col = where[0], where[1]
     copies = [
         pltpu.make_async_copy(grad_out.at[:, pl.ds(OFFSETS[p], WIDTHS[p])], outs[p].at[0], sem.at[p])
         for p in range(CHAINS)
     ]
     half = SHARDS * ROWS // 8
-    for z in range(4):
-        here = pre.at[pl.ds(pl.multiple_of(row % 2 * half, half), half), pl.ds(z * HID, HID)]
-        copies.append(pltpu.make_async_copy(here, chunks.at[z], sem.at[CHAINS + z]))
+    for j, mask in enumerate(HOPS):
+        here = pre.at[
+            pl.ds(pl.multiple_of(row % 2 * half, half), half), pl.ds(pl.multiple_of((col ^ mask) * HID, HID), HID)
+        ]
+        copies.append(pltpu.make_async_copy(here, chunks[j], sem.at[CHAINS + j]))
     for c in copies:
         c.start()
     for c in copies:
@@ -78,27 +82,27 @@
     return pl.pallas_call(
         cut_kernel,
         out_shape=[jax.ShapeDtypeStruct((1, ROWS, w), jnp.bfloat16) for w in WIDTHS]
-        + [jax.ShapeDtypeStruct((4, SHARDS * ROWS // 8, HID), jnp.bfloat16)],
+        + [jax.ShapeDtypeStruct((SHARDS * ROWS // 8, HID), jnp.bfloat16)] * len(HOPS),
         in_specs=[SMEM, ANY, ANY],
-        out_specs=[ANY] * (CHAINS + 1),
-        scratch_shapes=[pltpu.SemaphoreType.DMA((CHAINS + 4,))],
+        out_specs=[ANY] * (CHAINS + len(HOPS)),
+        scratch_shapes=[pltpu.SemaphoreType.DMA((CHAINS + len(HOPS),))],
         compiler_params=params(1),
         cost_estimate=TINY,
         name="cut",
     )(where, in_hbm(grad_out), in_hbm(pre))
 
 
-def grow_kernel(rows, *refs):
-    own, got, sem = refs[:CHAINS], refs[CHAINS : 2 * CHAINS], refs[-1]
-    outs = refs[-1 - len(rows) * CHAINS : -1]
+def grow_kernel(rows, own, got, *refs):
+    outs, sem = refs[-1 - len(rows) : -1], refs[-1]
+    blocks = own.shape[0]
     copies = []
-    for part, (at, n) in enumerate(rows):
-        for p in range(CHAINS):
-            out = outs[part * CHAINS + p]
-            blocks = own[p].shape[0]
-            for side, src in enumerate((own[p], got[p])):
-                copies.append((src.at[:, pl.ds(at, n)], out.at[pl.ds(side * blocks, blocks)]))
-    copies = [pltpu.make_async_copy(*c, sem.at[i]) for i, c in enumerate(copies)]
+    for out, (at, n) in zip(outs, rows):
+        for side, src in enumerate((own, got)):
+            copies.append(
+                pltpu.make_async_copy(
+                    src.at[:, pl.ds(at, n)], out.at[pl.ds(side * blocks, blocks)], sem.at[len(copies)]
+                )
+            )
     for c in copies:
         c.start()
     for c in copies:
@@ -106,31 +110,37 @@
 
 
 def grow_call(own, got, rows=((0, ROWS),), after=()):
-    blocks = own[0].shape[0]
+    blocks, _, w = own.shape
     shape = pltpu.HBM if len(rows) > 1 else jax.ShapeDtypeStruct
     return pl.pallas_call(
         functools.partial(grow_kernel, rows),
-        out_shape=[shape((2 * blocks, n, w), jnp.bfloat16) for _, n in rows for w in WIDTHS],
-        in_specs=[ANY] * (2 * CHAINS + len(after)),
-        out_specs=[ANY] * (len(rows) * CHAINS),
-        scratch_shapes=[pltpu.SemaphoreType.DMA((2 * CHAINS * len(rows),))],
+        out_shape=[shape((2 * blocks, n, w), jnp.bfloat16) for _, n in rows],
+        in_specs=[ANY] * (2 + len(after)),
+        out_specs=[ANY] * len(rows),
+        scratch_shapes=[pltpu.SemaphoreType.DMA((2 * len(rows),))],
         compiler_params=params(1),
         cost_estimate=TINY,
         name="grow",
-    )(*own, *got, *after)
-
-
-def gelu_kernel(where, table, fetched, other, *refs):
+    )(own, got, *after)
+
+
+def gelu_kernel(where, table, pre, got_a, got_b, got_c, other, *refs):
     outs, (buf, sems), acts = refs[:4], refs[4:6], refs[6:]
     act_t, slopes = outs[:2], outs[2:]
-    row, mine = where[0], where[2]
+    row, col, mine = where[0], where[1], where[2]
     core = row % 2
     quarter, half = SHARDS * ROWS // 4, SHARDS * ROWS // 8
-    copies = []
-    for z in range(4):
-        for side, src in ((core, fetched), (1 - core, other)):
-            at = pl.multiple_of(z * quarter + side * half, half)
-            copies.append(pltpu.make_async_copy(src.at[z], buf.at[pl.ds(at, half)], sems.at[len(copies)]))
+    copies = [
+        pltpu.make_async_copy(
+            pre.at[:, pl.ds(pl.multiple_of(col * HID, HID), HID)],
+            buf.at[pl.ds(pl.multiple_of(col * quarter, quarter), quarter)],
+            sems.at[0],
+        )
+    ]
+    for j, got in enumerate((got_a, got_b, got_c)):
+        for side, src in ((core, got), (1 - core, other.at[pl.ds(j * half, half)])):
+            at = pl.multiple_of((col ^ HOPS[j]) * quarter + side * half, half)
+            copies.append(pltpu.make_async_copy(src, buf.at[pl.ds(at, half)], sems.at[len(copies)]))
     for c in copies:
         c.start()
     for c in copies:
@@ -169,33 +179,33 @@
         lax.fori_loop(0, SHARDS * PARTS[part] // 128, one_turn, 0)
 
 
-def gelu_call(where, table, fetched, other):
+def gelu_call(where, table, pre, fetched, other):
     tokens = [SHARDS * n for n in PARTS]
     return pl.pallas_call(
         gelu_kernel,
         out_shape=[jax.ShapeDtypeStruct((HID, t), jnp.bfloat16) for t in tokens]
         + [jax.ShapeDtypeStruct((SHARDS // 4, n, HID), jnp.float32) for n in PARTS],
-        in_specs=[SMEM, SMEM, ANY, ANY],
+        in_specs=[SMEM, SMEM] + [ANY] * 5,
         out_specs=[VMEM] * 4,
-        scratch_shapes=[pltpu.VMEM((SHARDS * ROWS, HID), jnp.bfloat16), pltpu.SemaphoreType.DMA((8,))]
+        scratch_shapes=[pltpu.VMEM((SHARDS * ROWS, HID), jnp.bfloat16), pltpu.SemaphoreType.DMA((7,))]
         + [pltpu.VMEM((t, HID), jnp.bfloat16) for t in tokens],
         compiler_params=params(20),
         cost_estimate=TINY,
         name="gelu",
-    )(where, table, fetched, other)
-
-
-def pieces(p, side):
+    )(where, table, in_hbm(pre), *fetched, other)
+
+
+def pieces(p, side, top):
     every = slice(None)
     if p == 0:
-        return [((every,) * 4, (side,) + (every,) * 4)]
+        return [((every,) * 4, (side,) + (every,) * 4)] if side == top else []
     if p == 1:
-        return [((every,) * 4, (every,) * 4 + (side,))]
+        return [((top,) + (every,) * 3, (top,) + (every,) * 3 + (side,))]
     if p == 2:
-        return [((i,) + (every,) * 3, (every,) * 3 + (side, i)) for i in range(2)]
+        return [((i, top) + (every,) * 2, (top,) + (every,) * 2 + (side, i)) for i in range(2)]
     if p == 3:
-        return [((every,) * 2 + (i, j), (i, j, side) + (every,) * 2) for i in range(2) for j in range(2)]
-    return [((every,) * 3 + (i,), (i, side) + (every,) * 3) for i in range(2)]
+        return [((every,) * 2 + (top, j), (top, j, side) + (every,) * 2) for j in range(2)]
+    return [((every,) * 3 + (top,), (top, side) + (every,) * 3)]
 
 
 def hidden_kernel(n, where, w_far, *refs):
@@ -203,25 +213,38 @@
     keep, send, gathered, g, w, hs, sems = refs[-7:]
     row, mine = where[0], where[2]
     per = SHARDS // 4
-    weights = pltpu.make_async_copy(w_far, w, sems.at[0])
-    weights.start()
-    for p in range(CHAINS):
-        for side in range(2):
-            for src, dst in pieces(p, side):
-                pltpu.make_async_copy(
-                    blocks[2 * p + side].at[src],
-                    g.at[dst + (slice(None), pl.ds(OFFSETS[p], WIDTHS[p]))],
-                    sems.at[1],
-                ).start()
-    pltpu.make_async_copy(g, g, sems.at[1]).wait()
-    weights.wait()
-    out = pltpu.make_async_copy(g, gathered, sems.at[2])
-    out.start()
+    step = HID // 3
+    weights = [
+        pltpu.make_async_copy(w_far.at[pl.ds(k * step, step)], w.at[pl.ds(k * step, step)], sems.at[3 + k])
+        for k in range(3)
+    ]
+    for top in range(2):
+        for p in range(CHAINS):
+            for side in range(2):
+                for src, dst in pieces(p, side, top):
+                    pltpu.make_async_copy(
+                        blocks[2 * p + side].at[src],
+                        g.at[dst + (slice(None), pl.ds(OFFSETS[p], WIDTHS[p]))],
+                        sems.at[top],
+                    ).start()
+        if top == 0:
+            for c in weights:
+                c.start()
+    outs = []
     for i in range(2):
-        h = lax.dot_general(
-            g[i].reshape(2 * per * n, FEATS), w[...], (((1,), (1,)), ((), ())), preferred_element_type=jnp.float32
-        )
-        hs[i] = h.reshape(2, per, n, HID)
+        pltpu.make_async_copy(g.at[i], g.at[i], sems.at[i]).wait()
+        outs.append(pltpu.make_async_copy(g.at[i], gathered.at[i], sems.at[2 if i else 6]))
+        outs[-1].start()
+        for k in range(3):
+            if i == 0:
+                weights[k].wait()
+            h = lax.dot_general(
+                g[i].reshape(2 * per * n, FEATS),
+                w[k * step : (k + 1) * step, :],
+                (((1,), (1,)), ((), ())),
+                preferred_element_type=jnp.float32,
+            )
+            hs[i, :, :, :, k * step : (k + 1) * step] = h.reshape(2, per, n, step)
     for a, b in ((1, 1), (0, 1), (1, 0), (0, 0)):
         off_x = (mine // 16) ^ (row // 2) ^ a
         off_y = (mine // 8 % 2) ^ (row % 2) ^ b
@@ -231,7 +254,8 @@
                 send[a, slot] = hs[off_x, off_y, j].astype(jnp.bfloat16)
             else:
                 keep[a, slot] = hs[off_x, off_y, j]
-    out.wait()
+    for out in outs:
+        out.wait()
 
 
 def hidden_call(part, where, w, blocks, after=()):
@@ -250,7 +274,7 @@
             pltpu.VMEM((2,) * 5 + (n, FEATS), jnp.bfloat16),
             pltpu.VMEM((HID, FEATS), jnp.bfloat16),
             pltpu.VMEM((2, 2, per, n, HID), jnp.float32),
-            pltpu.SemaphoreType.DMA((3,)),
+            pltpu.SemaphoreType.DMA((7,)),
         ],
         compiler_params=params(14 + n // 2),
         cost_estimate=pl.CostEstimate(
@@ -319,23 +343,28 @@
     where = jnp.stack([row, col, depth * 4 + col]).astype(jnp.int32)
     table = jnp.asarray([mask_of(c) for c in range(SHARDS)], jnp.int32)
 
-    *blocks, chunks = cut_call(where, grad_out, pre_act)
-    fetched = lax.all_to_all(chunks, "col", split_axis=0, concat_axis=0, tiled=True)
-    got = [swap(blocks[p], ORDERS[p][0]) for p in range(CHAINS)]
-    blocks = grow_call(blocks, got)
-    got = [swap(blocks[p], ORDERS[p][1]) for p in range(CHAINS)]
-    blocks = grow_call(blocks, got, after=(fetched,))
-    got = [swap(blocks[p], ORDERS[p][2]) for p in range(CHAINS)]
-    other = swap_row(fetched, 1)
-    blocks = grow_call(blocks, got, after=(other,))
+    cuts = cut_call(where, grad_out, pre_act)
+    blocks, chunks = cuts[:CHAINS], cuts[CHAINS:]
+    fetched = []
+    for k in range(3):
+        got = [swap(blocks[p], ORDERS[p][k]) for p in range(CHAINS)]
+        fetched.append(swap(chunks[k], HOPS[k]))
+        blocks = [
+            grow_call(b, r, after=(fetched[k],))[0] if p == TIED else jnp.concatenate([b, r], 0)
+            for p, (b, r) in enumerate(zip(blocks, got))
+        ]
     got = [swap(blocks[p], ORDERS[p][3]) for p in range(CHAINS)]
-    act_a, act_b, slope_a, slope_b = gelu_call(where, table, fetched, other)
-    grown = grow_call(blocks, got, tuple(zip(STARTS, PARTS)), after=(slope_a,))
-    own = grown[:CHAINS], grown[CHAINS:]
+    other = swap_row(jnp.concatenate(fetched, 0), 1)
+    grown = [
+        grow_call(b, r, tuple(zip(STARTS, PARTS)), after=(other,) if p == TIED else ())
+        for p, (b, r) in enumerate(zip(blocks, got))
+    ]
+    own = [[grown[p][part] for p in range(CHAINS)] for part in range(2)]
     came = [[swap(own[part][p], ORDERS[p][4]) for p in range(CHAINS)] for part in range(2)]
+    act_a, act_b, slope_a, slope_b = gelu_call(where, table, pre_act, fetched, other)
 
     pairs = [[b for p in range(CHAINS) for b in (own[part][p], came[part][p])] for part in range(2)]
-    keep_a, send_a, g_a = hidden_call(0, where, w_down, pairs[0])
+    keep_a, send_a, g_a = hidden_call(0, where, w_down, pairs[0], after=(slope_a,))
     keep_b, send_b, g_b = hidden_call(1, where, w_down, pairs[1], after=(keep_a,))
     mine_a, far_a = total_call(keep_a, swap_row(send_a, 1), after=(keep_b,))
     far_a = swap_row(far_a, 2)

time: 157 us -> 162 us (1.032)
  blocking collectives: 25.5 us -> 0 us
  starting transfers between devices: 45 us -> 62.6 us
  waiting for transfers between devices: 35.1 us -> 42 us
  Pallas kernels: 48.8 us -> 53.7 us
    all_to_all x1 -> x0, blocking collectives: 25.5 us -> none  [local(): lax.all_to_all(chunks, 'col', split_axis=0, concat_axis=0, tiled=True)]
    ppermute x12 -> x15, starting transfers between devices: 9.96 us -> 19.5 us  [swap(): return lax.ppermute(x, 'col', [(i, i ^ mask) for i in range(4)])]
    ppermute x18, starting transfers between devices: 16.1 us -> 24.8 us  [swap(): return lax.ppermute(x, 'depth', [(i, i ^ mask >> 2) for i in range(8)])]
    pallas_call x2, Pallas kernels: 16 us -> 22.2 us  [hidden_call(): pl.pallas_call(functools.partial(hidden_kernel, n), out_shape=[jax.ShapeD...]
    ppermute x18, waiting for transfers between devices: 21.3 us -> 25.6 us  [swap(): return lax.ppermute(x, 'depth', [(i, i ^ mask >> 2) for i in range(8)])]
    ppermute x12 -> x15, waiting for transfers between devices: 6.72 us -> 9.34 us  [swap(): return lax.ppermute(x, 'col', [(i, i ^ mask) for i in range(4)])]
    pallas_call x4 -> x8, Pallas kernels: 6.96 us -> 6.29 us  [grow_call(): pl.pallas_call(functools.partial(grow_kernel, rows), out_shape=[shape((2...]
  transfers between devices with their start and end apart: 35 -> 38, of which waited for: 17 -> 10; matrix products, arithmetic and copies ran while one was open for 0% -> 0% of each run, Pallas kernels for 27% -> 32%
where the time goes in v4:
time: 162 us; the launch traced here: 161 us
  starting transfers between devices  62.6 us (39%)
  Pallas kernels  53.7 us (33%)
  waiting for transfers between devices  42 us (26%)
    ppermute x18, waiting for transfers between devices, swap(): return lax.ppermute(x, 'depth', [(i, i ^ mask >> 2) for i in range(8)])  25.6 us
    ppermute x18, starting transfers between devices, swap(): return lax.ppermute(x, 'depth', [(i, i ^ mask >> 2) for i in range(8)])  24.8 us
    pallas_call x2, Pallas kernels, hidden_call(): pl.pallas_call(functools.partial(hidden_kernel, n), out_shape=[jax.ShapeD...  22.2 us
    ppermute x15, starting transfers between devices, swap(): return lax.ppermute(x, 'col', [(i, i ^ mask) for i in range(4)])  19.5 us
    ppermute x5, starting transfers between devices, swap_row(): return lax.ppermute(x, 'row', [(i, i ^ mask) for i in range(4)])  18.4 us
    pallas_call x2, Pallas kernels, down_call(): pl.pallas_call(down_kernel, grid=(count,), out_shape=pltpu.HBM((HID, FEAT...  15.7 us
    ppermute x15, waiting for transfers between devices, swap(): return lax.ppermute(x, 'col', [(i, i ^ mask) for i in range(4)])  9.34 us
    pallas_call x1, Pallas kernels, gelu_call(): pl.pallas_call(gelu_kernel, out_shape=[jax.ShapeDtypeStruct((HID, t), jnp...  7.23 us
  transfers between devices with their start and end apart: 38, of which 10 were waited for; matrix products, arithmetic and copies ran while one was open for 0% of the time, Pallas kernels for 32%

profile of v4, /device:TPU:1, one launch (start us, length us, event | category | flops | bytes accessed | tf_op | source)
XLA Modules:
  0.0 161.4 jit_solution(12971276127356435390)
XLA Ops:
  0.7 2.0 %cut.1 = (bf16[1,64,512]{2,1,0:T(8,128)(2,1)S(1)}, bf16[1,64,640]{2,1,0:T(8,128)(2,1)S(1)}, bf16[1,64,640]{2,1,0:T(8,128)(2,1)S(1)}, bf16[1,64,640]{2,1,0:T(8,12...) custom-call(s32[3]{0:T(128)S(1)} %pad_add_fusion.where, ...), custom_call_target="tpu_custom_call" | custom-call | flops 1 | bytes 1 | tf_op jit(solution)/shard_map/cut/pallas_call | solution.py:82
  2.8 2.5 %collective-permute-start = (bf16[1,64,512]{2,1,0:T(8,128)(2,1)S(1)}, bf16[1,64,512]{2,1,0:T(8,128)(2,1)S(1)}, u32[]{:S(2)}, u32[]{:S(2)}) collective-permute-start(bf16[1,64,512]{2,1,0:T(8,128)(2,1)S(1)} %get-tuple-element.34), channel_id=1, source_target_pairs={{0,1},{1,0},{2,3},{3,2},{4,5},{5,4},{6,7},{7,6},{8,9},{9,8},{10,11... | collective-permute-start | bytes 196616 | tf_op jit(solution)/shard_map/ppermute | solution.py:41
  6.6 2.2 %collective-permute-start.10 = (bf16[1,64,640]{2,1,0:T(8,128)(2,1)S(1)}, bf16[1,64,640]{2,1,0:T(8,128)(2,1)S(1)}, u32[]{:S(2)}, u32[]{:S(2)}) collective-permute-start(bf16[1,64,640]{2,1,0:T(8,128)(2,1)S(1)} %get-tuple-element.38), channel_id=1, source_target_pairs={{0,3},{1,2},{2,1},{3,0},{4,7},{5,6},{6,5},{7,4},{8,11},{9,10},{10,... | collective-permute-start | bytes 245768 | tf_op jit(solution)/shard_map/ppermute | solution.py:41
  16.2 2.5 %collective-permute-done.1 = bf16[2,64,512]{2,1,0:T(8,128)(2,1)S(1)} collective-permute-done((bf16[2,64,512]{2,1,0:T(8,128)(2,1)S(1)}, bf16[2,64,512]{2,1,0:T(8,128)(2,1)S(1)}, u32[]{:S(2)}, u32[]{:S(2)}) %collective-permute-start.1) | collective-permute-done | bytes 131104 | tf_op jit(solution)/shard_map/ppermute | solution.py:40
  20.6 2.1 %collective-permute-start.6 = (bf16[2,64,640]{2,1,0:T(8,128)(2,1)S(1)}, bf16[2,64,640]{2,1,0:T(8,128)(2,1)S(1)}, u32[]{:S(2)}, u32[]{:S(2)}) collective-permute-start(bf16[2,64,640]{2,1,0:T(8,128)(2,1)S(1)} %pad_maximum_fusion.6), channel_id=1, source_target_pairs={{0,3},{1,2},{2,1},{3,0},{4,7},{5,6},{6,5},{7,4},{8,11},{9,10},{10,... | collective-permute-start | bytes 491528 | tf_op jit(solution)/shard_map/ppermute | solution.py:41
  24.8 9.3 %collective-permute-done.6 = bf16[2,64,640]{2,1,0:T(8,128)(2,1)S(1)} collective-permute-done((bf16[2,64,640]{2,1,0:T(8,128)(2,1)S(1)}, bf16[2,64,640]{2,1,0:T(8,128)(2,1)S(1)}, u32[]{:S(2)}, u32[]{:S(2)}) %collective-permute-start.6) | collective-permute-done | bytes 163872 | tf_op jit(solution)/shard_map/ppermute | solution.py:41
  35.4 2.0 %collective-permute-done.20.got = bf16[1,64,640]{2,1,0:T(8,128)(2,1)S(1)} collective-permute-done((bf16[1,64,640]{2,1,0:T(8,128)(2,1)S(1)}, bf16[1,64,640]{2,1,0:T(8,128)(2,1)S(1)}, u32[]{:S(2)}, u32[]{:S(2)}) %collective-permute-start.20) | collective-permute-done | bytes 81952 | tf_op jit(solution)/shard_map/ppermute | solution.py:40
  40.3 3.7 %collective-permute-start.27 = (bf16[768,768]{1,0:T(8,128)(2,1)S(1)}, bf16[768,768]{1,0:T(8,128)(2,1)S(1)}, u32[]{:S(2)}, u32[]{:S(2)}) collective-permute-start(bf16[768,768]{1,0:T(8,128)(2,1)S(1)} %pad_maximum_fusion), channel_id=1, source_target_pairs={{0,4},{4,0},{8,12},{12,8},{1,5},{5,1},{9,13},{13,9},{2,6},{6,2},{1... | collective-permute-start | bytes 3538952 | tf_op jit(solution)/shard_map/ppermute | solution.py:45
  48.5 11.3 %collective-permute-done.24.got = bf16[4,64,640]{2,1,0:T(8,128)(2,1)S(1)} collective-permute-done((bf16[4,64,640]{2,1,0:T(8,128)(2,1)S(1)}, bf16[4,64,640]{2,1,0:T(8,128)(2,1)S(1)}, u32[]{:S(2)}, u32[]{:S(2)}) %collective-permute-start.24) | collective-permute-done | bytes 327712 | tf_op jit(solution)/shard_map/ppermute | solution.py:40
  60.3 2.6 %collective-permute-start.26 = (bf16[8,64,640]{2,1,0:T(8,128)(2,1)S(1)}, bf16[8,64,640]{2,1,0:T(8,128)(2,1)S(1)}, u32[]{:S(2)}, u32[]{:S(2)}) collective-permute-start(bf16[8,64,640]{2,1,0:T(8,128)(2,1)S(1)} %grow.14.own), channel_id=1, source_target_pairs={{0,3},{1,2},{2,1},{3,0},{4,7},{5,6},{6,5},{7,4},{8,11},{9,10},{10,... | collective-permute-start | bytes 1966088 | tf_op jit(solution)/shard_map/ppermute | solution.py:41
  63.0 2.6 %collective-permute-start.3 = (bf16[8,64,512]{2,1,0:T(8,128)(2,1)S(1)}, bf16[8,64,512]{2,1,0:T(8,128)(2,1)S(1)}, u32[]{:S(2)}, u32[]{:S(2)}) collective-permute-start(bf16[8,64,512]{2,1,0:T(8,128)(2,1)S(1)} %constant_dynamic-update-slice_fusion.own), channel_id=1, source_target_pairs={{0,48},{16,32},{32,16},{48,0},{64,112},{80,96},{96,80},{112,64},{1... | collective-permute-start | bytes 1572872 | tf_op jit(solution)/shard_map/ppermute | solution.py:40
  68.0 3.5 %collective-permute-done.8.got = bf16[8,64,640]{2,1,0:T(8,128)(2,1)S(1)} collective-permute-done((bf16[8,64,640]{2,1,0:T(8,128)(2,1)S(1)}, bf16[8,64,640]{2,1,0:T(8,128)(2,1)S(1)}, u32[]{:S(2)}, u32[]{:S(2)}) %collective-permute-start.8) | collective-permute-done | bytes 655392 | tf_op jit(solution)/shard_map/ppermute | solution.py:40
  77.8 2.6 %collective-permute-start.28 = (bf16[16,32,640]{2,1,0:T(8,128)(2,1)}, bf16[16,32,640]{2,1,0:T(8,128)(2,1)S(1)}, u32[]{:S(2)}, u32[]{:S(2)}) collective-permute-start(bf16[16,32,640]{2,1,0:T(8,128)(2,1)} %get-tuple-element.46), channel_id=1, source_target_pairs={{0,48},{16,32},{32,16},{48,0},{64,112},{80,96},{96,80},{112,64},{1... | collective-permute-start | bytes 1966088 | tf_op jit(solution)/shard_map/ppermute | solution.py:40
  80.4 3.6 %collective-permute-done.4 = bf16[16,32,512]{2,1,0:T(8,128)(2,1)S(1)} collective-permute-done((bf16[16,32,512]{2,1,0:T(8,128)(2,1)}, bf16[16,32,512]{2,1,0:T(8,128)(2,1)S(1)}, u32[]{:S(2)}, u32[]{:S(2)}) %collective-permute-start.4) | collective-permute-done | bytes 524320 | tf_op jit(solution)/shard_map/ppermute | solution.py:40
  84.0 3.2 %collective-permute-start.33 = (bf16[16,32,640]{2,1,0:T(8,128)(2,1)S(1)}, bf16[16,32,640]{2,1,0:T(8,128)(2,1)S(1)}, u32[]{:S(2)}, u32[]{:S(2)}) collective-permute-start(bf16[16,32,640]{2,1,0:T(8,128)(2,1)S(1)} %copy-done.1), channel_id=1, source_target_pairs={{0,3},{1,2},{2,1},{3,0},{4,7},{5,6},{6,5},{7,4},{8,11},{9,10},{10,... | collective-permute-start | bytes 1966088 | tf_op jit(solution)/shard_map/ppermute | solution.py:41
  88.7 2.9 %collective-permute-start.34 = (bf16[16,32,640]{2,1,0:T(8,128)(2,1)}, bf16[16,32,640]{2,1,0:T(8,128)(2,1)S(1)}, u32[]{:S(2)}, u32[]{:S(2)}) collective-permute-start(bf16[16,32,640]{2,1,0:T(8,128)(2,1)} %get-tuple-element.54), channel_id=1, source_target_pairs={{0,48},{16,32},{32,16},{48,0},{64,112},{80,96},{96,80},{112,64},{1... | collective-permute-start | bytes 1966088 | tf_op jit(solution)/shard_map/ppermute | solution.py:40
  92.9 7.2 %gelu.1 = (bf16[768,1024]{1,0:T(8,128)(2,1)S(1)}, bf16[768,1024]{1,0:T(8,128)(2,1)S(1)}, f32[8,32,768]{2,1,0:T(8,128)S(1)}, f32[8,32,768]{2,1,0:T(8,128)S(1)}) custom-call(s32[3]{0:T(128)S(1)} %pad_add_fusion.where, s32[32]{0:T(128)S(1)} %copy-done, bf16[512,3072]{1,0:T(8,128)(2,1)} %pre.3, bf16[256,768]{1,0:T(8,128)(2,1)S(1)} %collective-permute-done.21.refs_0_.got_a, ...), custom_call_target="tpu_custom_call" | custom-call | flops 1 | bytes 1 | tf_op jit(solution)/shard_map/gelu/pallas_call | solution.py:184
  100.1 11.1 %hidden.2 = (f32[2,8,32,768]{3,2,1,0:T(8,128)S(1)}, bf16[2,8,32,768]{3,2,1,0:T(8,128)(2,1)S(1)}, bf16[2,2,2,2,2,32,3072]{6,5,4,3,2,1,0:T(8,128)(2,1)}) custom-call(s32[3]{0:T(128)S(1)} %pad_add_fusion.where, bf16[768,3072]{1,0:T(8,128)(2,1)S(1)} %bitcast.27, bf16[2,2,2,2,32,512]{5,4,3,2,1,0:T(8,128)(2,1)} %bitcast.52, ...), custom_call_target="tpu_custom_call" | custom-call | flops 4831838208 | bytes 12582912 | tf_op jit(solution)/shard_map/hidden/pallas_call | solution.py:264
  111.2 11.2 %collective-permute-start.29 = (bf16[2,8,32,768]{3,2,1,0:T(8,128)(2,1)S(1)}, bf16[2,8,32,768]{3,2,1,0:T(8,128)(2,1)S(1)}, u32[]{:S(2)}, u32[]{:S(2)}) collective-permute-start(bf16[2,8,32,768]{3,2,1,0:T(8,128)(2,1)S(1)} %get-tuple-element.49), channel_id=1, source_target_pairs={{0,4},{4,0},{8,12},{12,8},{1,5},{5,1},{9,13},{13,9},{2,6},{6,2},{1... | collective-permute-start | bytes 2359304 | tf_op jit(solution)/shard_map/ppermute | solution.py:45
  122.5 11.1 %hidden.3 = (f32[2,8,32,768]{3,2,1,0:T(8,128)S(1)}, bf16[2,8,32,768]{3,2,1,0:T(8,128)(2,1)S(1)}, bf16[2,2,2,2,2,32,3072]{6,5,4,3,2,1,0:T(8,128)(2,1)}) custom-call(s32[3]{0:T(128)S(1)} %pad_add_fusion.where, bf16[768,3072]{1,0:T(8,128)(2,1)S(1)} %bitcast.27, bf16[2,2,2,2,32,512]{5,4,3,2,1,0:T(8,128)(2,1)} %bitcast.51, ...), custom_call_target="tpu_custom_call" | custom-call | flops 4831838208 | bytes 12582912 | tf_op jit(solution)/shard_map/hidden/pallas_call | solution.py:264
  133.9 6.0 %down.2.refs_0_ = bf16[768,3072]{1,0:T(8,128)(2,1)} custom-call(bf16[768,1024]{1,0:T(8,128)(2,1)S(1)} %get-tuple-element.59.at_a, bf16[768,1024]{1,0:T(8,128)(2,1)S(1)} %get-tuple-element.60.at_b, bf16[1024,3072]{1,0:T(8,128)(2,1)} %bitcast.38, bf16[1024,3072]{1,0:T(8,128)(2,1)} %bitcast.40), custom_call_target="tpu_custom_call" | custom-call | flops 3221225472 | bytes 5767168 | tf_op jit(solution)/shard_map/down/pallas_call | solution.py:326
  140.1 2.7 %collective-permute-start.35 = (bf16[8,32,768]{2,1,0:T(8,128)(2,1)S(1)}, bf16[8,32,768]{2,1,0:T(8,128)(2,1)S(1)}, u32[]{:S(2)}, u32[]{:S(2)}) collective-permute-start(bf16[8,32,768]{2,1,0:T(8,128)(2,1)S(1)} %get-tuple-element.57), channel_id=1, source_target_pairs={{0,8},{4,12},{8,0},{12,4},{1,9},{5,13},{9,1},{13,5},{2,10},{6,14},... | collective-permute-start | bytes 1179656 | tf_op jit(solution)/shard_map/ppermute | solution.py:45
  143.3 9.7 %down.3 = bf16[768,3072]{1,0:T(8,128)(2,1)} custom-call(bf16[768,1024]{1,0:T(8,128)(2,1)S(1)} %get-tuple-element.59.at_a, bf16[768,1024]{1,0:T(8,128)(2,1)S(1)} %get-tuple-element.60.at_b, bf16[1024,3072]{1,0:T(8,128)(2,1)} %bitcast.39, bf16[1024,3072]{1,0:T(8,128)(2,1)} %bitcast.41, bf16[768,3072]{1,0:T(8,128)(2,1)} %down.2.refs_0_), custom_call_target="tpu_custom_call", output_to_operand_aliasing={{}: (4, {})} | custom-call | flops 6442450944 | bytes 11534336 | tf_op jit(solution)/shard_map/down/pallas_call | solution.py:326
  153.2 7.1 %collective-permute-done.37 = bf16[8,32,768]{2,1,0:T(8,128)(2,1)S(1)} collective-permute-done((bf16[8,32,768]{2,1,0:T(8,128)(2,1)S(1)}, bf16[8,32,768]{2,1,0:T(8,128)(2,1)S(1)}, u32[]{:S(2)}, u32[]{:S(2)}) %collective-permute-start.37) | collective-permute-done | bytes 393248 | tf_op jit(solution)/shard_map/ppermute | solution.py:45
  (111 shorter events, 35.4 us)
Async XLA Ops:
  10.8 27.5 %collective-permute-start.21 = (bf16[256,768]{1,0:T(8,128)(2,1)S(1)}, bf16[256,768]{1,0:T(8,128)(2,1)S(1)}, u32[]{:S(2)}, u32[]{:S(2)}) collective-permute-start(bf16[256,768]{1,0:T(8,128)(2,1)S(1)} %get-tuple-element.43), channel_id=1, source_target_pairs={{0,1},{1,0},{2,3},{3,2},{4,5},{5,4},{6,7},{7,6},{8,9},{9,8},{10,11... | collective-permute-start | bytes 1179656 | tf_op jit(solution)/shard_map/ppermute | solution.py:41
  11.6 28.5 %collective-permute-start.23 = (bf16[256,768]{1,0:T(8,128)(2,1)S(1)}, bf16[256,768]{1,0:T(8,128)(2,1)S(1)}, u32[]{:S(2)}, u32[]{:S(2)}) collective-permute-start(bf16[256,768]{1,0:T(8,128)(2,1)S(1)} %get-tuple-element.44), channel_id=1, source_target_pairs={{0,3},{1,2},{2,1},{3,0},{4,7},{5,6},{6,5},{7,4},{8,11},{9,10},{10,... | collective-permute-start | bytes 1179656 | tf_op jit(solution)/shard_map/ppermute | solution.py:41
  13.4 26.8 %collective-permute-start.25 = (bf16[256,768]{1,0:T(8,128)(2,1)S(1)}, bf16[256,768]{1,0:T(8,128)(2,1)S(1)}, u32[]{:S(2)}, u32[]{:S(2)}) collective-permute-start(bf16[256,768]{1,0:T(8,128)(2,1)S(1)} %get-tuple-element.45), channel_id=1, source_target_pairs={{0,2},{1,3},{2,0},{3,1},{4,6},{5,7},{6,4},{7,5},{8,10},{9,11},{10,... | collective-permute-start | bytes 1179656 | tf_op jit(solution)/shard_map/ppermute | solution.py:41
  20.6 13.5 %collective-permute-start.6 = (bf16[2,64,640]{2,1,0:T(8,128)(2,1)S(1)}, bf16[2,64,640]{2,1,0:T(8,128)(2,1)S(1)}, u32[]{:S(2)}, u32[]{:S(2)}) collective-permute-start(bf16[2,64,640]{2,1,0:T(8,128)(2,1)S(1)} %pad_maximum_fusion.6), channel_id=1, source_target_pairs={{0,3},{1,2},{2,1},{3,0},{4,7},{5,6},{6,5},{7,4},{8,11},{9,10},{10,... | collective-permute-start | bytes 491528 | tf_op jit(solution)/shard_map/ppermute | solution.py:41
  24.3 15.3 %collective-permute-start.17 = (bf16[4,64,640]{2,1,0:T(8,128)(2,1)S(1)}, bf16[4,64,640]{2,1,0:T(8,128)(2,1)S(1)}, u32[]{:S(2)}, u32[]{:S(2)}) collective-permute-start(bf16[4,64,640]{2,1,0:T(8,128)(2,1)S(1)} %pad_maximum_fusion.4), channel_id=1, source_target_pairs={{0,1},{1,0},{2,3},{3,2},{4,5},{5,4},{6,7},{7,6},{8,9},{9,8},{10,11... | collective-permute-start | bytes 983048 | tf_op jit(solution)/shard_map/ppermute | solution.py:41
  40.1 22.9 %collective-permute-start.18 = (bf16[8,64,640]{2,1,0:T(8,128)(2,1)S(1)}, bf16[8,64,640]{2,1,0:T(8,128)(2,1)S(1)}, u32[]{:S(2)}, u32[]{:S(2)}) collective-permute-start(bf16[8,64,640]{2,1,0:T(8,128)(2,1)S(1)} %constant_dynamic-update-slice_fusion.12.own), channel_id=1, source_target_pairs={{0,16},{16,0},{32,48},{48,32},{64,80},{80,64},{96,112},{112,96},{1... | collective-permute-start | bytes 1966088 | tf_op jit(solution)/shard_map/ppermute | solution.py:40
  40.3 36.4 %collective-permute-start.27 = (bf16[768,768]{1,0:T(8,128)(2,1)S(1)}, bf16[768,768]{1,0:T(8,128)(2,1)S(1)}, u32[]{:S(2)}, u32[]{:S(2)}) collective-permute-start(bf16[768,768]{1,0:T(8,128)(2,1)S(1)} %pad_maximum_fusion), channel_id=1, source_target_pairs={{0,4},{4,0},{8,12},{12,8},{1,5},{5,1},{9,13},{13,9},{2,6},{6,2},{1... | collective-permute-start | bytes 3538952 | tf_op jit(solution)/shard_map/ppermute | solution.py:45
  44.4 15.4 %collective-permute-start.24 = (bf16[4,64,640]{2,1,0:T(8,128)(2,1)S(1)}, bf16[4,64,640]{2,1,0:T(8,128)(2,1)S(1)}, u32[]{:S(2)}, u32[]{:S(2)}) collective-permute-start(bf16[4,64,640]{2,1,0:T(8,128)(2,1)S(1)} %grow.13.own), channel_id=1, source_target_pairs={{0,16},{16,0},{32,48},{48,32},{64,80},{80,64},{96,112},{112,96},{1... | collective-permute-start | bytes 983048 | tf_op jit(solution)/shard_map/ppermute | solution.py:40
  46.2 14.1 %collective-permute-start.2 = (bf16[4,64,512]{2,1,0:T(8,128)(2,1)S(1)}, bf16[4,64,512]{2,1,0:T(8,128)(2,1)S(1)}, u32[]{:S(2)}, u32[]{:S(2)}) collective-permute-start(bf16[4,64,512]{2,1,0:T(8,128)(2,1)S(1)} %pad_maximum_fusion.5), channel_id=1, source_target_pairs={{0,3},{1,2},{2,1},{3,0},{4,7},{5,6},{6,5},{7,4},{8,11},{9,10},{10,... | collective-permute-start | bytes 786440 | tf_op jit(solution)/shard_map/ppermute | solution.py:41
  47.6 19.1 %collective-permute-start.13 = (bf16[8,64,640]{2,1,0:T(8,128)(2,1)S(1)}, bf16[8,64,640]{2,1,0:T(8,128)(2,1)S(1)}, u32[]{:S(2)}, u32[]{:S(2)}) collective-permute-start(bf16[8,64,640]{2,1,0:T(8,128)(2,1)S(1)} %constant_dynamic-update-slice_fusion.8.own), channel_id=1, source_target_pairs={{0,1},{1,0},{2,3},{3,2},{4,5},{5,4},{6,7},{7,6},{8,9},{9,8},{10,11... | collective-permute-start | bytes 1966088 | tf_op jit(solution)/shard_map/ppermute | solution.py:41
  59.8 11.7 %collective-permute-start.8 = (bf16[8,64,640]{2,1,0:T(8,128)(2,1)S(1)}, bf16[8,64,640]{2,1,0:T(8,128)(2,1)S(1)}, u32[]{:S(2)}, u32[]{:S(2)}) collective-permute-start(bf16[8,64,640]{2,1,0:T(8,128)(2,1)S(1)} %constant_dynamic-update-slice_fusion.4.own), channel_id=1, source_target_pairs={{0,64},{16,80},{32,96},{48,112},{64,0},{80,16},{96,32},{112,48},{1... | collective-permute-start | bytes 1966088 | tf_op jit(solution)/shard_map/ppermute | solution.py:40
  60.3 15.0 %collective-permute-start.26 = (bf16[8,64,640]{2,1,0:T(8,128)(2,1)S(1)}, bf16[8,64,640]{2,1,0:T(8,128)(2,1)S(1)}, u32[]{:S(2)}, u32[]{:S(2)}) collective-permute-start(bf16[8,64,640]{2,1,0:T(8,128)(2,1)S(1)} %grow.14.own), channel_id=1, source_target_pairs={{0,3},{1,2},{2,1},{3,0},{4,7},{5,6},{6,5},{7,4},{8,11},{9,10},{10,... | collective-permute-start | bytes 1966088 | tf_op jit(solution)/shard_map/ppermute | solution.py:41
  66.7 20.5 %collective-permute-start.19 = (bf16[16,32,640]{2,1,0:T(8,128)(2,1)}, bf16[16,32,640]{2,1,0:T(8,128)(2,1)S(1)}, u32[]{:S(2)}, u32[]{:S(2)}) collective-permute-start(bf16[16,32,640]{2,1,0:T(8,128)(2,1)} %get-tuple-element.41), channel_id=1, source_target_pairs={{0,3},{1,2},{2,1},{3,0},{4,7},{5,6},{6,5},{7,4},{8,11},{9,10},{10,... | collective-permute-start | bytes 1966088 | tf_op jit(solution)/shard_map/ppermute | solution.py:41
  71.5 17.2 %collective-permute-start.14 = (bf16[16,32,640]{2,1,0:T(8,128)(2,1)}, bf16[16,32,640]{2,1,0:T(8,128)(2,1)S(1)}, u32[]{:S(2)}, u32[]{:S(2)}) collective-permute-start(bf16[16,32,640]{2,1,0:T(8,128)(2,1)} %get-tuple-element.39), channel_id=1, source_target_pairs={{0,16},{16,0},{32,48},{48,32},{64,80},{80,64},{96,112},{112,96},{1... | collective-permute-start | bytes 1966088 | tf_op jit(solution)/shard_map/ppermute | solution.py:40
  73.2 15.5 %collective-permute-start.9 = (bf16[16,32,640]{2,1,0:T(8,128)(2,1)}, bf16[16,32,640]{2,1,0:T(8,128)(2,1)S(1)}, u32[]{:S(2)}, u32[]{:S(2)}) collective-permute-start(bf16[16,32,640]{2,1,0:T(8,128)(2,1)} %get-tuple-element.37), channel_id=1, source_target_pairs={{0,1},{1,0},{2,3},{3,2},{4,5},{5,4},{6,7},{7,6},{8,9},{9,8},{10,11... | collective-permute-start | bytes 1966088 | tf_op jit(solution)/shard_map/ppermute | solution.py:41
  77.8 13.9 %collective-permute-start.28 = (bf16[16,32,640]{2,1,0:T(8,128)(2,1)}, bf16[16,32,640]{2,1,0:T(8,128)(2,1)S(1)}, u32[]{:S(2)}, u32[]{:S(2)}) collective-permute-start(bf16[16,32,640]{2,1,0:T(8,128)(2,1)} %get-tuple-element.46), channel_id=1, source_target_pairs={{0,48},{16,32},{32,16},{48,0},{64,112},{80,96},{96,80},{112,64},{1... | collective-permute-start | bytes 1966088 | tf_op jit(solution)/shard_map/ppermute | solution.py:40
  84.0 38.5 %collective-permute-start.33 = (bf16[16,32,640]{2,1,0:T(8,128)(2,1)S(1)}, bf16[16,32,640]{2,1,0:T(8,128)(2,1)S(1)}, u32[]{:S(2)}, u32[]{:S(2)}) collective-permute-start(bf16[16,32,640]{2,1,0:T(8,128)(2,1)S(1)} %copy-done.1), channel_id=1, source_target_pairs={{0,3},{1,2},{2,1},{3,0},{4,7},{5,6},{6,5},{7,4},{8,11},{9,10},{10,... | collective-permute-start | bytes 1966088 | tf_op jit(solution)/shard_map/ppermute | solution.py:41
  87.2 35.3 %collective-permute-start.32 = (bf16[16,32,640]{2,1,0:T(8,128)(2,1)S(1)}, bf16[16,32,640]{2,1,0:T(8,128)(2,1)S(1)}, u32[]{:S(2)}, u32[]{:S(2)}) collective-permute-start(bf16[16,32,640]{2,1,0:T(8,128)(2,1)S(1)} %copy-done.2), channel_id=1, source_target_pairs={{0,16},{16,0},{32,48},{48,32},{64,80},{80,64},{96,112},{112,96},{1... | collective-permute-start | bytes 1966088 | tf_op jit(solution)/shard_map/ppermute | solution.py:40
  88.7 33.8 %collective-permute-start.31 = (bf16[16,32,640]{2,1,0:T(8,128)(2,1)S(1)}, bf16[16,32,640]{2,1,0:T(8,128)(2,1)S(1)}, u32[]{:S(2)}, u32[]{:S(2)}) collective-permute-start(bf16[16,32,640]{2,1,0:T(8,128)(2,1)S(1)} %copy-done.3), channel_id=1, source_target_pairs={{0,1},{1,0},{2,3},{3,2},{4,5},{5,4},{6,7},{7,6},{8,9},{9,8},{10,11... | collective-permute-start | bytes 1966088 | tf_op jit(solution)/shard_map/ppermute | solution.py:41
  88.7 33.7 %collective-permute-start.34 = (bf16[16,32,640]{2,1,0:T(8,128)(2,1)}, bf16[16,32,640]{2,1,0:T(8,128)(2,1)S(1)}, u32[]{:S(2)}, u32[]{:S(2)}) collective-permute-start(bf16[16,32,640]{2,1,0:T(8,128)(2,1)} %get-tuple-element.54), channel_id=1, source_target_pairs={{0,48},{16,32},{32,16},{48,0},{64,112},{80,96},{96,80},{112,64},{1... | collective-permute-start | bytes 1966088 | tf_op jit(solution)/shard_map/ppermute | solution.py:40
  91.7 19.6 %collective-permute-start.30 = (bf16[16,32,512]{2,1,0:T(8,128)(2,1)S(1)}, bf16[16,32,512]{2,1,0:T(8,128)(2,1)S(1)}, u32[]{:S(2)}, u32[]{:S(2)}) collective-permute-start(bf16[16,32,512]{2,1,0:T(8,128)(2,1)S(1)} %copy-done.4), channel_id=1, source_target_pairs={{0,64},{16,80},{32,96},{48,112},{64,0},{80,16},{96,32},{112,48},{1... | collective-permute-start | bytes 1572872 | tf_op jit(solution)/shard_map/ppermute | solution.py:40
  111.2 28.7 %collective-permute-start.29 = (bf16[2,8,32,768]{3,2,1,0:T(8,128)(2,1)S(1)}, bf16[2,8,32,768]{3,2,1,0:T(8,128)(2,1)S(1)}, u32[]{:S(2)}, u32[]{:S(2)}) collective-permute-start(bf16[2,8,32,768]{3,2,1,0:T(8,128)(2,1)S(1)} %get-tuple-element.49), channel_id=1, source_target_pairs={{0,4},{4,0},{8,12},{12,8},{1,5},{5,1},{9,13},{13,9},{2,6},{6,2},{1... | collective-permute-start | bytes 2359304 | tf_op jit(solution)/shard_map/ppermute | solution.py:45
  140.1 13.0 %collective-permute-start.35 = (bf16[8,32,768]{2,1,0:T(8,128)(2,1)S(1)}, bf16[8,32,768]{2,1,0:T(8,128)(2,1)S(1)}, u32[]{:S(2)}, u32[]{:S(2)}) collective-permute-start(bf16[8,32,768]{2,1,0:T(8,128)(2,1)S(1)} %get-tuple-element.57), channel_id=1, source_target_pairs={{0,8},{4,12},{8,0},{12,4},{1,9},{5,13},{9,1},{13,5},{2,10},{6,14},... | collective-permute-start | bytes 1179656 | tf_op jit(solution)/shard_map/ppermute | solution.py:45
  142.9 17.4 %collective-permute-start.37 = (bf16[8,32,768]{2,1,0:T(8,128)(2,1)S(1)}, bf16[8,32,768]{2,1,0:T(8,128)(2,1)S(1)}, u32[]{:S(2)}, u32[]{:S(2)}) collective-permute-start(bf16[8,32,768]{2,1,0:T(8,128)(2,1)S(1)} %get-tuple-element.64), channel_id=1, source_target_pairs={{0,8},{4,12},{8,0},{12,4},{1,9},{5,13},{9,1},{13,5},{2,10},{6,14},... | collective-permute-start | bytes 1179656 | tf_op jit(solution)/shard_map/ppermute | solution.py:45
  (21 other events, 238.0 us)

commit v5 on v4

--- a/solution.py
+++ b/solution.py
@@ -16,13 +16,11 @@
 FEATS = 3072
 HID = 768
 X, Y0, Y1, Z0, Z1 = 16, 4, 12, 1, 3
-DIMS = (Z0, Y0, Z1, Y1, X)
-WIDTHS = (512, 640, 640, 640, 640)
-OFFSETS = tuple(int(v) for v in np.cumsum((0,) + WIDTHS)[:-1])
-CHAINS = len(WIDTHS)
+DIMS = (X, Z0, Y0, Z1, Y1)
+CHAINS = 4
+WIDTH = FEATS // CHAINS
+ORDERS = tuple(tuple(DIMS[1 + (p + k) % 4] for k in range(4)) for p in range(CHAINS))
 HOPS = (Z0, Z1, Z0 ^ Z1)
-ORDERS = tuple(tuple(DIMS[(p + k) % 5] for k in range(5)) for p in range(CHAINS))
-TIED = 4
 PARTS = (32, 32)
 STARTS = (0, 32)
 
@@ -59,69 +57,94 @@
 SMEM = pl.BlockSpec(memory_space=pltpu.SMEM)
 
 
-def cut_kernel(where, grad_out, pre, *refs):
-    outs, chunks, sem = refs[:CHAINS], refs[CHAINS:-1], refs[-1]
+def cut_kernel(where, pre, *refs):
+    chunks, sem = refs[:-1], refs[-1]
     row, col = where[0], where[1]
-    copies = [
-        pltpu.make_async_copy(grad_out.at[:, pl.ds(OFFSETS[p], WIDTHS[p])], outs[p].at[0], sem.at[p])
-        for p in range(CHAINS)
-    ]
     half = SHARDS * ROWS // 8
+    copies = []
     for j, mask in enumerate(HOPS):
         here = pre.at[
             pl.ds(pl.multiple_of(row % 2 * half, half), half), pl.ds(pl.multiple_of((col ^ mask) * HID, HID), HID)
         ]
-        copies.append(pltpu.make_async_copy(here, chunks[j], sem.at[CHAINS + j]))
+        copies.append(pltpu.make_async_copy(here, chunks[j], sem.at[j]))
     for c in copies:
         c.start()
     for c in copies:
         c.wait()
 
 
-def cut_call(where, grad_out, pre):
+def cut_call(where, pre):
     return pl.pallas_call(
         cut_kernel,
-        out_shape=[jax.ShapeDtypeStruct((1, ROWS, w), jnp.bfloat16) for w in WIDTHS]
-        + [jax.ShapeDtypeStruct((SHARDS * ROWS // 8, HID), jnp.bfloat16)] * len(HOPS),
-        in_specs=[SMEM, ANY, ANY],
-        out_specs=[ANY] * (CHAINS + len(HOPS)),
-        scratch_shapes=[pltpu.SemaphoreType.DMA((CHAINS + len(HOPS),))],
+        out_shape=[jax.ShapeDtypeStruct((SHARDS * ROWS // 8, HID), jnp.bfloat16)] * len(HOPS),
+        in_specs=[SMEM, ANY],
+        out_specs=[ANY] * len(HOPS),
+        scratch_shapes=[pltpu.SemaphoreType.DMA((len(HOPS),))],
         compiler_params=params(1),
         cost_estimate=TINY,
         name="cut",
-    )(where, in_hbm(grad_out), in_hbm(pre))
-
-
-def grow_kernel(rows, own, got, *refs):
-    outs, sem = refs[-1 - len(rows) : -1], refs[-1]
-    blocks = own.shape[0]
+    )(where, in_hbm(pre))
+
+
+def split_kernel(own, got, *refs):
+    outs, sem = refs[-1 - CHAINS : -1], refs[-1]
     copies = []
-    for out, (at, n) in zip(outs, rows):
+    for p in range(CHAINS):
         for side, src in enumerate((own, got)):
-            copies.append(
-                pltpu.make_async_copy(
-                    src.at[:, pl.ds(at, n)], out.at[pl.ds(side * blocks, blocks)], sem.at[len(copies)]
-                )
-            )
+            here = src.at[:, pl.ds(p * WIDTH, WIDTH)]
+            copies.append(pltpu.make_async_copy(here, outs[p].at[side], sem.at[len(copies)]))
     for c in copies:
         c.start()
     for c in copies:
         c.wait()
 
 
-def grow_call(own, got, rows=((0, ROWS),), after=()):
-    blocks, _, w = own.shape
+def split_call(own, got, after=()):
+    return pl.pallas_call(
+        split_kernel,
+        out_shape=[jax.ShapeDtypeStruct((2, ROWS, WIDTH), jnp.bfloat16)] * CHAINS,
+        in_specs=[ANY] * (2 + len(after)),
+        out_specs=[ANY] * CHAINS,
+        scratch_shapes=[pltpu.SemaphoreType.DMA((2 * CHAINS,))],
+        compiler_params=params(1),
+        cost_estimate=TINY,
+        name="split",
+    )(in_hbm(own), got, *after)
+
+
+def grow_kernel(rows, joined, *refs):
+    own, got, sem = refs[:CHAINS], refs[CHAINS : 2 * CHAINS], refs[-1]
+    outs = refs[-1 - len(rows) * CHAINS - (joined > 0) : -1]
+    copies = []
+    for part, (at, n) in enumerate(rows):
+        for p in range(CHAINS):
+            blocks = own[p].shape[0]
+            for side, src in enumerate((own[p], got[p])):
+                there = outs[part * CHAINS + p].at[pl.ds(side * blocks, blocks)]
+                copies.append(pltpu.make_async_copy(src.at[:, pl.ds(at, n)], there, sem.at[len(copies)]))
+    for j in range(joined):
+        src = refs[2 * CHAINS + j]
+        copies.append(pltpu.make_async_copy(src, outs[-1].at[j], sem.at[len(copies)]))
+    for c in copies:
+        c.start()
+    for c in copies:
+        c.wait()
+
+
+def grow_call(own, got, rows=((0, ROWS),), join=(), after=()):
+    blocks = own[0].shape[0]
     shape = pltpu.HBM if len(rows) > 1 else jax.ShapeDtypeStruct
     return pl.pallas_call(
-        functools.partial(grow_kernel, rows),
-        out_shape=[shape((2 * blocks, n, w), jnp.bfloat16) for _, n in rows],
-        in_specs=[ANY] * (2 + len(after)),
-        out_specs=[ANY] * len(rows),
-        scratch_shapes=[pltpu.SemaphoreType.DMA((2 * len(rows),))],
+        functools.partial(grow_kernel, rows, len(join)),
+        out_shape=[shape((2 * blocks, n, WIDTH), jnp.bfloat16) for _, n in rows for _ in range(CHAINS)]
+        + [jax.ShapeDtypeStruct((len(join), *j.shape), jnp.bfloat16) for j in join[:1]],
+        in_specs=[ANY] * (2 * CHAINS + len(join) + len(after)),
+        out_specs=[ANY] * (len(rows) * CHAINS + (len(join) > 0)),
+        scratch_shapes=[pltpu.SemaphoreType.DMA((2 * CHAINS * len(rows) + len(join),))],
         compiler_params=params(1),
         cost_estimate=TINY,
         name="grow",
-    )(own, got, *after)
+    )(*own, *got, *join, *after)
 
 
 def gelu_kernel(where, table, pre, got_a, got_b, got_c, other, *refs):
@@ -138,7 +161,7 @@
         )
     ]
     for j, got in enumerate((got_a, got_b, got_c)):
-        for side, src in ((core, got), (1 - core, other.at[pl.ds(j * half, half)])):
+        for side, src in ((core, got), (1 - core, other.at[j])):
             at = pl.multiple_of((col ^ HOPS[j]) * quarter + side * half, half)
             copies.append(pltpu.make_async_copy(src, buf.at[pl.ds(at, half)], sems.at[len(copies)]))
     for c in copies:
@@ -200,12 +223,10 @@
     if p == 0:
         return [((every,) * 4, (side,) + (every,) * 4)] if side == top else []
     if p == 1:
-        return [((top,) + (every,) * 3, (top,) + (every,) * 3 + (side,))]
+        return [((top,) + (every,) * 3, (top,) + (every,) * 2 + (side, every))]
     if p == 2:
-        return [((i, top) + (every,) * 2, (top,) + (every,) * 2 + (side, i)) for i in range(2)]
-    if p == 3:
-        return [((every,) * 2 + (top, j), (top, j, side) + (every,) * 2) for j in range(2)]
-    return [((every,) * 3 + (top,), (top, side) + (every,) * 3)]
+        return [((i, top) + (every,) * 2, (top, every, side, i, every)) for i in range(2)]
+    return [((every,) * 2 + (top, every), (top, side) + (every,) * 3)]
 
 
 def hidden_kernel(n, where, w_far, *refs):
@@ -213,47 +234,38 @@
     keep, send, gathered, g, w, hs, sems = refs[-7:]
     row, mine = where[0], where[2]
     per = SHARDS // 4
-    step = HID // 3
-    weights = [
-        pltpu.make_async_copy(w_far.at[pl.ds(k * step, step)], w.at[pl.ds(k * step, step)], sems.at[3 + k])
-        for k in range(3)
-    ]
+    weights = pltpu.make_async_copy(w_far, w, sems.at[4])
+    weights.start()
     for top in range(2):
         for p in range(CHAINS):
             for side in range(2):
                 for src, dst in pieces(p, side, top):
                     pltpu.make_async_copy(
                         blocks[2 * p + side].at[src],
-                        g.at[dst + (slice(None), pl.ds(OFFSETS[p], WIDTHS[p]))],
+                        g.at[dst + (slice(None), pl.ds(p * WIDTH, WIDTH))],
                         sems.at[top],
                     ).start()
-        if top == 0:
-            for c in weights:
-                c.start()
     outs = []
     for i in range(2):
         pltpu.make_async_copy(g.at[i], g.at[i], sems.at[i]).wait()
-        outs.append(pltpu.make_async_copy(g.at[i], gathered.at[i], sems.at[2 if i else 6]))
+        if i == 0:
+            weights.wait()
+        outs.append(pltpu.make_async_copy(g.at[i], gathered.at[i], sems.at[2 + i]))
         outs[-1].start()
-        for k in range(3):
-            if i == 0:
-                weights[k].wait()
-            h = lax.dot_general(
-                g[i].reshape(2 * per * n, FEATS),
-                w[k * step : (k + 1) * step, :],
-                (((1,), (1,)), ((), ())),
-                preferred_element_type=jnp.float32,
-            )
-            hs[i, :, :, :, k * step : (k + 1) * step] = h.reshape(2, per, n, step)
+        h = lax.dot_general(
+            g[i].reshape(2 * per * n, FEATS), w[...], (((1,), (1,)), ((), ())), preferred_element_type=jnp.float32
+        )
+        hs[i] = h.reshape(2, 2, 2, 2, n, HID)
     for a, b in ((1, 1), (0, 1), (1, 0), (0, 0)):
         off_x = (mine // 16) ^ (row // 2) ^ a
         off_y = (mine // 8 % 2) ^ (row % 2) ^ b
         for j in range(per):
-            slot = (mine % 8) ^ (mask_of(j) % 8) ^ (off_y * 4)
+            slot = (mine % 8) ^ (mask_of(2 * j) % 8) ^ (off_y * 4)
+            here = hs[off_y, j // 4, j // 2 % 2, j % 2, off_x]
             if b:
-                send[a, slot] = hs[off_x, off_y, j].astype(jnp.bfloat16)
+                send[a, slot] = here.astype(jnp.bfloat16)
             else:
-                keep[a, slot] = hs[off_x, off_y, j]
+                keep[a, slot] = here
     for out in outs:
         out.wait()
 
@@ -273,8 +285,8 @@
         scratch_shapes=[
             pltpu.VMEM((2,) * 5 + (n, FEATS), jnp.bfloat16),
             pltpu.VMEM((HID, FEATS), jnp.bfloat16),
-            pltpu.VMEM((2, 2, per, n, HID), jnp.float32),
-            pltpu.SemaphoreType.DMA((7,)),
+            pltpu.VMEM((2,) * 5 + (n, HID), jnp.float32),
+            pltpu.SemaphoreType.DMA((5,)),
         ],
         compiler_params=params(14 + n // 2),
         cost_estimate=pl.CostEstimate(
@@ -343,28 +355,22 @@
     where = jnp.stack([row, col, depth * 4 + col]).astype(jnp.int32)
     table = jnp.asarray([mask_of(c) for c in range(SHARDS)], jnp.int32)
 
-    cuts = cut_call(where, grad_out, pre_act)
-    blocks, chunks = cuts[:CHAINS], cuts[CHAINS:]
-    fetched = []
-    for k in range(3):
-        got = [swap(blocks[p], ORDERS[p][k]) for p in range(CHAINS)]
-        fetched.append(swap(chunks[k], HOPS[k]))
-        blocks = [
-            grow_call(b, r, after=(fetched[k],))[0] if p == TIED else jnp.concatenate([b, r], 0)
-            for p, (b, r) in enumerate(zip(blocks, got))
-        ]
-    got = [swap(blocks[p], ORDERS[p][3]) for p in range(CHAINS)]
-    other = swap_row(jnp.concatenate(fetched, 0), 1)
-    grown = [
-        grow_call(b, r, tuple(zip(STARTS, PARTS)), after=(other,) if p == TIED else ())
-        for p, (b, r) in enumerate(zip(blocks, got))
-    ]
-    own = [[grown[p][part] for p in range(CHAINS)] for part in range(2)]
-    came = [[swap(own[part][p], ORDERS[p][4]) for p in range(CHAINS)] for part in range(2)]
+    got = swap(in_hbm(grad_out), X)
+    fetched = [swap(chunk, mask) for chunk, mask in zip(cut_call(where, pre_act), HOPS)]
+    blocks = split_call(grad_out, got)
+    got = [swap(blocks[p], ORDERS[p][0]) for p in range(CHAINS)]
+    *blocks, both = grow_call(blocks, got, join=fetched)
+    got = [swap(blocks[p], ORDERS[p][1]) for p in range(CHAINS)]
+    other = swap_row(both, 1)
+    blocks = grow_call(blocks, got, after=(other,))
+    got = [swap(blocks[p], ORDERS[p][2]) for p in range(CHAINS)]
     act_a, act_b, slope_a, slope_b = gelu_call(where, table, pre_act, fetched, other)
+    grown = grow_call(blocks, got, tuple(zip(STARTS, PARTS)), after=(slope_a,))
+    own = grown[:CHAINS], grown[CHAINS:]
+    came = [[swap(own[part][p], ORDERS[p][3]) for p in range(CHAINS)] for part in range(2)]
 
     pairs = [[b for p in range(CHAINS) for b in (own[part][p], came[part][p])] for part in range(2)]
-    keep_a, send_a, g_a = hidden_call(0, where, w_down, pairs[0], after=(slope_a,))
+    keep_a, send_a, g_a = hidden_call(0, where, w_down, pairs[0])
     keep_b, send_b, g_b = hidden_call(1, where, w_down, pairs[1], after=(keep_a,))
     mine_a, far_a = total_call(keep_a, swap_row(send_a, 1), after=(keep_b,))
     far_a = swap_row(far_a, 2)

time: 162 us -> 156 us (0.963)
  starting transfers between devices: 62.6 us -> 49.9 us
  waiting for transfers between devices: 42 us -> 50.9 us
    ppermute x15 -> x13, waiting for transfers between devices: 9.34 us -> 22.8 us  [swap(): return lax.ppermute(x, 'col', [(i, i ^ mask) for i in range(4)])]
    ppermute x18 -> x11, starting transfers between devices: 24.8 us -> 14.6 us  [swap(): return lax.ppermute(x, 'depth', [(i, i ^ mask >> 2) for i in range(8)])]
    ppermute x18 -> x11, waiting for transfers between devices: 25.6 us -> 20.5 us  [swap(): return lax.ppermute(x, 'depth', [(i, i ^ mask >> 2) for i in range(8)])]
    pallas_call x2, Pallas kernels: 22.2 us -> 18.8 us  [hidden_call(): pl.pallas_call(functools.partial(hidden_kernel, n), out_shape=[jax.ShapeD...]
    pallas_call x9 -> x5, Pallas kernels: 8.34 us -> 10.2 us  [the longest x3 7.09 us: grow_call(): pl.pallas_call(functools.partial(grow_kernel, rows, len(join)), out_shape...]
    ppermute x5, starting transfers between devices: 18.4 us -> 16.7 us  [swap_row(): return lax.ppermute(x, 'row', [(i, i ^ mask) for i in range(4)])]
    ppermute x15 -> x13, starting transfers between devices: 19.5 us -> 18.5 us  [swap(): return lax.ppermute(x, 'col', [(i, i ^ mask) for i in range(4)])]
  transfers between devices with their start and end apart: 38 -> 29, of which waited for: 10 -> 14; matrix products, arithmetic and copies ran while one was open for 0% -> 0% of each run, Pallas kernels for 32% -> 29%
where the time goes in v5:
time: 156 us
  Pallas kernels  52.3 us (34%)
  waiting for transfers between devices  50.9 us (33%)
  starting transfers between devices  49.9 us (32%)
    ppermute x13, waiting for transfers between devices, swap(): return lax.ppermute(x, 'col', [(i, i ^ mask) for i in range(4)])  22.8 us
    ppermute x11, waiting for transfers between devices, swap(): return lax.ppermute(x, 'depth', [(i, i ^ mask >> 2) for i in range(8)])  20.5 us
    pallas_call x2, Pallas kernels, hidden_call(): pl.pallas_call(functools.partial(hidden_kernel, n), out_shape=[jax.ShapeD...  18.8 us
    ppermute x13, starting transfers between devices, swap(): return lax.ppermute(x, 'col', [(i, i ^ mask) for i in range(4)])  18.5 us
    ppermute x5, starting transfers between devices, swap_row(): return lax.ppermute(x, 'row', [(i, i ^ mask) for i in range(4)])  16.7 us
    pallas_call x2, Pallas kernels, down_call(): pl.pallas_call(down_kernel, grid=(count,), out_shape=pltpu.HBM((HID, FEAT...  15.7 us
    ppermute x11, starting transfers between devices, swap(): return lax.ppermute(x, 'depth', [(i, i ^ mask >> 2) for i in range(8)])  14.6 us
    ppermute x5, waiting for transfers between devices, swap_row(): return lax.ppermute(x, 'row', [(i, i ^ mask) for i in range(4)])  7.63 us
  transfers between devices with their start and end apart: 29, of which 14 were waited for; matrix products, arithmetic and copies ran while one was open for 0% of the time, Pallas kernels for 29%

profile of v5, /device:TPU:1, one launch (start us, length us, event | category | flops | bytes accessed | tf_op | source)
XLA Modules:
  0.0 155.8 jit_solution(17012094485049342426)
XLA Ops:
  0.6 2.1 %collective-permute-start = (bf16[64,3072]{1,0:T(8,128)(2,1)}, bf16[64,3072]{1,0:T(8,128)(2,1)S(1)}, u32[]{:S(2)}, u32[]{:S(2)}) collective-permute-start(bf16[64,3072]{1,0:T(8,128)(2,1)} %own.1), channel_id=1, source_target_pairs={{0,64},{16,80},{32,96},{48,112},{64,0},{80,16},{96,32},{112,48},{1... | collective-permute-start | bytes 1179656 | tf_op jit(solution)/shard_map/ppermute | solution.py:38
  6.4 2.2 %collective-permute-start.6 = (bf16[256,768]{1,0:T(8,128)(2,1)S(1)}, bf16[256,768]{1,0:T(8,128)(2,1)S(1)}, u32[]{:S(2)}, u32[]{:S(2)}) collective-permute-start(bf16[256,768]{1,0:T(8,128)(2,1)S(1)} %get-tuple-element.45), channel_id=1, source_target_pairs={{0,3},{1,2},{2,1},{3,0},{4,7},{5,6},{6,5},{7,4},{8,11},{9,10},{10,... | collective-permute-start | bytes 1179656 | tf_op jit(solution)/shard_map/ppermute | solution.py:39
  13.3 2.1 %collective-permute-start.1 = (bf16[2,64,768]{2,1,0:T(8,128)(2,1)S(1)}, bf16[2,64,768]{2,1,0:T(8,128)(2,1)S(1)}, u32[]{:S(2)}, u32[]{:S(2)}) collective-permute-start(bf16[2,64,768]{2,1,0:T(8,128)(2,1)S(1)} %get-tuple-element.40.refs_0_), channel_id=1, source_target_pairs={{0,1},{1,0},{2,3},{3,2},{4,5},{5,4},{6,7},{7,6},{8,9},{9,8},{10,11... | collective-permute-start | bytes 589832 | tf_op jit(solution)/shard_map/ppermute | solution.py:39
  16.8 2.2 %collective-permute-start.3 = (bf16[2,64,768]{2,1,0:T(8,128)(2,1)S(1)}, bf16[2,64,768]{2,1,0:T(8,128)(2,1)S(1)}, u32[]{:S(2)}, u32[]{:S(2)}) collective-permute-start(bf16[2,64,768]{2,1,0:T(8,128)(2,1)S(1)} %get-tuple-element.42.refs_2_), channel_id=1, source_target_pairs={{0,3},{1,2},{2,1},{3,0},{4,7},{5,6},{6,5},{7,4},{8,11},{9,10},{10,... | collective-permute-start | bytes 589832 | tf_op jit(solution)/shard_map/ppermute | solution.py:39
  19.0 4.1 %collective-permute-done.6.refs_9_.got_b = bf16[256,768]{1,0:T(8,128)(2,1)S(1)} collective-permute-done((bf16[256,768]{1,0:T(8,128)(2,1)S(1)}, bf16[256,768]{1,0:T(8,128)(2,1)S(1)}, u32[]{:S(2)}, u32[]{:S(2)}) %collective-permute-start.6) | collective-permute-done | bytes 393248 | tf_op jit(solution)/shard_map/ppermute | solution.py:39
  23.1 2.7 %collective-permute-start.4 = (bf16[2,64,768]{2,1,0:T(8,128)(2,1)S(1)}, bf16[2,64,768]{2,1,0:T(8,128)(2,1)S(1)}, u32[]{:S(2)}, u32[]{:S(2)}) collective-permute-start(bf16[2,64,768]{2,1,0:T(8,128)(2,1)S(1)} %get-tuple-element.43.refs_3_), channel_id=1, source_target_pairs={{0,48},{16,32},{32,16},{48,0},{64,112},{80,96},{96,80},{112,64},{1... | collective-permute-start | bytes 589832 | tf_op jit(solution)/shard_map/ppermute | solution.py:38
  27.5 4.3 %collective-permute-done.3.refs_6_ = bf16[2,64,768]{2,1,0:T(8,128)(2,1)S(1)} collective-permute-done((bf16[2,64,768]{2,1,0:T(8,128)(2,1)S(1)}, bf16[2,64,768]{2,1,0:T(8,128)(2,1)S(1)}, u32[]{:S(2)}, u32[]{:S(2)}) %collective-permute-start.3) | collective-permute-done | bytes 196640 | tf_op jit(solution)/shard_map/ppermute | solution.py:39
  31.8 2.7 %grow.3 = (bf16[4,64,768]{2,1,0:T(8,128)(2,1)S(1)}, bf16[4,64,768]{2,1,0:T(8,128)(2,1)S(1)}, bf16[4,64,768]{2,1,0:T(8,128)(2,1)S(1)}, bf16[4,64,768]{2,1,0:T(8,128)(2,1)S(1)}, bf16[3,256,768]{2,1,0:T(8,128)(2,1)S(1)}) custom-call(bf16[2,64,768]{2,1,0:T(8,128)(2,1)S(1)} %get-tuple-element.40.refs_0_, bf16[2,64,768]{2,1,0:T(8,128)(2,1)S(1)} %get-tuple-element.41.refs_1_, ...), custom_call_target="tpu_custom_call" | custom-call | flops 1 | bytes 1 | tf_op jit(solution)/shard_map/grow/pallas_call | solution.py:137
  34.5 3.3 %collective-permute-start.12 = (bf16[3,256,768]{2,1,0:T(8,128)(2,1)S(1)}, bf16[3,256,768]{2,1,0:T(8,128)(2,1)S(1)}, u32[]{:S(2)}, u32[]{:S(2)}) collective-permute-start(bf16[3,256,768]{2,1,0:T(8,128)(2,1)S(1)} %get-tuple-element.51), channel_id=1, source_target_pairs={{0,4},{4,0},{8,12},{12,8},{1,5},{5,1},{9,13},{13,9},{2,6},{6,2},{1... | collective-permute-start | bytes 3538952 | tf_op jit(solution)/shard_map/ppermute | solution.py:43
  37.9 3.4 %collective-permute-start.9 = (bf16[4,64,768]{2,1,0:T(8,128)(2,1)S(1)}, bf16[4,64,768]{2,1,0:T(8,128)(2,1)S(1)}, u32[]{:S(2)}, u32[]{:S(2)}) collective-permute-start(bf16[4,64,768]{2,1,0:T(8,128)(2,1)S(1)} %get-tuple-element.48.refs_1_), channel_id=1, source_target_pairs={{0,3},{1,2},{2,1},{3,0},{4,7},{5,6},{6,5},{7,4},{8,11},{9,10},{10,... | collective-permute-start | bytes 1179656 | tf_op jit(solution)/shard_map/ppermute | solution.py:39
  41.3 2.6 %collective-permute-start.10 = (bf16[4,64,768]{2,1,0:T(8,128)(2,1)S(1)}, bf16[4,64,768]{2,1,0:T(8,128)(2,1)S(1)}, u32[]{:S(2)}, u32[]{:S(2)}) collective-permute-start(bf16[4,64,768]{2,1,0:T(8,128)(2,1)S(1)} %get-tuple-element.49.refs_2_), channel_id=1, source_target_pairs={{0,48},{16,32},{32,16},{48,0},{64,112},{80,96},{96,80},{112,64},{1... | collective-permute-start | bytes 1179656 | tf_op jit(solution)/shard_map/ppermute | solution.py:38
  43.9 4.5 %collective-permute-done.8.refs_4_ = bf16[4,64,768]{2,1,0:T(8,128)(2,1)S(1)} collective-permute-done((bf16[4,64,768]{2,1,0:T(8,128)(2,1)S(1)}, bf16[4,64,768]{2,1,0:T(8,128)(2,1)S(1)}, u32[]{:S(2)}, u32[]{:S(2)}) %collective-permute-start.8) | collective-permute-done | bytes 393248 | tf_op jit(solution)/shard_map/ppermute | solution.py:38
  58.1 7.2 %gelu.1 = (bf16[768,1024]{1,0:T(8,128)(2,1)S(1)}, bf16[768,1024]{1,0:T(8,128)(2,1)S(1)}, f32[8,32,768]{2,1,0:T(8,128)S(1)}, f32[8,32,768]{2,1,0:T(8,128)S(1)}) custom-call(s32[3]{0:T(128)S(1)} %pad_add_fusion.where, s32[32]{0:T(128)S(1)} %copy-done, bf16[512,3072]{1,0:T(8,128)(2,1)} %pre.3, bf16[256,768]{1,0:T(8,128)(2,1)S(1)} %collective-permute-done.5.refs_8_.got_a, ...), custom_call_target="tpu_custom_call" | custom-call | flops 1 | bytes 1 | tf_op jit(solution)/shard_map/gelu/pallas_call | solution.py:207
  65.3 8.8 %collective-permute-done.13.refs_4_ = bf16[8,64,768]{2,1,0:T(8,128)(2,1)S(1)} collective-permute-done((bf16[8,64,768]{2,1,0:T(8,128)(2,1)S(1)}, bf16[8,64,768]{2,1,0:T(8,128)(2,1)S(1)}, u32[]{:S(2)}, u32[]{:S(2)}) %collective-permute-start.13) | collective-permute-done | bytes 786464 | tf_op jit(solution)/shard_map/ppermute | solution.py:39
  74.9 2.8 %grow.5 = (bf16[16,32,768]{2,1,0:T(8,128)(2,1)}, bf16[16,32,768]{2,1,0:T(8,128)(2,1)}, bf16[16,32,768]{2,1,0:T(8,128)(2,1)}, bf16[16,32,768]{2,1,0:T(8,128)(2,1)...) custom-call(bf16[8,64,768]{2,1,0:T(8,128)(2,1)S(1)} %get-tuple-eleme, ...), custom_call_target="tpu_custom_call" | custom-call | flops 1 | bytes 1 | tf_op jit(solution)/shard_map/grow/pallas_call | solution.py:137
  79.6 2.2 %collective-permute-start.20 = (bf16[16,32,768]{2,1,0:T(8,128)(2,1)}, bf16[16,32,768]{2,1,0:T(8,128)(2,1)S(1)}, u32[]{:S(2)}, u32[]{:S(2)}) collective-permute-start(bf16[16,32,768]{2,1,0:T(8,128)(2,1)} %get-tuple-element.60), channel_id=1, source_target_pairs={{0,3},{1,2},{2,1},{3,0},{4,7},{5,6},{6,5},{7,4},{8,11},{9,10},{10,... | collective-permute-start | bytes 2359304 | tf_op jit(solution)/shard_map/ppermute | solution.py:39
  83.7 12.1 %collective-permute-done.17 = bf16[16,32,768]{2,1,0:T(8,128)(2,1)S(1)} collective-permute-done((bf16[16,32,768]{2,1,0:T(8,128)(2,1)}, bf16[16,32,768]{2,1,0:T(8,128)(2,1)S(1)}, u32[]{:S(2)}, u32[]{:S(2)}) %collective-permute-start.17) | collective-permute-done | bytes 786464 | tf_op jit(solution)/shard_map/ppermute | solution.py:38
  98.7 9.4 %hidden.2 = (f32[2,8,32,768]{3,2,1,0:T(8,128)S(1)}, bf16[2,8,32,768]{3,2,1,0:T(8,128)(2,1)S(1)}, bf16[2,2,2,2,2,32,3072]{6,5,4,3,2,1,0:T(8,128)(2,1)}) custom-call(s32[3]{0:T(128)S(1)} %pad_add_fusion.where, bf16[768,3072]{1,0:T(8,128)(2,1)S(1)} %bitcast.23, bf16[2,2,2,2,32,768]{5,4,3,2,1,0:T(8,128)(2,1)} %bitcast.41, ...), custom_call_target="tpu_custom_call" | custom-call | flops 4831838208 | bytes 12582912 | tf_op jit(solution)/shard_map/hidden/pallas_call | solution.py:276
  108.1 8.2 %collective-permute-start.21 = (bf16[2,8,32,768]{3,2,1,0:T(8,128)(2,1)S(1)}, bf16[2,8,32,768]{3,2,1,0:T(8,128)(2,1)S(1)}, u32[]{:S(2)}, u32[]{:S(2)}) collective-permute-start(bf16[2,8,32,768]{3,2,1,0:T(8,128)(2,1)S(1)} %get-tuple-element.62), channel_id=1, source_target_pairs={{0,4},{4,0},{8,12},{12,8},{1,5},{5,1},{9,13},{13,9},{2,6},{6,2},{1... | collective-permute-start | bytes 2359304 | tf_op jit(solution)/shard_map/ppermute | solution.py:43
  116.3 9.4 %hidden.3 = (f32[2,8,32,768]{3,2,1,0:T(8,128)S(1)}, bf16[2,8,32,768]{3,2,1,0:T(8,128)(2,1)S(1)}, bf16[2,2,2,2,2,32,3072]{6,5,4,3,2,1,0:T(8,128)(2,1)}) custom-call(s32[3]{0:T(128)S(1)} %pad_add_fusion.where, bf16[768,3072]{1,0:T(8,128)(2,1)S(1)} %bitcast.23, bf16[2,2,2,2,32,768]{5,4,3,2,1,0:T(8,128)(2,1)} %bitcast.37, ...), custom_call_target="tpu_custom_call" | custom-call | flops 4831838208 | bytes 12582912 | tf_op jit(solution)/shard_map/hidden/pallas_call | solution.py:276
  127.8 6.0 %down.2.refs_0_ = bf16[768,3072]{1,0:T(8,128)(2,1)} custom-call(bf16[768,1024]{1,0:T(8,128)(2,1)S(1)} %get-tuple-element.71.at_a, bf16[768,1024]{1,0:T(8,128)(2,1)S(1)} %get-tuple-element.72.at_b, bf16[1024,3072]{1,0:T(8,128)(2,1)} %bitcast.32, bf16[1024,3072]{1,0:T(8,128)(2,1)} %bitcast.34), custom_call_target="tpu_custom_call" | custom-call | flops 3221225472 | bytes 5767168 | tf_op jit(solution)/shard_map/down/pallas_call | solution.py:338
  134.0 2.5 %collective-permute-start.26 = (bf16[8,32,768]{2,1,0:T(8,128)(2,1)S(1)}, bf16[8,32,768]{2,1,0:T(8,128)(2,1)S(1)}, u32[]{:S(2)}, u32[]{:S(2)}) collective-permute-start(bf16[8,32,768]{2,1,0:T(8,128)(2,1)S(1)} %get-tuple-element.69), channel_id=1, source_target_pairs={{0,8},{4,12},{8,0},{12,4},{1,9},{5,13},{9,1},{13,5},{2,10},{6,14},... | collective-permute-start | bytes 1179656 | tf_op jit(solution)/shard_map/ppermute | solution.py:43
  137.3 9.7 %down.3 = bf16[768,3072]{1,0:T(8,128)(2,1)} custom-call(bf16[768,1024]{1,0:T(8,128)(2,1)S(1)} %get-tuple-element.71.at_a, bf16[768,1024]{1,0:T(8,128)(2,1)S(1)} %get-tuple-element.72.at_b, bf16[1024,3072]{1,0:T(8,128)(2,1)} %bitcast.33, bf16[1024,3072]{1,0:T(8,128)(2,1)} %bitcast.35, bf16[768,3072]{1,0:T(8,128)(2,1)} %down.2.refs_0_), custom_call_target="tpu_custom_call", output_to_operand_aliasing={{}: (4, {})} | custom-call | flops 6442450944 | bytes 11534336 | tf_op jit(solution)/shard_map/down/pallas_call | solution.py:338
  147.1 7.6 %collective-permute-done.28 = bf16[8,32,768]{2,1,0:T(8,128)(2,1)S(1)} collective-permute-done((bf16[8,32,768]{2,1,0:T(8,128)(2,1)S(1)}, bf16[8,32,768]{2,1,0:T(8,128)(2,1)S(1)}, u32[]{:S(2)}, u32[]{:S(2)}) %collective-permute-start.28) | collective-permute-done | bytes 393248 | tf_op jit(solution)/shard_map/ppermute | solution.py:43
  (59 shorter events, 32.4 us)
Async XLA Ops:
  4.6 12.1 %collective-permute-start.5 = (bf16[256,768]{1,0:T(8,128)(2,1)S(1)}, bf16[256,768]{1,0:T(8,128)(2,1)S(1)}, u32[]{:S(2)}, u32[]{:S(2)}) collective-permute-start(bf16[256,768]{1,0:T(8,128)(2,1)S(1)} %get-tuple-element.44), channel_id=1, source_target_pairs={{0,1},{1,0},{2,3},{3,2},{4,5},{5,4},{6,7},{7,6},{8,9},{9,8},{10,11... | collective-permute-start | bytes 1179656 | tf_op jit(solution)/shard_map/ppermute | solution.py:39
  6.4 16.8 %collective-permute-start.6 = (bf16[256,768]{1,0:T(8,128)(2,1)S(1)}, bf16[256,768]{1,0:T(8,128)(2,1)S(1)}, u32[]{:S(2)}, u32[]{:S(2)}) collective-permute-start(bf16[256,768]{1,0:T(8,128)(2,1)S(1)} %get-tuple-element.45), channel_id=1, source_target_pairs={{0,3},{1,2},{2,1},{3,0},{4,7},{5,6},{6,5},{7,4},{8,11},{9,10},{10,... | collective-permute-start | bytes 1179656 | tf_op jit(solution)/shard_map/ppermute | solution.py:39
  8.6 17.7 %collective-permute-start.7 = (bf16[256,768]{1,0:T(8,128)(2,1)S(1)}, bf16[256,768]{1,0:T(8,128)(2,1)S(1)}, u32[]{:S(2)}, u32[]{:S(2)}) collective-permute-start(bf16[256,768]{1,0:T(8,128)(2,1)S(1)} %get-tuple-element.46), channel_id=1, source_target_pairs={{0,2},{1,3},{2,0},{3,1},{4,6},{5,7},{6,4},{7,5},{8,10},{9,11},{10,... | collective-permute-start | bytes 1179656 | tf_op jit(solution)/shard_map/ppermute | solution.py:39
  13.3 14.1 %collective-permute-start.1 = (bf16[2,64,768]{2,1,0:T(8,128)(2,1)S(1)}, bf16[2,64,768]{2,1,0:T(8,128)(2,1)S(1)}, u32[]{:S(2)}, u32[]{:S(2)}) collective-permute-start(bf16[2,64,768]{2,1,0:T(8,128)(2,1)S(1)} %get-tuple-element.40.refs_0_), channel_id=1, source_target_pairs={{0,1},{1,0},{2,3},{3,2},{4,5},{5,4},{6,7},{7,6},{8,9},{9,8},{10,11... | collective-permute-start | bytes 589832 | tf_op jit(solution)/shard_map/ppermute | solution.py:39
  15.5 12.0 %collective-permute-start.2 = (bf16[2,64,768]{2,1,0:T(8,128)(2,1)S(1)}, bf16[2,64,768]{2,1,0:T(8,128)(2,1)S(1)}, u32[]{:S(2)}, u32[]{:S(2)}) collective-permute-start(bf16[2,64,768]{2,1,0:T(8,128)(2,1)S(1)} %get-tuple-element.41.refs_1_), channel_id=1, source_target_pairs={{0,16},{16,0},{32,48},{48,32},{64,80},{80,64},{96,112},{112,96},{1... | collective-permute-start | bytes 589832 | tf_op jit(solution)/shard_map/ppermute | solution.py:38
  16.8 15.0 %collective-permute-start.3 = (bf16[2,64,768]{2,1,0:T(8,128)(2,1)S(1)}, bf16[2,64,768]{2,1,0:T(8,128)(2,1)S(1)}, u32[]{:S(2)}, u32[]{:S(2)}) collective-permute-start(bf16[2,64,768]{2,1,0:T(8,128)(2,1)S(1)} %get-tuple-element.42.refs_2_), channel_id=1, source_target_pairs={{0,3},{1,2},{2,1},{3,0},{4,7},{5,6},{6,5},{7,4},{8,11},{9,10},{10,... | collective-permute-start | bytes 589832 | tf_op jit(solution)/shard_map/ppermute | solution.py:39
  34.5 19.3 %collective-permute-start.12 = (bf16[3,256,768]{2,1,0:T(8,128)(2,1)S(1)}, bf16[3,256,768]{2,1,0:T(8,128)(2,1)S(1)}, u32[]{:S(2)}, u32[]{:S(2)}) collective-permute-start(bf16[3,256,768]{2,1,0:T(8,128)(2,1)S(1)} %get-tuple-element.51), channel_id=1, source_target_pairs={{0,4},{4,0},{8,12},{12,8},{1,5},{5,1},{9,13},{13,9},{2,6},{6,2},{1... | collective-permute-start | bytes 3538952 | tf_op jit(solution)/shard_map/ppermute | solution.py:43
  37.9 12.6 %collective-permute-start.9 = (bf16[4,64,768]{2,1,0:T(8,128)(2,1)S(1)}, bf16[4,64,768]{2,1,0:T(8,128)(2,1)S(1)}, u32[]{:S(2)}, u32[]{:S(2)}) collective-permute-start(bf16[4,64,768]{2,1,0:T(8,128)(2,1)S(1)} %get-tuple-element.48.refs_1_), channel_id=1, source_target_pairs={{0,3},{1,2},{2,1},{3,0},{4,7},{5,6},{6,5},{7,4},{8,11},{9,10},{10,... | collective-permute-start | bytes 1179656 | tf_op jit(solution)/shard_map/ppermute | solution.py:39
  41.3 11.2 %collective-permute-start.10 = (bf16[4,64,768]{2,1,0:T(8,128)(2,1)S(1)}, bf16[4,64,768]{2,1,0:T(8,128)(2,1)S(1)}, u32[]{:S(2)}, u32[]{:S(2)}) collective-permute-start(bf16[4,64,768]{2,1,0:T(8,128)(2,1)S(1)} %get-tuple-element.49.refs_2_), channel_id=1, source_target_pairs={{0,48},{16,32},{32,16},{48,0},{64,112},{80,96},{96,80},{112,64},{1... | collective-permute-start | bytes 1179656 | tf_op jit(solution)/shard_map/ppermute | solution.py:38
  55.4 18.7 %collective-permute-start.13 = (bf16[8,64,768]{2,1,0:T(8,128)(2,1)S(1)}, bf16[8,64,768]{2,1,0:T(8,128)(2,1)S(1)}, u32[]{:S(2)}, u32[]{:S(2)}) collective-permute-start(bf16[8,64,768]{2,1,0:T(8,128)(2,1)S(1)} %get-tuple-element.52.refs_0_), channel_id=1, source_target_pairs={{0,3},{1,2},{2,1},{3,0},{4,7},{5,6},{6,5},{7,4},{8,11},{9,10},{10,... | collective-permute-start | bytes 2359304 | tf_op jit(solution)/shard_map/ppermute | solution.py:39
  55.7 18.6 %collective-permute-start.14 = (bf16[8,64,768]{2,1,0:T(8,128)(2,1)S(1)}, bf16[8,64,768]{2,1,0:T(8,128)(2,1)S(1)}, u32[]{:S(2)}, u32[]{:S(2)}) collective-permute-start(bf16[8,64,768]{2,1,0:T(8,128)(2,1)S(1)} %get-tuple-element.53.refs_1_), channel_id=1, source_target_pairs={{0,48},{16,32},{32,16},{48,0},{64,112},{80,96},{96,80},{112,64},{1... | collective-permute-start | bytes 2359304 | tf_op jit(solution)/shard_map/ppermute | solution.py:38
  57.4 17.5 %collective-permute-start.15 = (bf16[8,64,768]{2,1,0:T(8,128)(2,1)S(1)}, bf16[8,64,768]{2,1,0:T(8,128)(2,1)S(1)}, u32[]{:S(2)}, u32[]{:S(2)}) collective-permute-start(bf16[8,64,768]{2,1,0:T(8,128)(2,1)S(1)} %get-tuple-element.54.refs_2_), channel_id=1, source_target_pairs={{0,1},{1,0},{2,3},{3,2},{4,5},{5,4},{6,7},{7,6},{8,9},{9,8},{10,11... | collective-permute-start | bytes 2359304 | tf_op jit(solution)/shard_map/ppermute | solution.py:39
  57.4 17.5 %collective-permute-start.16 = (bf16[8,64,768]{2,1,0:T(8,128)(2,1)S(1)}, bf16[8,64,768]{2,1,0:T(8,128)(2,1)S(1)}, u32[]{:S(2)}, u32[]{:S(2)}) collective-permute-start(bf16[8,64,768]{2,1,0:T(8,128)(2,1)S(1)} %get-tuple-element.55.refs_3_), channel_id=1, source_target_pairs={{0,16},{16,0},{32,48},{48,32},{64,80},{80,64},{96,112},{112,96},{1... | collective-permute-start | bytes 2359304 | tf_op jit(solution)/shard_map/ppermute | solution.py:38
  77.7 18.1 %collective-permute-start.17 = (bf16[16,32,768]{2,1,0:T(8,128)(2,1)}, bf16[16,32,768]{2,1,0:T(8,128)(2,1)S(1)}, u32[]{:S(2)}, u32[]{:S(2)}) collective-permute-start(bf16[16,32,768]{2,1,0:T(8,128)(2,1)} %get-tuple-element.57), channel_id=1, source_target_pairs={{0,48},{16,32},{32,16},{48,0},{64,112},{80,96},{96,80},{112,64},{1... | collective-permute-start | bytes 2359304 | tf_op jit(solution)/shard_map/ppermute | solution.py:38
  79.3 17.4 %collective-permute-start.18 = (bf16[16,32,768]{2,1,0:T(8,128)(2,1)}, bf16[16,32,768]{2,1,0:T(8,128)(2,1)S(1)}, u32[]{:S(2)}, u32[]{:S(2)}) collective-permute-start(bf16[16,32,768]{2,1,0:T(8,128)(2,1)} %get-tuple-element.58), channel_id=1, source_target_pairs={{0,1},{1,0},{2,3},{3,2},{4,5},{5,4},{6,7},{7,6},{8,9},{9,8},{10,11... | collective-permute-start | bytes 2359304 | tf_op jit(solution)/shard_map/ppermute | solution.py:39
  79.6 17.1 %collective-permute-start.19 = (bf16[16,32,768]{2,1,0:T(8,128)(2,1)}, bf16[16,32,768]{2,1,0:T(8,128)(2,1)S(1)}, u32[]{:S(2)}, u32[]{:S(2)}) collective-permute-start(bf16[16,32,768]{2,1,0:T(8,128)(2,1)} %get-tuple-element.59), channel_id=1, source_target_pairs={{0,16},{16,0},{32,48},{48,32},{64,80},{80,64},{96,112},{112,96},{1... | collective-permute-start | bytes 2359304 | tf_op jit(solution)/shard_map/ppermute | solution.py:38
  79.6 19.1 %collective-permute-start.20 = (bf16[16,32,768]{2,1,0:T(8,128)(2,1)}, bf16[16,32,768]{2,1,0:T(8,128)(2,1)S(1)}, u32[]{:S(2)}, u32[]{:S(2)}) collective-permute-start(bf16[16,32,768]{2,1,0:T(8,128)(2,1)} %get-tuple-element.60), channel_id=1, source_target_pairs={{0,3},{1,2},{2,1},{3,0},{4,7},{5,6},{6,5},{7,4},{8,11},{9,10},{10,... | collective-permute-start | bytes 2359304 | tf_op jit(solution)/shard_map/ppermute | solution.py:39
  81.8 34.5 %collective-permute-start.22 = (bf16[16,32,768]{2,1,0:T(8,128)(2,1)}, bf16[16,32,768]{2,1,0:T(8,128)(2,1)S(1)}, u32[]{:S(2)}, u32[]{:S(2)}) collective-permute-start(bf16[16,32,768]{2,1,0:T(8,128)(2,1)} %get-tuple-element.63), channel_id=1, source_target_pairs={{0,48},{16,32},{32,16},{48,0},{64,112},{80,96},{96,80},{112,64},{1... | collective-permute-start | bytes 2359304 | tf_op jit(solution)/shard_map/ppermute | solution.py:38
  95.8 20.6 %collective-permute-start.23 = (bf16[16,32,768]{2,1,0:T(8,128)(2,1)}, bf16[16,32,768]{2,1,0:T(8,128)(2,1)S(1)}, u32[]{:S(2)}, u32[]{:S(2)}) collective-permute-start(bf16[16,32,768]{2,1,0:T(8,128)(2,1)} %get-tuple-element.64), channel_id=1, source_target_pairs={{0,1},{1,0},{2,3},{3,2},{4,5},{5,4},{6,7},{7,6},{8,9},{9,8},{10,11... | collective-permute-start | bytes 2359304 | tf_op jit(solution)/shard_map/ppermute | solution.py:39
  96.7 19.6 %collective-permute-start.24 = (bf16[16,32,768]{2,1,0:T(8,128)(2,1)}, bf16[16,32,768]{2,1,0:T(8,128)(2,1)S(1)}, u32[]{:S(2)}, u32[]{:S(2)}) collective-permute-start(bf16[16,32,768]{2,1,0:T(8,128)(2,1)} %get-tuple-element.65), channel_id=1, source_target_pairs={{0,16},{16,0},{32,48},{48,32},{64,80},{80,64},{96,112},{112,96},{1... | collective-permute-start | bytes 2359304 | tf_op jit(solution)/shard_map/ppermute | solution.py:38
  96.7 19.6 %collective-permute-start.25 = (bf16[16,32,768]{2,1,0:T(8,128)(2,1)}, bf16[16,32,768]{2,1,0:T(8,128)(2,1)S(1)}, u32[]{:S(2)}, u32[]{:S(2)}) collective-permute-start(bf16[16,32,768]{2,1,0:T(8,128)(2,1)} %get-tuple-element.66), channel_id=1, source_target_pairs={{0,3},{1,2},{2,1},{3,0},{4,7},{5,6},{6,5},{7,4},{8,11},{9,10},{10,... | collective-permute-start | bytes 2359304 | tf_op jit(solution)/shard_map/ppermute | solution.py:39
  108.1 25.8 %collective-permute-start.21 = (bf16[2,8,32,768]{3,2,1,0:T(8,128)(2,1)S(1)}, bf16[2,8,32,768]{3,2,1,0:T(8,128)(2,1)S(1)}, u32[]{:S(2)}, u32[]{:S(2)}) collective-permute-start(bf16[2,8,32,768]{3,2,1,0:T(8,128)(2,1)S(1)} %get-tuple-element.62), channel_id=1, source_target_pairs={{0,4},{4,0},{8,12},{12,8},{1,5},{5,1},{9,13},{13,9},{2,6},{6,2},{1... | collective-permute-start | bytes 2359304 | tf_op jit(solution)/shard_map/ppermute | solution.py:43
  134.0 13.0 %collective-permute-start.26 = (bf16[8,32,768]{2,1,0:T(8,128)(2,1)S(1)}, bf16[8,32,768]{2,1,0:T(8,128)(2,1)S(1)}, u32[]{:S(2)}, u32[]{:S(2)}) collective-permute-start(bf16[8,32,768]{2,1,0:T(8,128)(2,1)S(1)} %get-tuple-element.69), channel_id=1, source_target_pairs={{0,8},{4,12},{8,0},{12,4},{1,9},{5,13},{9,1},{13,5},{2,10},{6,14},... | collective-permute-start | bytes 1179656 | tf_op jit(solution)/shard_map/ppermute | solution.py:43
  136.7 18.1 %collective-permute-start.28 = (bf16[8,32,768]{2,1,0:T(8,128)(2,1)S(1)}, bf16[8,32,768]{2,1,0:T(8,128)(2,1)S(1)}, u32[]{:S(2)}, u32[]{:S(2)}) collective-permute-start(bf16[8,32,768]{2,1,0:T(8,128)(2,1)S(1)} %get-tuple-element.76), channel_id=1, source_target_pairs={{0,8},{4,12},{8,0},{12,4},{1,9},{5,13},{9,1},{13,5},{2,10},{6,14},... | collective-permute-start | bytes 1179656 | tf_op jit(solution)/shard_map/ppermute | solution.py:43
  (9 other events, 151.6 us)

commit v6 on v5

--- a/solution.py
+++ b/solution.py
@@ -21,6 +21,7 @@
 WIDTH = FEATS // CHAINS
 ORDERS = tuple(tuple(DIMS[1 + (p + k) % 4] for k in range(4)) for p in range(CHAINS))
 HOPS = (Z0, Z1, Z0 ^ Z1)
+SLICE = SHARDS * ROWS // 16
 PARTS = (32, 32)
 STARTS = (0, 32)
 
@@ -60,11 +61,10 @@
 def cut_kernel(where, pre, *refs):
     chunks, sem = refs[:-1], refs[-1]
     row, col = where[0], where[1]
-    half = SHARDS * ROWS // 8
     copies = []
     for j, mask in enumerate(HOPS):
         here = pre.at[
-            pl.ds(pl.multiple_of(row % 2 * half, half), half), pl.ds(pl.multiple_of((col ^ mask) * HID, HID), HID)
+            pl.ds(pl.multiple_of(row * SLICE, SLICE), SLICE), pl.ds(pl.multiple_of((col ^ mask) * HID, HID), HID)
         ]
         copies.append(pltpu.make_async_copy(here, chunks[j], sem.at[j]))
     for c in copies:
@@ -76,7 +76,7 @@
 def cut_call(where, pre):
     return pl.pallas_call(
         cut_kernel,
-        out_shape=[jax.ShapeDtypeStruct((SHARDS * ROWS // 8, HID), jnp.bfloat16)] * len(HOPS),
+        out_shape=[jax.ShapeDtypeStruct((SLICE, HID), jnp.bfloat16)] * len(HOPS),
         in_specs=[SMEM, ANY],
         out_specs=[ANY] * len(HOPS),
         scratch_shapes=[pltpu.SemaphoreType.DMA((len(HOPS),))],
@@ -112,47 +112,43 @@
     )(in_hbm(own), got, *after)
 
 
-def grow_kernel(rows, joined, *refs):
-    own, got, sem = refs[:CHAINS], refs[CHAINS : 2 * CHAINS], refs[-1]
-    outs = refs[-1 - len(rows) * CHAINS - (joined > 0) : -1]
-    copies = []
-    for part, (at, n) in enumerate(rows):
-        for p in range(CHAINS):
-            blocks = own[p].shape[0]
-            for side, src in enumerate((own[p], got[p])):
-                there = outs[part * CHAINS + p].at[pl.ds(side * blocks, blocks)]
-                copies.append(pltpu.make_async_copy(src.at[:, pl.ds(at, n)], there, sem.at[len(copies)]))
+def grow_kernel(chains, at, n, joined, *refs):
+    outs, sem = refs[-1 - chains - (joined > 0) : -1], refs[-1]
+    pairs = []
+    for p in range(chains):
+        blocks = refs[2 * p].shape[0]
+        for side in range(2):
+            pairs.append((refs[2 * p + side].at[:, pl.ds(at, n)], outs[p].at[pl.ds(side * blocks, blocks)]))
     for j in range(joined):
-        src = refs[2 * CHAINS + j]
-        copies.append(pltpu.make_async_copy(src, outs[-1].at[j], sem.at[len(copies)]))
+        pairs.append((refs[2 * chains + j], outs[-1].at[j]))
+    copies = [pltpu.make_async_copy(*pair, sem.at[i]) for i, pair in enumerate(pairs)]
     for c in copies:
         c.start()
     for c in copies:
         c.wait()
 
 
-def grow_call(own, got, rows=((0, ROWS),), join=(), after=()):
-    blocks = own[0].shape[0]
-    shape = pltpu.HBM if len(rows) > 1 else jax.ShapeDtypeStruct
-    return pl.pallas_call(
-        functools.partial(grow_kernel, rows, len(join)),
-        out_shape=[shape((2 * blocks, n, WIDTH), jnp.bfloat16) for _, n in rows for _ in range(CHAINS)]
+def grow_call(pairs, at=0, n=ROWS, join=(), after=()):
+    blocks = pairs[0][0].shape[0]
+    shape = jax.ShapeDtypeStruct if n == ROWS else pltpu.HBM
+    return pl.pallas_call(
+        functools.partial(grow_kernel, len(pairs), at, n, len(join)),
+        out_shape=[shape((2 * blocks, n, WIDTH), jnp.bfloat16)] * len(pairs)
         + [jax.ShapeDtypeStruct((len(join), *j.shape), jnp.bfloat16) for j in join[:1]],
-        in_specs=[ANY] * (2 * CHAINS + len(join) + len(after)),
-        out_specs=[ANY] * (len(rows) * CHAINS + (len(join) > 0)),
-        scratch_shapes=[pltpu.SemaphoreType.DMA((2 * CHAINS * len(rows) + len(join),))],
+        in_specs=[ANY] * (2 * len(pairs) + len(join) + len(after)),
+        out_specs=[ANY] * (len(pairs) + (len(join) > 0)),
+        scratch_shapes=[pltpu.SemaphoreType.DMA((2 * len(pairs) + len(join),))],
         compiler_params=params(1),
         cost_estimate=TINY,
         name="grow",
-    )(*own, *got, *join, *after)
-
-
-def gelu_kernel(where, table, pre, got_a, got_b, got_c, other, *refs):
+    )(*(x for pair in pairs for x in pair), *join, *after)
+
+
+def gelu_kernel(where, table, pre, near, far, *refs):
     outs, (buf, sems), acts = refs[:4], refs[4:6], refs[6:]
     act_t, slopes = outs[:2], outs[2:]
     row, col, mine = where[0], where[1], where[2]
-    core = row % 2
-    quarter, half = SHARDS * ROWS // 4, SHARDS * ROWS // 8
+    quarter = SHARDS * ROWS // 4
     copies = [
         pltpu.make_async_copy(
             pre.at[:, pl.ds(pl.multiple_of(col * HID, HID), HID)],
@@ -160,10 +156,11 @@
             sems.at[0],
         )
     ]
-    for j, got in enumerate((got_a, got_b, got_c)):
-        for side, src in ((core, got), (1 - core, other.at[j])):
-            at = pl.multiple_of((col ^ HOPS[j]) * quarter + side * half, half)
-            copies.append(pltpu.make_async_copy(src, buf.at[pl.ds(at, half)], sems.at[len(copies)]))
+    for side, src in enumerate((near, far)):
+        for i in range(2):
+            for j, mask in enumerate(HOPS):
+                at = pl.multiple_of((col ^ mask) * quarter + (row ^ (2 * side + i)) * SLICE, SLICE)
+                copies.append(pltpu.make_async_copy(src.at[i, j], buf.at[pl.ds(at, SLICE)], sems.at[len(copies)]))
     for c in copies:
         c.start()
     for c in copies:
@@ -202,20 +199,20 @@
         lax.fori_loop(0, SHARDS * PARTS[part] // 128, one_turn, 0)
 
 
-def gelu_call(where, table, pre, fetched, other):
+def gelu_call(where, table, pre, near, far):
     tokens = [SHARDS * n for n in PARTS]
     return pl.pallas_call(
         gelu_kernel,
         out_shape=[jax.ShapeDtypeStruct((HID, t), jnp.bfloat16) for t in tokens]
         + [jax.ShapeDtypeStruct((SHARDS // 4, n, HID), jnp.float32) for n in PARTS],
-        in_specs=[SMEM, SMEM] + [ANY] * 5,
+        in_specs=[SMEM, SMEM] + [ANY] * 3,
         out_specs=[VMEM] * 4,
-        scratch_shapes=[pltpu.VMEM((SHARDS * ROWS, HID), jnp.bfloat16), pltpu.SemaphoreType.DMA((7,))]
+        scratch_shapes=[pltpu.VMEM((SHARDS * ROWS, HID), jnp.bfloat16), pltpu.SemaphoreType.DMA((13,))]
         + [pltpu.VMEM((t, HID), jnp.bfloat16) for t in tokens],
         compiler_params=params(20),
         cost_estimate=TINY,
         name="gelu",
-    )(where, table, in_hbm(pre), *fetched, other)
+    )(where, table, in_hbm(pre), near, far)
 
 
 def pieces(p, side, top):
@@ -324,7 +321,7 @@
     out[...] = acc.astype(jnp.bfloat16)
 
 
-def down_call(acts, gathered, first, count, base=None):
+def down_call(acts, gathered, first, count, base=None, after=()):
     wide = 512
     tokens = [SHARDS * n for n in PARTS]
     in_specs = [pl.BlockSpec((HID, t), lambda j: (0, 0)) for t in tokens]
@@ -335,6 +332,8 @@
         in_specs.append(ANY)
         args.append(in_hbm(base))
         aliases = {4: 0}
+    in_specs += [ANY] * len(after)
+    args += after
     return pl.pallas_call(
         down_kernel,
         grid=(count,),
@@ -358,23 +357,29 @@
     got = swap(in_hbm(grad_out), X)
     fetched = [swap(chunk, mask) for chunk, mask in zip(cut_call(where, pre_act), HOPS)]
     blocks = split_call(grad_out, got)
-    got = [swap(blocks[p], ORDERS[p][0]) for p in range(CHAINS)]
-    *blocks, both = grow_call(blocks, got, join=fetched)
-    got = [swap(blocks[p], ORDERS[p][1]) for p in range(CHAINS)]
-    other = swap_row(both, 1)
-    blocks = grow_call(blocks, got, after=(other,))
-    got = [swap(blocks[p], ORDERS[p][2]) for p in range(CHAINS)]
-    act_a, act_b, slope_a, slope_b = gelu_call(where, table, pre_act, fetched, other)
-    grown = grow_call(blocks, got, tuple(zip(STARTS, PARTS)), after=(slope_a,))
-    own = grown[:CHAINS], grown[CHAINS:]
-    came = [[swap(own[part][p], ORDERS[p][3]) for p in range(CHAINS)] for part in range(2)]
+    for k in range(2):
+        pairs = [(b, swap(b, ORDERS[p][k])) for p, b in enumerate(blocks)]
+        last = grow_call(pairs[-1:], join=fetched) if k == 0 else grow_call(pairs[-1:], join=[fetched, other])
+        blocks = [grow_call([pair])[0] for pair in pairs[:-1]] + [last[0]]
+        if k == 0:
+            fetched = last[1]
+            other = swap_row(fetched, 1)
+    near = last[1]
+    far = swap_row(near, 2)
+    pairs = [(b, swap(b, ORDERS[p][2])) for p, b in enumerate(blocks)]
+    own_a = [grow_call([pair], STARTS[0], PARTS[0])[0] for pair in pairs]
+    came_a = [swap(own_a[p], ORDERS[p][3]) for p in range(CHAINS)]
+    act_a, act_b, slope_a, slope_b = gelu_call(where, table, pre_act, near, far)
+    own_b = grow_call(pairs, STARTS[1], PARTS[1], after=(slope_a,))
+    came_b = [swap(own_b[p], ORDERS[p][3]) for p in range(CHAINS)]
+    own, came = (own_a, own_b), (came_a, came_b)
 
     pairs = [[b for p in range(CHAINS) for b in (own[part][p], came[part][p])] for part in range(2)]
     keep_a, send_a, g_a = hidden_call(0, where, w_down, pairs[0])
     keep_b, send_b, g_b = hidden_call(1, where, w_down, pairs[1], after=(keep_a,))
     mine_a, far_a = total_call(keep_a, swap_row(send_a, 1), after=(keep_b,))
     far_a = swap_row(far_a, 2)
-    grad_down = down_call((act_a, act_b), (g_a, g_b), 0, 2)
+    grad_down = down_call((act_a, act_b), (g_a, g_b), 0, 2, after=(mine_a,))
     mine_b, far_b = total_call(keep_b, swap_row(send_b, 1), after=(in_hbm(grad_down),))
     far_b = swap_row(far_b, 2)
     grad_down = down_call((act_a, act_b), (g_a, g_b), 2, 4, grad_down)

time: 156 us -> 145 us (0.929)
  waiting for transfers between devices: 50.9 us -> 34.2 us
  Pallas kernels: 52.3 us -> 57 us
    ppermute x11, waiting for transfers between devices: 20.5 us -> 6.96 us  [swap(): return lax.ppermute(x, 'depth', [(i, i ^ mask >> 2) for i in range(8)])]
    ppermute x13, waiting for transfers between devices: 22.8 us -> 18.6 us  [swap(): return lax.ppermute(x, 'col', [(i, i ^ mask) for i in range(4)])]
    ppermute x11, starting transfers between devices: 14.6 us -> 11.7 us  [swap(): return lax.ppermute(x, 'depth', [(i, i ^ mask >> 2) for i in range(8)])]
    ppermute x5 -> x6, starting transfers between devices: 16.7 us -> 19.6 us  [swap_row(): return lax.ppermute(x, 'row', [(i, i ^ mask) for i in range(4)])]
    pallas_call x4 -> x14, Pallas kernels: 8.9 us -> 11.7 us  [the longest x13 10.1 us: grow_call(): pl.pallas_call(functools.partial(grow_kernel, len(pairs), at, n, len(join...]
    pallas_call x1, Pallas kernels: 7.23 us -> 9.19 us  [gelu_call(): pl.pallas_call(gelu_kernel, out_shape=[jax.ShapeDtypeStruct((HID, t), jnp...]
    ppermute x5 -> x6, waiting for transfers between devices: 7.63 us -> 8.59 us  [swap_row(): return lax.ppermute(x, 'row', [(i, i ^ mask) for i in range(4)])]
  transfers between devices with their start and end apart: 29 -> 30, of which waited for: 14 -> 11; matrix products, arithmetic and copies ran while one was open for 0% -> 0% of each run, Pallas kernels for 29% -> 39%
where the time goes in v6:
time: 145 us; the launch traced here: 144 us
  Pallas kernels  57 us (39%)
  starting transfers between devices  50.4 us (35%)
  waiting for transfers between devices  34.2 us (24%)
    ppermute x6, starting transfers between devices, swap_row(): return lax.ppermute(x, 'row', [(i, i ^ mask) for i in range(4)])  19.6 us
    ppermute x13, starting transfers between devices, swap(): return lax.ppermute(x, 'col', [(i, i ^ mask) for i in range(4)])  19.1 us
    pallas_call x2, Pallas kernels, hidden_call(): pl.pallas_call(functools.partial(hidden_kernel, n), out_shape=[jax.ShapeD...  18.8 us
    ppermute x13, waiting for transfers between devices, swap(): return lax.ppermute(x, 'col', [(i, i ^ mask) for i in range(4)])  18.6 us
    pallas_call x2, Pallas kernels, down_call(): pl.pallas_call(down_kernel, grid=(count,), out_shape=pltpu.HBM((HID, FEAT...  15.7 us
    ppermute x11, starting transfers between devices, swap(): return lax.ppermute(x, 'depth', [(i, i ^ mask >> 2) for i in range(8)])  11.7 us
    pallas_call x13, Pallas kernels, grow_call(): pl.pallas_call(functools.partial(grow_kernel, len(pairs), at, n, len(join...  10.1 us
    pallas_call x1, Pallas kernels, gelu_call(): pl.pallas_call(gelu_kernel, out_shape=[jax.ShapeDtypeStruct((HID, t), jnp...  9.19 us
  transfers between devices with their start and end apart: 30, of which 11 were waited for; matrix products, arithmetic and copies ran while one was open for 0% of the time, Pallas kernels for 39%

profile of v6, /device:TPU:1, one launch (start us, length us, event | category | flops | bytes accessed | tf_op | source)
XLA Modules:
  0.0 144.5 jit_solution(5869309815948940636)
XLA Ops:
  0.6 2.1 %collective-permute-start = (bf16[64,3072]{1,0:T(8,128)(2,1)}, bf16[64,3072]{1,0:T(8,128)(2,1)S(1)}, u32[]{:S(2)}, u32[]{:S(2)}) collective-permute-start(bf16[64,3072]{1,0:T(8,128)(2,1)} %own.1), channel_id=1, source_target_pairs={{0,64},{16,80},{32,96},{48,112},{64,0},{80,16},{96,32},{112,48},{1... | collective-permute-start | bytes 1179656 | tf_op jit(solution)/shard_map/ppermute | solution.py:39
  6.2 5.1 %collective-permute-done.got = bf16[64,3072]{1,0:T(8,128)(2,1)S(1)} collective-permute-done((bf16[64,3072]{1,0:T(8,128)(2,1)}, bf16[64,3072]{1,0:T(8,128)(2,1)S(1)}, u32[]{:S(2)}, u32[]{:S(2)}) %collective-permute-start) | collective-permute-done | bytes 393248 | tf_op jit(solution)/shard_map/ppermute | solution.py:39
  13.3 2.1 %collective-permute-start.1 = (bf16[2,64,768]{2,1,0:T(8,128)(2,1)S(1)}, bf16[2,64,768]{2,1,0:T(8,128)(2,1)S(1)}, u32[]{:S(2)}, u32[]{:S(2)}) collective-permute-start(bf16[2,64,768]{2,1,0:T(8,128)(2,1)S(1)} %get-tuple-element.31.refs_0_), channel_id=1, source_target_pairs={{0,1},{1,0},{2,3},{3,2},{4,5},{5,4},{6,7},{7,6},{8,9},{9,8},{10,11... | collective-permute-start | bytes 589832 | tf_op jit(solution)/shard_map/ppermute | solution.py:40
  16.8 2.2 %collective-permute-start.9 = (bf16[2,64,768]{2,1,0:T(8,128)(2,1)S(1)}, bf16[2,64,768]{2,1,0:T(8,128)(2,1)S(1)}, u32[]{:S(2)}, u32[]{:S(2)}) collective-permute-start(bf16[2,64,768]{2,1,0:T(8,128)(2,1)S(1)} %get-tuple-element.33.refs_0_), channel_id=1, source_target_pairs={{0,3},{1,2},{2,1},{3,0},{4,7},{5,6},{6,5},{7,4},{8,11},{9,10},{10,... | collective-permute-start | bytes 589832 | tf_op jit(solution)/shard_map/ppermute | solution.py:40
  19.5 2.1 %collective-permute-start.16 = (bf16[128,768]{1,0:T(8,128)(2,1)S(1)}, bf16[128,768]{1,0:T(8,128)(2,1)S(1)}, u32[]{:S(2)}, u32[]{:S(2)}) collective-permute-start(bf16[128,768]{1,0:T(8,128)(2,1)S(1)} %get-tuple-element.37), channel_id=1, source_target_pairs={{0,2},{1,3},{2,0},{3,1},{4,6},{5,7},{6,4},{7,5},{8,10},{9,11},{10,... | collective-permute-start | bytes 589832 | tf_op jit(solution)/shard_map/ppermute | solution.py:40
  21.6 1.9 %collective-permute-start.13 = (bf16[2,64,768]{2,1,0:T(8,128)(2,1)S(1)}, bf16[2,64,768]{2,1,0:T(8,128)(2,1)S(1)}, u32[]{:S(2)}, u32[]{:S(2)}) collective-permute-start(bf16[2,64,768]{2,1,0:T(8,128)(2,1)S(1)} %get-tuple-element.34.refs_0_), channel_id=1, source_target_pairs={{0,48},{16,32},{32,16},{48,0},{64,112},{80,96},{96,80},{112,64},{1... | collective-permute-start | bytes 589832 | tf_op jit(solution)/shard_map/ppermute | solution.py:39
  26.9 4.1 %collective-permute-done.15.refs_3_ = bf16[128,768]{1,0:T(8,128)(2,1)S(1)} collective-permute-done((bf16[128,768]{1,0:T(8,128)(2,1)S(1)}, bf16[128,768]{1,0:T(8,128)(2,1)S(1)}, u32[]{:S(2)}, u32[]{:S(2)}) %collective-permute-start.15) | collective-permute-done | bytes 196640 | tf_op jit(solution)/shard_map/ppermute | solution.py:40
  34.3 5.6 %collective-permute-start.18 = (bf16[3,128,768]{2,1,0:T(8,128)(2,1)S(1)}, bf16[3,128,768]{2,1,0:T(8,128)(2,1)S(1)}, u32[]{:S(2)}, u32[]{:S(2)}) collective-permute-start(bf16[3,128,768]{2,1,0:T(8,128)(2,1)S(1)} %get-tuple-element.39.refs_2_), channel_id=1, source_target_pairs={{0,4},{4,0},{8,12},{12,8},{1,5},{5,1},{9,13},{13,9},{2,6},{6,2},{1... | collective-permute-start | bytes 1769480 | tf_op jit(solution)/shard_map/ppermute | solution.py:44
  40.4 2.4 %collective-permute-start.3 = (bf16[8,64,768]{2,1,0:T(8,128)(2,1)S(1)}, bf16[8,64,768]{2,1,0:T(8,128)(2,1)S(1)}, u32[]{:S(2)}, u32[]{:S(2)}) collective-permute-start(bf16[8,64,768]{2,1,0:T(8,128)(2,1)S(1)} %grow.14.refs_0_), channel_id=1, source_target_pairs={{0,3},{1,2},{2,1},{3,0},{4,7},{5,6},{6,5},{7,4},{8,11},{9,10},{10,... | collective-permute-start | bytes 2359304 | tf_op jit(solution)/shard_map/ppermute | solution.py:40
  45.3 5.3 %collective-permute-done.17.refs_1_ = bf16[4,64,768]{2,1,0:T(8,128)(2,1)S(1)} collective-permute-done((bf16[4,64,768]{2,1,0:T(8,128)(2,1)S(1)}, bf16[4,64,768]{2,1,0:T(8,128)(2,1)S(1)}, u32[]{:S(2)}, u32[]{:S(2)}) %collective-permute-start.17) | collective-permute-done | bytes 393248 | tf_op jit(solution)/shard_map/ppermute | solution.py:40
  51.7 2.7 %collective-permute-start.22 = (bf16[2,3,128,768]{3,2,1,0:T(8,128)(2,1)S(1)}, bf16[2,3,128,768]{3,2,1,0:T(8,128)(2,1)S(1)}, u32[]{:S(2)}, u32[]{:S(2)}) collective-permute-start(bf16[2,3,128,768]{3,2,1,0:T(8,128)(2,1)S(1)} %get-tuple-element.43.near), channel_id=1, source_target_pairs={{0,8},{4,12},{8,0},{12,4},{1,9},{5,13},{9,1},{13,5},{2,10},{6,14},... | collective-permute-start | bytes 3538952 | tf_op jit(solution)/shard_map/ppermute | solution.py:44
  54.4 6.0 %collective-permute-done.3.refs_1_ = bf16[8,64,768]{2,1,0:T(8,128)(2,1)S(1)} collective-permute-done((bf16[8,64,768]{2,1,0:T(8,128)(2,1)S(1)}, bf16[8,64,768]{2,1,0:T(8,128)(2,1)S(1)}, u32[]{:S(2)}, u32[]{:S(2)}) %collective-permute-start.3) | collective-permute-done | bytes 786464 | tf_op jit(solution)/shard_map/ppermute | solution.py:40
  64.7 2.7 %collective-permute-done.11.refs_1_.refs_5_ = bf16[8,64,768]{2,1,0:T(8,128)(2,1)S(1)} collective-permute-done((bf16[8,64,768]{2,1,0:T(8,128)(2,1)S(1)}, bf16[8,64,768]{2,1,0:T(8,128)(2,1)S(1)}, u32[]{:S(2)}, u32[]{:S(2)}) %collective-permute-start.11) | collective-permute-done | bytes 786464 | tf_op jit(solution)/shard_map/ppermute | solution.py:40
  69.9 2.4 %collective-permute-start.20 = (bf16[16,32,768]{2,1,0:T(8,128)(2,1)}, bf16[16,32,768]{2,1,0:T(8,128)(2,1)S(1)}, u32[]{:S(2)}, u32[]{:S(2)}) collective-permute-start(bf16[16,32,768]{2,1,0:T(8,128)(2,1)} %grow.24), channel_id=1, source_target_pairs={{0,3},{1,2},{2,1},{3,0},{4,7},{5,6},{6,5},{7,4},{8,11},{9,10},{10,... | collective-permute-start | bytes 2359304 | tf_op jit(solution)/shard_map/ppermute | solution.py:40
  72.3 6.7 %collective-permute-done.22.far = bf16[2,3,128,768]{3,2,1,0:T(8,128)(2,1)S(1)} collective-permute-done((bf16[2,3,128,768]{3,2,1,0:T(8,128)(2,1)S(1)}, bf16[2,3,128,768]{3,2,1,0:T(8,128)(2,1)S(1)}, u32[]{:S(2)}, u32[]{:S(2)}) %collective-permute-start.22) | collective-permute-done | bytes 1179680 | tf_op jit(solution)/shard_map/ppermute | solution.py:44
  79.0 9.2 %gelu.1 = (bf16[768,1024]{1,0:T(8,128)(2,1)S(1)}, bf16[768,1024]{1,0:T(8,128)(2,1)S(1)}, f32[8,32,768]{2,1,0:T(8,128)S(1)}, f32[8,32,768]{2,1,0:T(8,128)S(1)}) custom-call(s32[3]{0:T(128)S(1)} %pad_add_fusion.where, s32[32]{0:T(128)S(1)} %copy-done, bf16[512,3072]{1,0:T(8,128)(2,1)} %pre.3, bf16[2,3,128,768]{3,2,1,0:T(8,128)(2,1)S(1)} %get-tuple-element.43.near, ...), custom_call_target="tpu_custom_call" | custom-call | flops 1 | bytes 1 | tf_op jit(solution)/shard_map/gelu/pallas_call | solution.py:204
  91.4 2.4 %collective-permute-start.26 = (bf16[16,32,768]{2,1,0:T(8,128)(2,1)}, bf16[16,32,768]{2,1,0:T(8,128)(2,1)S(1)}, u32[]{:S(2)}, u32[]{:S(2)}) collective-permute-start(bf16[16,32,768]{2,1,0:T(8,128)(2,1)} %get-tuple-element.48), channel_id=1, source_target_pairs={{0,3},{1,2},{2,1},{3,0},{4,7},{5,6},{6,5},{7,4},{8,11},{9,10},{10,... | collective-permute-start | bytes 2359304 | tf_op jit(solution)/shard_map/ppermute | solution.py:40
  93.8 9.4 %hidden.2 = (f32[2,8,32,768]{3,2,1,0:T(8,128)S(1)}, bf16[2,8,32,768]{3,2,1,0:T(8,128)(2,1)S(1)}, bf16[2,2,2,2,2,32,3072]{6,5,4,3,2,1,0:T(8,128)(2,1)}) custom-call(s32[3]{0:T(128)S(1)} %pad_add_fusion.where, bf16[768,3072]{1,0:T(8,128)(2,1)S(1)} %bitcast.23, bf16[2,2,2,2,32,768]{5,4,3,2,1,0:T(8,128)(2,1)} %bitcast.37, ...), custom_call_target="tpu_custom_call" | custom-call | flops 4831838208 | bytes 12582912 | tf_op jit(solution)/shard_map/hidden/pallas_call | solution.py:273
  103.2 3.7 %collective-permute-start.21 = (bf16[2,8,32,768]{3,2,1,0:T(8,128)(2,1)S(1)}, bf16[2,8,32,768]{3,2,1,0:T(8,128)(2,1)S(1)}, u32[]{:S(2)}, u32[]{:S(2)}) collective-permute-start(bf16[2,8,32,768]{3,2,1,0:T(8,128)(2,1)S(1)} %get-tuple-element.42), channel_id=1, source_target_pairs={{0,4},{4,0},{8,12},{12,8},{1,5},{5,1},{9,13},{13,9},{2,6},{6,2},{1... | collective-permute-start | bytes 2359304 | tf_op jit(solution)/shard_map/ppermute | solution.py:44
  108.5 9.4 %hidden.3 = (f32[2,8,32,768]{3,2,1,0:T(8,128)S(1)}, bf16[2,8,32,768]{3,2,1,0:T(8,128)(2,1)S(1)}, bf16[2,2,2,2,2,32,3072]{6,5,4,3,2,1,0:T(8,128)(2,1)}) custom-call(s32[3]{0:T(128)S(1)} %pad_add_fusion.where, bf16[768,3072]{1,0:T(8,128)(2,1)S(1)} %bitcast.23, bf16[2,2,2,2,32,768]{5,4,3,2,1,0:T(8,128)(2,1)} %bitcast.41, ...), custom_call_target="tpu_custom_call" | custom-call | flops 4831838208 | bytes 12582912 | tf_op jit(solution)/shard_map/hidden/pallas_call | solution.py:273
  117.9 4.4 %collective-permute-start.28 = (bf16[2,8,32,768]{3,2,1,0:T(8,128)(2,1)S(1)}, bf16[2,8,32,768]{3,2,1,0:T(8,128)(2,1)S(1)}, u32[]{:S(2)}, u32[]{:S(2)}) collective-permute-start(bf16[2,8,32,768]{3,2,1,0:T(8,128)(2,1)S(1)} %get-tuple-element.52), channel_id=1, source_target_pairs={{0,4},{4,0},{8,12},{12,8},{1,5},{5,1},{9,13},{13,9},{2,6},{6,2},{1... | collective-permute-start | bytes 2359304 | tf_op jit(solution)/shard_map/ppermute | solution.py:44
  122.4 2.8 %collective-permute-start.27 = (bf16[8,32,768]{2,1,0:T(8,128)(2,1)S(1)}, bf16[8,32,768]{2,1,0:T(8,128)(2,1)S(1)}, u32[]{:S(2)}, u32[]{:S(2)}) collective-permute-start(bf16[8,32,768]{2,1,0:T(8,128)(2,1)S(1)} %get-tuple-element.51), channel_id=1, source_target_pairs={{0,8},{4,12},{8,0},{12,4},{1,9},{5,13},{9,1},{13,5},{2,10},{6,14},... | collective-permute-start | bytes 1179656 | tf_op jit(solution)/shard_map/ppermute | solution.py:44
  125.2 6.0 %down.2.refs_0_ = bf16[768,3072]{1,0:T(8,128)(2,1)} custom-call(bf16[768,1024]{1,0:T(8,128)(2,1)S(1)} %get-tuple-element.53.at_a, bf16[768,1024]{1,0:T(8,128)(2,1)S(1)} %get-tuple-element.54.at_b, bf16[1024,3072]{1,0:T(8,128)(2,1)} %bitcast.32, bf16[1024,3072]{1,0:T(8,128)(2,1)} %bitcast.34, f32[8,32,768]{2,1,0:T(8,128)S(1)} %get-tuple-element.50.refs_0_), custom_call_target="tpu_custom_call" | custom-call | flops 3221225472 | bytes 5767168 | tf_op jit(solution)/shard_map/down/pallas_call | solution.py:337
  131.7 9.7 %down.3 = bf16[768,3072]{1,0:T(8,128)(2,1)} custom-call(bf16[768,1024]{1,0:T(8,128)(2,1)S(1)} %get-tuple-element.53.at_a, bf16[768,1024]{1,0:T(8,128)(2,1)S(1)} %get-tuple-element.54.at_b, bf16[1024,3072]{1,0:T(8,128)(2,1)} %bitcast.33, bf16[1024,3072]{1,0:T(8,128)(2,1)} %bitcast.35, bf16[768,3072]{1,0:T(8,128)(2,1)} %down.2.refs_0_), custom_call_target="tpu_custom_call", output_to_operand_aliasing={{}: (4, {})} | custom-call | flops 6442450944 | bytes 11534336 | tf_op jit(solution)/shard_map/down/pallas_call | solution.py:337
  (71 shorter events, 33.0 us)
Async XLA Ops:
  4.5 14.9 %collective-permute-start.14 = (bf16[128,768]{1,0:T(8,128)(2,1)S(1)}, bf16[128,768]{1,0:T(8,128)(2,1)S(1)}, u32[]{:S(2)}, u32[]{:S(2)}) collective-permute-start(bf16[128,768]{1,0:T(8,128)(2,1)S(1)} %get-tuple-element.35), channel_id=1, source_target_pairs={{0,1},{1,0},{2,3},{3,2},{4,5},{5,4},{6,7},{7,6},{8,9},{9,8},{10,11... | collective-permute-start | bytes 589832 | tf_op jit(solution)/shard_map/ppermute | solution.py:40
  19.0 12.0 %collective-permute-start.15 = (bf16[128,768]{1,0:T(8,128)(2,1)S(1)}, bf16[128,768]{1,0:T(8,128)(2,1)S(1)}, u32[]{:S(2)}, u32[]{:S(2)}) collective-permute-start(bf16[128,768]{1,0:T(8,128)(2,1)S(1)} %get-tuple-element.36), channel_id=1, source_target_pairs={{0,3},{1,2},{2,1},{3,0},{4,7},{5,6},{6,5},{7,4},{8,11},{9,10},{10,... | collective-permute-start | bytes 589832 | tf_op jit(solution)/shard_map/ppermute | solution.py:40
  19.5 13.5 %collective-permute-start.16 = (bf16[128,768]{1,0:T(8,128)(2,1)S(1)}, bf16[128,768]{1,0:T(8,128)(2,1)S(1)}, u32[]{:S(2)}, u32[]{:S(2)}) collective-permute-start(bf16[128,768]{1,0:T(8,128)(2,1)S(1)} %get-tuple-element.37), channel_id=1, source_target_pairs={{0,2},{1,3},{2,0},{3,1},{4,6},{5,7},{6,4},{7,5},{8,10},{9,11},{10,... | collective-permute-start | bytes 589832 | tf_op jit(solution)/shard_map/ppermute | solution.py:40
  24.0 16.0 %collective-permute-start.2 = (bf16[4,64,768]{2,1,0:T(8,128)(2,1)S(1)}, bf16[4,64,768]{2,1,0:T(8,128)(2,1)S(1)}, u32[]{:S(2)}, u32[]{:S(2)}) collective-permute-start(bf16[4,64,768]{2,1,0:T(8,128)(2,1)S(1)} %grow.13.refs_0_), channel_id=1, source_target_pairs={{0,16},{16,0},{32,48},{48,32},{64,80},{80,64},{96,112},{112,96},{1... | collective-permute-start | bytes 1179656 | tf_op jit(solution)/shard_map/ppermute | solution.py:39
  25.0 17.9 %collective-permute-start.6 = (bf16[4,64,768]{2,1,0:T(8,128)(2,1)S(1)}, bf16[4,64,768]{2,1,0:T(8,128)(2,1)S(1)}, u32[]{:S(2)}, u32[]{:S(2)}) collective-permute-start(bf16[4,64,768]{2,1,0:T(8,128)(2,1)S(1)} %grow.16.refs_0_), channel_id=1, source_target_pairs={{0,3},{1,2},{2,1},{3,0},{4,7},{5,6},{6,5},{7,4},{8,11},{9,10},{10,... | collective-permute-start | bytes 1179656 | tf_op jit(solution)/shard_map/ppermute | solution.py:40
  31.0 13.0 %collective-permute-start.10 = (bf16[4,64,768]{2,1,0:T(8,128)(2,1)S(1)}, bf16[4,64,768]{2,1,0:T(8,128)(2,1)S(1)}, u32[]{:S(2)}, u32[]{:S(2)}) collective-permute-start(bf16[4,64,768]{2,1,0:T(8,128)(2,1)S(1)} %grow.19.refs_0_), channel_id=1, source_target_pairs={{0,48},{16,32},{32,16},{48,0},{64,112},{80,96},{96,80},{112,64},{1... | collective-permute-start | bytes 1179656 | tf_op jit(solution)/shard_map/ppermute | solution.py:39
  34.3 16.3 %collective-permute-start.18 = (bf16[3,128,768]{2,1,0:T(8,128)(2,1)S(1)}, bf16[3,128,768]{2,1,0:T(8,128)(2,1)S(1)}, u32[]{:S(2)}, u32[]{:S(2)}) collective-permute-start(bf16[3,128,768]{2,1,0:T(8,128)(2,1)S(1)} %get-tuple-element.39.refs_2_), channel_id=1, source_target_pairs={{0,4},{4,0},{8,12},{12,8},{1,5},{5,1},{9,13},{13,9},{2,6},{6,2},{1... | collective-permute-start | bytes 1769480 | tf_op jit(solution)/shard_map/ppermute | solution.py:44
  40.4 20.1 %collective-permute-start.3 = (bf16[8,64,768]{2,1,0:T(8,128)(2,1)S(1)}, bf16[8,64,768]{2,1,0:T(8,128)(2,1)S(1)}, u32[]{:S(2)}, u32[]{:S(2)}) collective-permute-start(bf16[8,64,768]{2,1,0:T(8,128)(2,1)S(1)} %grow.14.refs_0_), channel_id=1, source_target_pairs={{0,3},{1,2},{2,1},{3,0},{4,7},{5,6},{6,5},{7,4},{8,11},{9,10},{10,... | collective-permute-start | bytes 2359304 | tf_op jit(solution)/shard_map/ppermute | solution.py:40
  43.2 19.7 %collective-permute-start.7 = (bf16[8,64,768]{2,1,0:T(8,128)(2,1)S(1)}, bf16[8,64,768]{2,1,0:T(8,128)(2,1)S(1)}, u32[]{:S(2)}, u32[]{:S(2)}) collective-permute-start(bf16[8,64,768]{2,1,0:T(8,128)(2,1)S(1)} %grow.17.refs_0_.refs_2_), channel_id=1, source_target_pairs={{0,48},{16,32},{32,16},{48,0},{64,112},{80,96},{96,80},{112,64},{1... | collective-permute-start | bytes 2359304 | tf_op jit(solution)/shard_map/ppermute | solution.py:39
  44.5 22.9 %collective-permute-start.11 = (bf16[8,64,768]{2,1,0:T(8,128)(2,1)S(1)}, bf16[8,64,768]{2,1,0:T(8,128)(2,1)S(1)}, u32[]{:S(2)}, u32[]{:S(2)}) collective-permute-start(bf16[8,64,768]{2,1,0:T(8,128)(2,1)S(1)} %grow.20.refs_0_.refs_4_), channel_id=1, source_target_pairs={{0,1},{1,0},{2,3},{3,2},{4,5},{5,4},{6,7},{7,6},{8,9},{9,8},{10,11... | collective-permute-start | bytes 2359304 | tf_op jit(solution)/shard_map/ppermute | solution.py:40
  51.2 17.8 %collective-permute-start.19 = (bf16[8,64,768]{2,1,0:T(8,128)(2,1)S(1)}, bf16[8,64,768]{2,1,0:T(8,128)(2,1)S(1)}, u32[]{:S(2)}, u32[]{:S(2)}) collective-permute-start(bf16[8,64,768]{2,1,0:T(8,128)(2,1)S(1)} %get-tuple-element.40.refs_0_.refs_6_), channel_id=1, source_target_pairs={{0,16},{16,0},{32,48},{48,32},{64,80},{80,64},{96,112},{112,96},{1... | collective-permute-start | bytes 2359304 | tf_op jit(solution)/shard_map/ppermute | solution.py:39
  51.7 27.3 %collective-permute-start.22 = (bf16[2,3,128,768]{3,2,1,0:T(8,128)(2,1)S(1)}, bf16[2,3,128,768]{3,2,1,0:T(8,128)(2,1)S(1)}, u32[]{:S(2)}, u32[]{:S(2)}) collective-permute-start(bf16[2,3,128,768]{3,2,1,0:T(8,128)(2,1)S(1)} %get-tuple-element.43.near), channel_id=1, source_target_pairs={{0,8},{4,12},{8,0},{12,4},{1,9},{5,13},{9,1},{13,5},{2,10},{6,14},... | collective-permute-start | bytes 3538952 | tf_op jit(solution)/shard_map/ppermute | solution.py:44
  61.3 29.3 %collective-permute-start.4 = (bf16[16,32,768]{2,1,0:T(8,128)(2,1)}, bf16[16,32,768]{2,1,0:T(8,128)(2,1)S(1)}, u32[]{:S(2)}, u32[]{:S(2)}) collective-permute-start(bf16[16,32,768]{2,1,0:T(8,128)(2,1)} %grow.15), channel_id=1, source_target_pairs={{0,48},{16,32},{32,16},{48,0},{64,112},{80,96},{96,80},{112,64},{1... | collective-permute-start | bytes 2359304 | tf_op jit(solution)/shard_map/ppermute | solution.py:39
  63.9 26.8 %collective-permute-start.8 = (bf16[16,32,768]{2,1,0:T(8,128)(2,1)}, bf16[16,32,768]{2,1,0:T(8,128)(2,1)S(1)}, u32[]{:S(2)}, u32[]{:S(2)}) collective-permute-start(bf16[16,32,768]{2,1,0:T(8,128)(2,1)} %grow.18), channel_id=1, source_target_pairs={{0,1},{1,0},{2,3},{3,2},{4,5},{5,4},{6,7},{7,6},{8,9},{9,8},{10,11... | collective-permute-start | bytes 2359304 | tf_op jit(solution)/shard_map/ppermute | solution.py:40
  68.4 23.0 %collective-permute-start.12 = (bf16[16,32,768]{2,1,0:T(8,128)(2,1)}, bf16[16,32,768]{2,1,0:T(8,128)(2,1)S(1)}, u32[]{:S(2)}, u32[]{:S(2)}) collective-permute-start(bf16[16,32,768]{2,1,0:T(8,128)(2,1)} %grow.21), channel_id=1, source_target_pairs={{0,16},{16,0},{32,48},{48,32},{64,80},{80,64},{96,112},{112,96},{1... | collective-permute-start | bytes 2359304 | tf_op jit(solution)/shard_map/ppermute | solution.py:39
  69.9 23.8 %collective-permute-start.20 = (bf16[16,32,768]{2,1,0:T(8,128)(2,1)}, bf16[16,32,768]{2,1,0:T(8,128)(2,1)S(1)}, u32[]{:S(2)}, u32[]{:S(2)}) collective-permute-start(bf16[16,32,768]{2,1,0:T(8,128)(2,1)} %grow.24), channel_id=1, source_target_pairs={{0,3},{1,2},{2,1},{3,0},{4,7},{5,6},{6,5},{7,4},{8,11},{9,10},{10,... | collective-permute-start | bytes 2359304 | tf_op jit(solution)/shard_map/ppermute | solution.py:40
  90.0 18.0 %collective-permute-start.23 = (bf16[16,32,768]{2,1,0:T(8,128)(2,1)}, bf16[16,32,768]{2,1,0:T(8,128)(2,1)S(1)}, u32[]{:S(2)}, u32[]{:S(2)}) collective-permute-start(bf16[16,32,768]{2,1,0:T(8,128)(2,1)} %get-tuple-element.45), channel_id=1, source_target_pairs={{0,48},{16,32},{32,16},{48,0},{64,112},{80,96},{96,80},{112,64},{1... | collective-permute-start | bytes 2359304 | tf_op jit(solution)/shard_map/ppermute | solution.py:39
  90.7 17.3 %collective-permute-start.24 = (bf16[16,32,768]{2,1,0:T(8,128)(2,1)}, bf16[16,32,768]{2,1,0:T(8,128)(2,1)S(1)}, u32[]{:S(2)}, u32[]{:S(2)}) collective-permute-start(bf16[16,32,768]{2,1,0:T(8,128)(2,1)} %get-tuple-element.46), channel_id=1, source_target_pairs={{0,1},{1,0},{2,3},{3,2},{4,5},{5,4},{6,7},{7,6},{8,9},{9,8},{10,11... | collective-permute-start | bytes 2359304 | tf_op jit(solution)/shard_map/ppermute | solution.py:40
  90.7 17.2 %collective-permute-start.25 = (bf16[16,32,768]{2,1,0:T(8,128)(2,1)}, bf16[16,32,768]{2,1,0:T(8,128)(2,1)S(1)}, u32[]{:S(2)}, u32[]{:S(2)}) collective-permute-start(bf16[16,32,768]{2,1,0:T(8,128)(2,1)} %get-tuple-element.47), channel_id=1, source_target_pairs={{0,16},{16,0},{32,48},{48,32},{64,80},{80,64},{96,112},{112,96},{1... | collective-permute-start | bytes 2359304 | tf_op jit(solution)/shard_map/ppermute | solution.py:39
  91.4 17.1 %collective-permute-start.26 = (bf16[16,32,768]{2,1,0:T(8,128)(2,1)}, bf16[16,32,768]{2,1,0:T(8,128)(2,1)S(1)}, u32[]{:S(2)}, u32[]{:S(2)}) collective-permute-start(bf16[16,32,768]{2,1,0:T(8,128)(2,1)} %get-tuple-element.48), channel_id=1, source_target_pairs={{0,3},{1,2},{2,1},{3,0},{4,7},{5,6},{6,5},{7,4},{8,11},{9,10},{10,... | collective-permute-start | bytes 2359304 | tf_op jit(solution)/shard_map/ppermute | solution.py:40
  103.2 19.1 %collective-permute-start.21 = (bf16[2,8,32,768]{3,2,1,0:T(8,128)(2,1)S(1)}, bf16[2,8,32,768]{3,2,1,0:T(8,128)(2,1)S(1)}, u32[]{:S(2)}, u32[]{:S(2)}) collective-permute-start(bf16[2,8,32,768]{3,2,1,0:T(8,128)(2,1)S(1)} %get-tuple-element.42), channel_id=1, source_target_pairs={{0,4},{4,0},{8,12},{12,8},{1,5},{5,1},{9,13},{13,9},{2,6},{6,2},{1... | collective-permute-start | bytes 2359304 | tf_op jit(solution)/shard_map/ppermute | solution.py:44
  117.9 13.4 %collective-permute-start.28 = (bf16[2,8,32,768]{3,2,1,0:T(8,128)(2,1)S(1)}, bf16[2,8,32,768]{3,2,1,0:T(8,128)(2,1)S(1)}, u32[]{:S(2)}, u32[]{:S(2)}) collective-permute-start(bf16[2,8,32,768]{3,2,1,0:T(8,128)(2,1)S(1)} %get-tuple-element.52), channel_id=1, source_target_pairs={{0,4},{4,0},{8,12},{12,8},{1,5},{5,1},{9,13},{13,9},{2,6},{6,2},{1... | collective-permute-start | bytes 2359304 | tf_op jit(solution)/shard_map/ppermute | solution.py:44
  122.4 19.0 %collective-permute-start.27 = (bf16[8,32,768]{2,1,0:T(8,128)(2,1)S(1)}, bf16[8,32,768]{2,1,0:T(8,128)(2,1)S(1)}, u32[]{:S(2)}, u32[]{:S(2)}) collective-permute-start(bf16[8,32,768]{2,1,0:T(8,128)(2,1)S(1)} %get-tuple-element.51), channel_id=1, source_target_pairs={{0,8},{4,12},{8,0},{12,4},{1,9},{5,13},{9,1},{13,5},{2,10},{6,14},... | collective-permute-start | bytes 1179656 | tf_op jit(solution)/shard_map/ppermute | solution.py:44
  131.4 12.0 %collective-permute-start.29 = (bf16[8,32,768]{2,1,0:T(8,128)(2,1)S(1)}, bf16[8,32,768]{2,1,0:T(8,128)(2,1)S(1)}, u32[]{:S(2)}, u32[]{:S(2)}) collective-permute-start(bf16[8,32,768]{2,1,0:T(8,128)(2,1)S(1)} %get-tuple-element.58), channel_id=1, source_target_pairs={{0,8},{4,12},{8,0},{12,4},{1,9},{5,13},{9,1},{13,5},{2,10},{6,14},... | collective-permute-start | bytes 1179656 | tf_op jit(solution)/shard_map/ppermute | solution.py:44
  (10 other events, 117.6 us)

commit v7 on v6

--- a/solution.py
+++ b/solution.py
@@ -87,29 +87,32 @@
 
 
 def split_kernel(own, got, *refs):
-    outs, sem = refs[-1 - CHAINS : -1], refs[-1]
-    copies = []
+    joined, outs, both, sem = refs[: len(HOPS)], refs[len(HOPS) : -2], refs[-2], refs[-1]
+    pairs = []
     for p in range(CHAINS):
         for side, src in enumerate((own, got)):
-            here = src.at[:, pl.ds(p * WIDTH, WIDTH)]
-            copies.append(pltpu.make_async_copy(here, outs[p].at[side], sem.at[len(copies)]))
+            pairs.append((src.at[:, pl.ds(p * WIDTH, WIDTH)], outs[p].at[side]))
+    for j, src in enumerate(joined):
+        pairs.append((src, both.at[j]))
+    copies = [pltpu.make_async_copy(*pair, sem.at[i]) for i, pair in enumerate(pairs)]
     for c in copies:
         c.start()
     for c in copies:
         c.wait()
 
 
-def split_call(own, got, after=()):
+def split_call(own, got, join):
     return pl.pallas_call(
         split_kernel,
-        out_shape=[jax.ShapeDtypeStruct((2, ROWS, WIDTH), jnp.bfloat16)] * CHAINS,
-        in_specs=[ANY] * (2 + len(after)),
-        out_specs=[ANY] * CHAINS,
-        scratch_shapes=[pltpu.SemaphoreType.DMA((2 * CHAINS,))],
+        out_shape=[jax.ShapeDtypeStruct((2, ROWS, WIDTH), jnp.bfloat16)] * CHAINS
+        + [jax.ShapeDtypeStruct((len(HOPS), SLICE, HID), jnp.bfloat16)],
+        in_specs=[ANY] * (2 + len(HOPS)),
+        out_specs=[ANY] * (CHAINS + 1),
+        scratch_shapes=[pltpu.SemaphoreType.DMA((2 * CHAINS + len(HOPS),))],
         compiler_params=params(1),
         cost_estimate=TINY,
         name="split",
-    )(in_hbm(own), got, *after)
+    )(in_hbm(own), got, *join)
 
 
 def grow_kernel(chains, at, n, joined, *refs):
@@ -145,7 +148,7 @@
 
 
 def gelu_kernel(where, table, pre, near, far, *refs):
-    outs, (buf, sems), acts = refs[:4], refs[4:6], refs[6:]
+    outs, (buf, sems), acts = refs[-8:-4], refs[-4:-2], refs[-2:]
     act_t, slopes = outs[:2], outs[2:]
     row, col, mine = where[0], where[1], where[2]
     quarter = SHARDS * ROWS // 4
@@ -199,31 +202,31 @@
         lax.fori_loop(0, SHARDS * PARTS[part] // 128, one_turn, 0)
 
 
-def gelu_call(where, table, pre, near, far):
+def gelu_call(where, table, pre, near, far, after=()):
     tokens = [SHARDS * n for n in PARTS]
     return pl.pallas_call(
         gelu_kernel,
         out_shape=[jax.ShapeDtypeStruct((HID, t), jnp.bfloat16) for t in tokens]
         + [jax.ShapeDtypeStruct((SHARDS // 4, n, HID), jnp.float32) for n in PARTS],
-        in_specs=[SMEM, SMEM] + [ANY] * 3,
+        in_specs=[SMEM, SMEM] + [ANY] * (3 + len(after)),
         out_specs=[VMEM] * 4,
         scratch_shapes=[pltpu.VMEM((SHARDS * ROWS, HID), jnp.bfloat16), pltpu.SemaphoreType.DMA((13,))]
         + [pltpu.VMEM((t, HID), jnp.bfloat16) for t in tokens],
         compiler_params=params(20),
         cost_estimate=TINY,
         name="gelu",
-    )(where, table, in_hbm(pre), near, far)
-
-
-def pieces(p, side, top):
+    )(where, table, in_hbm(pre), near, far, *after)
+
+
+def pieces(p, side):
     every = slice(None)
     if p == 0:
-        return [((every,) * 4, (side,) + (every,) * 4)] if side == top else []
+        return [((every,) * 4, (side,) + (every,) * 4)]
     if p == 1:
-        return [((top,) + (every,) * 3, (top,) + (every,) * 2 + (side, every))]
+        return [((every,) * 4, (every,) * 3 + (side, every))]
     if p == 2:
-        return [((i, top) + (every,) * 2, (top, every, side, i, every)) for i in range(2)]
-    return [((every,) * 2 + (top, every), (top, side) + (every,) * 3)]
+        return [((i,) + (every,) * 3, (every,) * 2 + (side, i, every)) for i in range(2)]
+    return [((every,) * 2 + (i, every), (i, side) + (every,) * 3) for i in range(2)]
 
 
 def hidden_kernel(n, where, w_far, *refs):
@@ -231,28 +234,31 @@
     keep, send, gathered, g, w, hs, sems = refs[-7:]
     row, mine = where[0], where[2]
     per = SHARDS // 4
-    weights = pltpu.make_async_copy(w_far, w, sems.at[4])
-    weights.start()
-    for top in range(2):
-        for p in range(CHAINS):
-            for side in range(2):
-                for src, dst in pieces(p, side, top):
-                    pltpu.make_async_copy(
-                        blocks[2 * p + side].at[src],
-                        g.at[dst + (slice(None), pl.ds(p * WIDTH, WIDTH))],
-                        sems.at[top],
-                    ).start()
-    outs = []
-    for i in range(2):
-        pltpu.make_async_copy(g.at[i], g.at[i], sems.at[i]).wait()
-        if i == 0:
-            weights.wait()
-        outs.append(pltpu.make_async_copy(g.at[i], gathered.at[i], sems.at[2 + i]))
+    every = (slice(None),) * 6
+    weights, outs = [], []
+    for p in range(CHAINS):
+        cols = pl.ds(p * WIDTH, WIDTH)
+        weights.append(pltpu.make_async_copy(w_far.at[:, cols], w.at[:, cols], sems.at[p]))
+        weights[-1].start()
+        for side in range(2):
+            for src, dst in pieces(p, side):
+                pltpu.make_async_copy(
+                    blocks[2 * p + side].at[src], g.at[dst + (slice(None), cols)], sems.at[CHAINS + p]
+                ).start()
+    for p in range(CHAINS):
+        cols = pl.ds(p * WIDTH, WIDTH)
+        here = g.at[every + (cols,)]
+        weights[p].wait()
+        pltpu.make_async_copy(here, here, sems.at[CHAINS + p]).wait()
+        outs.append(pltpu.make_async_copy(here, gathered.at[every + (cols,)], sems.at[2 * CHAINS + p]))
         outs[-1].start()
         h = lax.dot_general(
-            g[i].reshape(2 * per * n, FEATS), w[...], (((1,), (1,)), ((), ())), preferred_element_type=jnp.float32
-        )
-        hs[i] = h.reshape(2, 2, 2, 2, n, HID)
+            here[...].reshape(4 * per * n, WIDTH),
+            w[:, p * WIDTH : (p + 1) * WIDTH],
+            (((1,), (1,)), ((), ())),
+            preferred_element_type=jnp.float32,
+        ).reshape(hs.shape)
+        hs[...] = h if p == 0 else hs[...] + h
     for a, b in ((1, 1), (0, 1), (1, 0), (0, 0)):
         off_x = (mine // 16) ^ (row // 2) ^ a
         off_y = (mine // 8 % 2) ^ (row % 2) ^ b
@@ -283,7 +289,7 @@
             pltpu.VMEM((2,) * 5 + (n, FEATS), jnp.bfloat16),
             pltpu.VMEM((HID, FEATS), jnp.bfloat16),
             pltpu.VMEM((2,) * 5 + (n, HID), jnp.float32),
-            pltpu.SemaphoreType.DMA((5,)),
+            pltpu.SemaphoreType.DMA((3 * CHAINS,)),
         ],
         compiler_params=params(14 + n // 2),
         cost_estimate=pl.CostEstimate(
@@ -356,27 +362,28 @@
 
     got = swap(in_hbm(grad_out), X)
     fetched = [swap(chunk, mask) for chunk, mask in zip(cut_call(where, pre_act), HOPS)]
-    blocks = split_call(grad_out, got)
-    for k in range(2):
-        pairs = [(b, swap(b, ORDERS[p][k])) for p, b in enumerate(blocks)]
-        last = grow_call(pairs[-1:], join=fetched) if k == 0 else grow_call(pairs[-1:], join=[fetched, other])
-        blocks = [grow_call([pair])[0] for pair in pairs[:-1]] + [last[0]]
-        if k == 0:
-            fetched = last[1]
-            other = swap_row(fetched, 1)
-    near = last[1]
+    *blocks, fetched = split_call(grad_out, got, fetched)
+    other = swap_row(fetched, 1)
+    pairs = [(b, swap(b, ORDERS[p][0])) for p, b in enumerate(blocks)]
+    blocks = [grow_call([pair])[0] for pair in pairs]
+    near = jnp.stack([fetched, other])
     far = swap_row(near, 2)
+    pairs = [(b, swap(b, ORDERS[p][1])) for p, b in enumerate(blocks)]
+    blocks = [grow_call([pair])[0] for pair in pairs]
     pairs = [(b, swap(b, ORDERS[p][2])) for p, b in enumerate(blocks)]
-    own_a = [grow_call([pair], STARTS[0], PARTS[0])[0] for pair in pairs]
+    own_a = [
+        grow_call([pair], STARTS[0], PARTS[0], after=(far,) if p == CHAINS - 1 else ())[0]
+        for p, pair in enumerate(pairs)
+    ]
     came_a = [swap(own_a[p], ORDERS[p][3]) for p in range(CHAINS)]
-    act_a, act_b, slope_a, slope_b = gelu_call(where, table, pre_act, near, far)
-    own_b = grow_call(pairs, STARTS[1], PARTS[1], after=(slope_a,))
+    own_b = grow_call(pairs, STARTS[1], PARTS[1], after=(in_hbm(own_a[-1]),))
     came_b = [swap(own_b[p], ORDERS[p][3]) for p in range(CHAINS)]
     own, came = (own_a, own_b), (came_a, came_b)
 
     pairs = [[b for p in range(CHAINS) for b in (own[part][p], came[part][p])] for part in range(2)]
     keep_a, send_a, g_a = hidden_call(0, where, w_down, pairs[0])
-    keep_b, send_b, g_b = hidden_call(1, where, w_down, pairs[1], after=(keep_a,))
+    act_a, act_b, slope_a, slope_b = gelu_call(where, table, pre_act, near, far, after=(keep_a,))
+    keep_b, send_b, g_b = hidden_call(1, where, w_down, pairs[1], after=(slope_a,))
     mine_a, far_a = total_call(keep_a, swap_row(send_a, 1), after=(keep_b,))
     far_a = swap_row(far_a, 2)
     grad_down = down_call((act_a, act_b), (g_a, g_b), 0, 2, after=(mine_a,))

time: 145 us -> 143 us (0.986)
  starting transfers between devices: 50.4 us -> 42.1 us
  Pallas kernels: 57 us -> 60.2 us
  waiting for transfers between devices: 34.2 us -> 36.1 us
    ppermute x6, waiting for transfers between devices: 8.59 us -> 1.05 us  [swap_row(): return lax.ppermute(x, 'row', [(i, i ^ mask) for i in range(4)])]
    ppermute x13, waiting for transfers between devices: 18.6 us -> 25.4 us  [swap(): return lax.ppermute(x, 'col', [(i, i ^ mask) for i in range(4)])]
    ppermute x6, starting transfers between devices: 19.6 us -> 13.6 us  [swap_row(): return lax.ppermute(x, 'row', [(i, i ^ mask) for i in range(4)])]
    ppermute x13, starting transfers between devices: 19.1 us -> 13.8 us  [swap(): return lax.ppermute(x, 'col', [(i, i ^ mask) for i in range(4)])]
    pallas_call x2, Pallas kernels: 18.8 us -> 23.1 us  [hidden_call(): pl.pallas_call(functools.partial(hidden_kernel, n), out_shape=[jax.ShapeD...]
    ppermute x11, starting transfers between devices: 11.7 us -> 14.7 us  [swap(): return lax.ppermute(x, 'depth', [(i, i ^ mask >> 2) for i in range(8)])]
    ppermute x11, waiting for transfers between devices: 6.96 us -> 9.6 us  [swap(): return lax.ppermute(x, 'depth', [(i, i ^ mask >> 2) for i in range(8)])]
  transfers between devices with their start and end apart: 30 -> 30, of which waited for: 11 -> 12; matrix products, arithmetic and copies ran while one was open for 0% -> 0% of each run, Pallas kernels for 39% -> 42%
where the time goes in v7:
time: 143 us; the launch traced here: 141 us
  Pallas kernels  60.2 us (42%)
  starting transfers between devices  42.1 us (29%)
  waiting for transfers between devices  36.1 us (25%)
    ppermute x13, waiting for transfers between devices, swap(): return lax.ppermute(x, 'col', [(i, i ^ mask) for i in range(4)])  25.4 us
    pallas_call x2, Pallas kernels, hidden_call(): pl.pallas_call(functools.partial(hidden_kernel, n), out_shape=[jax.ShapeD...  23.1 us
    pallas_call x2, Pallas kernels, down_call(): pl.pallas_call(down_kernel, grid=(count,), out_shape=pltpu.HBM((HID, FEAT...  15.7 us
    ppermute x11, starting transfers between devices, swap(): return lax.ppermute(x, 'depth', [(i, i ^ mask >> 2) for i in range(8)])  14.7 us
    ppermute x13, starting transfers between devices, swap(): return lax.ppermute(x, 'col', [(i, i ^ mask) for i in range(4)])  13.8 us
    ppermute x6, starting transfers between devices, swap_row(): return lax.ppermute(x, 'row', [(i, i ^ mask) for i in range(4)])  13.6 us
    ppermute x11, waiting for transfers between devices, swap(): return lax.ppermute(x, 'depth', [(i, i ^ mask >> 2) for i in range(8)])  9.6 us
    pallas_call x1, Pallas kernels, gelu_call(): pl.pallas_call(gelu_kernel, out_shape=[jax.ShapeDtypeStruct((HID, t), jnp...  9.19 us
  transfers between devices with their start and end apart: 30, of which 12 were waited for; matrix products, arithmetic and copies ran while one was open for 0% of the time, Pallas kernels for 42%

profile of v7, /device:TPU:1, one launch (start us, length us, event | category | flops | bytes accessed | tf_op | source)
XLA Modules:
  0.0 141.4 jit_solution(15004966855784181795)
XLA Ops:
  0.6 2.1 %collective-permute-start = (bf16[64,3072]{1,0:T(8,128)(2,1)}, bf16[64,3072]{1,0:T(8,128)(2,1)S(1)}, u32[]{:S(2)}, u32[]{:S(2)}) collective-permute-start(bf16[64,3072]{1,0:T(8,128)(2,1)} %own.1), channel_id=1, source_target_pairs={{0,64},{16,80},{32,96},{48,112},{64,0},{80,16},{96,32},{112,48},{1... | collective-permute-start | bytes 1179656 | tf_op jit(solution)/shard_map/ppermute | solution.py:39
  4.5 1.7 %collective-permute-start.1 = (bf16[128,768]{1,0:T(8,128)(2,1)S(1)}, bf16[128,768]{1,0:T(8,128)(2,1)S(1)}, u32[]{:S(2)}, u32[]{:S(2)}) collective-permute-start(bf16[128,768]{1,0:T(8,128)(2,1)S(1)} %get-tuple-element.28), channel_id=1, source_target_pairs={{0,1},{1,0},{2,3},{3,2},{4,5},{5,4},{6,7},{7,6},{8,9},{9,8},{10,11... | collective-permute-start | bytes 589832 | tf_op jit(solution)/shard_map/ppermute | solution.py:40
  6.2 2.2 %collective-permute-start.2 = (bf16[128,768]{1,0:T(8,128)(2,1)S(1)}, bf16[128,768]{1,0:T(8,128)(2,1)S(1)}, u32[]{:S(2)}, u32[]{:S(2)}) collective-permute-start(bf16[128,768]{1,0:T(8,128)(2,1)S(1)} %get-tuple-element.29), channel_id=1, source_target_pairs={{0,3},{1,2},{2,1},{3,0},{4,7},{5,6},{6,5},{7,4},{8,11},{9,10},{10,... | collective-permute-start | bytes 589832 | tf_op jit(solution)/shard_map/ppermute | solution.py:40
  10.4 5.5 %collective-permute-done.2.refs_1_ = bf16[128,768]{1,0:T(8,128)(2,1)S(1)} collective-permute-done((bf16[128,768]{1,0:T(8,128)(2,1)S(1)}, bf16[128,768]{1,0:T(8,128)(2,1)S(1)}, u32[]{:S(2)}, u32[]{:S(2)}) %collective-permute-start.2) | collective-permute-done | bytes 196640 | tf_op jit(solution)/shard_map/ppermute | solution.py:40
  16.0 1.8 %collective-permute-done.3.refs_2_ = bf16[128,768]{1,0:T(8,128)(2,1)S(1)} collective-permute-done((bf16[128,768]{1,0:T(8,128)(2,1)S(1)}, bf16[128,768]{1,0:T(8,128)(2,1)S(1)}, u32[]{:S(2)}, u32[]{:S(2)}) %collective-permute-start.3) | collective-permute-done | bytes 196640 | tf_op jit(solution)/shard_map/ppermute | solution.py:40
  19.8 1.9 %collective-permute-start.19 = (bf16[3,128,768]{2,1,0:T(8,128)(2,1)S(1)}, bf16[3,128,768]{2,1,0:T(8,128)(2,1)S(1)}, u32[]{:S(2)}, u32[]{:S(2)}) collective-permute-start(bf16[3,128,768]{2,1,0:T(8,128)(2,1)S(1)} %get-tuple-element.35), channel_id=1, source_target_pairs={{0,4},{4,0},{8,12},{12,8},{1,5},{5,1},{9,13},{13,9},{2,6},{6,2},{1... | collective-permute-start | bytes 1769480 | tf_op jit(solution)/shard_map/ppermute | solution.py:44
  23.1 1.8 %collective-permute-start.12 = (bf16[2,64,768]{2,1,0:T(8,128)(2,1)S(1)}, bf16[2,64,768]{2,1,0:T(8,128)(2,1)S(1)}, u32[]{:S(2)}, u32[]{:S(2)}) collective-permute-start(bf16[2,64,768]{2,1,0:T(8,128)(2,1)S(1)} %get-tuple-element.33.refs_0_), channel_id=1, source_target_pairs={{0,3},{1,2},{2,1},{3,0},{4,7},{5,6},{6,5},{7,4},{8,11},{9,10},{10,... | collective-permute-start | bytes 589832 | tf_op jit(solution)/shard_map/ppermute | solution.py:40
  24.8 1.9 %collective-permute-start.16 = (bf16[2,64,768]{2,1,0:T(8,128)(2,1)S(1)}, bf16[2,64,768]{2,1,0:T(8,128)(2,1)S(1)}, u32[]{:S(2)}, u32[]{:S(2)}) collective-permute-start(bf16[2,64,768]{2,1,0:T(8,128)(2,1)S(1)} %get-tuple-element.34.refs_0_), channel_id=1, source_target_pairs={{0,48},{16,32},{32,16},{48,0},{64,112},{80,96},{96,80},{112,64},{1... | collective-permute-start | bytes 589832 | tf_op jit(solution)/shard_map/ppermute | solution.py:39
  30.6 1.7 %collective-permute-start.9 = (bf16[4,64,768]{2,1,0:T(8,128)(2,1)S(1)}, bf16[4,64,768]{2,1,0:T(8,128)(2,1)S(1)}, u32[]{:S(2)}, u32[]{:S(2)}) collective-permute-start(bf16[4,64,768]{2,1,0:T(8,128)(2,1)S(1)} %grow.16.refs_0_), channel_id=1, source_target_pairs={{0,3},{1,2},{2,1},{3,0},{4,7},{5,6},{6,5},{7,4},{8,11},{9,10},{10,... | collective-permute-start | bytes 1179656 | tf_op jit(solution)/shard_map/ppermute | solution.py:40
  32.8 2.0 %collective-permute-start.13 = (bf16[4,64,768]{2,1,0:T(8,128)(2,1)S(1)}, bf16[4,64,768]{2,1,0:T(8,128)(2,1)S(1)}, u32[]{:S(2)}, u32[]{:S(2)}) collective-permute-start(bf16[4,64,768]{2,1,0:T(8,128)(2,1)S(1)} %grow.19.refs_0_), channel_id=1, source_target_pairs={{0,48},{16,32},{32,16},{48,0},{64,112},{80,96},{96,80},{112,64},{1... | collective-permute-start | bytes 1179656 | tf_op jit(solution)/shard_map/ppermute | solution.py:39
  35.6 2.5 %collective-permute-start.20 = (bf16[2,3,128,768]{3,2,1,0:T(8,128)(2,1)S(1)}, bf16[2,3,128,768]{3,2,1,0:T(8,128)(2,1)S(1)}, u32[]{:S(2)}, u32[]{:S(2)}) collective-permute-start(bf16[2,3,128,768]{3,2,1,0:T(8,128)(2,1)S(1)} %pad_maximum_fusion.near), channel_id=1, source_target_pairs={{0,8},{4,12},{8,0},{12,4},{1,9},{5,13},{9,1},{13,5},{2,10},{6,14},... | collective-permute-start | bytes 3538952 | tf_op jit(solution)/shard_map/ppermute | solution.py:44
  41.8 2.1 %collective-permute-start.10 = (bf16[8,64,768]{2,1,0:T(8,128)(2,1)S(1)}, bf16[8,64,768]{2,1,0:T(8,128)(2,1)S(1)}, u32[]{:S(2)}, u32[]{:S(2)}) collective-permute-start(bf16[8,64,768]{2,1,0:T(8,128)(2,1)S(1)} %grow.17.refs_0_.refs_2_), channel_id=1, source_target_pairs={{0,48},{16,32},{32,16},{48,0},{64,112},{80,96},{96,80},{112,64},{1... | collective-permute-start | bytes 2359304 | tf_op jit(solution)/shard_map/ppermute | solution.py:39
  45.2 12.5 %collective-permute-done.6.refs_1_ = bf16[8,64,768]{2,1,0:T(8,128)(2,1)S(1)} collective-permute-done((bf16[8,64,768]{2,1,0:T(8,128)(2,1)S(1)}, bf16[8,64,768]{2,1,0:T(8,128)(2,1)S(1)}, u32[]{:S(2)}, u32[]{:S(2)}) %collective-permute-start.6) | collective-permute-done | bytes 786464 | tf_op jit(solution)/shard_map/ppermute | solution.py:40
  58.6 2.6 %collective-permute-start.7 = (bf16[16,32,768]{2,1,0:T(8,128)(2,1)}, bf16[16,32,768]{2,1,0:T(8,128)(2,1)S(1)}, u32[]{:S(2)}, u32[]{:S(2)}) collective-permute-start(bf16[16,32,768]{2,1,0:T(8,128)(2,1)} %grow.15), channel_id=1, source_target_pairs={{0,48},{16,32},{32,16},{48,0},{64,112},{80,96},{96,80},{112,64},{1... | collective-permute-start | bytes 2359304 | tf_op jit(solution)/shard_map/ppermute | solution.py:39
  65.9 1.7 %grow.25 = (bf16[16,32,768]{2,1,0:T(8,128)(2,1)}, bf16[16,32,768]{2,1,0:T(8,128)(2,1)}, bf16[16,32,768]{2,1,0:T(8,128)(2,1)}, bf16[16,32,768]{2,1,0:T(8,128)(2,1)}) custom-call(bf16[8,64,768]{2,1,0:T(8,128)(2,1)S(1)} %grow.14.refs_0_, bf16[8,64,768]{2,1,0:T(8,128)(2,1)S(1)} %collective-permute-done.6.refs_1_, bf16[8,64,768]{2,1,0:T(8,128)(2,1)S(1)} %grow.17.refs_0_.refs_2_, ...), custom_call_target="tpu_custom_call" | custom-call | flops 1 | bytes 1 | tf_op jit(solution)/shard_map/grow/pallas_call | solution.py:137
  68.4 8.1 %collective-permute-done.7 = bf16[16,32,768]{2,1,0:T(8,128)(2,1)S(1)} collective-permute-done((bf16[16,32,768]{2,1,0:T(8,128)(2,1)}, bf16[16,32,768]{2,1,0:T(8,128)(2,1)S(1)}, u32[]{:S(2)}, u32[]{:S(2)}) %collective-permute-start.7) | collective-permute-done | bytes 786464 | tf_op jit(solution)/shard_map/ppermute | solution.py:39
  76.5 2.0 %collective-permute-done.11 = bf16[16,32,768]{2,1,0:T(8,128)(2,1)S(1)} collective-permute-done((bf16[16,32,768]{2,1,0:T(8,128)(2,1)}, bf16[16,32,768]{2,1,0:T(8,128)(2,1)S(1)}, u32[]{:S(2)}, u32[]{:S(2)}) %collective-permute-start.11) | collective-permute-done | bytes 786464 | tf_op jit(solution)/shard_map/ppermute | solution.py:40
  81.7 11.5 %hidden.2 = (f32[2,8,32,768]{3,2,1,0:T(8,128)S(1)}, bf16[2,8,32,768]{3,2,1,0:T(8,128)(2,1)S(1)}, bf16[2,2,2,2,2,32,3072]{6,5,4,3,2,1,0:T(8,128)(2,1)}) custom-call(s32[3]{0:T(128)S(1)} %pad_add_fusion.where, bf16[768,3072]{1,0:T(8,128)(2,1)S(1)} %bitcast.26, bf16[2,2,2,2,32,768]{5,4,3,2,1,0:T(8,128)(2,1)} %bitcast.41, ...), custom_call_target="tpu_custom_call" | custom-call | flops 4831838208 | bytes 12582912 | tf_op jit(solution)/shard_map/hidden/pallas_call | solution.py:279
  93.2 5.9 %collective-permute-start.22 = (bf16[2,8,32,768]{3,2,1,0:T(8,128)(2,1)S(1)}, bf16[2,8,32,768]{3,2,1,0:T(8,128)(2,1)S(1)}, u32[]{:S(2)}, u32[]{:S(2)}) collective-permute-start(bf16[2,8,32,768]{3,2,1,0:T(8,128)(2,1)S(1)} %get-tuple-element.37), channel_id=1, source_target_pairs={{0,4},{4,0},{8,12},{12,8},{1,5},{5,1},{9,13},{13,9},{2,6},{6,2},{1... | collective-permute-start | bytes 2359304 | tf_op jit(solution)/shard_map/ppermute | solution.py:44
  99.1 9.2 %gelu.1 = (bf16[768,1024]{1,0:T(8,128)(2,1)S(1)}, bf16[768,1024]{1,0:T(8,128)(2,1)S(1)}, f32[8,32,768]{2,1,0:T(8,128)S(1)}, f32[8,32,768]{2,1,0:T(8,128)S(1)}) custom-call(s32[3]{0:T(128)S(1)} %pad_add_fusion.where, s32[32]{0:T(128)S(1)} %copy-done, bf16[512,3072]{1,0:T(8,128)(2,1)} %pre.3, bf16[2,3,128,768]{3,2,1,0:T(8,128)(2,1)S(1)} %pad_maximum_fusion.near, ...), custom_call_target="tpu_custom_call" | custom-call | flops 1 | bytes 1 | tf_op jit(solution)/shard_map/gelu/pallas_call | solution.py:207
  108.4 11.5 %hidden.3 = (f32[2,8,32,768]{3,2,1,0:T(8,128)S(1)}, bf16[2,8,32,768]{3,2,1,0:T(8,128)(2,1)S(1)}, bf16[2,2,2,2,2,32,3072]{6,5,4,3,2,1,0:T(8,128)(2,1)}) custom-call(s32[3]{0:T(128)S(1)} %pad_add_fusion.where, bf16[768,3072]{1,0:T(8,128)(2,1)S(1)} %bitcast.26, bf16[2,2,2,2,32,768]{5,4,3,2,1,0:T(8,128)(2,1)} %bitcast.45, ...), custom_call_target="tpu_custom_call" | custom-call | flops 4831838208 | bytes 12582912 | tf_op jit(solution)/shard_map/hidden/pallas_call | solution.py:279
  120.2 2.5 %collective-permute-start.27 = (bf16[8,32,768]{2,1,0:T(8,128)(2,1)S(1)}, bf16[8,32,768]{2,1,0:T(8,128)(2,1)S(1)}, u32[]{:S(2)}, u32[]{:S(2)}) collective-permute-start(bf16[8,32,768]{2,1,0:T(8,128)(2,1)S(1)} %get-tuple-element.45), channel_id=1, source_target_pairs={{0,8},{4,12},{8,0},{12,4},{1,9},{5,13},{9,1},{13,5},{2,10},{6,14},... | collective-permute-start | bytes 1179656 | tf_op jit(solution)/shard_map/ppermute | solution.py:44
  122.7 6.0 %down.2.refs_0_ = bf16[768,3072]{1,0:T(8,128)(2,1)} custom-call(bf16[768,1024]{1,0:T(8,128)(2,1)S(1)} %get-tuple-element.47.at_a, bf16[768,1024]{1,0:T(8,128)(2,1)S(1)} %get-tuple-element.48.at_b, bf16[1024,3072]{1,0:T(8,128)(2,1)} %bitcast.35, bf16[1024,3072]{1,0:T(8,128)(2,1)} %bitcast.37, f32[8,32,768]{2,1,0:T(8,128)S(1)} %get-tuple-element.44.refs_0_), custom_call_target="tpu_custom_call" | custom-call | flops 3221225472 | bytes 5767168 | tf_op jit(solution)/shard_map/down/pallas_call | solution.py:343
  129.5 9.7 %down.3 = bf16[768,3072]{1,0:T(8,128)(2,1)} custom-call(bf16[768,1024]{1,0:T(8,128)(2,1)S(1)} %get-tuple-element.47.at_a, bf16[768,1024]{1,0:T(8,128)(2,1)S(1)} %get-tuple-element.48.at_b, bf16[1024,3072]{1,0:T(8,128)(2,1)} %bitcast.36, bf16[1024,3072]{1,0:T(8,128)(2,1)} %bitcast.38, bf16[768,3072]{1,0:T(8,128)(2,1)} %down.2.refs_0_), custom_call_target="tpu_custom_call", output_to_operand_aliasing={{}: (4, {})} | custom-call | flops 6442450944 | bytes 11534336 | tf_op jit(solution)/shard_map/down/pallas_call | solution.py:343
  (72 shorter events, 29.8 us)
Async XLA Ops:
  0.6 17.1 %collective-permute-start = (bf16[64,3072]{1,0:T(8,128)(2,1)}, bf16[64,3072]{1,0:T(8,128)(2,1)S(1)}, u32[]{:S(2)}, u32[]{:S(2)}) collective-permute-start(bf16[64,3072]{1,0:T(8,128)(2,1)} %own.1), channel_id=1, source_target_pairs={{0,64},{16,80},{32,96},{48,112},{64,0},{80,16},{96,32},{112,48},{1... | collective-permute-start | bytes 1179656 | tf_op jit(solution)/shard_map/ppermute | solution.py:39
  6.2 9.7 %collective-permute-start.2 = (bf16[128,768]{1,0:T(8,128)(2,1)S(1)}, bf16[128,768]{1,0:T(8,128)(2,1)S(1)}, u32[]{:S(2)}, u32[]{:S(2)}) collective-permute-start(bf16[128,768]{1,0:T(8,128)(2,1)S(1)} %get-tuple-element.29), channel_id=1, source_target_pairs={{0,3},{1,2},{2,1},{3,0},{4,7},{5,6},{6,5},{7,4},{8,11},{9,10},{10,... | collective-permute-start | bytes 589832 | tf_op jit(solution)/shard_map/ppermute | solution.py:40
  19.8 15.6 %collective-permute-start.19 = (bf16[3,128,768]{2,1,0:T(8,128)(2,1)S(1)}, bf16[3,128,768]{2,1,0:T(8,128)(2,1)S(1)}, u32[]{:S(2)}, u32[]{:S(2)}) collective-permute-start(bf16[3,128,768]{2,1,0:T(8,128)(2,1)S(1)} %get-tuple-element.35), channel_id=1, source_target_pairs={{0,4},{4,0},{8,12},{12,8},{1,5},{5,1},{9,13},{13,9},{2,6},{6,2},{1... | collective-permute-start | bytes 1769480 | tf_op jit(solution)/shard_map/ppermute | solution.py:44
  23.1 9.3 %collective-permute-start.12 = (bf16[2,64,768]{2,1,0:T(8,128)(2,1)S(1)}, bf16[2,64,768]{2,1,0:T(8,128)(2,1)S(1)}, u32[]{:S(2)}, u32[]{:S(2)}) collective-permute-start(bf16[2,64,768]{2,1,0:T(8,128)(2,1)S(1)} %get-tuple-element.33.refs_0_), channel_id=1, source_target_pairs={{0,3},{1,2},{2,1},{3,0},{4,7},{5,6},{6,5},{7,4},{8,11},{9,10},{10,... | collective-permute-start | bytes 589832 | tf_op jit(solution)/shard_map/ppermute | solution.py:40
  24.8 10.0 %collective-permute-start.16 = (bf16[2,64,768]{2,1,0:T(8,128)(2,1)S(1)}, bf16[2,64,768]{2,1,0:T(8,128)(2,1)S(1)}, u32[]{:S(2)}, u32[]{:S(2)}) collective-permute-start(bf16[2,64,768]{2,1,0:T(8,128)(2,1)S(1)} %get-tuple-element.34.refs_0_), channel_id=1, source_target_pairs={{0,48},{16,32},{32,16},{48,0},{64,112},{80,96},{96,80},{112,64},{1... | collective-permute-start | bytes 589832 | tf_op jit(solution)/shard_map/ppermute | solution.py:39
  28.7 9.8 %collective-permute-start.5 = (bf16[4,64,768]{2,1,0:T(8,128)(2,1)S(1)}, bf16[4,64,768]{2,1,0:T(8,128)(2,1)S(1)}, u32[]{:S(2)}, u32[]{:S(2)}) collective-permute-start(bf16[4,64,768]{2,1,0:T(8,128)(2,1)S(1)} %grow.13.refs_0_), channel_id=1, source_target_pairs={{0,16},{16,0},{32,48},{48,32},{64,80},{80,64},{96,112},{112,96},{1... | collective-permute-start | bytes 1179656 | tf_op jit(solution)/shard_map/ppermute | solution.py:39
  30.6 10.7 %collective-permute-start.9 = (bf16[4,64,768]{2,1,0:T(8,128)(2,1)S(1)}, bf16[4,64,768]{2,1,0:T(8,128)(2,1)S(1)}, u32[]{:S(2)}, u32[]{:S(2)}) collective-permute-start(bf16[4,64,768]{2,1,0:T(8,128)(2,1)S(1)} %grow.16.refs_0_), channel_id=1, source_target_pairs={{0,3},{1,2},{2,1},{3,0},{4,7},{5,6},{6,5},{7,4},{8,11},{9,10},{10,... | collective-permute-start | bytes 1179656 | tf_op jit(solution)/shard_map/ppermute | solution.py:40
  32.8 11.0 %collective-permute-start.13 = (bf16[4,64,768]{2,1,0:T(8,128)(2,1)S(1)}, bf16[4,64,768]{2,1,0:T(8,128)(2,1)S(1)}, u32[]{:S(2)}, u32[]{:S(2)}) collective-permute-start(bf16[4,64,768]{2,1,0:T(8,128)(2,1)S(1)} %grow.19.refs_0_), channel_id=1, source_target_pairs={{0,48},{16,32},{32,16},{48,0},{64,112},{80,96},{96,80},{112,64},{1... | collective-permute-start | bytes 1179656 | tf_op jit(solution)/shard_map/ppermute | solution.py:39
  35.6 27.7 %collective-permute-start.20 = (bf16[2,3,128,768]{3,2,1,0:T(8,128)(2,1)S(1)}, bf16[2,3,128,768]{3,2,1,0:T(8,128)(2,1)S(1)}, u32[]{:S(2)}, u32[]{:S(2)}) collective-permute-start(bf16[2,3,128,768]{3,2,1,0:T(8,128)(2,1)S(1)} %pad_maximum_fusion.near), channel_id=1, source_target_pairs={{0,8},{4,12},{8,0},{12,4},{1,9},{5,13},{9,1},{13,5},{2,10},{6,14},... | collective-permute-start | bytes 3538952 | tf_op jit(solution)/shard_map/ppermute | solution.py:44
  39.0 18.7 %collective-permute-start.6 = (bf16[8,64,768]{2,1,0:T(8,128)(2,1)S(1)}, bf16[8,64,768]{2,1,0:T(8,128)(2,1)S(1)}, u32[]{:S(2)}, u32[]{:S(2)}) collective-permute-start(bf16[8,64,768]{2,1,0:T(8,128)(2,1)S(1)} %grow.14.refs_0_), channel_id=1, source_target_pairs={{0,3},{1,2},{2,1},{3,0},{4,7},{5,6},{6,5},{7,4},{8,11},{9,10},{10,... | collective-permute-start | bytes 2359304 | tf_op jit(solution)/shard_map/ppermute | solution.py:40
  41.8 19.5 %collective-permute-start.10 = (bf16[8,64,768]{2,1,0:T(8,128)(2,1)S(1)}, bf16[8,64,768]{2,1,0:T(8,128)(2,1)S(1)}, u32[]{:S(2)}, u32[]{:S(2)}) collective-permute-start(bf16[8,64,768]{2,1,0:T(8,128)(2,1)S(1)} %grow.17.refs_0_.refs_2_), channel_id=1, source_target_pairs={{0,48},{16,32},{32,16},{48,0},{64,112},{80,96},{96,80},{112,64},{1... | collective-permute-start | bytes 2359304 | tf_op jit(solution)/shard_map/ppermute | solution.py:39
  44.3 18.0 %collective-permute-start.14 = (bf16[8,64,768]{2,1,0:T(8,128)(2,1)S(1)}, bf16[8,64,768]{2,1,0:T(8,128)(2,1)S(1)}, u32[]{:S(2)}, u32[]{:S(2)}) collective-permute-start(bf16[8,64,768]{2,1,0:T(8,128)(2,1)S(1)} %grow.20.refs_0_.refs_4_), channel_id=1, source_target_pairs={{0,1},{1,0},{2,3},{3,2},{4,5},{5,4},{6,7},{7,6},{8,9},{9,8},{10,11... | collective-permute-start | bytes 2359304 | tf_op jit(solution)/shard_map/ppermute | solution.py:40
  44.8 18.5 %collective-permute-start.18 = (bf16[8,64,768]{2,1,0:T(8,128)(2,1)S(1)}, bf16[8,64,768]{2,1,0:T(8,128)(2,1)S(1)}, u32[]{:S(2)}, u32[]{:S(2)}) collective-permute-start(bf16[8,64,768]{2,1,0:T(8,128)(2,1)S(1)} %grow.23.refs_0_.refs_6_), channel_id=1, source_target_pairs={{0,16},{16,0},{32,48},{48,32},{64,80},{80,64},{96,112},{112,96},{1... | collective-permute-start | bytes 2359304 | tf_op jit(solution)/shard_map/ppermute | solution.py:39
  58.6 17.9 %collective-permute-start.7 = (bf16[16,32,768]{2,1,0:T(8,128)(2,1)}, bf16[16,32,768]{2,1,0:T(8,128)(2,1)S(1)}, u32[]{:S(2)}, u32[]{:S(2)}) collective-permute-start(bf16[16,32,768]{2,1,0:T(8,128)(2,1)} %grow.15), channel_id=1, source_target_pairs={{0,48},{16,32},{32,16},{48,0},{64,112},{80,96},{96,80},{112,64},{1... | collective-permute-start | bytes 2359304 | tf_op jit(solution)/shard_map/ppermute | solution.py:39
  62.1 16.4 %collective-permute-start.11 = (bf16[16,32,768]{2,1,0:T(8,128)(2,1)}, bf16[16,32,768]{2,1,0:T(8,128)(2,1)S(1)}, u32[]{:S(2)}, u32[]{:S(2)}) collective-permute-start(bf16[16,32,768]{2,1,0:T(8,128)(2,1)} %grow.18), channel_id=1, source_target_pairs={{0,1},{1,0},{2,3},{3,2},{4,5},{5,4},{6,7},{7,6},{8,9},{9,8},{10,11... | collective-permute-start | bytes 2359304 | tf_op jit(solution)/shard_map/ppermute | solution.py:40
  63.2 16.4 %collective-permute-start.15 = (bf16[16,32,768]{2,1,0:T(8,128)(2,1)}, bf16[16,32,768]{2,1,0:T(8,128)(2,1)S(1)}, u32[]{:S(2)}, u32[]{:S(2)}) collective-permute-start(bf16[16,32,768]{2,1,0:T(8,128)(2,1)} %grow.21), channel_id=1, source_target_pairs={{0,16},{16,0},{32,48},{48,32},{64,80},{80,64},{96,112},{112,96},{1... | collective-permute-start | bytes 2359304 | tf_op jit(solution)/shard_map/ppermute | solution.py:39
  64.2 17.5 %collective-permute-start.21 = (bf16[16,32,768]{2,1,0:T(8,128)(2,1)}, bf16[16,32,768]{2,1,0:T(8,128)(2,1)S(1)}, u32[]{:S(2)}, u32[]{:S(2)}) collective-permute-start(bf16[16,32,768]{2,1,0:T(8,128)(2,1)} %grow.24.refs_8_), channel_id=1, source_target_pairs={{0,3},{1,2},{2,1},{3,0},{4,7},{5,6},{6,5},{7,4},{8,11},{9,10},{10,... | collective-permute-start | bytes 2359304 | tf_op jit(solution)/shard_map/ppermute | solution.py:40
  67.7 40.7 %collective-permute-start.23 = (bf16[16,32,768]{2,1,0:T(8,128)(2,1)}, bf16[16,32,768]{2,1,0:T(8,128)(2,1)S(1)}, u32[]{:S(2)}, u32[]{:S(2)}) collective-permute-start(bf16[16,32,768]{2,1,0:T(8,128)(2,1)} %get-tuple-element.38), channel_id=1, source_target_pairs={{0,48},{16,32},{32,16},{48,0},{64,112},{80,96},{96,80},{112,64},{1... | collective-permute-start | bytes 2359304 | tf_op jit(solution)/shard_map/ppermute | solution.py:39
  76.5 31.9 %collective-permute-start.24 = (bf16[16,32,768]{2,1,0:T(8,128)(2,1)}, bf16[16,32,768]{2,1,0:T(8,128)(2,1)S(1)}, u32[]{:S(2)}, u32[]{:S(2)}) collective-permute-start(bf16[16,32,768]{2,1,0:T(8,128)(2,1)} %get-tuple-element.39), channel_id=1, source_target_pairs={{0,1},{1,0},{2,3},{3,2},{4,5},{5,4},{6,7},{7,6},{8,9},{9,8},{10,11... | collective-permute-start | bytes 2359304 | tf_op jit(solution)/shard_map/ppermute | solution.py:40
  78.5 29.9 %collective-permute-start.25 = (bf16[16,32,768]{2,1,0:T(8,128)(2,1)}, bf16[16,32,768]{2,1,0:T(8,128)(2,1)S(1)}, u32[]{:S(2)}, u32[]{:S(2)}) collective-permute-start(bf16[16,32,768]{2,1,0:T(8,128)(2,1)} %get-tuple-element.40), channel_id=1, source_target_pairs={{0,16},{16,0},{32,48},{48,32},{64,80},{80,64},{96,112},{112,96},{1... | collective-permute-start | bytes 2359304 | tf_op jit(solution)/shard_map/ppermute | solution.py:39
  79.5 28.9 %collective-permute-start.26 = (bf16[16,32,768]{2,1,0:T(8,128)(2,1)}, bf16[16,32,768]{2,1,0:T(8,128)(2,1)S(1)}, u32[]{:S(2)}, u32[]{:S(2)}) collective-permute-start(bf16[16,32,768]{2,1,0:T(8,128)(2,1)} %get-tuple-element.41), channel_id=1, source_target_pairs={{0,3},{1,2},{2,1},{3,0},{4,7},{5,6},{6,5},{7,4},{8,11},{9,10},{10,... | collective-permute-start | bytes 2359304 | tf_op jit(solution)/shard_map/ppermute | solution.py:40
  93.2 26.8 %collective-permute-start.22 = (bf16[2,8,32,768]{3,2,1,0:T(8,128)(2,1)S(1)}, bf16[2,8,32,768]{3,2,1,0:T(8,128)(2,1)S(1)}, u32[]{:S(2)}, u32[]{:S(2)}) collective-permute-start(bf16[2,8,32,768]{3,2,1,0:T(8,128)(2,1)S(1)} %get-tuple-element.37), channel_id=1, source_target_pairs={{0,4},{4,0},{8,12},{12,8},{1,5},{5,1},{9,13},{13,9},{2,6},{6,2},{1... | collective-permute-start | bytes 2359304 | tf_op jit(solution)/shard_map/ppermute | solution.py:44
  120.2 19.0 %collective-permute-start.27 = (bf16[8,32,768]{2,1,0:T(8,128)(2,1)S(1)}, bf16[8,32,768]{2,1,0:T(8,128)(2,1)S(1)}, u32[]{:S(2)}, u32[]{:S(2)}) collective-permute-start(bf16[8,32,768]{2,1,0:T(8,128)(2,1)S(1)} %get-tuple-element.45), channel_id=1, source_target_pairs={{0,8},{4,12},{8,0},{12,4},{1,9},{5,13},{9,1},{13,5},{2,10},{6,14},... | collective-permute-start | bytes 1179656 | tf_op jit(solution)/shard_map/ppermute | solution.py:44
  128.9 11.5 %collective-permute-start.29 = (bf16[8,32,768]{2,1,0:T(8,128)(2,1)S(1)}, bf16[8,32,768]{2,1,0:T(8,128)(2,1)S(1)}, u32[]{:S(2)}, u32[]{:S(2)}) collective-permute-start(bf16[8,32,768]{2,1,0:T(8,128)(2,1)S(1)} %get-tuple-element.52), channel_id=1, source_target_pairs={{0,8},{4,12},{8,0},{12,4},{1,9},{5,13},{9,1},{13,5},{2,10},{6,14},... | collective-permute-start | bytes 1179656 | tf_op jit(solution)/shard_map/ppermute | solution.py:44
  (10 other events, 105.0 us)

commit v8 on v7

--- a/solution.py
+++ b/solution.py
@@ -22,8 +22,8 @@
 ORDERS = tuple(tuple(DIMS[1 + (p + k) % 4] for k in range(4)) for p in range(CHAINS))
 HOPS = (Z0, Z1, Z0 ^ Z1)
 SLICE = SHARDS * ROWS // 16
-PARTS = (32, 32)
-STARTS = (0, 32)
+PARTS = (48, 16)
+STARTS = (0, 48)
 
 
 def mask_of(c):
@@ -234,31 +234,23 @@
     keep, send, gathered, g, w, hs, sems = refs[-7:]
     row, mine = where[0], where[2]
     per = SHARDS // 4
-    every = (slice(None),) * 6
-    weights, outs = [], []
+    weights = pltpu.make_async_copy(w_far, w, sems.at[0])
+    weights.start()
     for p in range(CHAINS):
-        cols = pl.ds(p * WIDTH, WIDTH)
-        weights.append(pltpu.make_async_copy(w_far.at[:, cols], w.at[:, cols], sems.at[p]))
-        weights[-1].start()
         for side in range(2):
             for src, dst in pieces(p, side):
                 pltpu.make_async_copy(
-                    blocks[2 * p + side].at[src], g.at[dst + (slice(None), cols)], sems.at[CHAINS + p]
+                    blocks[2 * p + side].at[src], g.at[dst + (slice(None), pl.ds(p * WIDTH, WIDTH))], sems.at[1]
                 ).start()
-    for p in range(CHAINS):
-        cols = pl.ds(p * WIDTH, WIDTH)
-        here = g.at[every + (cols,)]
-        weights[p].wait()
-        pltpu.make_async_copy(here, here, sems.at[CHAINS + p]).wait()
-        outs.append(pltpu.make_async_copy(here, gathered.at[every + (cols,)], sems.at[2 * CHAINS + p]))
-        outs[-1].start()
+    pltpu.make_async_copy(g, g, sems.at[1]).wait()
+    weights.wait()
+    outs = [pltpu.make_async_copy(g, gathered, sems.at[2])]
+    outs[0].start()
+    for i in range(2):
         h = lax.dot_general(
-            here[...].reshape(4 * per * n, WIDTH),
-            w[:, p * WIDTH : (p + 1) * WIDTH],
-            (((1,), (1,)), ((), ())),
-            preferred_element_type=jnp.float32,
-        ).reshape(hs.shape)
-        hs[...] = h if p == 0 else hs[...] + h
+            g[i].reshape(2 * per * n, FEATS), w[...], (((1,), (1,)), ((), ())), preferred_element_type=jnp.float32
+        )
+        hs[i] = h.reshape(2, 2, 2, 2, n, HID)
     for a, b in ((1, 1), (0, 1), (1, 0), (0, 0)):
         off_x = (mine // 16) ^ (row // 2) ^ a
         off_y = (mine // 8 % 2) ^ (row % 2) ^ b
@@ -289,7 +281,7 @@
             pltpu.VMEM((2,) * 5 + (n, FEATS), jnp.bfloat16),
             pltpu.VMEM((HID, FEATS), jnp.bfloat16),
             pltpu.VMEM((2,) * 5 + (n, HID), jnp.float32),
-            pltpu.SemaphoreType.DMA((3 * CHAINS,)),
+            pltpu.SemaphoreType.DMA((3,)),
         ],
         compiler_params=params(14 + n // 2),
         cost_estimate=pl.CostEstimate(
@@ -376,14 +368,14 @@
         for p, pair in enumerate(pairs)
     ]
     came_a = [swap(own_a[p], ORDERS[p][3]) for p in range(CHAINS)]
-    own_b = grow_call(pairs, STARTS[1], PARTS[1], after=(in_hbm(own_a[-1]),))
+    act_a, act_b, slope_a, slope_b = gelu_call(where, table, pre_act, near, far, after=(in_hbm(own_a[-1]),))
+    own_b = grow_call(pairs, STARTS[1], PARTS[1], after=(slope_a,))
     came_b = [swap(own_b[p], ORDERS[p][3]) for p in range(CHAINS)]
     own, came = (own_a, own_b), (came_a, came_b)
 
     pairs = [[b for p in range(CHAINS) for b in (own[part][p], came[part][p])] for part in range(2)]
     keep_a, send_a, g_a = hidden_call(0, where, w_down, pairs[0])
-    act_a, act_b, slope_a, slope_b = gelu_call(where, table, pre_act, near, far, after=(keep_a,))
-    keep_b, send_b, g_b = hidden_call(1, where, w_down, pairs[1], after=(slope_a,))
+    keep_b, send_b, g_b = hidden_call(1, where, w_down, pairs[1], after=(keep_a,))
     mine_a, far_a = total_call(keep_a, swap_row(send_a, 1), after=(keep_b,))
     far_a = swap_row(far_a, 2)
     grad_down = down_call((act_a, act_b), (g_a, g_b), 0, 2, after=(mine_a,))

time: 143 us -> 164 us (1.15)
  waiting for transfers between devices: 36.1 us -> 68.6 us
  Pallas kernels: 60.2 us -> 52.9 us
  starting transfers between devices: 42.1 us -> 38.7 us
    ppermute x11, waiting for transfers between devices: 9.6 us -> 38.3 us  [swap(): return lax.ppermute(x, 'depth', [(i, i ^ mask >> 2) for i in range(8)])]
    pallas_call x2, Pallas kernels: 23.1 us -> 16 us  [hidden_call(): pl.pallas_call(functools.partial(hidden_kernel, n), out_shape=[jax.ShapeD...]
    ppermute x11, starting transfers between devices: 14.7 us -> 11.3 us  [swap(): return lax.ppermute(x, 'depth', [(i, i ^ mask >> 2) for i in range(8)])]
    ppermute x13, waiting for transfers between devices: 25.4 us -> 28.3 us  [swap(): return lax.ppermute(x, 'col', [(i, i ^ mask) for i in range(4)])]
  transfers between devices with their start and end apart: 30 -> 30, of which waited for: 12 -> 14; matrix products, arithmetic and copies ran while one was open for 0% -> 0% of each run, Pallas kernels for 42% -> 25%
where the time goes in v8:
time: 164 us; the launch traced here: 163 us
  waiting for transfers between devices  68.6 us (42%)
  Pallas kernels  52.9 us (32%)
  starting transfers between devices  38.7 us (24%)
    ppermute x11, waiting for transfers between devices, swap(): return lax.ppermute(x, 'depth', [(i, i ^ mask >> 2) for i in range(8)])  38.3 us
    ppermute x13, waiting for transfers between devices, swap(): return lax.ppermute(x, 'col', [(i, i ^ mask) for i in range(4)])  28.3 us
    pallas_call x2, Pallas kernels, hidden_call(): pl.pallas_call(functools.partial(hidden_kernel, n), out_shape=[jax.ShapeD...  16 us
    pallas_call x2, Pallas kernels, down_call(): pl.pallas_call(down_kernel, grid=(count,), out_shape=pltpu.HBM((HID, FEAT...  15.6 us
    ppermute x6, starting transfers between devices, swap_row(): return lax.ppermute(x, 'row', [(i, i ^ mask) for i in range(4)])  14.3 us
    ppermute x13, starting transfers between devices, swap(): return lax.ppermute(x, 'col', [(i, i ^ mask) for i in range(4)])  13.1 us
    ppermute x11, starting transfers between devices, swap(): return lax.ppermute(x, 'depth', [(i, i ^ mask >> 2) for i in range(8)])  11.3 us
    pallas_call x1, Pallas kernels, gelu_call(): pl.pallas_call(gelu_kernel, out_shape=[jax.ShapeDtypeStruct((HID, t), jnp...  9.09 us
  transfers between devices with their start and end apart: 30, of which 14 were waited for; matrix products, arithmetic and copies ran while one was open for 0% of the time, Pallas kernels for 25%

profile of v8, /device:TPU:1, one launch (start us, length us, event | category | flops | bytes accessed | tf_op | source)
XLA Modules:
  0.0 163.3 jit_solution(6693661950422771761)
XLA Ops:
  0.6 2.1 %collective-permute-start = (bf16[64,3072]{1,0:T(8,128)(2,1)}, bf16[64,3072]{1,0:T(8,128)(2,1)S(1)}, u32[]{:S(2)}, u32[]{:S(2)}) collective-permute-start(bf16[64,3072]{1,0:T(8,128)(2,1)} %own.1), channel_id=1, source_target_pairs={{0,64},{16,80},{32,96},{48,112},{64,0},{80,16},{96,32},{112,48},{1... | collective-permute-start | bytes 1179656 | tf_op jit(solution)/shard_map/ppermute | solution.py:39
  4.5 1.7 %collective-permute-start.1 = (bf16[128,768]{1,0:T(8,128)(2,1)S(1)}, bf16[128,768]{1,0:T(8,128)(2,1)S(1)}, u32[]{:S(2)}, u32[]{:S(2)}) collective-permute-start(bf16[128,768]{1,0:T(8,128)(2,1)S(1)} %get-tuple-element.28), channel_id=1, source_target_pairs={{0,1},{1,0},{2,3},{3,2},{4,5},{5,4},{6,7},{7,6},{8,9},{9,8},{10,11... | collective-permute-start | bytes 589832 | tf_op jit(solution)/shard_map/ppermute | solution.py:40
  6.2 2.2 %collective-permute-start.2 = (bf16[128,768]{1,0:T(8,128)(2,1)S(1)}, bf16[128,768]{1,0:T(8,128)(2,1)S(1)}, u32[]{:S(2)}, u32[]{:S(2)}) collective-permute-start(bf16[128,768]{1,0:T(8,128)(2,1)S(1)} %get-tuple-element.29), channel_id=1, source_target_pairs={{0,3},{1,2},{2,1},{3,0},{4,7},{5,6},{6,5},{7,4},{8,11},{9,10},{10,... | collective-permute-start | bytes 589832 | tf_op jit(solution)/shard_map/ppermute | solution.py:40
  10.4 5.5 %collective-permute-done.2.refs_1_ = bf16[128,768]{1,0:T(8,128)(2,1)S(1)} collective-permute-done((bf16[128,768]{1,0:T(8,128)(2,1)S(1)}, bf16[128,768]{1,0:T(8,128)(2,1)S(1)}, u32[]{:S(2)}, u32[]{:S(2)}) %collective-permute-start.2) | collective-permute-done | bytes 196640 | tf_op jit(solution)/shard_map/ppermute | solution.py:40
  16.0 1.8 %collective-permute-done.3.refs_2_ = bf16[128,768]{1,0:T(8,128)(2,1)S(1)} collective-permute-done((bf16[128,768]{1,0:T(8,128)(2,1)S(1)}, bf16[128,768]{1,0:T(8,128)(2,1)S(1)}, u32[]{:S(2)}, u32[]{:S(2)}) %collective-permute-start.3) | collective-permute-done | bytes 196640 | tf_op jit(solution)/shard_map/ppermute | solution.py:40
  19.8 1.9 %collective-permute-start.19 = (bf16[3,128,768]{2,1,0:T(8,128)(2,1)S(1)}, bf16[3,128,768]{2,1,0:T(8,128)(2,1)S(1)}, u32[]{:S(2)}, u32[]{:S(2)}) collective-permute-start(bf16[3,128,768]{2,1,0:T(8,128)(2,1)S(1)} %get-tuple-element.35), channel_id=1, source_target_pairs={{0,4},{4,0},{8,12},{12,8},{1,5},{5,1},{9,13},{13,9},{2,6},{6,2},{1... | collective-permute-start | bytes 1769480 | tf_op jit(solution)/shard_map/ppermute | solution.py:44
  21.8 2.7 %collective-permute-start.16 = (bf16[2,64,768]{2,1,0:T(8,128)(2,1)S(1)}, bf16[2,64,768]{2,1,0:T(8,128)(2,1)S(1)}, u32[]{:S(2)}, u32[]{:S(2)}) collective-permute-start(bf16[2,64,768]{2,1,0:T(8,128)(2,1)S(1)} %get-tuple-element.34.refs_0_), channel_id=1, source_target_pairs={{0,48},{16,32},{32,16},{48,0},{64,112},{80,96},{96,80},{112,64},{1... | collective-permute-start | bytes 589832 | tf_op jit(solution)/shard_map/ppermute | solution.py:39
  26.1 3.4 %collective-permute-done.16.refs_1_ = bf16[2,64,768]{2,1,0:T(8,128)(2,1)S(1)} collective-permute-done((bf16[2,64,768]{2,1,0:T(8,128)(2,1)S(1)}, bf16[2,64,768]{2,1,0:T(8,128)(2,1)S(1)}, u32[]{:S(2)}, u32[]{:S(2)}) %collective-permute-start.16) | collective-permute-done | bytes 196640 | tf_op jit(solution)/shard_map/ppermute | solution.py:39
  33.9 1.8 %collective-permute-start.9 = (bf16[4,64,768]{2,1,0:T(8,128)(2,1)S(1)}, bf16[4,64,768]{2,1,0:T(8,128)(2,1)S(1)}, u32[]{:S(2)}, u32[]{:S(2)}) collective-permute-start(bf16[4,64,768]{2,1,0:T(8,128)(2,1)S(1)} %grow.16.refs_0_), channel_id=1, source_target_pairs={{0,3},{1,2},{2,1},{3,0},{4,7},{5,6},{6,5},{7,4},{8,11},{9,10},{10,... | collective-permute-start | bytes 1179656 | tf_op jit(solution)/shard_map/ppermute | solution.py:40
  36.4 2.5 %collective-permute-start.20 = (bf16[2,3,128,768]{3,2,1,0:T(8,128)(2,1)S(1)}, bf16[2,3,128,768]{3,2,1,0:T(8,128)(2,1)S(1)}, u32[]{:S(2)}, u32[]{:S(2)}) collective-permute-start(bf16[2,3,128,768]{3,2,1,0:T(8,128)(2,1)S(1)} %pad_maximum_fusion.near), channel_id=1, source_target_pairs={{0,8},{4,12},{8,0},{12,4},{1,9},{5,13},{9,1},{13,5},{2,10},{6,14},... | collective-permute-start | bytes 3538952 | tf_op jit(solution)/shard_map/ppermute | solution.py:44
  39.0 6.2 %collective-permute-done.5.refs_1_ = bf16[4,64,768]{2,1,0:T(8,128)(2,1)S(1)} collective-permute-done((bf16[4,64,768]{2,1,0:T(8,128)(2,1)S(1)}, bf16[4,64,768]{2,1,0:T(8,128)(2,1)S(1)}, u32[]{:S(2)}, u32[]{:S(2)}) %collective-permute-start.5) | collective-permute-done | bytes 393248 | tf_op jit(solution)/shard_map/ppermute | solution.py:39
  49.8 13.5 %collective-permute-done.6.refs_1_ = bf16[8,64,768]{2,1,0:T(8,128)(2,1)S(1)} collective-permute-done((bf16[8,64,768]{2,1,0:T(8,128)(2,1)S(1)}, bf16[8,64,768]{2,1,0:T(8,128)(2,1)S(1)}, u32[]{:S(2)}, u32[]{:S(2)}) %collective-permute-start.6) | collective-permute-done | bytes 786464 | tf_op jit(solution)/shard_map/ppermute | solution.py:40
  70.7 19.1 %collective-permute-done.7 = bf16[16,48,768]{2,1,0:T(8,128)(2,1)S(1)} collective-permute-done((bf16[16,48,768]{2,1,0:T(8,128)(2,1)}, bf16[16,48,768]{2,1,0:T(8,128)(2,1)S(1)}, u32[]{:S(2)}, u32[]{:S(2)}) %collective-permute-start.7) | collective-permute-done | bytes 1179680 | tf_op jit(solution)/shard_map/ppermute | solution.py:39
  92.1 2.5 %collective-permute-done.21 = bf16[16,48,768]{2,1,0:T(8,128)(2,1)S(1)} collective-permute-done((bf16[16,48,768]{2,1,0:T(8,128)(2,1)}, bf16[16,48,768]{2,1,0:T(8,128)(2,1)S(1)}, u32[]{:S(2)}, u32[]{:S(2)}) %collective-permute-start.21) | collective-permute-done | bytes 1179680 | tf_op jit(solution)/shard_map/ppermute | solution.py:40
  94.6 11.0 %hidden.2 = (f32[2,8,48,768]{3,2,1,0:T(8,128)S(1)}, bf16[2,8,48,768]{3,2,1,0:T(8,128)(2,1)S(1)}, bf16[2,2,2,2,2,48,3072]{6,5,4,3,2,1,0:T(8,128)(2,1)}) custom-call(s32[3]{0:T(128)S(1)} %pad_add_fusion.where, bf16[768,3072]{1,0:T(8,128)(2,1)S(1)} %bitcast.25, bf16[2,2,2,2,48,768]{5,4,3,2,1,0:T(8,128)(2,1)} %bitcast.40, ...), custom_call_target="tpu_custom_call" | custom-call | flops 7247757312 | bytes 18874368 | tf_op jit(solution)/shard_map/hidden/pallas_call | solution.py:271
  105.7 4.9 %collective-permute-start.22 = (bf16[2,8,48,768]{3,2,1,0:T(8,128)(2,1)S(1)}, bf16[2,8,48,768]{3,2,1,0:T(8,128)(2,1)S(1)}, u32[]{:S(2)}, u32[]{:S(2)}) collective-permute-start(bf16[2,8,48,768]{3,2,1,0:T(8,128)(2,1)S(1)} %get-tuple-element.37), channel_id=1, source_target_pairs={{0,4},{4,0},{8,12},{12,8},{1,5},{5,1},{9,13},{13,9},{2,6},{6,2},{1... | collective-permute-start | bytes 3538952 | tf_op jit(solution)/shard_map/ppermute | solution.py:44
  110.6 9.1 %gelu.1 = (bf16[768,1536]{1,0:T(8,128)(2,1)S(1)}, bf16[768,512]{1,0:T(8,128)(2,1)S(1)}, f32[8,48,768]{2,1,0:T(8,128)S(1)}, f32[8,16,768]{2,1,0:T(8,128)S(1)}) custom-call(s32[3]{0:T(128)S(1)} %pad_add_fusion.where, s32[32]{0:T(128)S(1)} %copy-done, bf16[512,3072]{1,0:T(8,128)(2,1)} %pre.3, bf16[2,3,128,768]{3,2,1,0:T(8,128)(2,1)S(1)} %pad_maximum_fusion.near, ...), custom_call_target="tpu_custom_call" | custom-call | flops 1 | bytes 1 | tf_op jit(solution)/shard_map/gelu/pallas_call | solution.py:207
  124.7 8.4 %collective-permute-done.23 = bf16[16,16,768]{2,1,0:T(8,128)(2,1)S(1)} collective-permute-done((bf16[16,16,768]{2,1,0:T(8,128)(2,1)}, bf16[16,16,768]{2,1,0:T(8,128)(2,1)S(1)}, u32[]{:S(2)}, u32[]{:S(2)}) %collective-permute-start.23) | collective-permute-done | bytes 393248 | tf_op jit(solution)/shard_map/ppermute | solution.py:39
  134.3 5.0 %hidden.3 = (f32[2,8,16,768]{3,2,1,0:T(8,128)S(1)}, bf16[2,8,16,768]{3,2,1,0:T(8,128)(2,1)S(1)}, bf16[2,2,2,2,2,16,3072]{6,5,4,3,2,1,0:T(8,128)(2,1)}) custom-call(s32[3]{0:T(128)S(1)} %pad_add_fusion.where, bf16[768,3072]{1,0:T(8,128)(2,1)S(1)} %bitcast.25, bf16[2,2,2,2,16,768]{5,4,3,2,1,0:T(8,128)(2,1)} %bitcast.45, ...), custom_call_target="tpu_custom_call" | custom-call | flops 2415919104 | bytes 6291456 | tf_op jit(solution)/shard_map/hidden/pallas_call | solution.py:271
  139.3 1.8 %collective-permute-start.28 = (bf16[2,8,16,768]{3,2,1,0:T(8,128)(2,1)S(1)}, bf16[2,8,16,768]{3,2,1,0:T(8,128)(2,1)S(1)}, u32[]{:S(2)}, u32[]{:S(2)}) collective-permute-start(bf16[2,8,16,768]{3,2,1,0:T(8,128)(2,1)S(1)} %get-tuple-element.46), channel_id=1, source_target_pairs={{0,4},{4,0},{8,12},{12,8},{1,5},{5,1},{9,13},{13,9},{2,6},{6,2},{1... | collective-permute-start | bytes 1179656 | tf_op jit(solution)/shard_map/ppermute | solution.py:44
  141.3 2.5 %collective-permute-start.27 = (bf16[8,48,768]{2,1,0:T(8,128)(2,1)S(1)}, bf16[8,48,768]{2,1,0:T(8,128)(2,1)S(1)}, u32[]{:S(2)}, u32[]{:S(2)}) collective-permute-start(bf16[8,48,768]{2,1,0:T(8,128)(2,1)S(1)} %get-tuple-element.45), channel_id=1, source_target_pairs={{0,8},{4,12},{8,0},{12,4},{1,9},{5,13},{9,1},{13,5},{2,10},{6,14},... | collective-permute-start | bytes 1769480 | tf_op jit(solution)/shard_map/ppermute | solution.py:44
  143.9 6.0 %down.2.refs_0_ = bf16[768,3072]{1,0:T(8,128)(2,1)} custom-call(bf16[768,1536]{1,0:T(8,128)(2,1)S(1)} %get-tuple-element.47.at_a, bf16[768,512]{1,0:T(8,128)(2,1)S(1)} %get-tuple-element.48.at_b, bf16[1536,3072]{1,0:T(8,128)(2,1)} %bitcast.35, bf16[512,3072]{1,0:T(8,128)(2,1)} %bitcast.37, f32[8,48,768]{2,1,0:T(8,128)S(1)} %get-tuple-element.44.refs_0_), custom_call_target="tpu_custom_call" | custom-call | flops 3221225472 | bytes 5767168 | tf_op jit(solution)/shard_map/down/pallas_call | solution.py:335
  150.5 9.6 %down.3 = bf16[768,3072]{1,0:T(8,128)(2,1)} custom-call(bf16[768,1536]{1,0:T(8,128)(2,1)S(1)} %get-tuple-element.47.at_a, bf16[768,512]{1,0:T(8,128)(2,1)S(1)} %get-tuple-element.48.at_b, bf16[1536,3072]{1,0:T(8,128)(2,1)} %bitcast.36, bf16[512,3072]{1,0:T(8,128)(2,1)} %bitcast.38, bf16[768,3072]{1,0:T(8,128)(2,1)} %down.2.refs_0_), custom_call_target="tpu_custom_call", output_to_operand_aliasing={{}: (4, {})} | custom-call | flops 6442450944 | bytes 11534336 | tf_op jit(solution)/shard_map/down/pallas_call | solution.py:335
  160.1 1.9 %collective-permute-done.29 = bf16[8,16,768]{2,1,0:T(8,128)(2,1)S(1)} collective-permute-done((bf16[8,16,768]{2,1,0:T(8,128)(2,1)S(1)}, bf16[8,16,768]{2,1,0:T(8,128)(2,1)S(1)}, u32[]{:S(2)}, u32[]{:S(2)}) %collective-permute-start.29) | collective-permute-done | bytes 196640 | tf_op jit(solution)/shard_map/ppermute | solution.py:44
  (72 shorter events, 35.0 us)
Async XLA Ops:
  0.6 17.1 %collective-permute-start = (bf16[64,3072]{1,0:T(8,128)(2,1)}, bf16[64,3072]{1,0:T(8,128)(2,1)S(1)}, u32[]{:S(2)}, u32[]{:S(2)}) collective-permute-start(bf16[64,3072]{1,0:T(8,128)(2,1)} %own.1), channel_id=1, source_target_pairs={{0,64},{16,80},{32,96},{48,112},{64,0},{80,16},{96,32},{112,48},{1... | collective-permute-start | bytes 1179656 | tf_op jit(solution)/shard_map/ppermute | solution.py:39
  6.2 9.7 %collective-permute-start.2 = (bf16[128,768]{1,0:T(8,128)(2,1)S(1)}, bf16[128,768]{1,0:T(8,128)(2,1)S(1)}, u32[]{:S(2)}, u32[]{:S(2)}) collective-permute-start(bf16[128,768]{1,0:T(8,128)(2,1)S(1)} %get-tuple-element.29), channel_id=1, source_target_pairs={{0,3},{1,2},{2,1},{3,0},{4,7},{5,6},{6,5},{7,4},{8,11},{9,10},{10,... | collective-permute-start | bytes 589832 | tf_op jit(solution)/shard_map/ppermute | solution.py:40
  19.8 16.5 %collective-permute-start.19 = (bf16[3,128,768]{2,1,0:T(8,128)(2,1)S(1)}, bf16[3,128,768]{2,1,0:T(8,128)(2,1)S(1)}, u32[]{:S(2)}, u32[]{:S(2)}) collective-permute-start(bf16[3,128,768]{2,1,0:T(8,128)(2,1)S(1)} %get-tuple-element.35), channel_id=1, source_target_pairs={{0,4},{4,0},{8,12},{12,8},{1,5},{5,1},{9,13},{13,9},{2,6},{6,2},{1... | collective-permute-start | bytes 1769480 | tf_op jit(solution)/shard_map/ppermute | solution.py:44
  26.1 9.6 %collective-permute-start.4 = (bf16[2,64,768]{2,1,0:T(8,128)(2,1)S(1)}, bf16[2,64,768]{2,1,0:T(8,128)(2,1)S(1)}, u32[]{:S(2)}, u32[]{:S(2)}) collective-permute-start(bf16[2,64,768]{2,1,0:T(8,128)(2,1)S(1)} %get-tuple-element.31.refs_0_), channel_id=1, source_target_pairs={{0,1},{1,0},{2,3},{3,2},{4,5},{5,4},{6,7},{7,6},{8,9},{9,8},{10,11... | collective-permute-start | bytes 589832 | tf_op jit(solution)/shard_map/ppermute | solution.py:40
  30.0 19.3 %collective-permute-start.17 = (bf16[4,64,768]{2,1,0:T(8,128)(2,1)S(1)}, bf16[4,64,768]{2,1,0:T(8,128)(2,1)S(1)}, u32[]{:S(2)}, u32[]{:S(2)}) collective-permute-start(bf16[4,64,768]{2,1,0:T(8,128)(2,1)S(1)} %grow.22.refs_0_), channel_id=1, source_target_pairs={{0,1},{1,0},{2,3},{3,2},{4,5},{5,4},{6,7},{7,6},{8,9},{9,8},{10,11... | collective-permute-start | bytes 1179656 | tf_op jit(solution)/shard_map/ppermute | solution.py:40
  32.3 16.4 %collective-permute-start.13 = (bf16[4,64,768]{2,1,0:T(8,128)(2,1)S(1)}, bf16[4,64,768]{2,1,0:T(8,128)(2,1)S(1)}, u32[]{:S(2)}, u32[]{:S(2)}) collective-permute-start(bf16[4,64,768]{2,1,0:T(8,128)(2,1)S(1)} %grow.19.refs_0_), channel_id=1, source_target_pairs={{0,48},{16,32},{32,16},{48,0},{64,112},{80,96},{96,80},{112,64},{1... | collective-permute-start | bytes 1179656 | tf_op jit(solution)/shard_map/ppermute | solution.py:39
  33.9 13.0 %collective-permute-start.9 = (bf16[4,64,768]{2,1,0:T(8,128)(2,1)S(1)}, bf16[4,64,768]{2,1,0:T(8,128)(2,1)S(1)}, u32[]{:S(2)}, u32[]{:S(2)}) collective-permute-start(bf16[4,64,768]{2,1,0:T(8,128)(2,1)S(1)} %grow.16.refs_0_), channel_id=1, source_target_pairs={{0,3},{1,2},{2,1},{3,0},{4,7},{5,6},{6,5},{7,4},{8,11},{9,10},{10,... | collective-permute-start | bytes 1179656 | tf_op jit(solution)/shard_map/ppermute | solution.py:40
  36.4 31.9 %collective-permute-start.20 = (bf16[2,3,128,768]{3,2,1,0:T(8,128)(2,1)S(1)}, bf16[2,3,128,768]{3,2,1,0:T(8,128)(2,1)S(1)}, u32[]{:S(2)}, u32[]{:S(2)}) collective-permute-start(bf16[2,3,128,768]{3,2,1,0:T(8,128)(2,1)S(1)} %pad_maximum_fusion.near), channel_id=1, source_target_pairs={{0,8},{4,12},{8,0},{12,4},{1,9},{5,13},{9,1},{13,5},{2,10},{6,14},... | collective-permute-start | bytes 3538952 | tf_op jit(solution)/shard_map/ppermute | solution.py:44
  45.6 17.7 %collective-permute-start.6 = (bf16[8,64,768]{2,1,0:T(8,128)(2,1)S(1)}, bf16[8,64,768]{2,1,0:T(8,128)(2,1)S(1)}, u32[]{:S(2)}, u32[]{:S(2)}) collective-permute-start(bf16[8,64,768]{2,1,0:T(8,128)(2,1)S(1)} %grow.14.refs_0_), channel_id=1, source_target_pairs={{0,3},{1,2},{2,1},{3,0},{4,7},{5,6},{6,5},{7,4},{8,11},{9,10},{10,... | collective-permute-start | bytes 2359304 | tf_op jit(solution)/shard_map/ppermute | solution.py:40
  47.3 18.6 %collective-permute-start.10 = (bf16[8,64,768]{2,1,0:T(8,128)(2,1)S(1)}, bf16[8,64,768]{2,1,0:T(8,128)(2,1)S(1)}, u32[]{:S(2)}, u32[]{:S(2)}) collective-permute-start(bf16[8,64,768]{2,1,0:T(8,128)(2,1)S(1)} %grow.17.refs_0_.refs_2_), channel_id=1, source_target_pairs={{0,48},{16,32},{32,16},{48,0},{64,112},{80,96},{96,80},{112,64},{1... | collective-permute-start | bytes 2359304 | tf_op jit(solution)/shard_map/ppermute | solution.py:39
  49.2 17.9 %collective-permute-start.14 = (bf16[8,64,768]{2,1,0:T(8,128)(2,1)S(1)}, bf16[8,64,768]{2,1,0:T(8,128)(2,1)S(1)}, u32[]{:S(2)}, u32[]{:S(2)}) collective-permute-start(bf16[8,64,768]{2,1,0:T(8,128)(2,1)S(1)} %grow.20.refs_0_.refs_4_), channel_id=1, source_target_pairs={{0,1},{1,0},{2,3},{3,2},{4,5},{5,4},{6,7},{7,6},{8,9},{9,8},{10,11... | collective-permute-start | bytes 2359304 | tf_op jit(solution)/shard_map/ppermute | solution.py:40
  49.7 18.6 %collective-permute-start.18 = (bf16[8,64,768]{2,1,0:T(8,128)(2,1)S(1)}, bf16[8,64,768]{2,1,0:T(8,128)(2,1)S(1)}, u32[]{:S(2)}, u32[]{:S(2)}) collective-permute-start(bf16[8,64,768]{2,1,0:T(8,128)(2,1)S(1)} %grow.23.refs_0_.refs_6_), channel_id=1, source_target_pairs={{0,16},{16,0},{32,48},{48,32},{64,80},{80,64},{96,112},{112,96},{1... | collective-permute-start | bytes 2359304 | tf_op jit(solution)/shard_map/ppermute | solution.py:39
  64.3 25.4 %collective-permute-start.7 = (bf16[16,48,768]{2,1,0:T(8,128)(2,1)}, bf16[16,48,768]{2,1,0:T(8,128)(2,1)S(1)}, u32[]{:S(2)}, u32[]{:S(2)}) collective-permute-start(bf16[16,48,768]{2,1,0:T(8,128)(2,1)} %grow.15), channel_id=1, source_target_pairs={{0,48},{16,32},{32,16},{48,0},{64,112},{80,96},{96,80},{112,64},{1... | collective-permute-start | bytes 3538952 | tf_op jit(solution)/shard_map/ppermute | solution.py:39
  67.0 23.9 %collective-permute-start.11 = (bf16[16,48,768]{2,1,0:T(8,128)(2,1)}, bf16[16,48,768]{2,1,0:T(8,128)(2,1)S(1)}, u32[]{:S(2)}, u32[]{:S(2)}) collective-permute-start(bf16[16,48,768]{2,1,0:T(8,128)(2,1)} %grow.18), channel_id=1, source_target_pairs={{0,1},{1,0},{2,3},{3,2},{4,5},{5,4},{6,7},{7,6},{8,9},{9,8},{10,11... | collective-permute-start | bytes 3538952 | tf_op jit(solution)/shard_map/ppermute | solution.py:40
  68.2 23.9 %collective-permute-start.15 = (bf16[16,48,768]{2,1,0:T(8,128)(2,1)}, bf16[16,48,768]{2,1,0:T(8,128)(2,1)S(1)}, u32[]{:S(2)}, u32[]{:S(2)}) collective-permute-start(bf16[16,48,768]{2,1,0:T(8,128)(2,1)} %grow.21), channel_id=1, source_target_pairs={{0,16},{16,0},{32,48},{48,32},{64,80},{80,64},{96,112},{112,96},{1... | collective-permute-start | bytes 3538952 | tf_op jit(solution)/shard_map/ppermute | solution.py:39
  69.4 25.3 %collective-permute-start.21 = (bf16[16,48,768]{2,1,0:T(8,128)(2,1)}, bf16[16,48,768]{2,1,0:T(8,128)(2,1)S(1)}, u32[]{:S(2)}, u32[]{:S(2)}) collective-permute-start(bf16[16,48,768]{2,1,0:T(8,128)(2,1)} %grow.24.refs_0_), channel_id=1, source_target_pairs={{0,3},{1,2},{2,1},{3,0},{4,7},{5,6},{6,5},{7,4},{8,11},{9,10},{10,... | collective-permute-start | bytes 3538952 | tf_op jit(solution)/shard_map/ppermute | solution.py:40
  105.7 35.5 %collective-permute-start.22 = (bf16[2,8,48,768]{3,2,1,0:T(8,128)(2,1)S(1)}, bf16[2,8,48,768]{3,2,1,0:T(8,128)(2,1)S(1)}, u32[]{:S(2)}, u32[]{:S(2)}) collective-permute-start(bf16[2,8,48,768]{3,2,1,0:T(8,128)(2,1)S(1)} %get-tuple-element.37), channel_id=1, source_target_pairs={{0,4},{4,0},{8,12},{12,8},{1,5},{5,1},{9,13},{13,9},{2,6},{6,2},{1... | collective-permute-start | bytes 3538952 | tf_op jit(solution)/shard_map/ppermute | solution.py:44
  120.9 12.2 %collective-permute-start.23 = (bf16[16,16,768]{2,1,0:T(8,128)(2,1)}, bf16[16,16,768]{2,1,0:T(8,128)(2,1)S(1)}, u32[]{:S(2)}, u32[]{:S(2)}) collective-permute-start(bf16[16,16,768]{2,1,0:T(8,128)(2,1)} %get-tuple-element.39), channel_id=1, source_target_pairs={{0,48},{16,32},{32,16},{48,0},{64,112},{80,96},{96,80},{112,64},{1... | collective-permute-start | bytes 1179656 | tf_op jit(solution)/shard_map/ppermute | solution.py:39
  122.1 11.0 %collective-permute-start.24 = (bf16[16,16,768]{2,1,0:T(8,128)(2,1)}, bf16[16,16,768]{2,1,0:T(8,128)(2,1)S(1)}, u32[]{:S(2)}, u32[]{:S(2)}) collective-permute-start(bf16[16,16,768]{2,1,0:T(8,128)(2,1)} %get-tuple-element.40), channel_id=1, source_target_pairs={{0,1},{1,0},{2,3},{3,2},{4,5},{5,4},{6,7},{7,6},{8,9},{9,8},{10,11... | collective-permute-start | bytes 1179656 | tf_op jit(solution)/shard_map/ppermute | solution.py:40
  122.3 10.8 %collective-permute-start.25 = (bf16[16,16,768]{2,1,0:T(8,128)(2,1)}, bf16[16,16,768]{2,1,0:T(8,128)(2,1)S(1)}, u32[]{:S(2)}, u32[]{:S(2)}) collective-permute-start(bf16[16,16,768]{2,1,0:T(8,128)(2,1)} %get-tuple-element.41), channel_id=1, source_target_pairs={{0,16},{16,0},{32,48},{48,32},{64,80},{80,64},{96,112},{112,96},{1... | collective-permute-start | bytes 1179656 | tf_op jit(solution)/shard_map/ppermute | solution.py:39
  123.1 11.2 %collective-permute-start.26 = (bf16[16,16,768]{2,1,0:T(8,128)(2,1)}, bf16[16,16,768]{2,1,0:T(8,128)(2,1)S(1)}, u32[]{:S(2)}, u32[]{:S(2)}) collective-permute-start(bf16[16,16,768]{2,1,0:T(8,128)(2,1)} %get-tuple-element.42), channel_id=1, source_target_pairs={{0,3},{1,2},{2,1},{3,0},{4,7},{5,6},{6,5},{7,4},{8,11},{9,10},{10,... | collective-permute-start | bytes 1179656 | tf_op jit(solution)/shard_map/ppermute | solution.py:40
  139.3 10.6 %collective-permute-start.28 = (bf16[2,8,16,768]{3,2,1,0:T(8,128)(2,1)S(1)}, bf16[2,8,16,768]{3,2,1,0:T(8,128)(2,1)S(1)}, u32[]{:S(2)}, u32[]{:S(2)}) collective-permute-start(bf16[2,8,16,768]{3,2,1,0:T(8,128)(2,1)S(1)} %get-tuple-element.46), channel_id=1, source_target_pairs={{0,4},{4,0},{8,12},{12,8},{1,5},{5,1},{9,13},{13,9},{2,6},{6,2},{1... | collective-permute-start | bytes 1179656 | tf_op jit(solution)/shard_map/ppermute | solution.py:44
  141.3 20.8 %collective-permute-start.27 = (bf16[8,48,768]{2,1,0:T(8,128)(2,1)S(1)}, bf16[8,48,768]{2,1,0:T(8,128)(2,1)S(1)}, u32[]{:S(2)}, u32[]{:S(2)}) collective-permute-start(bf16[8,48,768]{2,1,0:T(8,128)(2,1)S(1)} %get-tuple-element.45), channel_id=1, source_target_pairs={{0,8},{4,12},{8,0},{12,4},{1,9},{5,13},{9,1},{13,5},{2,10},{6,14},... | collective-permute-start | bytes 1769480 | tf_op jit(solution)/shard_map/ppermute | solution.py:44
  149.9 12.1 %collective-permute-start.29 = (bf16[8,16,768]{2,1,0:T(8,128)(2,1)S(1)}, bf16[8,16,768]{2,1,0:T(8,128)(2,1)S(1)}, u32[]{:S(2)}, u32[]{:S(2)}) collective-permute-start(bf16[8,16,768]{2,1,0:T(8,128)(2,1)S(1)} %get-tuple-element.52), channel_id=1, source_target_pairs={{0,8},{4,12},{8,0},{12,4},{1,9},{5,13},{9,1},{13,5},{2,10},{6,14},... | collective-permute-start | bytes 589832 | tf_op jit(solution)/shard_map/ppermute | solution.py:44
  (10 other events, 138.9 us)

commit v9 on v8

--- a/solution.py
+++ b/solution.py
@@ -22,8 +22,8 @@
 ORDERS = tuple(tuple(DIMS[1 + (p + k) % 4] for k in range(4)) for p in range(CHAINS))
 HOPS = (Z0, Z1, Z0 ^ Z1)
 SLICE = SHARDS * ROWS // 16
-PARTS = (48, 16)
-STARTS = (0, 48)
+PARTS = (32, 32)
+STARTS = (0, 32)
 
 
 def mask_of(c):
@@ -374,7 +374,7 @@
     own, came = (own_a, own_b), (came_a, came_b)
 
     pairs = [[b for p in range(CHAINS) for b in (own[part][p], came[part][p])] for part in range(2)]
-    keep_a, send_a, g_a = hidden_call(0, where, w_down, pairs[0])
+    keep_a, send_a, g_a = hidden_call(0, where, w_down, pairs[0], after=(in_hbm(own_b[0]),))
     keep_b, send_b, g_b = hidden_call(1, where, w_down, pairs[1], after=(keep_a,))
     mine_a, far_a = total_call(keep_a, swap_row(send_a, 1), after=(keep_b,))
     far_a = swap_row(far_a, 2)

time: 164 us -> 133 us (0.81)
  waiting for transfers between devices: 68.6 us -> 28.2 us
  starting transfers between devices: 38.7 us -> 48.1 us
    ppermute x11, waiting for transfers between devices: 38.3 us -> 1.35 us  [swap(): return lax.ppermute(x, 'depth', [(i, i ^ mask >> 2) for i in range(8)])]
    ppermute x11, starting transfers between devices: 11.3 us -> 16.2 us  [swap(): return lax.ppermute(x, 'depth', [(i, i ^ mask >> 2) for i in range(8)])]
    ppermute x6, starting transfers between devices: 14.3 us -> 17.8 us  [swap_row(): return lax.ppermute(x, 'row', [(i, i ^ mask) for i in range(4)])]
    ppermute x13, waiting for transfers between devices: 28.3 us -> 25.4 us  [swap(): return lax.ppermute(x, 'col', [(i, i ^ mask) for i in range(4)])]
  transfers between devices with their start and end apart: 30 -> 30, of which waited for: 14 -> 12; matrix products, arithmetic and copies ran while one was open for 0% -> 0% of each run, Pallas kernels for 25% -> 39%
where the time goes in v9:
time: 133 us
  Pallas kernels  53.2 us (40%)
  starting transfers between devices  48.1 us (36%)
  waiting for transfers between devices  28.2 us (21%)
  other arithmetic  1.4 us (1%)
    ppermute x13, waiting for transfers between devices, swap(): return lax.ppermute(x, 'col', [(i, i ^ mask) for i in range(4)])  25.4 us
    ppermute x6, starting transfers between devices, swap_row(): return lax.ppermute(x, 'row', [(i, i ^ mask) for i in range(4)])  17.8 us
    ppermute x11, starting transfers between devices, swap(): return lax.ppermute(x, 'depth', [(i, i ^ mask >> 2) for i in range(8)])  16.2 us
    pallas_call x2, Pallas kernels, hidden_call(): pl.pallas_call(functools.partial(hidden_kernel, n), out_shape=[jax.ShapeD...  16 us
    pallas_call x2, Pallas kernels, down_call(): pl.pallas_call(down_kernel, grid=(count,), out_shape=pltpu.HBM((HID, FEAT...  15.7 us
    ppermute x13, starting transfers between devices, swap(): return lax.ppermute(x, 'col', [(i, i ^ mask) for i in range(4)])  14.1 us
    pallas_call x1, Pallas kernels, gelu_call(): pl.pallas_call(gelu_kernel, out_shape=[jax.ShapeDtypeStruct((HID, t), jnp...  9.19 us
    pallas_call x13, Pallas kernels, grow_call(): pl.pallas_call(functools.partial(grow_kernel, len(pairs), at, n, len(join...  9.04 us
  transfers between devices with their start and end apart: 30, of which 12 were waited for; matrix products, arithmetic and copies ran while one was open for 0% of the time, Pallas kernels for 39%

profile of v9, /device:TPU:1, one launch (start us, length us, event | category | flops | bytes accessed | tf_op | source)
XLA Modules:
  0.0 132.6 jit_solution(15213830427689473217)
XLA Ops:
  0.6 2.1 %collective-permute-start = (bf16[64,3072]{1,0:T(8,128)(2,1)}, bf16[64,3072]{1,0:T(8,128)(2,1)S(1)}, u32[]{:S(2)}, u32[]{:S(2)}) collective-permute-start(bf16[64,3072]{1,0:T(8,128)(2,1)} %own.1), channel_id=1, source_target_pairs={{0,64},{16,80},{32,96},{48,112},{64,0},{80,16},{96,32},{112,48},{1... | collective-permute-start | bytes 1179656 | tf_op jit(solution)/shard_map/ppermute | solution.py:39
  4.5 1.7 %collective-permute-start.1 = (bf16[128,768]{1,0:T(8,128)(2,1)S(1)}, bf16[128,768]{1,0:T(8,128)(2,1)S(1)}, u32[]{:S(2)}, u32[]{:S(2)}) collective-permute-start(bf16[128,768]{1,0:T(8,128)(2,1)S(1)} %get-tuple-element.28), channel_id=1, source_target_pairs={{0,1},{1,0},{2,3},{3,2},{4,5},{5,4},{6,7},{7,6},{8,9},{9,8},{10,11... | collective-permute-start | bytes 589832 | tf_op jit(solution)/shard_map/ppermute | solution.py:40
  6.2 2.2 %collective-permute-start.2 = (bf16[128,768]{1,0:T(8,128)(2,1)S(1)}, bf16[128,768]{1,0:T(8,128)(2,1)S(1)}, u32[]{:S(2)}, u32[]{:S(2)}) collective-permute-start(bf16[128,768]{1,0:T(8,128)(2,1)S(1)} %get-tuple-element.29), channel_id=1, source_target_pairs={{0,3},{1,2},{2,1},{3,0},{4,7},{5,6},{6,5},{7,4},{8,11},{9,10},{10,... | collective-permute-start | bytes 589832 | tf_op jit(solution)/shard_map/ppermute | solution.py:40
  10.4 5.5 %collective-permute-done.2.refs_1_ = bf16[128,768]{1,0:T(8,128)(2,1)S(1)} collective-permute-done((bf16[128,768]{1,0:T(8,128)(2,1)S(1)}, bf16[128,768]{1,0:T(8,128)(2,1)S(1)}, u32[]{:S(2)}, u32[]{:S(2)}) %collective-permute-start.2) | collective-permute-done | bytes 196640 | tf_op jit(solution)/shard_map/ppermute | solution.py:40
  16.0 1.8 %collective-permute-done.3.refs_2_ = bf16[128,768]{1,0:T(8,128)(2,1)S(1)} collective-permute-done((bf16[128,768]{1,0:T(8,128)(2,1)S(1)}, bf16[128,768]{1,0:T(8,128)(2,1)S(1)}, u32[]{:S(2)}, u32[]{:S(2)}) %collective-permute-start.3) | collective-permute-done | bytes 196640 | tf_op jit(solution)/shard_map/ppermute | solution.py:40
  19.8 1.9 %collective-permute-start.19 = (bf16[3,128,768]{2,1,0:T(8,128)(2,1)S(1)}, bf16[3,128,768]{2,1,0:T(8,128)(2,1)S(1)}, u32[]{:S(2)}, u32[]{:S(2)}) collective-permute-start(bf16[3,128,768]{2,1,0:T(8,128)(2,1)S(1)} %get-tuple-element.35), channel_id=1, source_target_pairs={{0,4},{4,0},{8,12},{12,8},{1,5},{5,1},{9,13},{13,9},{2,6},{6,2},{1... | collective-permute-start | bytes 1769480 | tf_op jit(solution)/shard_map/ppermute | solution.py:44
  23.1 1.8 %collective-permute-start.12 = (bf16[2,64,768]{2,1,0:T(8,128)(2,1)S(1)}, bf16[2,64,768]{2,1,0:T(8,128)(2,1)S(1)}, u32[]{:S(2)}, u32[]{:S(2)}) collective-permute-start(bf16[2,64,768]{2,1,0:T(8,128)(2,1)S(1)} %get-tuple-element.33.refs_0_), channel_id=1, source_target_pairs={{0,3},{1,2},{2,1},{3,0},{4,7},{5,6},{6,5},{7,4},{8,11},{9,10},{10,... | collective-permute-start | bytes 589832 | tf_op jit(solution)/shard_map/ppermute | solution.py:40
  24.8 1.9 %collective-permute-start.16 = (bf16[2,64,768]{2,1,0:T(8,128)(2,1)S(1)}, bf16[2,64,768]{2,1,0:T(8,128)(2,1)S(1)}, u32[]{:S(2)}, u32[]{:S(2)}) collective-permute-start(bf16[2,64,768]{2,1,0:T(8,128)(2,1)S(1)} %get-tuple-element.34.refs_0_), channel_id=1, source_target_pairs={{0,48},{16,32},{32,16},{48,0},{64,112},{80,96},{96,80},{112,64},{1... | collective-permute-start | bytes 589832 | tf_op jit(solution)/shard_map/ppermute | solution.py:39
  30.6 1.7 %collective-permute-start.9 = (bf16[4,64,768]{2,1,0:T(8,128)(2,1)S(1)}, bf16[4,64,768]{2,1,0:T(8,128)(2,1)S(1)}, u32[]{:S(2)}, u32[]{:S(2)}) collective-permute-start(bf16[4,64,768]{2,1,0:T(8,128)(2,1)S(1)} %grow.16.refs_0_), channel_id=1, source_target_pairs={{0,3},{1,2},{2,1},{3,0},{4,7},{5,6},{6,5},{7,4},{8,11},{9,10},{10,... | collective-permute-start | bytes 1179656 | tf_op jit(solution)/shard_map/ppermute | solution.py:40
  32.8 2.0 %collective-permute-start.13 = (bf16[4,64,768]{2,1,0:T(8,128)(2,1)S(1)}, bf16[4,64,768]{2,1,0:T(8,128)(2,1)S(1)}, u32[]{:S(2)}, u32[]{:S(2)}) collective-permute-start(bf16[4,64,768]{2,1,0:T(8,128)(2,1)S(1)} %grow.19.refs_0_), channel_id=1, source_target_pairs={{0,48},{16,32},{32,16},{48,0},{64,112},{80,96},{96,80},{112,64},{1... | collective-permute-start | bytes 1179656 | tf_op jit(solution)/shard_map/ppermute | solution.py:39
  35.6 2.5 %collective-permute-start.20 = (bf16[2,3,128,768]{3,2,1,0:T(8,128)(2,1)S(1)}, bf16[2,3,128,768]{3,2,1,0:T(8,128)(2,1)S(1)}, u32[]{:S(2)}, u32[]{:S(2)}) collective-permute-start(bf16[2,3,128,768]{3,2,1,0:T(8,128)(2,1)S(1)} %pad_maximum_fusion.near), channel_id=1, source_target_pairs={{0,8},{4,12},{8,0},{12,4},{1,9},{5,13},{9,1},{13,5},{2,10},{6,14},... | collective-permute-start | bytes 3538952 | tf_op jit(solution)/shard_map/ppermute | solution.py:44
  39.0 1.7 %collective-permute-start.6 = (bf16[8,64,768]{2,1,0:T(8,128)(2,1)S(1)}, bf16[8,64,768]{2,1,0:T(8,128)(2,1)S(1)}, u32[]{:S(2)}, u32[]{:S(2)}) collective-permute-start(bf16[8,64,768]{2,1,0:T(8,128)(2,1)S(1)} %grow.14.refs_0_), channel_id=1, source_target_pairs={{0,3},{1,2},{2,1},{3,0},{4,7},{5,6},{6,5},{7,4},{8,11},{9,10},{10,... | collective-permute-start | bytes 2359304 | tf_op jit(solution)/shard_map/ppermute | solution.py:40
  41.8 2.1 %collective-permute-start.10 = (bf16[8,64,768]{2,1,0:T(8,128)(2,1)S(1)}, bf16[8,64,768]{2,1,0:T(8,128)(2,1)S(1)}, u32[]{:S(2)}, u32[]{:S(2)}) collective-permute-start(bf16[8,64,768]{2,1,0:T(8,128)(2,1)S(1)} %grow.17.refs_0_.refs_2_), channel_id=1, source_target_pairs={{0,48},{16,32},{32,16},{48,0},{64,112},{80,96},{96,80},{112,64},{1... | collective-permute-start | bytes 2359304 | tf_op jit(solution)/shard_map/ppermute | solution.py:39
  45.2 12.5 %collective-permute-done.6.refs_1_ = bf16[8,64,768]{2,1,0:T(8,128)(2,1)S(1)} collective-permute-done((bf16[8,64,768]{2,1,0:T(8,128)(2,1)S(1)}, bf16[8,64,768]{2,1,0:T(8,128)(2,1)S(1)}, u32[]{:S(2)}, u32[]{:S(2)}) %collective-permute-start.6) | collective-permute-done | bytes 786464 | tf_op jit(solution)/shard_map/ppermute | solution.py:40
  58.6 2.6 %collective-permute-start.7 = (bf16[16,32,768]{2,1,0:T(8,128)(2,1)}, bf16[16,32,768]{2,1,0:T(8,128)(2,1)S(1)}, u32[]{:S(2)}, u32[]{:S(2)}) collective-permute-start(bf16[16,32,768]{2,1,0:T(8,128)(2,1)} %grow.15), channel_id=1, source_target_pairs={{0,48},{16,32},{32,16},{48,0},{64,112},{80,96},{96,80},{112,64},{1... | collective-permute-start | bytes 2359304 | tf_op jit(solution)/shard_map/ppermute | solution.py:39
  66.0 9.2 %gelu.1 = (bf16[768,1024]{1,0:T(8,128)(2,1)S(1)}, bf16[768,1024]{1,0:T(8,128)(2,1)S(1)}, f32[8,32,768]{2,1,0:T(8,128)S(1)}, f32[8,32,768]{2,1,0:T(8,128)S(1)}) custom-call(s32[3]{0:T(128)S(1)} %pad_add_fusion.where, s32[32]{0:T(128)S(1)} %copy-done, bf16[512,3072]{1,0:T(8,128)(2,1)} %pre.3, bf16[2,3,128,768]{3,2,1,0:T(8,128)(2,1)S(1)} %pad_maximum_fusion.near, ...), custom_call_target="tpu_custom_call" | custom-call | flops 1 | bytes 1 | tf_op jit(solution)/shard_map/gelu/pallas_call | solution.py:207
  75.2 1.7 %grow.25 = (bf16[16,32,768]{2,1,0:T(8,128)(2,1)}, bf16[16,32,768]{2,1,0:T(8,128)(2,1)}, bf16[16,32,768]{2,1,0:T(8,128)(2,1)}, bf16[16,32,768]{2,1,0:T(8,128)(2,1)}) custom-call(bf16[8,64,768]{2,1,0:T(8,128)(2,1)S(1)} %grow.14.refs_0_, bf16[8,64,768]{2,1,0:T(8,128)(2,1)S(1)} %collective-permute-done.6.refs_1_, bf16[8,64,768]{2,1,0:T(8,128)(2,1)S(1)} %grow.17.refs_0_.refs_2_, ...), custom_call_target="tpu_custom_call" | custom-call | flops 1 | bytes 1 | tf_op jit(solution)/shard_map/grow/pallas_call | solution.py:137
  81.8 8.0 %hidden.2 = (f32[2,8,32,768]{3,2,1,0:T(8,128)S(1)}, bf16[2,8,32,768]{3,2,1,0:T(8,128)(2,1)S(1)}, bf16[2,2,2,2,2,32,3072]{6,5,4,3,2,1,0:T(8,128)(2,1)}) custom-call(s32[3]{0:T(128)S(1)} %pad_add_fusion.where, bf16[768,3072]{1,0:T(8,128)(2,1)S(1)} %bitcast.26, bf16[2,2,2,2,32,768]{5,4,3,2,1,0:T(8,128)(2,1)} %bitcast.41, ...), custom_call_target="tpu_custom_call" | custom-call | flops 4831838208 | bytes 12582912 | tf_op jit(solution)/shard_map/hidden/pallas_call | solution.py:271
  89.8 6.0 %collective-permute-start.22 = (bf16[2,8,32,768]{3,2,1,0:T(8,128)(2,1)S(1)}, bf16[2,8,32,768]{3,2,1,0:T(8,128)(2,1)S(1)}, u32[]{:S(2)}, u32[]{:S(2)}) collective-permute-start(bf16[2,8,32,768]{3,2,1,0:T(8,128)(2,1)S(1)} %get-tuple-element.39), channel_id=1, source_target_pairs={{0,4},{4,0},{8,12},{12,8},{1,5},{5,1},{9,13},{13,9},{2,6},{6,2},{1... | collective-permute-start | bytes 2359304 | tf_op jit(solution)/shard_map/ppermute | solution.py:44
  98.6 8.0 %hidden.3 = (f32[2,8,32,768]{3,2,1,0:T(8,128)S(1)}, bf16[2,8,32,768]{3,2,1,0:T(8,128)(2,1)S(1)}, bf16[2,2,2,2,2,32,3072]{6,5,4,3,2,1,0:T(8,128)(2,1)}) custom-call(s32[3]{0:T(128)S(1)} %pad_add_fusion.where, bf16[768,3072]{1,0:T(8,128)(2,1)S(1)} %bitcast.26, bf16[2,2,2,2,32,768]{5,4,3,2,1,0:T(8,128)(2,1)} %bitcast.45, ...), custom_call_target="tpu_custom_call" | custom-call | flops 4831838208 | bytes 12582912 | tf_op jit(solution)/shard_map/hidden/pallas_call | solution.py:271
  106.6 4.2 %collective-permute-start.28 = (bf16[2,8,32,768]{3,2,1,0:T(8,128)(2,1)S(1)}, bf16[2,8,32,768]{3,2,1,0:T(8,128)(2,1)S(1)}, u32[]{:S(2)}, u32[]{:S(2)}) collective-permute-start(bf16[2,8,32,768]{3,2,1,0:T(8,128)(2,1)S(1)} %get-tuple-element.46), channel_id=1, source_target_pairs={{0,4},{4,0},{8,12},{12,8},{1,5},{5,1},{9,13},{13,9},{2,6},{6,2},{1... | collective-permute-start | bytes 2359304 | tf_op jit(solution)/shard_map/ppermute | solution.py:44
  110.9 2.5 %collective-permute-start.27 = (bf16[8,32,768]{2,1,0:T(8,128)(2,1)S(1)}, bf16[8,32,768]{2,1,0:T(8,128)(2,1)S(1)}, u32[]{:S(2)}, u32[]{:S(2)}) collective-permute-start(bf16[8,32,768]{2,1,0:T(8,128)(2,1)S(1)} %get-tuple-element.45), channel_id=1, source_target_pairs={{0,8},{4,12},{8,0},{12,4},{1,9},{5,13},{9,1},{13,5},{2,10},{6,14},... | collective-permute-start | bytes 1179656 | tf_op jit(solution)/shard_map/ppermute | solution.py:44
  113.4 6.0 %down.2.refs_0_ = bf16[768,3072]{1,0:T(8,128)(2,1)} custom-call(bf16[768,1024]{1,0:T(8,128)(2,1)S(1)} %get-tuple-element.47.at_a, bf16[768,1024]{1,0:T(8,128)(2,1)S(1)} %get-tuple-element.48.at_b, bf16[1024,3072]{1,0:T(8,128)(2,1)} %bitcast.35, bf16[1024,3072]{1,0:T(8,128)(2,1)} %bitcast.37, f32[8,32,768]{2,1,0:T(8,128)S(1)} %get-tuple-element.44.refs_0_), custom_call_target="tpu_custom_call" | custom-call | flops 3221225472 | bytes 5767168 | tf_op jit(solution)/shard_map/down/pallas_call | solution.py:335
  120.2 9.7 %down.3 = bf16[768,3072]{1,0:T(8,128)(2,1)} custom-call(bf16[768,1024]{1,0:T(8,128)(2,1)S(1)} %get-tuple-element.47.at_a, bf16[768,1024]{1,0:T(8,128)(2,1)S(1)} %get-tuple-element.48.at_b, bf16[1024,3072]{1,0:T(8,128)(2,1)} %bitcast.36, bf16[1024,3072]{1,0:T(8,128)(2,1)} %bitcast.38, bf16[768,3072]{1,0:T(8,128)(2,1)} %down.2.refs_0_), custom_call_target="tpu_custom_call", output_to_operand_aliasing={{}: (4, {})} | custom-call | flops 6442450944 | bytes 11534336 | tf_op jit(solution)/shard_map/down/pallas_call | solution.py:335
  (72 shorter events, 32.2 us)
Async XLA Ops:
  0.6 17.1 %collective-permute-start = (bf16[64,3072]{1,0:T(8,128)(2,1)}, bf16[64,3072]{1,0:T(8,128)(2,1)S(1)}, u32[]{:S(2)}, u32[]{:S(2)}) collective-permute-start(bf16[64,3072]{1,0:T(8,128)(2,1)} %own.1), channel_id=1, source_target_pairs={{0,64},{16,80},{32,96},{48,112},{64,0},{80,16},{96,32},{112,48},{1... | collective-permute-start | bytes 1179656 | tf_op jit(solution)/shard_map/ppermute | solution.py:39
  6.2 9.7 %collective-permute-start.2 = (bf16[128,768]{1,0:T(8,128)(2,1)S(1)}, bf16[128,768]{1,0:T(8,128)(2,1)S(1)}, u32[]{:S(2)}, u32[]{:S(2)}) collective-permute-start(bf16[128,768]{1,0:T(8,128)(2,1)S(1)} %get-tuple-element.29), channel_id=1, source_target_pairs={{0,3},{1,2},{2,1},{3,0},{4,7},{5,6},{6,5},{7,4},{8,11},{9,10},{10,... | collective-permute-start | bytes 589832 | tf_op jit(solution)/shard_map/ppermute | solution.py:40
  19.8 15.6 %collective-permute-start.19 = (bf16[3,128,768]{2,1,0:T(8,128)(2,1)S(1)}, bf16[3,128,768]{2,1,0:T(8,128)(2,1)S(1)}, u32[]{:S(2)}, u32[]{:S(2)}) collective-permute-start(bf16[3,128,768]{2,1,0:T(8,128)(2,1)S(1)} %get-tuple-element.35), channel_id=1, source_target_pairs={{0,4},{4,0},{8,12},{12,8},{1,5},{5,1},{9,13},{13,9},{2,6},{6,2},{1... | collective-permute-start | bytes 1769480 | tf_op jit(solution)/shard_map/ppermute | solution.py:44
  24.8 10.0 %collective-permute-start.16 = (bf16[2,64,768]{2,1,0:T(8,128)(2,1)S(1)}, bf16[2,64,768]{2,1,0:T(8,128)(2,1)S(1)}, u32[]{:S(2)}, u32[]{:S(2)}) collective-permute-start(bf16[2,64,768]{2,1,0:T(8,128)(2,1)S(1)} %get-tuple-element.34.refs_0_), channel_id=1, source_target_pairs={{0,48},{16,32},{32,16},{48,0},{64,112},{80,96},{96,80},{112,64},{1... | collective-permute-start | bytes 589832 | tf_op jit(solution)/shard_map/ppermute | solution.py:39
  28.7 9.8 %collective-permute-start.5 = (bf16[4,64,768]{2,1,0:T(8,128)(2,1)S(1)}, bf16[4,64,768]{2,1,0:T(8,128)(2,1)S(1)}, u32[]{:S(2)}, u32[]{:S(2)}) collective-permute-start(bf16[4,64,768]{2,1,0:T(8,128)(2,1)S(1)} %grow.13.refs_0_), channel_id=1, source_target_pairs={{0,16},{16,0},{32,48},{48,32},{64,80},{80,64},{96,112},{112,96},{1... | collective-permute-start | bytes 1179656 | tf_op jit(solution)/shard_map/ppermute | solution.py:39
  30.6 10.7 %collective-permute-start.9 = (bf16[4,64,768]{2,1,0:T(8,128)(2,1)S(1)}, bf16[4,64,768]{2,1,0:T(8,128)(2,1)S(1)}, u32[]{:S(2)}, u32[]{:S(2)}) collective-permute-start(bf16[4,64,768]{2,1,0:T(8,128)(2,1)S(1)} %grow.16.refs_0_), channel_id=1, source_target_pairs={{0,3},{1,2},{2,1},{3,0},{4,7},{5,6},{6,5},{7,4},{8,11},{9,10},{10,... | collective-permute-start | bytes 1179656 | tf_op jit(solution)/shard_map/ppermute | solution.py:40
  32.8 11.0 %collective-permute-start.13 = (bf16[4,64,768]{2,1,0:T(8,128)(2,1)S(1)}, bf16[4,64,768]{2,1,0:T(8,128)(2,1)S(1)}, u32[]{:S(2)}, u32[]{:S(2)}) collective-permute-start(bf16[4,64,768]{2,1,0:T(8,128)(2,1)S(1)} %grow.19.refs_0_), channel_id=1, source_target_pairs={{0,48},{16,32},{32,16},{48,0},{64,112},{80,96},{96,80},{112,64},{1... | collective-permute-start | bytes 1179656 | tf_op jit(solution)/shard_map/ppermute | solution.py:39
  35.6 27.9 %collective-permute-start.20 = (bf16[2,3,128,768]{3,2,1,0:T(8,128)(2,1)S(1)}, bf16[2,3,128,768]{3,2,1,0:T(8,128)(2,1)S(1)}, u32[]{:S(2)}, u32[]{:S(2)}) collective-permute-start(bf16[2,3,128,768]{3,2,1,0:T(8,128)(2,1)S(1)} %pad_maximum_fusion.near), channel_id=1, source_target_pairs={{0,8},{4,12},{8,0},{12,4},{1,9},{5,13},{9,1},{13,5},{2,10},{6,14},... | collective-permute-start | bytes 3538952 | tf_op jit(solution)/shard_map/ppermute | solution.py:44
  39.0 18.7 %collective-permute-start.6 = (bf16[8,64,768]{2,1,0:T(8,128)(2,1)S(1)}, bf16[8,64,768]{2,1,0:T(8,128)(2,1)S(1)}, u32[]{:S(2)}, u32[]{:S(2)}) collective-permute-start(bf16[8,64,768]{2,1,0:T(8,128)(2,1)S(1)} %grow.14.refs_0_), channel_id=1, source_target_pairs={{0,3},{1,2},{2,1},{3,0},{4,7},{5,6},{6,5},{7,4},{8,11},{9,10},{10,... | collective-permute-start | bytes 2359304 | tf_op jit(solution)/shard_map/ppermute | solution.py:40
  41.8 19.5 %collective-permute-start.10 = (bf16[8,64,768]{2,1,0:T(8,128)(2,1)S(1)}, bf16[8,64,768]{2,1,0:T(8,128)(2,1)S(1)}, u32[]{:S(2)}, u32[]{:S(2)}) collective-permute-start(bf16[8,64,768]{2,1,0:T(8,128)(2,1)S(1)} %grow.17.refs_0_.refs_2_), channel_id=1, source_target_pairs={{0,48},{16,32},{32,16},{48,0},{64,112},{80,96},{96,80},{112,64},{1... | collective-permute-start | bytes 2359304 | tf_op jit(solution)/shard_map/ppermute | solution.py:39
  44.3 18.0 %collective-permute-start.14 = (bf16[8,64,768]{2,1,0:T(8,128)(2,1)S(1)}, bf16[8,64,768]{2,1,0:T(8,128)(2,1)S(1)}, u32[]{:S(2)}, u32[]{:S(2)}) collective-permute-start(bf16[8,64,768]{2,1,0:T(8,128)(2,1)S(1)} %grow.20.refs_0_.refs_4_), channel_id=1, source_target_pairs={{0,1},{1,0},{2,3},{3,2},{4,5},{5,4},{6,7},{7,6},{8,9},{9,8},{10,11... | collective-permute-start | bytes 2359304 | tf_op jit(solution)/shard_map/ppermute | solution.py:40
  44.8 18.6 %collective-permute-start.18 = (bf16[8,64,768]{2,1,0:T(8,128)(2,1)S(1)}, bf16[8,64,768]{2,1,0:T(8,128)(2,1)S(1)}, u32[]{:S(2)}, u32[]{:S(2)}) collective-permute-start(bf16[8,64,768]{2,1,0:T(8,128)(2,1)S(1)} %grow.23.refs_0_.refs_6_), channel_id=1, source_target_pairs={{0,16},{16,0},{32,48},{48,32},{64,80},{80,64},{96,112},{112,96},{1... | collective-permute-start | bytes 2359304 | tf_op jit(solution)/shard_map/ppermute | solution.py:39
  58.6 19.3 %collective-permute-start.7 = (bf16[16,32,768]{2,1,0:T(8,128)(2,1)}, bf16[16,32,768]{2,1,0:T(8,128)(2,1)S(1)}, u32[]{:S(2)}, u32[]{:S(2)}) collective-permute-start(bf16[16,32,768]{2,1,0:T(8,128)(2,1)} %grow.15), channel_id=1, source_target_pairs={{0,48},{16,32},{32,16},{48,0},{64,112},{80,96},{96,80},{112,64},{1... | collective-permute-start | bytes 2359304 | tf_op jit(solution)/shard_map/ppermute | solution.py:39
  62.2 17.1 %collective-permute-start.11 = (bf16[16,32,768]{2,1,0:T(8,128)(2,1)}, bf16[16,32,768]{2,1,0:T(8,128)(2,1)S(1)}, u32[]{:S(2)}, u32[]{:S(2)}) collective-permute-start(bf16[16,32,768]{2,1,0:T(8,128)(2,1)} %grow.18), channel_id=1, source_target_pairs={{0,1},{1,0},{2,3},{3,2},{4,5},{5,4},{6,7},{7,6},{8,9},{9,8},{10,11... | collective-permute-start | bytes 2359304 | tf_op jit(solution)/shard_map/ppermute | solution.py:40
  63.3 17.1 %collective-permute-start.15 = (bf16[16,32,768]{2,1,0:T(8,128)(2,1)}, bf16[16,32,768]{2,1,0:T(8,128)(2,1)S(1)}, u32[]{:S(2)}, u32[]{:S(2)}) collective-permute-start(bf16[16,32,768]{2,1,0:T(8,128)(2,1)} %grow.21), channel_id=1, source_target_pairs={{0,16},{16,0},{32,48},{48,32},{64,80},{80,64},{96,112},{112,96},{1... | collective-permute-start | bytes 2359304 | tf_op jit(solution)/shard_map/ppermute | solution.py:39
  64.3 17.5 %collective-permute-start.21 = (bf16[16,32,768]{2,1,0:T(8,128)(2,1)}, bf16[16,32,768]{2,1,0:T(8,128)(2,1)S(1)}, u32[]{:S(2)}, u32[]{:S(2)}) collective-permute-start(bf16[16,32,768]{2,1,0:T(8,128)(2,1)} %grow.24.refs_0_), channel_id=1, source_target_pairs={{0,3},{1,2},{2,1},{3,0},{4,7},{5,6},{6,5},{7,4},{8,11},{9,10},{10,... | collective-permute-start | bytes 2359304 | tf_op jit(solution)/shard_map/ppermute | solution.py:40
  77.0 19.9 %collective-permute-start.24 = (bf16[16,32,768]{2,1,0:T(8,128)(2,1)}, bf16[16,32,768]{2,1,0:T(8,128)(2,1)S(1)}, u32[]{:S(2)}, u32[]{:S(2)}) collective-permute-start(bf16[16,32,768]{2,1,0:T(8,128)(2,1)} %get-tuple-element.40), channel_id=1, source_target_pairs={{0,1},{1,0},{2,3},{3,2},{4,5},{5,4},{6,7},{7,6},{8,9},{9,8},{10,11... | collective-permute-start | bytes 2359304 | tf_op jit(solution)/shard_map/ppermute | solution.py:40
  77.9 19.8 %collective-permute-start.25 = (bf16[16,32,768]{2,1,0:T(8,128)(2,1)}, bf16[16,32,768]{2,1,0:T(8,128)(2,1)S(1)}, u32[]{:S(2)}, u32[]{:S(2)}) collective-permute-start(bf16[16,32,768]{2,1,0:T(8,128)(2,1)} %get-tuple-element.41), channel_id=1, source_target_pairs={{0,16},{16,0},{32,48},{48,32},{64,80},{80,64},{96,112},{112,96},{1... | collective-permute-start | bytes 2359304 | tf_op jit(solution)/shard_map/ppermute | solution.py:39
  79.4 19.2 %collective-permute-start.26 = (bf16[16,32,768]{2,1,0:T(8,128)(2,1)}, bf16[16,32,768]{2,1,0:T(8,128)(2,1)S(1)}, u32[]{:S(2)}, u32[]{:S(2)}) collective-permute-start(bf16[16,32,768]{2,1,0:T(8,128)(2,1)} %get-tuple-element.42), channel_id=1, source_target_pairs={{0,3},{1,2},{2,1},{3,0},{4,7},{5,6},{6,5},{7,4},{8,11},{9,10},{10,... | collective-permute-start | bytes 2359304 | tf_op jit(solution)/shard_map/ppermute | solution.py:40
  80.4 18.2 %collective-permute-start.23 = (bf16[16,32,768]{2,1,0:T(8,128)(2,1)}, bf16[16,32,768]{2,1,0:T(8,128)(2,1)S(1)}, u32[]{:S(2)}, u32[]{:S(2)}) collective-permute-start(bf16[16,32,768]{2,1,0:T(8,128)(2,1)} %get-tuple-element.37.refs_8_), channel_id=1, source_target_pairs={{0,48},{16,32},{32,16},{48,0},{64,112},{80,96},{96,80},{112,64},{1... | collective-permute-start | bytes 2359304 | tf_op jit(solution)/shard_map/ppermute | solution.py:39
  89.8 20.9 %collective-permute-start.22 = (bf16[2,8,32,768]{3,2,1,0:T(8,128)(2,1)S(1)}, bf16[2,8,32,768]{3,2,1,0:T(8,128)(2,1)S(1)}, u32[]{:S(2)}, u32[]{:S(2)}) collective-permute-start(bf16[2,8,32,768]{3,2,1,0:T(8,128)(2,1)S(1)} %get-tuple-element.39), channel_id=1, source_target_pairs={{0,4},{4,0},{8,12},{12,8},{1,5},{5,1},{9,13},{13,9},{2,6},{6,2},{1... | collective-permute-start | bytes 2359304 | tf_op jit(solution)/shard_map/ppermute | solution.py:44
  106.6 12.9 %collective-permute-start.28 = (bf16[2,8,32,768]{3,2,1,0:T(8,128)(2,1)S(1)}, bf16[2,8,32,768]{3,2,1,0:T(8,128)(2,1)S(1)}, u32[]{:S(2)}, u32[]{:S(2)}) collective-permute-start(bf16[2,8,32,768]{3,2,1,0:T(8,128)(2,1)S(1)} %get-tuple-element.46), channel_id=1, source_target_pairs={{0,4},{4,0},{8,12},{12,8},{1,5},{5,1},{9,13},{13,9},{2,6},{6,2},{1... | collective-permute-start | bytes 2359304 | tf_op jit(solution)/shard_map/ppermute | solution.py:44
  110.9 19.0 %collective-permute-start.27 = (bf16[8,32,768]{2,1,0:T(8,128)(2,1)S(1)}, bf16[8,32,768]{2,1,0:T(8,128)(2,1)S(1)}, u32[]{:S(2)}, u32[]{:S(2)}) collective-permute-start(bf16[8,32,768]{2,1,0:T(8,128)(2,1)S(1)} %get-tuple-element.45), channel_id=1, source_target_pairs={{0,8},{4,12},{8,0},{12,4},{1,9},{5,13},{9,1},{13,5},{2,10},{6,14},... | collective-permute-start | bytes 1179656 | tf_op jit(solution)/shard_map/ppermute | solution.py:44
  119.6 12.0 %collective-permute-start.29 = (bf16[8,32,768]{2,1,0:T(8,128)(2,1)S(1)}, bf16[8,32,768]{2,1,0:T(8,128)(2,1)S(1)}, u32[]{:S(2)}, u32[]{:S(2)}) collective-permute-start(bf16[8,32,768]{2,1,0:T(8,128)(2,1)S(1)} %get-tuple-element.52), channel_id=1, source_target_pairs={{0,8},{4,12},{8,0},{12,4},{1,9},{5,13},{9,1},{13,5},{2,10},{6,14},... | collective-permute-start | bytes 1179656 | tf_op jit(solution)/shard_map/ppermute | solution.py:44
  (10 other events, 87.6 us)

commit v10 on v9

--- a/solution.py
+++ b/solution.py
@@ -231,7 +231,7 @@
 
 def hidden_kernel(n, where, w_far, *refs):
     blocks = refs[: 2 * CHAINS]
-    keep, send, gathered, g, w, hs, sems = refs[-7:]
+    keeps, sends, (gathered, g, w, hs, sems) = refs[-9:-7], refs[-7:-5], refs[-5:]
     row, mine = where[0], where[2]
     per = SHARDS // 4
     weights = pltpu.make_async_copy(w_far, w, sems.at[0])
@@ -258,9 +258,9 @@
             slot = (mine % 8) ^ (mask_of(2 * j) % 8) ^ (off_y * 4)
             here = hs[off_y, j // 4, j // 2 % 2, j % 2, off_x]
             if b:
-                send[a, slot] = here.astype(jnp.bfloat16)
+                sends[a][slot] = here.astype(jnp.bfloat16)
             else:
-                keep[a, slot] = here
+                keeps[a][slot] = here
     for out in outs:
         out.wait()
 
@@ -271,12 +271,14 @@
     return pl.pallas_call(
         functools.partial(hidden_kernel, n),
         out_shape=[
-            jax.ShapeDtypeStruct((2, per, n, HID), jnp.float32),
-            jax.ShapeDtypeStruct((2, per, n, HID), jnp.bfloat16),
+            jax.ShapeDtypeStruct((per, n, HID), jnp.float32),
+            jax.ShapeDtypeStruct((per, n, HID), jnp.float32),
+            jax.ShapeDtypeStruct((per, n, HID), jnp.bfloat16),
+            jax.ShapeDtypeStruct((per, n, HID), jnp.bfloat16),
             pltpu.HBM((2,) * 5 + (n, FEATS), jnp.bfloat16),
         ],
         in_specs=[SMEM] + [ANY] * (1 + 2 * CHAINS + len(after)),
-        out_specs=[VMEM, VMEM, ANY],
+        out_specs=[VMEM] * 4 + [ANY],
         scratch_shapes=[
             pltpu.VMEM((2,) * 5 + (n, FEATS), jnp.bfloat16),
             pltpu.VMEM((HID, FEATS), jnp.bfloat16),
@@ -292,20 +294,15 @@
 
 
 def total_kernel(keep, got, *refs):
-    mine, far = refs[-2:]
-    mine[...] = keep[0] + got[0].astype(jnp.float32)
-    far[...] = (keep[1] + got[1].astype(jnp.float32)).astype(jnp.bfloat16)
+    refs[-1][...] = (keep[...].astype(jnp.float32) + got[...].astype(jnp.float32)).astype(jnp.bfloat16)
 
 
 def total_call(keep, got, after=()):
     return pl.pallas_call(
         total_kernel,
-        out_shape=[
-            jax.ShapeDtypeStruct(keep.shape[1:], jnp.float32),
-            jax.ShapeDtypeStruct(keep.shape[1:], jnp.bfloat16),
-        ],
+        out_shape=jax.ShapeDtypeStruct(keep.shape, jnp.bfloat16),
         in_specs=[VMEM, VMEM] + [ANY] * len(after),
-        out_specs=[VMEM, VMEM],
+        out_specs=VMEM,
         compiler_params=params(8),
         cost_estimate=TINY,
         name="total",
@@ -374,18 +371,19 @@
     own, came = (own_a, own_b), (came_a, came_b)
 
     pairs = [[b for p in range(CHAINS) for b in (own[part][p], came[part][p])] for part in range(2)]
-    keep_a, send_a, g_a = hidden_call(0, where, w_down, pairs[0], after=(in_hbm(own_b[0]),))
-    keep_b, send_b, g_b = hidden_call(1, where, w_down, pairs[1], after=(keep_a,))
-    mine_a, far_a = total_call(keep_a, swap_row(send_a, 1), after=(keep_b,))
-    far_a = swap_row(far_a, 2)
-    grad_down = down_call((act_a, act_b), (g_a, g_b), 0, 2, after=(mine_a,))
-    mine_b, far_b = total_call(keep_b, swap_row(send_b, 1), after=(in_hbm(grad_down),))
-    far_b = swap_row(far_b, 2)
-    grad_down = down_call((act_a, act_b), (g_a, g_b), 2, 4, grad_down)
-    done = (mine_a, far_a), (mine_b, far_b)
+    keep_a, keep_far, send_a, send_far, g_a = hidden_call(0, where, w_down, pairs[0], after=(in_hbm(own_b[0]),))
+    leave_a = total_call(keep_far, swap_row(send_far, 1))
+    keep_b, keep_far, send_b, send_far, g_b = hidden_call(1, where, w_down, pairs[1], after=(leave_a,))
+    far_a, near_a = swap_row(leave_a, 2), swap_row(send_a, 1)
+    near_b = swap_row(send_b, 1)
+    grad_down = down_call((act_a, act_b), (g_a, g_b), 0, 1, after=(far_a,))
+    leave_b = total_call(keep_far, swap_row(send_far, 1), after=(in_hbm(grad_down),))
+    far_b = swap_row(leave_b, 2)
+    grad_down = down_call((act_a, act_b), (g_a, g_b), 1, 5, grad_down)
+    done = (keep_a, near_a, far_a), (keep_b, near_b, far_b)
     parts = [
-        ((mine + far.astype(jnp.float32)) * slope).astype(jnp.bfloat16)
-        for (mine, far), slope in zip(done, (slope_a, slope_b))
+        ((mine + near.astype(jnp.float32) + far.astype(jnp.float32)) * slope).astype(jnp.bfloat16)
+        for (mine, near, far), slope in zip(done, (slope_a, slope_b))
     ]
     grad_pre = jnp.concatenate(parts, 1).reshape(512, HID)
     return (grad_pre, grad_down)

time: 133 us -> 133 us (level)
    ppermute x11, waiting for transfers between devices: 1.35 us -> 5.34 us  [swap(): return lax.ppermute(x, 'depth', [(i, i ^ mask >> 2) for i in range(8)])]
    ppermute x13, waiting for transfers between devices: 25.4 us -> 21.9 us  [swap(): return lax.ppermute(x, 'col', [(i, i ^ mask) for i in range(4)])]
    ppermute x11, starting transfers between devices: 16.2 us -> 14.1 us  [swap(): return lax.ppermute(x, 'depth', [(i, i ^ mask >> 2) for i in range(8)])]
    ppermute x6 -> x8, starting transfers between devices: 17.8 us -> 19.2 us  [swap_row(): return lax.ppermute(x, 'row', [(i, i ^ mask) for i in range(4)])]
  transfers between devices with their start and end apart: 30 -> 32, of which waited for: 12 -> 11; matrix products, arithmetic and copies ran while one was open for 0% -> 0% of each run, Pallas kernels for 39% -> 39%
where the time goes in v10:
time: 133 us
  Pallas kernels  53.1 us (40%)
  starting transfers between devices  47.9 us (36%)
  waiting for transfers between devices  28.6 us (22%)
  other arithmetic  1.46 us (1%)
    ppermute x13, waiting for transfers between devices, swap(): return lax.ppermute(x, 'col', [(i, i ^ mask) for i in range(4)])  21.9 us
    ppermute x8, starting transfers between devices, swap_row(): return lax.ppermute(x, 'row', [(i, i ^ mask) for i in range(4)])  19.2 us
    pallas_call x2, Pallas kernels, hidden_call(): pl.pallas_call(functools.partial(hidden_kernel, n), out_shape=[jax.ShapeD...  16 us
    pallas_call x2, Pallas kernels, down_call(): pl.pallas_call(down_kernel, grid=(count,), out_shape=pltpu.HBM((HID, FEAT...  15.7 us
    ppermute x13, starting transfers between devices, swap(): return lax.ppermute(x, 'col', [(i, i ^ mask) for i in range(4)])  14.6 us
    ppermute x11, starting transfers between devices, swap(): return lax.ppermute(x, 'depth', [(i, i ^ mask >> 2) for i in range(8)])  14.1 us
    pallas_call x1, Pallas kernels, gelu_call(): pl.pallas_call(gelu_kernel, out_shape=[jax.ShapeDtypeStruct((HID, t), jnp...  9.19 us
    pallas_call x13, Pallas kernels, grow_call(): pl.pallas_call(functools.partial(grow_kernel, len(pairs), at, n, len(join...  9.05 us
  transfers between devices with their start and end apart: 32, of which 11 were waited for; matrix products, arithmetic and copies ran while one was open for 0% of the time, Pallas kernels for 39%

profile of v10, /device:TPU:1, one launch (start us, length us, event | category | flops | bytes accessed | tf_op | source)
XLA Modules:
  0.0 132.8 jit_solution(5594963900725898518)
XLA Ops:
  0.6 2.1 %collective-permute-start = (bf16[64,3072]{1,0:T(8,128)(2,1)}, bf16[64,3072]{1,0:T(8,128)(2,1)S(1)}, u32[]{:S(2)}, u32[]{:S(2)}) collective-permute-start(bf16[64,3072]{1,0:T(8,128)(2,1)} %own.1), channel_id=1, source_target_pairs={{0,64},{16,80},{32,96},{48,112},{64,0},{80,16},{96,32},{112,48},{1... | collective-permute-start | bytes 1179656 | tf_op jit(solution)/shard_map/ppermute | solution.py:39
  4.5 1.7 %collective-permute-start.1 = (bf16[128,768]{1,0:T(8,128)(2,1)S(1)}, bf16[128,768]{1,0:T(8,128)(2,1)S(1)}, u32[]{:S(2)}, u32[]{:S(2)}) collective-permute-start(bf16[128,768]{1,0:T(8,128)(2,1)S(1)} %get-tuple-element.28), channel_id=1, source_target_pairs={{0,1},{1,0},{2,3},{3,2},{4,5},{5,4},{6,7},{7,6},{8,9},{9,8},{10,11... | collective-permute-start | bytes 589832 | tf_op jit(solution)/shard_map/ppermute | solution.py:40
  6.2 2.2 %collective-permute-start.2 = (bf16[128,768]{1,0:T(8,128)(2,1)S(1)}, bf16[128,768]{1,0:T(8,128)(2,1)S(1)}, u32[]{:S(2)}, u32[]{:S(2)}) collective-permute-start(bf16[128,768]{1,0:T(8,128)(2,1)S(1)} %get-tuple-element.29), channel_id=1, source_target_pairs={{0,3},{1,2},{2,1},{3,0},{4,7},{5,6},{6,5},{7,4},{8,11},{9,10},{10,... | collective-permute-start | bytes 589832 | tf_op jit(solution)/shard_map/ppermute | solution.py:40
  10.4 5.5 %collective-permute-done.2.refs_1_ = bf16[128,768]{1,0:T(8,128)(2,1)S(1)} collective-permute-done((bf16[128,768]{1,0:T(8,128)(2,1)S(1)}, bf16[128,768]{1,0:T(8,128)(2,1)S(1)}, u32[]{:S(2)}, u32[]{:S(2)}) %collective-permute-start.2) | collective-permute-done | bytes 196640 | tf_op jit(solution)/shard_map/ppermute | solution.py:40
  16.0 1.8 %collective-permute-done.3.refs_2_ = bf16[128,768]{1,0:T(8,128)(2,1)S(1)} collective-permute-done((bf16[128,768]{1,0:T(8,128)(2,1)S(1)}, bf16[128,768]{1,0:T(8,128)(2,1)S(1)}, u32[]{:S(2)}, u32[]{:S(2)}) %collective-permute-start.3) | collective-permute-done | bytes 196640 | tf_op jit(solution)/shard_map/ppermute | solution.py:40
  19.8 1.9 %collective-permute-start.19 = (bf16[3,128,768]{2,1,0:T(8,128)(2,1)S(1)}, bf16[3,128,768]{2,1,0:T(8,128)(2,1)S(1)}, u32[]{:S(2)}, u32[]{:S(2)}) collective-permute-start(bf16[3,128,768]{2,1,0:T(8,128)(2,1)S(1)} %get-tuple-element.35), channel_id=1, source_target_pairs={{0,4},{4,0},{8,12},{12,8},{1,5},{5,1},{9,13},{13,9},{2,6},{6,2},{1... | collective-permute-start | bytes 1769480 | tf_op jit(solution)/shard_map/ppermute | solution.py:44
  21.8 2.7 %collective-permute-start.16 = (bf16[2,64,768]{2,1,0:T(8,128)(2,1)S(1)}, bf16[2,64,768]{2,1,0:T(8,128)(2,1)S(1)}, u32[]{:S(2)}, u32[]{:S(2)}) collective-permute-start(bf16[2,64,768]{2,1,0:T(8,128)(2,1)S(1)} %get-tuple-element.34.refs_0_), channel_id=1, source_target_pairs={{0,48},{16,32},{32,16},{48,0},{64,112},{80,96},{96,80},{112,64},{1... | collective-permute-start | bytes 589832 | tf_op jit(solution)/shard_map/ppermute | solution.py:39
  24.5 1.8 %collective-permute-start.12 = (bf16[2,64,768]{2,1,0:T(8,128)(2,1)S(1)}, bf16[2,64,768]{2,1,0:T(8,128)(2,1)S(1)}, u32[]{:S(2)}, u32[]{:S(2)}) collective-permute-start(bf16[2,64,768]{2,1,0:T(8,128)(2,1)S(1)} %get-tuple-element.33.refs_0_), channel_id=1, source_target_pairs={{0,3},{1,2},{2,1},{3,0},{4,7},{5,6},{6,5},{7,4},{8,11},{9,10},{10,... | collective-permute-start | bytes 589832 | tf_op jit(solution)/shard_map/ppermute | solution.py:40
  26.3 3.3 %collective-permute-done.16.refs_1_ = bf16[2,64,768]{2,1,0:T(8,128)(2,1)S(1)} collective-permute-done((bf16[2,64,768]{2,1,0:T(8,128)(2,1)S(1)}, bf16[2,64,768]{2,1,0:T(8,128)(2,1)S(1)}, u32[]{:S(2)}, u32[]{:S(2)}) %collective-permute-start.16) | collective-permute-done | bytes 196640 | tf_op jit(solution)/shard_map/ppermute | solution.py:39
  34.0 2.3 %collective-permute-start.13 = (bf16[4,64,768]{2,1,0:T(8,128)(2,1)S(1)}, bf16[4,64,768]{2,1,0:T(8,128)(2,1)S(1)}, u32[]{:S(2)}, u32[]{:S(2)}) collective-permute-start(bf16[4,64,768]{2,1,0:T(8,128)(2,1)S(1)} %grow.19.refs_0_), channel_id=1, source_target_pairs={{0,48},{16,32},{32,16},{48,0},{64,112},{80,96},{96,80},{112,64},{1... | collective-permute-start | bytes 1179656 | tf_op jit(solution)/shard_map/ppermute | solution.py:39
  36.5 2.5 %collective-permute-start.20 = (bf16[2,3,128,768]{3,2,1,0:T(8,128)(2,1)S(1)}, bf16[2,3,128,768]{3,2,1,0:T(8,128)(2,1)S(1)}, u32[]{:S(2)}, u32[]{:S(2)}) collective-permute-start(bf16[2,3,128,768]{3,2,1,0:T(8,128)(2,1)S(1)} %pad_maximum_fusion.near), channel_id=1, source_target_pairs={{0,8},{4,12},{8,0},{12,4},{1,9},{5,13},{9,1},{13,5},{2,10},{6,14},... | collective-permute-start | bytes 3538952 | tf_op jit(solution)/shard_map/ppermute | solution.py:44
  43.1 2.4 %collective-permute-start.10 = (bf16[8,64,768]{2,1,0:T(8,128)(2,1)S(1)}, bf16[8,64,768]{2,1,0:T(8,128)(2,1)S(1)}, u32[]{:S(2)}, u32[]{:S(2)}) collective-permute-start(bf16[8,64,768]{2,1,0:T(8,128)(2,1)S(1)} %grow.17.refs_0_.refs_2_), channel_id=1, source_target_pairs={{0,48},{16,32},{32,16},{48,0},{64,112},{80,96},{96,80},{112,64},{1... | collective-permute-start | bytes 2359304 | tf_op jit(solution)/shard_map/ppermute | solution.py:39
  47.2 12.0 %collective-permute-done.6.refs_1_ = bf16[8,64,768]{2,1,0:T(8,128)(2,1)S(1)} collective-permute-done((bf16[8,64,768]{2,1,0:T(8,128)(2,1)S(1)}, bf16[8,64,768]{2,1,0:T(8,128)(2,1)S(1)}, u32[]{:S(2)}, u32[]{:S(2)}) %collective-permute-start.6) | collective-permute-done | bytes 786464 | tf_op jit(solution)/shard_map/ppermute | solution.py:40
  60.2 2.9 %collective-permute-start.7 = (bf16[16,32,768]{2,1,0:T(8,128)(2,1)}, bf16[16,32,768]{2,1,0:T(8,128)(2,1)S(1)}, u32[]{:S(2)}, u32[]{:S(2)}) collective-permute-start(bf16[16,32,768]{2,1,0:T(8,128)(2,1)} %grow.15), channel_id=1, source_target_pairs={{0,48},{16,32},{32,16},{48,0},{64,112},{80,96},{96,80},{112,64},{1... | collective-permute-start | bytes 2359304 | tf_op jit(solution)/shard_map/ppermute | solution.py:39
  67.9 9.2 %gelu.1 = (bf16[768,1024]{1,0:T(8,128)(2,1)S(1)}, bf16[768,1024]{1,0:T(8,128)(2,1)S(1)}, f32[8,32,768]{2,1,0:T(8,128)S(1)}, f32[8,32,768]{2,1,0:T(8,128)S(1)}) custom-call(s32[3]{0:T(128)S(1)} %pad_add_fusion.where, s32[32]{0:T(128)S(1)} %copy-done, bf16[512,3072]{1,0:T(8,128)(2,1)} %pre.3, bf16[2,3,128,768]{3,2,1,0:T(8,128)(2,1)S(1)} %pad_maximum_fusion.near, ...), custom_call_target="tpu_custom_call" | custom-call | flops 1 | bytes 1 | tf_op jit(solution)/shard_map/gelu/pallas_call | solution.py:207
  77.2 1.7 %grow.25 = (bf16[16,32,768]{2,1,0:T(8,128)(2,1)}, bf16[16,32,768]{2,1,0:T(8,128)(2,1)}, bf16[16,32,768]{2,1,0:T(8,128)(2,1)}, bf16[16,32,768]{2,1,0:T(8,128)(2,1)}) custom-call(bf16[8,64,768]{2,1,0:T(8,128)(2,1)S(1)} %grow.14.refs_0_, bf16[8,64,768]{2,1,0:T(8,128)(2,1)S(1)} %collective-permute-done.6.refs_1_, bf16[8,64,768]{2,1,0:T(8,128)(2,1)S(1)} %grow.17.refs_0_.refs_2_, ...), custom_call_target="tpu_custom_call" | custom-call | flops 1 | bytes 1 | tf_op jit(solution)/shard_map/grow/pallas_call | solution.py:137
  83.5 8.0 %hidden.2 = (f32[8,32,768]{2,1,0:T(8,128)S(1)}, f32[8,32,768]{2,1,0:T(8,128)S(1)}, bf16[8,32,768]{2,1,0:T(8,128)(2,1)S(1)}, bf16[8,32,768]{2,1,0:T(8,128)(2,1)S(1)}, bf16[2,2,2,2,2,32,3072]{6,5,4,3,2,1,0:T(8,128)(2,1)}) custom-call(s32[3]{0:T(128)S(1)} %pad_add_fusion.where, bf16[768,3072]{1,0:T(8,128)(2,1)S(1)} %bitcast.26, ...), custom_call_target="tpu_custom_call" | custom-call | flops 4831838208 | bytes 12582912 | tf_op jit(solution)/shard_map/hidden/pallas_call | solution.py:271
  91.5 6.1 %collective-permute-start.23 = (bf16[8,32,768]{2,1,0:T(8,128)(2,1)S(1)}, bf16[8,32,768]{2,1,0:T(8,128)(2,1)S(1)}, u32[]{:S(2)}, u32[]{:S(2)}) collective-permute-start(bf16[8,32,768]{2,1,0:T(8,128)(2,1)S(1)} %get-tuple-element.41), channel_id=1, source_target_pairs={{0,4},{4,0},{8,12},{12,8},{1,5},{5,1},{9,13},{13,9},{2,6},{6,2},{1... | collective-permute-start | bytes 1179656 | tf_op jit(solution)/shard_map/ppermute | solution.py:44
  99.0 2.5 %collective-permute-start.24 = (bf16[8,32,768]{2,1,0:T(8,128)(2,1)S(1)}, bf16[8,32,768]{2,1,0:T(8,128)(2,1)S(1)}, u32[]{:S(2)}, u32[]{:S(2)}) collective-permute-start(bf16[8,32,768]{2,1,0:T(8,128)(2,1)S(1)} %total.2.refs_8_), channel_id=1, source_target_pairs={{0,8},{4,12},{8,0},{12,4},{1,9},{5,13},{9,1},{13,5},{2,10},{6,14},... | collective-permute-start | bytes 1179656 | tf_op jit(solution)/shard_map/ppermute | solution.py:44
  101.5 8.0 %hidden.3 = (f32[8,32,768]{2,1,0:T(8,128)S(1)}, f32[8,32,768]{2,1,0:T(8,128)S(1)}, bf16[8,32,768]{2,1,0:T(8,128)(2,1)S(1)}, bf16[8,32,768]{2,1,0:T(8,128)(2,1)S(1)}, bf16[2,2,2,2,2,32,3072]{6,5,4,3,2,1,0:T(8,128)(2,1)}) custom-call(s32[3]{0:T(128)S(1)} %pad_add_fusion.where, bf16[768,3072]{1,0:T(8,128)(2,1)S(1)} %bitcast.26, ...), custom_call_target="tpu_custom_call" | custom-call | flops 4831838208 | bytes 12582912 | tf_op jit(solution)/shard_map/hidden/pallas_call | solution.py:271
  109.6 3.1 %collective-permute-start.30 = (bf16[8,32,768]{2,1,0:T(8,128)(2,1)S(1)}, bf16[8,32,768]{2,1,0:T(8,128)(2,1)S(1)}, u32[]{:S(2)}, u32[]{:S(2)}) collective-permute-start(bf16[8,32,768]{2,1,0:T(8,128)(2,1)S(1)} %get-tuple-element.48), channel_id=1, source_target_pairs={{0,4},{4,0},{8,12},{12,8},{1,5},{5,1},{9,13},{13,9},{2,6},{6,2},{1... | collective-permute-start | bytes 1179656 | tf_op jit(solution)/shard_map/ppermute | solution.py:44
  113.2 4.2 %down.2.refs_0_ = bf16[768,3072]{1,0:T(8,128)(2,1)} custom-call(bf16[768,1024]{1,0:T(8,128)(2,1)S(1)} %get-tuple-element.49.at_a, bf16[768,1024]{1,0:T(8,128)(2,1)S(1)} %get-tuple-element.50.at_b, bf16[1024,3072]{1,0:T(8,128)(2,1)} %bitcast.35, bf16[1024,3072]{1,0:T(8,128)(2,1)} %bitcast.37, bf16[8,32,768]{2,1,0:T(8,128)(2,1)S(1)} %collective-permute-done.24.refs_0_), custom_call_target="tpu_custom_call" | custom-call | flops 1610612736 | bytes 2883584 | tf_op jit(solution)/shard_map/down/pallas_call | solution.py:332
  117.5 2.5 %collective-permute-start.31 = (bf16[8,32,768]{2,1,0:T(8,128)(2,1)S(1)}, bf16[8,32,768]{2,1,0:T(8,128)(2,1)S(1)}, u32[]{:S(2)}, u32[]{:S(2)}) collective-permute-start(bf16[8,32,768]{2,1,0:T(8,128)(2,1)S(1)} %total.3), channel_id=1, source_target_pairs={{0,8},{4,12},{8,0},{12,4},{1,9},{5,13},{9,1},{13,5},{2,10},{6,14},... | collective-permute-start | bytes 1179656 | tf_op jit(solution)/shard_map/ppermute | solution.py:44
  120.0 11.5 %down.3 = bf16[768,3072]{1,0:T(8,128)(2,1)} custom-call(bf16[768,1024]{1,0:T(8,128)(2,1)S(1)} %get-tuple-element.49.at_a, bf16[768,1024]{1,0:T(8,128)(2,1)S(1)} %get-tuple-element.50.at_b, bf16[1024,3072]{1,0:T(8,128)(2,1)} %bitcast.36, bf16[1024,3072]{1,0:T(8,128)(2,1)} %bitcast.38, bf16[768,3072]{1,0:T(8,128)(2,1)} %down.2.refs_0_), custom_call_target="tpu_custom_call", output_to_operand_aliasing={{}: (4, {})} | custom-call | flops 8053063680 | bytes 14417920 | tf_op jit(solution)/shard_map/down/pallas_call | solution.py:332
  (76 shorter events, 29.7 us)
Async XLA Ops:
  0.6 17.1 %collective-permute-start = (bf16[64,3072]{1,0:T(8,128)(2,1)}, bf16[64,3072]{1,0:T(8,128)(2,1)S(1)}, u32[]{:S(2)}, u32[]{:S(2)}) collective-permute-start(bf16[64,3072]{1,0:T(8,128)(2,1)} %own.1), channel_id=1, source_target_pairs={{0,64},{16,80},{32,96},{48,112},{64,0},{80,16},{96,32},{112,48},{1... | collective-permute-start | bytes 1179656 | tf_op jit(solution)/shard_map/ppermute | solution.py:39
  6.2 9.7 %collective-permute-start.2 = (bf16[128,768]{1,0:T(8,128)(2,1)S(1)}, bf16[128,768]{1,0:T(8,128)(2,1)S(1)}, u32[]{:S(2)}, u32[]{:S(2)}) collective-permute-start(bf16[128,768]{1,0:T(8,128)(2,1)S(1)} %get-tuple-element.29), channel_id=1, source_target_pairs={{0,3},{1,2},{2,1},{3,0},{4,7},{5,6},{6,5},{7,4},{8,11},{9,10},{10,... | collective-permute-start | bytes 589832 | tf_op jit(solution)/shard_map/ppermute | solution.py:40
  19.8 16.5 %collective-permute-start.19 = (bf16[3,128,768]{2,1,0:T(8,128)(2,1)S(1)}, bf16[3,128,768]{2,1,0:T(8,128)(2,1)S(1)}, u32[]{:S(2)}, u32[]{:S(2)}) collective-permute-start(bf16[3,128,768]{2,1,0:T(8,128)(2,1)S(1)} %get-tuple-element.35), channel_id=1, source_target_pairs={{0,4},{4,0},{8,12},{12,8},{1,5},{5,1},{9,13},{13,9},{2,6},{6,2},{1... | collective-permute-start | bytes 1769480 | tf_op jit(solution)/shard_map/ppermute | solution.py:44
  30.0 16.7 %collective-permute-start.17 = (bf16[4,64,768]{2,1,0:T(8,128)(2,1)S(1)}, bf16[4,64,768]{2,1,0:T(8,128)(2,1)S(1)}, u32[]{:S(2)}, u32[]{:S(2)}) collective-permute-start(bf16[4,64,768]{2,1,0:T(8,128)(2,1)S(1)} %grow.22.refs_0_), channel_id=1, source_target_pairs={{0,1},{1,0},{2,3},{3,2},{4,5},{5,4},{6,7},{7,6},{8,9},{9,8},{10,11... | collective-permute-start | bytes 1179656 | tf_op jit(solution)/shard_map/ppermute | solution.py:40
  31.1 9.5 %collective-permute-start.5 = (bf16[4,64,768]{2,1,0:T(8,128)(2,1)S(1)}, bf16[4,64,768]{2,1,0:T(8,128)(2,1)S(1)}, u32[]{:S(2)}, u32[]{:S(2)}) collective-permute-start(bf16[4,64,768]{2,1,0:T(8,128)(2,1)S(1)} %grow.13.refs_0_), channel_id=1, source_target_pairs={{0,16},{16,0},{32,48},{48,32},{64,80},{80,64},{96,112},{112,96},{1... | collective-permute-start | bytes 1179656 | tf_op jit(solution)/shard_map/ppermute | solution.py:39
  31.8 11.0 %collective-permute-start.9 = (bf16[4,64,768]{2,1,0:T(8,128)(2,1)S(1)}, bf16[4,64,768]{2,1,0:T(8,128)(2,1)S(1)}, u32[]{:S(2)}, u32[]{:S(2)}) collective-permute-start(bf16[4,64,768]{2,1,0:T(8,128)(2,1)S(1)} %grow.16.refs_0_), channel_id=1, source_target_pairs={{0,3},{1,2},{2,1},{3,0},{4,7},{5,6},{6,5},{7,4},{8,11},{9,10},{10,... | collective-permute-start | bytes 1179656 | tf_op jit(solution)/shard_map/ppermute | solution.py:40
  34.0 11.5 %collective-permute-start.13 = (bf16[4,64,768]{2,1,0:T(8,128)(2,1)S(1)}, bf16[4,64,768]{2,1,0:T(8,128)(2,1)S(1)}, u32[]{:S(2)}, u32[]{:S(2)}) collective-permute-start(bf16[4,64,768]{2,1,0:T(8,128)(2,1)S(1)} %grow.19.refs_0_), channel_id=1, source_target_pairs={{0,48},{16,32},{32,16},{48,0},{64,112},{80,96},{96,80},{112,64},{1... | collective-permute-start | bytes 1179656 | tf_op jit(solution)/shard_map/ppermute | solution.py:39
  36.5 28.9 %collective-permute-start.20 = (bf16[2,3,128,768]{3,2,1,0:T(8,128)(2,1)S(1)}, bf16[2,3,128,768]{3,2,1,0:T(8,128)(2,1)S(1)}, u32[]{:S(2)}, u32[]{:S(2)}) collective-permute-start(bf16[2,3,128,768]{3,2,1,0:T(8,128)(2,1)S(1)} %pad_maximum_fusion.near), channel_id=1, source_target_pairs={{0,8},{4,12},{8,0},{12,4},{1,9},{5,13},{9,1},{13,5},{2,10},{6,14},... | collective-permute-start | bytes 3538952 | tf_op jit(solution)/shard_map/ppermute | solution.py:44
  41.0 18.2 %collective-permute-start.6 = (bf16[8,64,768]{2,1,0:T(8,128)(2,1)S(1)}, bf16[8,64,768]{2,1,0:T(8,128)(2,1)S(1)}, u32[]{:S(2)}, u32[]{:S(2)}) collective-permute-start(bf16[8,64,768]{2,1,0:T(8,128)(2,1)S(1)} %grow.14.refs_0_), channel_id=1, source_target_pairs={{0,3},{1,2},{2,1},{3,0},{4,7},{5,6},{6,5},{7,4},{8,11},{9,10},{10,... | collective-permute-start | bytes 2359304 | tf_op jit(solution)/shard_map/ppermute | solution.py:40
  43.1 20.0 %collective-permute-start.10 = (bf16[8,64,768]{2,1,0:T(8,128)(2,1)S(1)}, bf16[8,64,768]{2,1,0:T(8,128)(2,1)S(1)}, u32[]{:S(2)}, u32[]{:S(2)}) collective-permute-start(bf16[8,64,768]{2,1,0:T(8,128)(2,1)S(1)} %grow.17.refs_0_.refs_2_), channel_id=1, source_target_pairs={{0,48},{16,32},{32,16},{48,0},{64,112},{80,96},{96,80},{112,64},{1... | collective-permute-start | bytes 2359304 | tf_op jit(solution)/shard_map/ppermute | solution.py:39
  45.9 18.2 %collective-permute-start.14 = (bf16[8,64,768]{2,1,0:T(8,128)(2,1)S(1)}, bf16[8,64,768]{2,1,0:T(8,128)(2,1)S(1)}, u32[]{:S(2)}, u32[]{:S(2)}) collective-permute-start(bf16[8,64,768]{2,1,0:T(8,128)(2,1)S(1)} %grow.20.refs_0_.refs_4_), channel_id=1, source_target_pairs={{0,1},{1,0},{2,3},{3,2},{4,5},{5,4},{6,7},{7,6},{8,9},{9,8},{10,11... | collective-permute-start | bytes 2359304 | tf_op jit(solution)/shard_map/ppermute | solution.py:40
  47.1 18.2 %collective-permute-start.18 = (bf16[8,64,768]{2,1,0:T(8,128)(2,1)S(1)}, bf16[8,64,768]{2,1,0:T(8,128)(2,1)S(1)}, u32[]{:S(2)}, u32[]{:S(2)}) collective-permute-start(bf16[8,64,768]{2,1,0:T(8,128)(2,1)S(1)} %grow.23.refs_0_.refs_6_), channel_id=1, source_target_pairs={{0,16},{16,0},{32,48},{48,32},{64,80},{80,64},{96,112},{112,96},{1... | collective-permute-start | bytes 2359304 | tf_op jit(solution)/shard_map/ppermute | solution.py:39
  60.2 19.4 %collective-permute-start.7 = (bf16[16,32,768]{2,1,0:T(8,128)(2,1)}, bf16[16,32,768]{2,1,0:T(8,128)(2,1)S(1)}, u32[]{:S(2)}, u32[]{:S(2)}) collective-permute-start(bf16[16,32,768]{2,1,0:T(8,128)(2,1)} %grow.15), channel_id=1, source_target_pairs={{0,48},{16,32},{32,16},{48,0},{64,112},{80,96},{96,80},{112,64},{1... | collective-permute-start | bytes 2359304 | tf_op jit(solution)/shard_map/ppermute | solution.py:39
  64.1 16.4 %collective-permute-start.11 = (bf16[16,32,768]{2,1,0:T(8,128)(2,1)}, bf16[16,32,768]{2,1,0:T(8,128)(2,1)S(1)}, u32[]{:S(2)}, u32[]{:S(2)}) collective-permute-start(bf16[16,32,768]{2,1,0:T(8,128)(2,1)} %grow.18), channel_id=1, source_target_pairs={{0,1},{1,0},{2,3},{3,2},{4,5},{5,4},{6,7},{7,6},{8,9},{9,8},{10,11... | collective-permute-start | bytes 2359304 | tf_op jit(solution)/shard_map/ppermute | solution.py:40
  65.2 16.2 %collective-permute-start.15 = (bf16[16,32,768]{2,1,0:T(8,128)(2,1)}, bf16[16,32,768]{2,1,0:T(8,128)(2,1)S(1)}, u32[]{:S(2)}, u32[]{:S(2)}) collective-permute-start(bf16[16,32,768]{2,1,0:T(8,128)(2,1)} %grow.21), channel_id=1, source_target_pairs={{0,16},{16,0},{32,48},{48,32},{64,80},{80,64},{96,112},{112,96},{1... | collective-permute-start | bytes 2359304 | tf_op jit(solution)/shard_map/ppermute | solution.py:39
  66.2 17.2 %collective-permute-start.21 = (bf16[16,32,768]{2,1,0:T(8,128)(2,1)}, bf16[16,32,768]{2,1,0:T(8,128)(2,1)S(1)}, u32[]{:S(2)}, u32[]{:S(2)}) collective-permute-start(bf16[16,32,768]{2,1,0:T(8,128)(2,1)} %grow.24.refs_0_), channel_id=1, source_target_pairs={{0,3},{1,2},{2,1},{3,0},{4,7},{5,6},{6,5},{7,4},{8,11},{9,10},{10,... | collective-permute-start | bytes 2359304 | tf_op jit(solution)/shard_map/ppermute | solution.py:40
  78.9 22.6 %collective-permute-start.25 = (bf16[16,32,768]{2,1,0:T(8,128)(2,1)}, bf16[16,32,768]{2,1,0:T(8,128)(2,1)S(1)}, u32[]{:S(2)}, u32[]{:S(2)}) collective-permute-start(bf16[16,32,768]{2,1,0:T(8,128)(2,1)} %get-tuple-element.37.refs_8_), channel_id=1, source_target_pairs={{0,48},{16,32},{32,16},{48,0},{64,112},{80,96},{96,80},{112,64},{1... | collective-permute-start | bytes 2359304 | tf_op jit(solution)/shard_map/ppermute | solution.py:39
  79.6 21.9 %collective-permute-start.26 = (bf16[16,32,768]{2,1,0:T(8,128)(2,1)}, bf16[16,32,768]{2,1,0:T(8,128)(2,1)S(1)}, u32[]{:S(2)}, u32[]{:S(2)}) collective-permute-start(bf16[16,32,768]{2,1,0:T(8,128)(2,1)} %get-tuple-element.42), channel_id=1, source_target_pairs={{0,1},{1,0},{2,3},{3,2},{4,5},{5,4},{6,7},{7,6},{8,9},{9,8},{10,11... | collective-permute-start | bytes 2359304 | tf_op jit(solution)/shard_map/ppermute | solution.py:40
  80.4 21.1 %collective-permute-start.27 = (bf16[16,32,768]{2,1,0:T(8,128)(2,1)}, bf16[16,32,768]{2,1,0:T(8,128)(2,1)S(1)}, u32[]{:S(2)}, u32[]{:S(2)}) collective-permute-start(bf16[16,32,768]{2,1,0:T(8,128)(2,1)} %get-tuple-element.43), channel_id=1, source_target_pairs={{0,16},{16,0},{32,48},{48,32},{64,80},{80,64},{96,112},{112,96},{1... | collective-permute-start | bytes 2359304 | tf_op jit(solution)/shard_map/ppermute | solution.py:39
  81.3 20.2 %collective-permute-start.28 = (bf16[16,32,768]{2,1,0:T(8,128)(2,1)}, bf16[16,32,768]{2,1,0:T(8,128)(2,1)S(1)}, u32[]{:S(2)}, u32[]{:S(2)}) collective-permute-start(bf16[16,32,768]{2,1,0:T(8,128)(2,1)} %get-tuple-element.44), channel_id=1, source_target_pairs={{0,3},{1,2},{2,1},{3,0},{4,7},{5,6},{6,5},{7,4},{8,11},{9,10},{10,... | collective-permute-start | bytes 2359304 | tf_op jit(solution)/shard_map/ppermute | solution.py:40
  99.0 14.2 %collective-permute-start.24 = (bf16[8,32,768]{2,1,0:T(8,128)(2,1)S(1)}, bf16[8,32,768]{2,1,0:T(8,128)(2,1)S(1)}, u32[]{:S(2)}, u32[]{:S(2)}) collective-permute-start(bf16[8,32,768]{2,1,0:T(8,128)(2,1)S(1)} %total.2.refs_8_), channel_id=1, source_target_pairs={{0,8},{4,12},{8,0},{12,4},{1,9},{5,13},{9,1},{13,5},{2,10},{6,14},... | collective-permute-start | bytes 1179656 | tf_op jit(solution)/shard_map/ppermute | solution.py:44
  112.6 18.9 %collective-permute-start.22 = (bf16[8,32,768]{2,1,0:T(8,128)(2,1)S(1)}, bf16[8,32,768]{2,1,0:T(8,128)(2,1)S(1)}, u32[]{:S(2)}, u32[]{:S(2)}) collective-permute-start(bf16[8,32,768]{2,1,0:T(8,128)(2,1)S(1)} %get-tuple-element.39), channel_id=1, source_target_pairs={{0,4},{4,0},{8,12},{12,8},{1,5},{5,1},{9,13},{13,9},{2,6},{6,2},{1... | collective-permute-start | bytes 1179656 | tf_op jit(solution)/shard_map/ppermute | solution.py:44
  112.7 18.9 %collective-permute-start.29 = (bf16[8,32,768]{2,1,0:T(8,128)(2,1)S(1)}, bf16[8,32,768]{2,1,0:T(8,128)(2,1)S(1)}, u32[]{:S(2)}, u32[]{:S(2)}) collective-permute-start(bf16[8,32,768]{2,1,0:T(8,128)(2,1)S(1)} %get-tuple-element.46), channel_id=1, source_target_pairs={{0,4},{4,0},{8,12},{12,8},{1,5},{5,1},{9,13},{13,9},{2,6},{6,2},{1... | collective-permute-start | bytes 1179656 | tf_op jit(solution)/shard_map/ppermute | solution.py:44
  117.5 14.2 %collective-permute-start.31 = (bf16[8,32,768]{2,1,0:T(8,128)(2,1)S(1)}, bf16[8,32,768]{2,1,0:T(8,128)(2,1)S(1)}, u32[]{:S(2)}, u32[]{:S(2)}) collective-permute-start(bf16[8,32,768]{2,1,0:T(8,128)(2,1)S(1)} %total.3), channel_id=1, source_target_pairs={{0,8},{4,12},{8,0},{12,4},{1,9},{5,13},{9,1},{13,5},{2,10},{6,14},... | collective-permute-start | bytes 1179656 | tf_op jit(solution)/shard_map/ppermute | solution.py:44
  (12 other events, 99.0 us)

commit v11 on v10

--- a/solution.py
+++ b/solution.py
@@ -170,27 +170,24 @@
         c.wait()
 
     def one_shard(s, carry):
-        v = buf[pl.ds(pl.multiple_of((mine ^ table[s]) * ROWS, ROWS), ROWS), :].astype(jnp.float32)
+        shard = mine ^ table[s]
+        v = buf[pl.ds(pl.multiple_of(shard * ROWS, ROWS), ROWS), :].astype(jnp.float32)
         bend = jnp.tanh(gelu_const * (v + 0.044715 * v * v * v))
         a = (0.5 * v * (1.0 + bend)).astype(jnp.bfloat16)
         for part in range(2):
             n, at = PARTS[part], STARTS[part]
             acts[part][pl.ds(pl.multiple_of(s * n, 16), n), :] = a[at : at + n]
+
+        @pl.when(shard // 8 == row)
+        def _():
+            d = 0.5 * (1.0 + bend) + 0.5 * v * (1.0 - bend * bend) * gelu_const * (1.0 + 3.0 * 0.044715 * v * v)
+            for part in range(2):
+                n, at = PARTS[part], STARTS[part]
+                slopes[part][shard % 8] = d[at : at + n]
+
         return carry
 
     lax.fori_loop(0, SHARDS, one_shard, 0)
-
-    def one_slope(s, carry):
-        at_row = pl.multiple_of(row * quarter + s * ROWS, ROWS)
-        v = buf[pl.ds(at_row, ROWS), :].astype(jnp.float32)
-        bend = jnp.tanh(gelu_const * (v + 0.044715 * v * v * v))
-        d = 0.5 * (1.0 + bend) + 0.5 * v * (1.0 - bend * bend) * gelu_const * (1.0 + 3.0 * 0.044715 * v * v)
-        for part in range(2):
-            n, at = PARTS[part], STARTS[part]
-            slopes[part][s] = d[at : at + n]
-        return carry
-
-    lax.fori_loop(0, SHARDS // 4, one_slope, 0)
 
     for part in range(2):
 
@@ -317,7 +314,7 @@
 
 
 def down_call(acts, gathered, first, count, base=None, after=()):
-    wide = 512
+    wide = 768
     tokens = [SHARDS * n for n in PARTS]
     in_specs = [pl.BlockSpec((HID, t), lambda j: (0, 0)) for t in tokens]
     in_specs += [pl.BlockSpec((t, wide), lambda j: (0, j + first)) for t in tokens]
@@ -379,7 +376,7 @@
     grad_down = down_call((act_a, act_b), (g_a, g_b), 0, 1, after=(far_a,))
     leave_b = total_call(keep_far, swap_row(send_far, 1), after=(in_hbm(grad_down),))
     far_b = swap_row(leave_b, 2)
-    grad_down = down_call((act_a, act_b), (g_a, g_b), 1, 5, grad_down)
+    grad_down = down_call((act_a, act_b), (g_a, g_b), 1, 3, grad_down)
     done = (keep_a, near_a, far_a), (keep_b, near_b, far_b)
     parts = [
         ((mine + near.astype(jnp.float32) + far.astype(jnp.float32)) * slope).astype(jnp.bfloat16)

time: 133 us -> 134 us (level)
  no operation moved by 1% of the time
where the time goes in v11:
time: 134 us; the launch traced here: 133 us
  Pallas kernels  53.4 us (40%)
  starting transfers between devices  47.6 us (36%)
  waiting for transfers between devices  29.2 us (22%)
  other arithmetic  1.46 us (1%)
    ppermute x13, waiting for transfers between devices, swap(): return lax.ppermute(x, 'col', [(i, i ^ mask) for i in range(4)])  22.3 us
    ppermute x8, starting transfers between devices, swap_row(): return lax.ppermute(x, 'row', [(i, i ^ mask) for i in range(4)])  19.2 us
    pallas_call x2, Pallas kernels, down_call(): pl.pallas_call(down_kernel, grid=(count,), out_shape=pltpu.HBM((HID, FEAT...  16.3 us
    pallas_call x2, Pallas kernels, hidden_call(): pl.pallas_call(functools.partial(hidden_kernel, n), out_shape=[jax.ShapeD...  16 us
    ppermute x13, starting transfers between devices, swap(): return lax.ppermute(x, 'col', [(i, i ^ mask) for i in range(4)])  14.5 us
    ppermute x11, starting transfers between devices, swap(): return lax.ppermute(x, 'depth', [(i, i ^ mask >> 2) for i in range(8)])  13.9 us
    pallas_call x13, Pallas kernels, grow_call(): pl.pallas_call(functools.partial(grow_kernel, len(pairs), at, n, len(join...  9.05 us
    pallas_call x1, Pallas kernels, gelu_call(): pl.pallas_call(gelu_kernel, out_shape=[jax.ShapeDtypeStruct((HID, t), jnp...  8.9 us
  transfers between devices with their start and end apart: 32, of which 11 were waited for; matrix products, arithmetic and copies ran while one was open for 0% of the time, Pallas kernels for 39%

profile of v11, /device:TPU:1, one launch (start us, length us, event | category | flops | bytes accessed | tf_op | source)
XLA Modules:
  0.0 133.4 jit_solution(15457507257487709667)
XLA Ops:
  0.6 2.1 %collective-permute-start = (bf16[64,3072]{1,0:T(8,128)(2,1)}, bf16[64,3072]{1,0:T(8,128)(2,1)S(1)}, u32[]{:S(2)}, u32[]{:S(2)}) collective-permute-start(bf16[64,3072]{1,0:T(8,128)(2,1)} %own.1), channel_id=1, source_target_pairs={{0,64},{16,80},{32,96},{48,112},{64,0},{80,16},{96,32},{112,48},{1... | collective-permute-start | bytes 1179656 | tf_op jit(solution)/shard_map/ppermute | solution.py:39
  4.5 1.7 %collective-permute-start.1 = (bf16[128,768]{1,0:T(8,128)(2,1)S(1)}, bf16[128,768]{1,0:T(8,128)(2,1)S(1)}, u32[]{:S(2)}, u32[]{:S(2)}) collective-permute-start(bf16[128,768]{1,0:T(8,128)(2,1)S(1)} %get-tuple-element.28), channel_id=1, source_target_pairs={{0,1},{1,0},{2,3},{3,2},{4,5},{5,4},{6,7},{7,6},{8,9},{9,8},{10,11... | collective-permute-start | bytes 589832 | tf_op jit(solution)/shard_map/ppermute | solution.py:40
  6.2 2.2 %collective-permute-start.2 = (bf16[128,768]{1,0:T(8,128)(2,1)S(1)}, bf16[128,768]{1,0:T(8,128)(2,1)S(1)}, u32[]{:S(2)}, u32[]{:S(2)}) collective-permute-start(bf16[128,768]{1,0:T(8,128)(2,1)S(1)} %get-tuple-element.29), channel_id=1, source_target_pairs={{0,3},{1,2},{2,1},{3,0},{4,7},{5,6},{6,5},{7,4},{8,11},{9,10},{10,... | collective-permute-start | bytes 589832 | tf_op jit(solution)/shard_map/ppermute | solution.py:40
  10.4 5.5 %collective-permute-done.2.refs_1_ = bf16[128,768]{1,0:T(8,128)(2,1)S(1)} collective-permute-done((bf16[128,768]{1,0:T(8,128)(2,1)S(1)}, bf16[128,768]{1,0:T(8,128)(2,1)S(1)}, u32[]{:S(2)}, u32[]{:S(2)}) %collective-permute-start.2) | collective-permute-done | bytes 196640 | tf_op jit(solution)/shard_map/ppermute | solution.py:40
  16.0 1.8 %collective-permute-done.3.refs_2_ = bf16[128,768]{1,0:T(8,128)(2,1)S(1)} collective-permute-done((bf16[128,768]{1,0:T(8,128)(2,1)S(1)}, bf16[128,768]{1,0:T(8,128)(2,1)S(1)}, u32[]{:S(2)}, u32[]{:S(2)}) %collective-permute-start.3) | collective-permute-done | bytes 196640 | tf_op jit(solution)/shard_map/ppermute | solution.py:40
  19.8 1.9 %collective-permute-start.19 = (bf16[3,128,768]{2,1,0:T(8,128)(2,1)S(1)}, bf16[3,128,768]{2,1,0:T(8,128)(2,1)S(1)}, u32[]{:S(2)}, u32[]{:S(2)}) collective-permute-start(bf16[3,128,768]{2,1,0:T(8,128)(2,1)S(1)} %get-tuple-element.35), channel_id=1, source_target_pairs={{0,4},{4,0},{8,12},{12,8},{1,5},{5,1},{9,13},{13,9},{2,6},{6,2},{1... | collective-permute-start | bytes 1769480 | tf_op jit(solution)/shard_map/ppermute | solution.py:44
  21.8 2.7 %collective-permute-start.16 = (bf16[2,64,768]{2,1,0:T(8,128)(2,1)S(1)}, bf16[2,64,768]{2,1,0:T(8,128)(2,1)S(1)}, u32[]{:S(2)}, u32[]{:S(2)}) collective-permute-start(bf16[2,64,768]{2,1,0:T(8,128)(2,1)S(1)} %get-tuple-element.34.refs_0_), channel_id=1, source_target_pairs={{0,48},{16,32},{32,16},{48,0},{64,112},{80,96},{96,80},{112,64},{1... | collective-permute-start | bytes 589832 | tf_op jit(solution)/shard_map/ppermute | solution.py:39
  24.5 1.8 %collective-permute-start.12 = (bf16[2,64,768]{2,1,0:T(8,128)(2,1)S(1)}, bf16[2,64,768]{2,1,0:T(8,128)(2,1)S(1)}, u32[]{:S(2)}, u32[]{:S(2)}) collective-permute-start(bf16[2,64,768]{2,1,0:T(8,128)(2,1)S(1)} %get-tuple-element.33.refs_0_), channel_id=1, source_target_pairs={{0,3},{1,2},{2,1},{3,0},{4,7},{5,6},{6,5},{7,4},{8,11},{9,10},{10,... | collective-permute-start | bytes 589832 | tf_op jit(solution)/shard_map/ppermute | solution.py:40
  26.3 3.3 %collective-permute-done.16.refs_1_ = bf16[2,64,768]{2,1,0:T(8,128)(2,1)S(1)} collective-permute-done((bf16[2,64,768]{2,1,0:T(8,128)(2,1)S(1)}, bf16[2,64,768]{2,1,0:T(8,128)(2,1)S(1)}, u32[]{:S(2)}, u32[]{:S(2)}) %collective-permute-start.16) | collective-permute-done | bytes 196640 | tf_op jit(solution)/shard_map/ppermute | solution.py:39
  34.0 2.3 %collective-permute-start.13 = (bf16[4,64,768]{2,1,0:T(8,128)(2,1)S(1)}, bf16[4,64,768]{2,1,0:T(8,128)(2,1)S(1)}, u32[]{:S(2)}, u32[]{:S(2)}) collective-permute-start(bf16[4,64,768]{2,1,0:T(8,128)(2,1)S(1)} %grow.19.refs_0_), channel_id=1, source_target_pairs={{0,48},{16,32},{32,16},{48,0},{64,112},{80,96},{96,80},{112,64},{1... | collective-permute-start | bytes 1179656 | tf_op jit(solution)/shard_map/ppermute | solution.py:39
  36.5 2.5 %collective-permute-start.20 = (bf16[2,3,128,768]{3,2,1,0:T(8,128)(2,1)S(1)}, bf16[2,3,128,768]{3,2,1,0:T(8,128)(2,1)S(1)}, u32[]{:S(2)}, u32[]{:S(2)}) collective-permute-start(bf16[2,3,128,768]{3,2,1,0:T(8,128)(2,1)S(1)} %pad_maximum_fusion.near), channel_id=1, source_target_pairs={{0,8},{4,12},{8,0},{12,4},{1,9},{5,13},{9,1},{13,5},{2,10},{6,14},... | collective-permute-start | bytes 3538952 | tf_op jit(solution)/shard_map/ppermute | solution.py:44
  43.1 2.4 %collective-permute-start.10 = (bf16[8,64,768]{2,1,0:T(8,128)(2,1)S(1)}, bf16[8,64,768]{2,1,0:T(8,128)(2,1)S(1)}, u32[]{:S(2)}, u32[]{:S(2)}) collective-permute-start(bf16[8,64,768]{2,1,0:T(8,128)(2,1)S(1)} %grow.17.refs_0_.refs_2_), channel_id=1, source_target_pairs={{0,48},{16,32},{32,16},{48,0},{64,112},{80,96},{96,80},{112,64},{1... | collective-permute-start | bytes 2359304 | tf_op jit(solution)/shard_map/ppermute | solution.py:39
  47.2 12.0 %collective-permute-done.6.refs_1_ = bf16[8,64,768]{2,1,0:T(8,128)(2,1)S(1)} collective-permute-done((bf16[8,64,768]{2,1,0:T(8,128)(2,1)S(1)}, bf16[8,64,768]{2,1,0:T(8,128)(2,1)S(1)}, u32[]{:S(2)}, u32[]{:S(2)}) %collective-permute-start.6) | collective-permute-done | bytes 786464 | tf_op jit(solution)/shard_map/ppermute | solution.py:40
  60.2 2.9 %collective-permute-start.7 = (bf16[16,32,768]{2,1,0:T(8,128)(2,1)}, bf16[16,32,768]{2,1,0:T(8,128)(2,1)S(1)}, u32[]{:S(2)}, u32[]{:S(2)}) collective-permute-start(bf16[16,32,768]{2,1,0:T(8,128)(2,1)} %grow.15), channel_id=1, source_target_pairs={{0,48},{16,32},{32,16},{48,0},{64,112},{80,96},{96,80},{112,64},{1... | collective-permute-start | bytes 2359304 | tf_op jit(solution)/shard_map/ppermute | solution.py:39
  67.9 8.9 %gelu.1 = (bf16[768,1024]{1,0:T(8,128)(2,1)S(1)}, bf16[768,1024]{1,0:T(8,128)(2,1)S(1)}, f32[8,32,768]{2,1,0:T(8,128)S(1)}, f32[8,32,768]{2,1,0:T(8,128)S(1)}) custom-call(s32[3]{0:T(128)S(1)} %pad_add_fusion.where, s32[32]{0:T(128)S(1)} %copy-done, bf16[512,3072]{1,0:T(8,128)(2,1)} %pre.3, bf16[2,3,128,768]{3,2,1,0:T(8,128)(2,1)S(1)} %pad_maximum_fusion.near, ...), custom_call_target="tpu_custom_call" | custom-call | flops 1 | bytes 1 | tf_op jit(solution)/shard_map/gelu/pallas_call | solution.py:204
  76.9 1.7 %grow.25 = (bf16[16,32,768]{2,1,0:T(8,128)(2,1)}, bf16[16,32,768]{2,1,0:T(8,128)(2,1)}, bf16[16,32,768]{2,1,0:T(8,128)(2,1)}, bf16[16,32,768]{2,1,0:T(8,128)(2,1)}) custom-call(bf16[8,64,768]{2,1,0:T(8,128)(2,1)S(1)} %grow.14.refs_0_, bf16[8,64,768]{2,1,0:T(8,128)(2,1)S(1)} %collective-permute-done.6.refs_1_, bf16[8,64,768]{2,1,0:T(8,128)(2,1)S(1)} %grow.17.refs_0_.refs_2_, ...), custom_call_target="tpu_custom_call" | custom-call | flops 1 | bytes 1 | tf_op jit(solution)/shard_map/grow/pallas_call | solution.py:137
  83.5 8.0 %hidden.2 = (f32[8,32,768]{2,1,0:T(8,128)S(1)}, f32[8,32,768]{2,1,0:T(8,128)S(1)}, bf16[8,32,768]{2,1,0:T(8,128)(2,1)S(1)}, bf16[8,32,768]{2,1,0:T(8,128)(2,1)S(1)}, bf16[2,2,2,2,2,32,3072]{6,5,4,3,2,1,0:T(8,128)(2,1)}) custom-call(s32[3]{0:T(128)S(1)} %pad_add_fusion.where, bf16[768,3072]{1,0:T(8,128)(2,1)S(1)} %bitcast.26, ...), custom_call_target="tpu_custom_call" | custom-call | flops 4831838208 | bytes 12582912 | tf_op jit(solution)/shard_map/hidden/pallas_call | solution.py:268
  91.5 6.1 %collective-permute-start.23 = (bf16[8,32,768]{2,1,0:T(8,128)(2,1)S(1)}, bf16[8,32,768]{2,1,0:T(8,128)(2,1)S(1)}, u32[]{:S(2)}, u32[]{:S(2)}) collective-permute-start(bf16[8,32,768]{2,1,0:T(8,128)(2,1)S(1)} %get-tuple-element.41), channel_id=1, source_target_pairs={{0,4},{4,0},{8,12},{12,8},{1,5},{5,1},{9,13},{13,9},{2,6},{6,2},{1... | collective-permute-start | bytes 1179656 | tf_op jit(solution)/shard_map/ppermute | solution.py:44
  99.0 2.5 %collective-permute-start.24 = (bf16[8,32,768]{2,1,0:T(8,128)(2,1)S(1)}, bf16[8,32,768]{2,1,0:T(8,128)(2,1)S(1)}, u32[]{:S(2)}, u32[]{:S(2)}) collective-permute-start(bf16[8,32,768]{2,1,0:T(8,128)(2,1)S(1)} %total.2.refs_8_), channel_id=1, source_target_pairs={{0,8},{4,12},{8,0},{12,4},{1,9},{5,13},{9,1},{13,5},{2,10},{6,14},... | collective-permute-start | bytes 1179656 | tf_op jit(solution)/shard_map/ppermute | solution.py:44
  101.5 8.0 %hidden.3 = (f32[8,32,768]{2,1,0:T(8,128)S(1)}, f32[8,32,768]{2,1,0:T(8,128)S(1)}, bf16[8,32,768]{2,1,0:T(8,128)(2,1)S(1)}, bf16[8,32,768]{2,1,0:T(8,128)(2,1)S(1)}, bf16[2,2,2,2,2,32,3072]{6,5,4,3,2,1,0:T(8,128)(2,1)}) custom-call(s32[3]{0:T(128)S(1)} %pad_add_fusion.where, bf16[768,3072]{1,0:T(8,128)(2,1)S(1)} %bitcast.26, ...), custom_call_target="tpu_custom_call" | custom-call | flops 4831838208 | bytes 12582912 | tf_op jit(solution)/shard_map/hidden/pallas_call | solution.py:268
  109.6 3.1 %collective-permute-start.30 = (bf16[8,32,768]{2,1,0:T(8,128)(2,1)S(1)}, bf16[8,32,768]{2,1,0:T(8,128)(2,1)S(1)}, u32[]{:S(2)}, u32[]{:S(2)}) collective-permute-start(bf16[8,32,768]{2,1,0:T(8,128)(2,1)S(1)} %get-tuple-element.48), channel_id=1, source_target_pairs={{0,4},{4,0},{8,12},{12,8},{1,5},{5,1},{9,13},{13,9},{2,6},{6,2},{1... | collective-permute-start | bytes 1179656 | tf_op jit(solution)/shard_map/ppermute | solution.py:44
  113.2 5.5 %down.2.refs_0_ = bf16[768,3072]{1,0:T(8,128)(2,1)} custom-call(bf16[768,1024]{1,0:T(8,128)(2,1)S(1)} %get-tuple-element.49.at_a, bf16[768,1024]{1,0:T(8,128)(2,1)S(1)} %get-tuple-element.50.at_b, bf16[1024,3072]{1,0:T(8,128)(2,1)} %bitcast.35, bf16[1024,3072]{1,0:T(8,128)(2,1)} %bitcast.37, bf16[8,32,768]{2,1,0:T(8,128)(2,1)S(1)} %collective-permute-done.24.refs_0_), custom_call_target="tpu_custom_call" | custom-call | flops 2415919104 | bytes 4325376 | tf_op jit(solution)/shard_map/down/pallas_call | solution.py:329
  118.7 2.5 %collective-permute-start.31 = (bf16[8,32,768]{2,1,0:T(8,128)(2,1)S(1)}, bf16[8,32,768]{2,1,0:T(8,128)(2,1)S(1)}, u32[]{:S(2)}, u32[]{:S(2)}) collective-permute-start(bf16[8,32,768]{2,1,0:T(8,128)(2,1)S(1)} %total.3), channel_id=1, source_target_pairs={{0,8},{4,12},{8,0},{12,4},{1,9},{5,13},{9,1},{13,5},{2,10},{6,14},... | collective-permute-start | bytes 1179656 | tf_op jit(solution)/shard_map/ppermute | solution.py:44
  121.3 10.8 %down.3 = bf16[768,3072]{1,0:T(8,128)(2,1)} custom-call(bf16[768,1024]{1,0:T(8,128)(2,1)S(1)} %get-tuple-element.49.at_a, bf16[768,1024]{1,0:T(8,128)(2,1)S(1)} %get-tuple-element.50.at_b, bf16[1024,3072]{1,0:T(8,128)(2,1)} %bitcast.36, bf16[1024,3072]{1,0:T(8,128)(2,1)} %bitcast.38, bf16[768,3072]{1,0:T(8,128)(2,1)} %down.2.refs_0_), custom_call_target="tpu_custom_call", output_to_operand_aliasing={{}: (4, {})} | custom-call | flops 7247757312 | bytes 12976128 | tf_op jit(solution)/shard_map/down/pallas_call | solution.py:329
  (76 shorter events, 30.0 us)
Async XLA Ops:
  0.6 17.1 %collective-permute-start = (bf16[64,3072]{1,0:T(8,128)(2,1)}, bf16[64,3072]{1,0:T(8,128)(2,1)S(1)}, u32[]{:S(2)}, u32[]{:S(2)}) collective-permute-start(bf16[64,3072]{1,0:T(8,128)(2,1)} %own.1), channel_id=1, source_target_pairs={{0,64},{16,80},{32,96},{48,112},{64,0},{80,16},{96,32},{112,48},{1... | collective-permute-start | bytes 1179656 | tf_op jit(solution)/shard_map/ppermute | solution.py:39
  6.2 9.7 %collective-permute-start.2 = (bf16[128,768]{1,0:T(8,128)(2,1)S(1)}, bf16[128,768]{1,0:T(8,128)(2,1)S(1)}, u32[]{:S(2)}, u32[]{:S(2)}) collective-permute-start(bf16[128,768]{1,0:T(8,128)(2,1)S(1)} %get-tuple-element.29), channel_id=1, source_target_pairs={{0,3},{1,2},{2,1},{3,0},{4,7},{5,6},{6,5},{7,4},{8,11},{9,10},{10,... | collective-permute-start | bytes 589832 | tf_op jit(solution)/shard_map/ppermute | solution.py:40
  19.8 16.5 %collective-permute-start.19 = (bf16[3,128,768]{2,1,0:T(8,128)(2,1)S(1)}, bf16[3,128,768]{2,1,0:T(8,128)(2,1)S(1)}, u32[]{:S(2)}, u32[]{:S(2)}) collective-permute-start(bf16[3,128,768]{2,1,0:T(8,128)(2,1)S(1)} %get-tuple-element.35), channel_id=1, source_target_pairs={{0,4},{4,0},{8,12},{12,8},{1,5},{5,1},{9,13},{13,9},{2,6},{6,2},{1... | collective-permute-start | bytes 1769480 | tf_op jit(solution)/shard_map/ppermute | solution.py:44
  30.0 16.7 %collective-permute-start.17 = (bf16[4,64,768]{2,1,0:T(8,128)(2,1)S(1)}, bf16[4,64,768]{2,1,0:T(8,128)(2,1)S(1)}, u32[]{:S(2)}, u32[]{:S(2)}) collective-permute-start(bf16[4,64,768]{2,1,0:T(8,128)(2,1)S(1)} %grow.22.refs_0_), channel_id=1, source_target_pairs={{0,1},{1,0},{2,3},{3,2},{4,5},{5,4},{6,7},{7,6},{8,9},{9,8},{10,11... | collective-permute-start | bytes 1179656 | tf_op jit(solution)/shard_map/ppermute | solution.py:40
  31.1 9.5 %collective-permute-start.5 = (bf16[4,64,768]{2,1,0:T(8,128)(2,1)S(1)}, bf16[4,64,768]{2,1,0:T(8,128)(2,1)S(1)}, u32[]{:S(2)}, u32[]{:S(2)}) collective-permute-start(bf16[4,64,768]{2,1,0:T(8,128)(2,1)S(1)} %grow.13.refs_0_), channel_id=1, source_target_pairs={{0,16},{16,0},{32,48},{48,32},{64,80},{80,64},{96,112},{112,96},{1... | collective-permute-start | bytes 1179656 | tf_op jit(solution)/shard_map/ppermute | solution.py:39
  31.8 11.0 %collective-permute-start.9 = (bf16[4,64,768]{2,1,0:T(8,128)(2,1)S(1)}, bf16[4,64,768]{2,1,0:T(8,128)(2,1)S(1)}, u32[]{:S(2)}, u32[]{:S(2)}) collective-permute-start(bf16[4,64,768]{2,1,0:T(8,128)(2,1)S(1)} %grow.16.refs_0_), channel_id=1, source_target_pairs={{0,3},{1,2},{2,1},{3,0},{4,7},{5,6},{6,5},{7,4},{8,11},{9,10},{10,... | collective-permute-start | bytes 1179656 | tf_op jit(solution)/shard_map/ppermute | solution.py:40
  34.0 11.5 %collective-permute-start.13 = (bf16[4,64,768]{2,1,0:T(8,128)(2,1)S(1)}, bf16[4,64,768]{2,1,0:T(8,128)(2,1)S(1)}, u32[]{:S(2)}, u32[]{:S(2)}) collective-permute-start(bf16[4,64,768]{2,1,0:T(8,128)(2,1)S(1)} %grow.19.refs_0_), channel_id=1, source_target_pairs={{0,48},{16,32},{32,16},{48,0},{64,112},{80,96},{96,80},{112,64},{1... | collective-permute-start | bytes 1179656 | tf_op jit(solution)/shard_map/ppermute | solution.py:39
  36.5 28.9 %collective-permute-start.20 = (bf16[2,3,128,768]{3,2,1,0:T(8,128)(2,1)S(1)}, bf16[2,3,128,768]{3,2,1,0:T(8,128)(2,1)S(1)}, u32[]{:S(2)}, u32[]{:S(2)}) collective-permute-start(bf16[2,3,128,768]{3,2,1,0:T(8,128)(2,1)S(1)} %pad_maximum_fusion.near), channel_id=1, source_target_pairs={{0,8},{4,12},{8,0},{12,4},{1,9},{5,13},{9,1},{13,5},{2,10},{6,14},... | collective-permute-start | bytes 3538952 | tf_op jit(solution)/shard_map/ppermute | solution.py:44
  41.0 18.2 %collective-permute-start.6 = (bf16[8,64,768]{2,1,0:T(8,128)(2,1)S(1)}, bf16[8,64,768]{2,1,0:T(8,128)(2,1)S(1)}, u32[]{:S(2)}, u32[]{:S(2)}) collective-permute-start(bf16[8,64,768]{2,1,0:T(8,128)(2,1)S(1)} %grow.14.refs_0_), channel_id=1, source_target_pairs={{0,3},{1,2},{2,1},{3,0},{4,7},{5,6},{6,5},{7,4},{8,11},{9,10},{10,... | collective-permute-start | bytes 2359304 | tf_op jit(solution)/shard_map/ppermute | solution.py:40
  43.1 20.0 %collective-permute-start.10 = (bf16[8,64,768]{2,1,0:T(8,128)(2,1)S(1)}, bf16[8,64,768]{2,1,0:T(8,128)(2,1)S(1)}, u32[]{:S(2)}, u32[]{:S(2)}) collective-permute-start(bf16[8,64,768]{2,1,0:T(8,128)(2,1)S(1)} %grow.17.refs_0_.refs_2_), channel_id=1, source_target_pairs={{0,48},{16,32},{32,16},{48,0},{64,112},{80,96},{96,80},{112,64},{1... | collective-permute-start | bytes 2359304 | tf_op jit(solution)/shard_map/ppermute | solution.py:39
  45.9 18.2 %collective-permute-start.14 = (bf16[8,64,768]{2,1,0:T(8,128)(2,1)S(1)}, bf16[8,64,768]{2,1,0:T(8,128)(2,1)S(1)}, u32[]{:S(2)}, u32[]{:S(2)}) collective-permute-start(bf16[8,64,768]{2,1,0:T(8,128)(2,1)S(1)} %grow.20.refs_0_.refs_4_), channel_id=1, source_target_pairs={{0,1},{1,0},{2,3},{3,2},{4,5},{5,4},{6,7},{7,6},{8,9},{9,8},{10,11... | collective-permute-start | bytes 2359304 | tf_op jit(solution)/shard_map/ppermute | solution.py:40
  47.1 18.2 %collective-permute-start.18 = (bf16[8,64,768]{2,1,0:T(8,128)(2,1)S(1)}, bf16[8,64,768]{2,1,0:T(8,128)(2,1)S(1)}, u32[]{:S(2)}, u32[]{:S(2)}) collective-permute-start(bf16[8,64,768]{2,1,0:T(8,128)(2,1)S(1)} %grow.23.refs_0_.refs_6_), channel_id=1, source_target_pairs={{0,16},{16,0},{32,48},{48,32},{64,80},{80,64},{96,112},{112,96},{1... | collective-permute-start | bytes 2359304 | tf_op jit(solution)/shard_map/ppermute | solution.py:39
  60.2 19.2 %collective-permute-start.7 = (bf16[16,32,768]{2,1,0:T(8,128)(2,1)}, bf16[16,32,768]{2,1,0:T(8,128)(2,1)S(1)}, u32[]{:S(2)}, u32[]{:S(2)}) collective-permute-start(bf16[16,32,768]{2,1,0:T(8,128)(2,1)} %grow.15), channel_id=1, source_target_pairs={{0,48},{16,32},{32,16},{48,0},{64,112},{80,96},{96,80},{112,64},{1... | collective-permute-start | bytes 2359304 | tf_op jit(solution)/shard_map/ppermute | solution.py:39
  64.1 16.4 %collective-permute-start.11 = (bf16[16,32,768]{2,1,0:T(8,128)(2,1)}, bf16[16,32,768]{2,1,0:T(8,128)(2,1)S(1)}, u32[]{:S(2)}, u32[]{:S(2)}) collective-permute-start(bf16[16,32,768]{2,1,0:T(8,128)(2,1)} %grow.18), channel_id=1, source_target_pairs={{0,1},{1,0},{2,3},{3,2},{4,5},{5,4},{6,7},{7,6},{8,9},{9,8},{10,11... | collective-permute-start | bytes 2359304 | tf_op jit(solution)/shard_map/ppermute | solution.py:40
  65.2 16.2 %collective-permute-start.15 = (bf16[16,32,768]{2,1,0:T(8,128)(2,1)}, bf16[16,32,768]{2,1,0:T(8,128)(2,1)S(1)}, u32[]{:S(2)}, u32[]{:S(2)}) collective-permute-start(bf16[16,32,768]{2,1,0:T(8,128)(2,1)} %grow.21), channel_id=1, source_target_pairs={{0,16},{16,0},{32,48},{48,32},{64,80},{80,64},{96,112},{112,96},{1... | collective-permute-start | bytes 2359304 | tf_op jit(solution)/shard_map/ppermute | solution.py:39
  66.2 17.2 %collective-permute-start.21 = (bf16[16,32,768]{2,1,0:T(8,128)(2,1)}, bf16[16,32,768]{2,1,0:T(8,128)(2,1)S(1)}, u32[]{:S(2)}, u32[]{:S(2)}) collective-permute-start(bf16[16,32,768]{2,1,0:T(8,128)(2,1)} %grow.24.refs_0_), channel_id=1, source_target_pairs={{0,3},{1,2},{2,1},{3,0},{4,7},{5,6},{6,5},{7,4},{8,11},{9,10},{10,... | collective-permute-start | bytes 2359304 | tf_op jit(solution)/shard_map/ppermute | solution.py:40
  78.6 22.9 %collective-permute-start.25 = (bf16[16,32,768]{2,1,0:T(8,128)(2,1)}, bf16[16,32,768]{2,1,0:T(8,128)(2,1)S(1)}, u32[]{:S(2)}, u32[]{:S(2)}) collective-permute-start(bf16[16,32,768]{2,1,0:T(8,128)(2,1)} %get-tuple-element.37.refs_8_), channel_id=1, source_target_pairs={{0,48},{16,32},{32,16},{48,0},{64,112},{80,96},{96,80},{112,64},{1... | collective-permute-start | bytes 2359304 | tf_op jit(solution)/shard_map/ppermute | solution.py:39
  79.3 22.2 %collective-permute-start.26 = (bf16[16,32,768]{2,1,0:T(8,128)(2,1)}, bf16[16,32,768]{2,1,0:T(8,128)(2,1)S(1)}, u32[]{:S(2)}, u32[]{:S(2)}) collective-permute-start(bf16[16,32,768]{2,1,0:T(8,128)(2,1)} %get-tuple-element.42), channel_id=1, source_target_pairs={{0,1},{1,0},{2,3},{3,2},{4,5},{5,4},{6,7},{7,6},{8,9},{9,8},{10,11... | collective-permute-start | bytes 2359304 | tf_op jit(solution)/shard_map/ppermute | solution.py:40
  80.4 21.1 %collective-permute-start.27 = (bf16[16,32,768]{2,1,0:T(8,128)(2,1)}, bf16[16,32,768]{2,1,0:T(8,128)(2,1)S(1)}, u32[]{:S(2)}, u32[]{:S(2)}) collective-permute-start(bf16[16,32,768]{2,1,0:T(8,128)(2,1)} %get-tuple-element.43), channel_id=1, source_target_pairs={{0,16},{16,0},{32,48},{48,32},{64,80},{80,64},{96,112},{112,96},{1... | collective-permute-start | bytes 2359304 | tf_op jit(solution)/shard_map/ppermute | solution.py:39
  81.3 20.2 %collective-permute-start.28 = (bf16[16,32,768]{2,1,0:T(8,128)(2,1)}, bf16[16,32,768]{2,1,0:T(8,128)(2,1)S(1)}, u32[]{:S(2)}, u32[]{:S(2)}) collective-permute-start(bf16[16,32,768]{2,1,0:T(8,128)(2,1)} %get-tuple-element.44), channel_id=1, source_target_pairs={{0,3},{1,2},{2,1},{3,0},{4,7},{5,6},{6,5},{7,4},{8,11},{9,10},{10,... | collective-permute-start | bytes 2359304 | tf_op jit(solution)/shard_map/ppermute | solution.py:40
  99.0 14.2 %collective-permute-start.24 = (bf16[8,32,768]{2,1,0:T(8,128)(2,1)S(1)}, bf16[8,32,768]{2,1,0:T(8,128)(2,1)S(1)}, u32[]{:S(2)}, u32[]{:S(2)}) collective-permute-start(bf16[8,32,768]{2,1,0:T(8,128)(2,1)S(1)} %total.2.refs_8_), channel_id=1, source_target_pairs={{0,8},{4,12},{8,0},{12,4},{1,9},{5,13},{9,1},{13,5},{2,10},{6,14},... | collective-permute-start | bytes 1179656 | tf_op jit(solution)/shard_map/ppermute | solution.py:44
  112.6 19.4 %collective-permute-start.22 = (bf16[8,32,768]{2,1,0:T(8,128)(2,1)S(1)}, bf16[8,32,768]{2,1,0:T(8,128)(2,1)S(1)}, u32[]{:S(2)}, u32[]{:S(2)}) collective-permute-start(bf16[8,32,768]{2,1,0:T(8,128)(2,1)S(1)} %get-tuple-element.39), channel_id=1, source_target_pairs={{0,4},{4,0},{8,12},{12,8},{1,5},{5,1},{9,13},{13,9},{2,6},{6,2},{1... | collective-permute-start | bytes 1179656 | tf_op jit(solution)/shard_map/ppermute | solution.py:44
  112.7 19.5 %collective-permute-start.29 = (bf16[8,32,768]{2,1,0:T(8,128)(2,1)S(1)}, bf16[8,32,768]{2,1,0:T(8,128)(2,1)S(1)}, u32[]{:S(2)}, u32[]{:S(2)}) collective-permute-start(bf16[8,32,768]{2,1,0:T(8,128)(2,1)S(1)} %get-tuple-element.46), channel_id=1, source_target_pairs={{0,4},{4,0},{8,12},{12,8},{1,5},{5,1},{9,13},{13,9},{2,6},{6,2},{1... | collective-permute-start | bytes 1179656 | tf_op jit(solution)/shard_map/ppermute | solution.py:44
  118.7 13.5 %collective-permute-start.31 = (bf16[8,32,768]{2,1,0:T(8,128)(2,1)S(1)}, bf16[8,32,768]{2,1,0:T(8,128)(2,1)S(1)}, u32[]{:S(2)}, u32[]{:S(2)}) collective-permute-start(bf16[8,32,768]{2,1,0:T(8,128)(2,1)S(1)} %total.3), channel_id=1, source_target_pairs={{0,8},{4,12},{8,0},{12,4},{1,9},{5,13},{9,1},{13,5},{2,10},{6,14},... | collective-permute-start | bytes 1179656 | tf_op jit(solution)/shard_map/ppermute | solution.py:44
  (12 other events, 100.3 us)

commit v12 on v11

--- a/solution.py
+++ b/solution.py
@@ -358,7 +358,7 @@
     blocks = [grow_call([pair])[0] for pair in pairs]
     pairs = [(b, swap(b, ORDERS[p][2])) for p, b in enumerate(blocks)]
     own_a = [
-        grow_call([pair], STARTS[0], PARTS[0], after=(far,) if p == CHAINS - 1 else ())[0]
+        grow_call([pair], STARTS[0], PARTS[0], after=(far,) if p == 0 else ())[0]
         for p, pair in enumerate(pairs)
     ]
     came_a = [swap(own_a[p], ORDERS[p][3]) for p in range(CHAINS)]

time: 134 us -> 135 us (level)
    ppermute x11, waiting for transfers between devices: 5.51 us -> 15.2 us  [swap(): return lax.ppermute(x, 'depth', [(i, i ^ mask >> 2) for i in range(8)])]
    ppermute x13, waiting for transfers between devices: 22.3 us -> 13 us  [swap(): return lax.ppermute(x, 'col', [(i, i ^ mask) for i in range(4)])]
where the time goes in v12:
time: 135 us; the launch traced here: 134 us
  Pallas kernels  53.4 us (40%)
  starting transfers between devices  48.3 us (36%)
  waiting for transfers between devices  29.6 us (22%)
  other arithmetic  1.46 us (1%)
    ppermute x8, starting transfers between devices, swap_row(): return lax.ppermute(x, 'row', [(i, i ^ mask) for i in range(4)])  20.4 us
    pallas_call x2, Pallas kernels, down_call(): pl.pallas_call(down_kernel, grid=(count,), out_shape=pltpu.HBM((HID, FEAT...  16.3 us
    pallas_call x2, Pallas kernels, hidden_call(): pl.pallas_call(functools.partial(hidden_kernel, n), out_shape=[jax.ShapeD...  16 us
    ppermute x11, waiting for transfers between devices, swap(): return lax.ppermute(x, 'depth', [(i, i ^ mask >> 2) for i in range(8)])  15.2 us
    ppermute x11, starting transfers between devices, swap(): return lax.ppermute(x, 'depth', [(i, i ^ mask >> 2) for i in range(8)])  14.3 us
    ppermute x13, starting transfers between devices, swap(): return lax.ppermute(x, 'col', [(i, i ^ mask) for i in range(4)])  13.6 us
    ppermute x13, waiting for transfers between devices, swap(): return lax.ppermute(x, 'col', [(i, i ^ mask) for i in range(4)])  13 us
    pallas_call x13, Pallas kernels, grow_call(): pl.pallas_call(functools.partial(grow_kernel, len(pairs), at, n, len(join...  9.05 us
  transfers between devices with their start and end apart: 32, of which 11 were waited for; matrix products, arithmetic and copies ran while one was open for 0% of the time, Pallas kernels for 39%

profile of v12, /device:TPU:1, one launch (start us, length us, event | category | flops | bytes accessed | tf_op | source)
XLA Modules:
  0.0 134.5 jit_solution(5755198236739878024)
XLA Ops:
  0.6 2.1 %collective-permute-start = (bf16[64,3072]{1,0:T(8,128)(2,1)}, bf16[64,3072]{1,0:T(8,128)(2,1)S(1)}, u32[]{:S(2)}, u32[]{:S(2)}) collective-permute-start(bf16[64,3072]{1,0:T(8,128)(2,1)} %own.1), channel_id=1, source_target_pairs={{0,64},{16,80},{32,96},{48,112},{64,0},{80,16},{96,32},{112,48},{1... | collective-permute-start | bytes 1179656 | tf_op jit(solution)/shard_map/ppermute | solution.py:39
  4.5 1.7 %collective-permute-start.1 = (bf16[128,768]{1,0:T(8,128)(2,1)S(1)}, bf16[128,768]{1,0:T(8,128)(2,1)S(1)}, u32[]{:S(2)}, u32[]{:S(2)}) collective-permute-start(bf16[128,768]{1,0:T(8,128)(2,1)S(1)} %get-tuple-element.28), channel_id=1, source_target_pairs={{0,1},{1,0},{2,3},{3,2},{4,5},{5,4},{6,7},{7,6},{8,9},{9,8},{10,11... | collective-permute-start | bytes 589832 | tf_op jit(solution)/shard_map/ppermute | solution.py:40
  6.2 2.2 %collective-permute-start.2 = (bf16[128,768]{1,0:T(8,128)(2,1)S(1)}, bf16[128,768]{1,0:T(8,128)(2,1)S(1)}, u32[]{:S(2)}, u32[]{:S(2)}) collective-permute-start(bf16[128,768]{1,0:T(8,128)(2,1)S(1)} %get-tuple-element.29), channel_id=1, source_target_pairs={{0,3},{1,2},{2,1},{3,0},{4,7},{5,6},{6,5},{7,4},{8,11},{9,10},{10,... | collective-permute-start | bytes 589832 | tf_op jit(solution)/shard_map/ppermute | solution.py:40
  10.4 5.5 %collective-permute-done.2.refs_1_ = bf16[128,768]{1,0:T(8,128)(2,1)S(1)} collective-permute-done((bf16[128,768]{1,0:T(8,128)(2,1)S(1)}, bf16[128,768]{1,0:T(8,128)(2,1)S(1)}, u32[]{:S(2)}, u32[]{:S(2)}) %collective-permute-start.2) | collective-permute-done | bytes 196640 | tf_op jit(solution)/shard_map/ppermute | solution.py:40
  16.0 1.8 %collective-permute-done.3.refs_2_ = bf16[128,768]{1,0:T(8,128)(2,1)S(1)} collective-permute-done((bf16[128,768]{1,0:T(8,128)(2,1)S(1)}, bf16[128,768]{1,0:T(8,128)(2,1)S(1)}, u32[]{:S(2)}, u32[]{:S(2)}) %collective-permute-start.3) | collective-permute-done | bytes 196640 | tf_op jit(solution)/shard_map/ppermute | solution.py:40
  19.8 1.9 %collective-permute-start.7 = (bf16[3,128,768]{2,1,0:T(8,128)(2,1)S(1)}, bf16[3,128,768]{2,1,0:T(8,128)(2,1)S(1)}, u32[]{:S(2)}, u32[]{:S(2)}) collective-permute-start(bf16[3,128,768]{2,1,0:T(8,128)(2,1)S(1)} %get-tuple-element.32), channel_id=1, source_target_pairs={{0,4},{4,0},{8,12},{12,8},{1,5},{5,1},{9,13},{13,9},{2,6},{6,2},{1... | collective-permute-start | bytes 1769480 | tf_op jit(solution)/shard_map/ppermute | solution.py:44
  21.8 2.7 %collective-permute-start.18 = (bf16[2,64,768]{2,1,0:T(8,128)(2,1)S(1)}, bf16[2,64,768]{2,1,0:T(8,128)(2,1)S(1)}, u32[]{:S(2)}, u32[]{:S(2)}) collective-permute-start(bf16[2,64,768]{2,1,0:T(8,128)(2,1)S(1)} %get-tuple-element.35.refs_0_), channel_id=1, source_target_pairs={{0,48},{16,32},{32,16},{48,0},{64,112},{80,96},{96,80},{112,64},{1... | collective-permute-start | bytes 589832 | tf_op jit(solution)/shard_map/ppermute | solution.py:39
  24.5 1.8 %collective-permute-start.14 = (bf16[2,64,768]{2,1,0:T(8,128)(2,1)S(1)}, bf16[2,64,768]{2,1,0:T(8,128)(2,1)S(1)}, u32[]{:S(2)}, u32[]{:S(2)}) collective-permute-start(bf16[2,64,768]{2,1,0:T(8,128)(2,1)S(1)} %get-tuple-element.34.refs_0_), channel_id=1, source_target_pairs={{0,3},{1,2},{2,1},{3,0},{4,7},{5,6},{6,5},{7,4},{8,11},{9,10},{10,... | collective-permute-start | bytes 589832 | tf_op jit(solution)/shard_map/ppermute | solution.py:40
  26.3 3.3 %collective-permute-done.18.refs_1_ = bf16[2,64,768]{2,1,0:T(8,128)(2,1)S(1)} collective-permute-done((bf16[2,64,768]{2,1,0:T(8,128)(2,1)S(1)}, bf16[2,64,768]{2,1,0:T(8,128)(2,1)S(1)}, u32[]{:S(2)}, u32[]{:S(2)}) %collective-permute-start.18) | collective-permute-done | bytes 196640 | tf_op jit(solution)/shard_map/ppermute | solution.py:39
  34.0 2.3 %collective-permute-start.15 = (bf16[4,64,768]{2,1,0:T(8,128)(2,1)S(1)}, bf16[4,64,768]{2,1,0:T(8,128)(2,1)S(1)}, u32[]{:S(2)}, u32[]{:S(2)}) collective-permute-start(bf16[4,64,768]{2,1,0:T(8,128)(2,1)S(1)} %grow.19.refs_0_), channel_id=1, source_target_pairs={{0,48},{16,32},{32,16},{48,0},{64,112},{80,96},{96,80},{112,64},{1... | collective-permute-start | bytes 1179656 | tf_op jit(solution)/shard_map/ppermute | solution.py:39
  36.5 2.5 %collective-permute-start.8 = (bf16[2,3,128,768]{3,2,1,0:T(8,128)(2,1)S(1)}, bf16[2,3,128,768]{3,2,1,0:T(8,128)(2,1)S(1)}, u32[]{:S(2)}, u32[]{:S(2)}) collective-permute-start(bf16[2,3,128,768]{3,2,1,0:T(8,128)(2,1)S(1)} %pad_maximum_fusion.near), channel_id=1, source_target_pairs={{0,8},{4,12},{8,0},{12,4},{1,9},{5,13},{9,1},{13,5},{2,10},{6,14},... | collective-permute-start | bytes 3538952 | tf_op jit(solution)/shard_map/ppermute | solution.py:44
  39.0 3.4 %collective-permute-done.11.refs_1_ = bf16[4,64,768]{2,1,0:T(8,128)(2,1)S(1)} collective-permute-done((bf16[4,64,768]{2,1,0:T(8,128)(2,1)S(1)}, bf16[4,64,768]{2,1,0:T(8,128)(2,1)S(1)}, u32[]{:S(2)}, u32[]{:S(2)}) %collective-permute-start.11) | collective-permute-done | bytes 393248 | tf_op jit(solution)/shard_map/ppermute | solution.py:40
  42.8 2.7 %collective-permute-start.12 = (bf16[8,64,768]{2,1,0:T(8,128)(2,1)S(1)}, bf16[8,64,768]{2,1,0:T(8,128)(2,1)S(1)}, u32[]{:S(2)}, u32[]{:S(2)}) collective-permute-start(bf16[8,64,768]{2,1,0:T(8,128)(2,1)S(1)} %grow.17.refs_0_.refs_2_), channel_id=1, source_target_pairs={{0,48},{16,32},{32,16},{48,0},{64,112},{80,96},{96,80},{112,64},{1... | collective-permute-start | bytes 2359304 | tf_op jit(solution)/shard_map/ppermute | solution.py:39
  49.0 11.9 %collective-permute-done.12.refs_1_.refs_3_ = bf16[8,64,768]{2,1,0:T(8,128)(2,1)S(1)} collective-permute-done((bf16[8,64,768]{2,1,0:T(8,128)(2,1)S(1)}, bf16[8,64,768]{2,1,0:T(8,128)(2,1)S(1)}, u32[]{:S(2)}, u32[]{:S(2)}) %collective-permute-start.12) | collective-permute-done | bytes 786464 | tf_op jit(solution)/shard_map/ppermute | solution.py:39
  67.3 2.0 %collective-permute-start.9 = (bf16[16,32,768]{2,1,0:T(8,128)(2,1)}, bf16[16,32,768]{2,1,0:T(8,128)(2,1)S(1)}, u32[]{:S(2)}, u32[]{:S(2)}) collective-permute-start(bf16[16,32,768]{2,1,0:T(8,128)(2,1)} %grow.15), channel_id=1, source_target_pairs={{0,48},{16,32},{32,16},{48,0},{64,112},{80,96},{96,80},{112,64},{1... | collective-permute-start | bytes 2359304 | tf_op jit(solution)/shard_map/ppermute | solution.py:39
  69.3 8.9 %gelu.1 = (bf16[768,1024]{1,0:T(8,128)(2,1)S(1)}, bf16[768,1024]{1,0:T(8,128)(2,1)S(1)}, f32[8,32,768]{2,1,0:T(8,128)S(1)}, f32[8,32,768]{2,1,0:T(8,128)S(1)}) custom-call(s32[3]{0:T(128)S(1)} %pad_add_fusion.where, s32[32]{0:T(128)S(1)} %copy-done, bf16[512,3072]{1,0:T(8,128)(2,1)} %pre.3, bf16[2,3,128,768]{3,2,1,0:T(8,128)(2,1)S(1)} %pad_maximum_fusion.near, ...), custom_call_target="tpu_custom_call" | custom-call | flops 1 | bytes 1 | tf_op jit(solution)/shard_map/gelu/pallas_call | solution.py:204
  78.2 1.7 %grow.25 = (bf16[16,32,768]{2,1,0:T(8,128)(2,1)}, bf16[16,32,768]{2,1,0:T(8,128)(2,1)}, bf16[16,32,768]{2,1,0:T(8,128)(2,1)}, bf16[16,32,768]{2,1,0:T(8,128)(2,1)}) custom-call(bf16[8,64,768]{2,1,0:T(8,128)(2,1)S(1)} %grow.14.refs_0_, bf16[8,64,768]{2,1,0:T(8,128)(2,1)S(1)} %collective-permute-done.6.refs_1_, bf16[8,64,768]{2,1,0:T(8,128)(2,1)S(1)} %grow.17.refs_0_.refs_2_, ...), custom_call_target="tpu_custom_call" | custom-call | flops 1 | bytes 1 | tf_op jit(solution)/shard_map/grow/pallas_call | solution.py:137
  83.3 8.0 %hidden.2 = (f32[8,32,768]{2,1,0:T(8,128)S(1)}, f32[8,32,768]{2,1,0:T(8,128)S(1)}, bf16[8,32,768]{2,1,0:T(8,128)(2,1)S(1)}, bf16[8,32,768]{2,1,0:T(8,128)(2,1)S(1)}, bf16[2,2,2,2,2,32,3072]{6,5,4,3,2,1,0:T(8,128)(2,1)}) custom-call(s32[3]{0:T(128)S(1)} %pad_add_fusion.where, bf16[768,3072]{1,0:T(8,128)(2,1)S(1)} %bitcast.26, ...), custom_call_target="tpu_custom_call" | custom-call | flops 4831838208 | bytes 12582912 | tf_op jit(solution)/shard_map/hidden/pallas_call | solution.py:268
  91.4 9.6 %collective-permute-start.23 = (bf16[8,32,768]{2,1,0:T(8,128)(2,1)S(1)}, bf16[8,32,768]{2,1,0:T(8,128)(2,1)S(1)}, u32[]{:S(2)}, u32[]{:S(2)}) collective-permute-start(bf16[8,32,768]{2,1,0:T(8,128)(2,1)S(1)} %get-tuple-element.41), channel_id=1, source_target_pairs={{0,4},{4,0},{8,12},{12,8},{1,5},{5,1},{9,13},{13,9},{2,6},{6,2},{1... | collective-permute-start | bytes 1179656 | tf_op jit(solution)/shard_map/ppermute | solution.py:44
  102.4 2.5 %collective-permute-start.24 = (bf16[8,32,768]{2,1,0:T(8,128)(2,1)S(1)}, bf16[8,32,768]{2,1,0:T(8,128)(2,1)S(1)}, u32[]{:S(2)}, u32[]{:S(2)}) collective-permute-start(bf16[8,32,768]{2,1,0:T(8,128)(2,1)S(1)} %total.2.refs_8_), channel_id=1, source_target_pairs={{0,8},{4,12},{8,0},{12,4},{1,9},{5,13},{9,1},{13,5},{2,10},{6,14},... | collective-permute-start | bytes 1179656 | tf_op jit(solution)/shard_map/ppermute | solution.py:44
  104.9 8.0 %hidden.3 = (f32[8,32,768]{2,1,0:T(8,128)S(1)}, f32[8,32,768]{2,1,0:T(8,128)S(1)}, bf16[8,32,768]{2,1,0:T(8,128)(2,1)S(1)}, bf16[8,32,768]{2,1,0:T(8,128)(2,1)S(1)}, bf16[2,2,2,2,2,32,3072]{6,5,4,3,2,1,0:T(8,128)(2,1)}) custom-call(s32[3]{0:T(128)S(1)} %pad_add_fusion.where, bf16[768,3072]{1,0:T(8,128)(2,1)S(1)} %bitcast.26, ...), custom_call_target="tpu_custom_call" | custom-call | flops 4831838208 | bytes 12582912 | tf_op jit(solution)/shard_map/hidden/pallas_call | solution.py:268
  114.3 5.5 %down.2.refs_0_ = bf16[768,3072]{1,0:T(8,128)(2,1)} custom-call(bf16[768,1024]{1,0:T(8,128)(2,1)S(1)} %get-tuple-element.49.at_a, bf16[768,1024]{1,0:T(8,128)(2,1)S(1)} %get-tuple-element.50.at_b, bf16[1024,3072]{1,0:T(8,128)(2,1)} %bitcast.35, bf16[1024,3072]{1,0:T(8,128)(2,1)} %bitcast.37, bf16[8,32,768]{2,1,0:T(8,128)(2,1)S(1)} %collective-permute-done.24.refs_0_), custom_call_target="tpu_custom_call" | custom-call | flops 2415919104 | bytes 4325376 | tf_op jit(solution)/shard_map/down/pallas_call | solution.py:329
  119.9 2.5 %collective-permute-start.31 = (bf16[8,32,768]{2,1,0:T(8,128)(2,1)S(1)}, bf16[8,32,768]{2,1,0:T(8,128)(2,1)S(1)}, u32[]{:S(2)}, u32[]{:S(2)}) collective-permute-start(bf16[8,32,768]{2,1,0:T(8,128)(2,1)S(1)} %total.3), channel_id=1, source_target_pairs={{0,8},{4,12},{8,0},{12,4},{1,9},{5,13},{9,1},{13,5},{2,10},{6,14},... | collective-permute-start | bytes 1179656 | tf_op jit(solution)/shard_map/ppermute | solution.py:44
  122.4 10.8 %down.3 = bf16[768,3072]{1,0:T(8,128)(2,1)} custom-call(bf16[768,1024]{1,0:T(8,128)(2,1)S(1)} %get-tuple-element.49.at_a, bf16[768,1024]{1,0:T(8,128)(2,1)S(1)} %get-tuple-element.50.at_b, bf16[1024,3072]{1,0:T(8,128)(2,1)} %bitcast.36, bf16[1024,3072]{1,0:T(8,128)(2,1)} %bitcast.38, bf16[768,3072]{1,0:T(8,128)(2,1)} %down.2.refs_0_), custom_call_target="tpu_custom_call", output_to_operand_aliasing={{}: (4, {})} | custom-call | flops 7247757312 | bytes 12976128 | tf_op jit(solution)/shard_map/down/pallas_call | solution.py:329
  (76 shorter events, 28.0 us)
Async XLA Ops:
  0.6 17.1 %collective-permute-start = (bf16[64,3072]{1,0:T(8,128)(2,1)}, bf16[64,3072]{1,0:T(8,128)(2,1)S(1)}, u32[]{:S(2)}, u32[]{:S(2)}) collective-permute-start(bf16[64,3072]{1,0:T(8,128)(2,1)} %own.1), channel_id=1, source_target_pairs={{0,64},{16,80},{32,96},{48,112},{64,0},{80,16},{96,32},{112,48},{1... | collective-permute-start | bytes 1179656 | tf_op jit(solution)/shard_map/ppermute | solution.py:39
  19.8 16.5 %collective-permute-start.7 = (bf16[3,128,768]{2,1,0:T(8,128)(2,1)S(1)}, bf16[3,128,768]{2,1,0:T(8,128)(2,1)S(1)}, u32[]{:S(2)}, u32[]{:S(2)}) collective-permute-start(bf16[3,128,768]{2,1,0:T(8,128)(2,1)S(1)} %get-tuple-element.32), channel_id=1, source_target_pairs={{0,4},{4,0},{8,12},{12,8},{1,5},{5,1},{9,13},{13,9},{2,6},{6,2},{1... | collective-permute-start | bytes 1769480 | tf_op jit(solution)/shard_map/ppermute | solution.py:44
  30.0 15.9 %collective-permute-start.19 = (bf16[4,64,768]{2,1,0:T(8,128)(2,1)S(1)}, bf16[4,64,768]{2,1,0:T(8,128)(2,1)S(1)}, u32[]{:S(2)}, u32[]{:S(2)}) collective-permute-start(bf16[4,64,768]{2,1,0:T(8,128)(2,1)S(1)} %grow.22.refs_0_), channel_id=1, source_target_pairs={{0,1},{1,0},{2,3},{3,2},{4,5},{5,4},{6,7},{7,6},{8,9},{9,8},{10,11... | collective-permute-start | bytes 1179656 | tf_op jit(solution)/shard_map/ppermute | solution.py:40
  31.1 15.8 %collective-permute-start.5 = (bf16[4,64,768]{2,1,0:T(8,128)(2,1)S(1)}, bf16[4,64,768]{2,1,0:T(8,128)(2,1)S(1)}, u32[]{:S(2)}, u32[]{:S(2)}) collective-permute-start(bf16[4,64,768]{2,1,0:T(8,128)(2,1)S(1)} %grow.13.refs_0_), channel_id=1, source_target_pairs={{0,16},{16,0},{32,48},{48,32},{64,80},{80,64},{96,112},{112,96},{1... | collective-permute-start | bytes 1179656 | tf_op jit(solution)/shard_map/ppermute | solution.py:39
  31.8 10.6 %collective-permute-start.11 = (bf16[4,64,768]{2,1,0:T(8,128)(2,1)S(1)}, bf16[4,64,768]{2,1,0:T(8,128)(2,1)S(1)}, u32[]{:S(2)}, u32[]{:S(2)}) collective-permute-start(bf16[4,64,768]{2,1,0:T(8,128)(2,1)S(1)} %grow.16.refs_0_), channel_id=1, source_target_pairs={{0,3},{1,2},{2,1},{3,0},{4,7},{5,6},{6,5},{7,4},{8,11},{9,10},{10,... | collective-permute-start | bytes 1179656 | tf_op jit(solution)/shard_map/ppermute | solution.py:40
  34.0 11.5 %collective-permute-start.15 = (bf16[4,64,768]{2,1,0:T(8,128)(2,1)S(1)}, bf16[4,64,768]{2,1,0:T(8,128)(2,1)S(1)}, u32[]{:S(2)}, u32[]{:S(2)}) collective-permute-start(bf16[4,64,768]{2,1,0:T(8,128)(2,1)S(1)} %grow.19.refs_0_), channel_id=1, source_target_pairs={{0,48},{16,32},{32,16},{48,0},{64,112},{80,96},{96,80},{112,64},{1... | collective-permute-start | bytes 1179656 | tf_op jit(solution)/shard_map/ppermute | solution.py:39
  36.5 29.9 %collective-permute-start.8 = (bf16[2,3,128,768]{3,2,1,0:T(8,128)(2,1)S(1)}, bf16[2,3,128,768]{3,2,1,0:T(8,128)(2,1)S(1)}, u32[]{:S(2)}, u32[]{:S(2)}) collective-permute-start(bf16[2,3,128,768]{3,2,1,0:T(8,128)(2,1)S(1)} %pad_maximum_fusion.near), channel_id=1, source_target_pairs={{0,8},{4,12},{8,0},{12,4},{1,9},{5,13},{9,1},{13,5},{2,10},{6,14},... | collective-permute-start | bytes 3538952 | tf_op jit(solution)/shard_map/ppermute | solution.py:44
  42.8 18.1 %collective-permute-start.12 = (bf16[8,64,768]{2,1,0:T(8,128)(2,1)S(1)}, bf16[8,64,768]{2,1,0:T(8,128)(2,1)S(1)}, u32[]{:S(2)}, u32[]{:S(2)}) collective-permute-start(bf16[8,64,768]{2,1,0:T(8,128)(2,1)S(1)} %grow.17.refs_0_.refs_2_), channel_id=1, source_target_pairs={{0,48},{16,32},{32,16},{48,0},{64,112},{80,96},{96,80},{112,64},{1... | collective-permute-start | bytes 2359304 | tf_op jit(solution)/shard_map/ppermute | solution.py:39
  45.9 17.1 %collective-permute-start.16 = (bf16[8,64,768]{2,1,0:T(8,128)(2,1)S(1)}, bf16[8,64,768]{2,1,0:T(8,128)(2,1)S(1)}, u32[]{:S(2)}, u32[]{:S(2)}) collective-permute-start(bf16[8,64,768]{2,1,0:T(8,128)(2,1)S(1)} %grow.20.refs_0_.refs_4_), channel_id=1, source_target_pairs={{0,1},{1,0},{2,3},{3,2},{4,5},{5,4},{6,7},{7,6},{8,9},{9,8},{10,11... | collective-permute-start | bytes 2359304 | tf_op jit(solution)/shard_map/ppermute | solution.py:40
  46.4 17.9 %collective-permute-start.20 = (bf16[8,64,768]{2,1,0:T(8,128)(2,1)S(1)}, bf16[8,64,768]{2,1,0:T(8,128)(2,1)S(1)}, u32[]{:S(2)}, u32[]{:S(2)}) collective-permute-start(bf16[8,64,768]{2,1,0:T(8,128)(2,1)S(1)} %grow.23.refs_0_.refs_6_), channel_id=1, source_target_pairs={{0,16},{16,0},{32,48},{48,32},{64,80},{80,64},{96,112},{112,96},{1... | collective-permute-start | bytes 2359304 | tf_op jit(solution)/shard_map/ppermute | solution.py:39
  47.4 19.0 %collective-permute-start.6 = (bf16[8,64,768]{2,1,0:T(8,128)(2,1)S(1)}, bf16[8,64,768]{2,1,0:T(8,128)(2,1)S(1)}, u32[]{:S(2)}, u32[]{:S(2)}) collective-permute-start(bf16[8,64,768]{2,1,0:T(8,128)(2,1)S(1)} %grow.14.refs_0_), channel_id=1, source_target_pairs={{0,3},{1,2},{2,1},{3,0},{4,7},{5,6},{6,5},{7,4},{8,11},{9,10},{10,... | collective-permute-start | bytes 2359304 | tf_op jit(solution)/shard_map/ppermute | solution.py:40
  61.9 18.9 %collective-permute-start.13 = (bf16[16,32,768]{2,1,0:T(8,128)(2,1)}, bf16[16,32,768]{2,1,0:T(8,128)(2,1)S(1)}, u32[]{:S(2)}, u32[]{:S(2)}) collective-permute-start(bf16[16,32,768]{2,1,0:T(8,128)(2,1)} %grow.18), channel_id=1, source_target_pairs={{0,1},{1,0},{2,3},{3,2},{4,5},{5,4},{6,7},{7,6},{8,9},{9,8},{10,11... | collective-permute-start | bytes 2359304 | tf_op jit(solution)/shard_map/ppermute | solution.py:40
  63.9 17.3 %collective-permute-start.17 = (bf16[16,32,768]{2,1,0:T(8,128)(2,1)}, bf16[16,32,768]{2,1,0:T(8,128)(2,1)S(1)}, u32[]{:S(2)}, u32[]{:S(2)}) collective-permute-start(bf16[16,32,768]{2,1,0:T(8,128)(2,1)} %grow.21), channel_id=1, source_target_pairs={{0,16},{16,0},{32,48},{48,32},{64,80},{80,64},{96,112},{112,96},{1... | collective-permute-start | bytes 2359304 | tf_op jit(solution)/shard_map/ppermute | solution.py:39
  65.2 16.7 %collective-permute-start.21 = (bf16[16,32,768]{2,1,0:T(8,128)(2,1)}, bf16[16,32,768]{2,1,0:T(8,128)(2,1)S(1)}, u32[]{:S(2)}, u32[]{:S(2)}) collective-permute-start(bf16[16,32,768]{2,1,0:T(8,128)(2,1)} %grow.24.refs_0_), channel_id=1, source_target_pairs={{0,3},{1,2},{2,1},{3,0},{4,7},{5,6},{6,5},{7,4},{8,11},{9,10},{10,... | collective-permute-start | bytes 2359304 | tf_op jit(solution)/shard_map/ppermute | solution.py:40
  67.3 16.0 %collective-permute-start.9 = (bf16[16,32,768]{2,1,0:T(8,128)(2,1)}, bf16[16,32,768]{2,1,0:T(8,128)(2,1)S(1)}, u32[]{:S(2)}, u32[]{:S(2)}) collective-permute-start(bf16[16,32,768]{2,1,0:T(8,128)(2,1)} %grow.15), channel_id=1, source_target_pairs={{0,48},{16,32},{32,16},{48,0},{64,112},{80,96},{96,80},{112,64},{1... | collective-permute-start | bytes 2359304 | tf_op jit(solution)/shard_map/ppermute | solution.py:39
  80.0 24.9 %collective-permute-start.25 = (bf16[16,32,768]{2,1,0:T(8,128)(2,1)}, bf16[16,32,768]{2,1,0:T(8,128)(2,1)S(1)}, u32[]{:S(2)}, u32[]{:S(2)}) collective-permute-start(bf16[16,32,768]{2,1,0:T(8,128)(2,1)} %get-tuple-element.37.refs_8_), channel_id=1, source_target_pairs={{0,48},{16,32},{32,16},{48,0},{64,112},{80,96},{96,80},{112,64},{1... | collective-permute-start | bytes 2359304 | tf_op jit(solution)/shard_map/ppermute | solution.py:39
  80.8 24.1 %collective-permute-start.26 = (bf16[16,32,768]{2,1,0:T(8,128)(2,1)}, bf16[16,32,768]{2,1,0:T(8,128)(2,1)S(1)}, u32[]{:S(2)}, u32[]{:S(2)}) collective-permute-start(bf16[16,32,768]{2,1,0:T(8,128)(2,1)} %get-tuple-element.42), channel_id=1, source_target_pairs={{0,1},{1,0},{2,3},{3,2},{4,5},{5,4},{6,7},{7,6},{8,9},{9,8},{10,11... | collective-permute-start | bytes 2359304 | tf_op jit(solution)/shard_map/ppermute | solution.py:40
  81.2 23.7 %collective-permute-start.27 = (bf16[16,32,768]{2,1,0:T(8,128)(2,1)}, bf16[16,32,768]{2,1,0:T(8,128)(2,1)S(1)}, u32[]{:S(2)}, u32[]{:S(2)}) collective-permute-start(bf16[16,32,768]{2,1,0:T(8,128)(2,1)} %get-tuple-element.43), channel_id=1, source_target_pairs={{0,16},{16,0},{32,48},{48,32},{64,80},{80,64},{96,112},{112,96},{1... | collective-permute-start | bytes 2359304 | tf_op jit(solution)/shard_map/ppermute | solution.py:39
  81.9 23.0 %collective-permute-start.28 = (bf16[16,32,768]{2,1,0:T(8,128)(2,1)}, bf16[16,32,768]{2,1,0:T(8,128)(2,1)S(1)}, u32[]{:S(2)}, u32[]{:S(2)}) collective-permute-start(bf16[16,32,768]{2,1,0:T(8,128)(2,1)} %get-tuple-element.44), channel_id=1, source_target_pairs={{0,3},{1,2},{2,1},{3,0},{4,7},{5,6},{6,5},{7,4},{8,11},{9,10},{10,... | collective-permute-start | bytes 2359304 | tf_op jit(solution)/shard_map/ppermute | solution.py:40
  91.4 10.9 %collective-permute-start.23 = (bf16[8,32,768]{2,1,0:T(8,128)(2,1)S(1)}, bf16[8,32,768]{2,1,0:T(8,128)(2,1)S(1)}, u32[]{:S(2)}, u32[]{:S(2)}) collective-permute-start(bf16[8,32,768]{2,1,0:T(8,128)(2,1)S(1)} %get-tuple-element.41), channel_id=1, source_target_pairs={{0,4},{4,0},{8,12},{12,8},{1,5},{5,1},{9,13},{13,9},{2,6},{6,2},{1... | collective-permute-start | bytes 1179656 | tf_op jit(solution)/shard_map/ppermute | solution.py:44
  102.4 11.9 %collective-permute-start.24 = (bf16[8,32,768]{2,1,0:T(8,128)(2,1)S(1)}, bf16[8,32,768]{2,1,0:T(8,128)(2,1)S(1)}, u32[]{:S(2)}, u32[]{:S(2)}) collective-permute-start(bf16[8,32,768]{2,1,0:T(8,128)(2,1)S(1)} %total.2.refs_8_), channel_id=1, source_target_pairs={{0,8},{4,12},{8,0},{12,4},{1,9},{5,13},{9,1},{13,5},{2,10},{6,14},... | collective-permute-start | bytes 1179656 | tf_op jit(solution)/shard_map/ppermute | solution.py:44
  113.7 19.4 %collective-permute-start.22 = (bf16[8,32,768]{2,1,0:T(8,128)(2,1)S(1)}, bf16[8,32,768]{2,1,0:T(8,128)(2,1)S(1)}, u32[]{:S(2)}, u32[]{:S(2)}) collective-permute-start(bf16[8,32,768]{2,1,0:T(8,128)(2,1)S(1)} %get-tuple-element.39), channel_id=1, source_target_pairs={{0,4},{4,0},{8,12},{12,8},{1,5},{5,1},{9,13},{13,9},{2,6},{6,2},{1... | collective-permute-start | bytes 1179656 | tf_op jit(solution)/shard_map/ppermute | solution.py:44
  113.8 19.5 %collective-permute-start.29 = (bf16[8,32,768]{2,1,0:T(8,128)(2,1)S(1)}, bf16[8,32,768]{2,1,0:T(8,128)(2,1)S(1)}, u32[]{:S(2)}, u32[]{:S(2)}) collective-permute-start(bf16[8,32,768]{2,1,0:T(8,128)(2,1)S(1)} %get-tuple-element.46), channel_id=1, source_target_pairs={{0,4},{4,0},{8,12},{12,8},{1,5},{5,1},{9,13},{13,9},{2,6},{6,2},{1... | collective-permute-start | bytes 1179656 | tf_op jit(solution)/shard_map/ppermute | solution.py:44
  119.9 13.5 %collective-permute-start.31 = (bf16[8,32,768]{2,1,0:T(8,128)(2,1)S(1)}, bf16[8,32,768]{2,1,0:T(8,128)(2,1)S(1)}, u32[]{:S(2)}, u32[]{:S(2)}) collective-permute-start(bf16[8,32,768]{2,1,0:T(8,128)(2,1)S(1)} %total.3), channel_id=1, source_target_pairs={{0,8},{4,12},{8,0},{12,4},{1,9},{5,13},{9,1},{13,5},{2,10},{6,14},... | collective-permute-start | bytes 1179656 | tf_op jit(solution)/shard_map/ppermute | solution.py:44
  (12 other events, 99.2 us)
